TPU v7x, 32 devices: a whole 2x2x4 slice. The times are simulated.
32 devices in a mesh: dp: 8 (over z, y), row: 2 (over x), col: 2 (over core).
Axes of the slice: x: 2, y: 2, z: 4, core: 2. Of those that a mesh axis runs over, the one named last changes fastest.
Arguments:
- block_in: bfloat16 [12288, 1600], P(('dp', 'col'), 'row'), may hold values from -6 to 6
- out_grad: bfloat16 [12288, 1600], P(('dp', 'col'), 'row'), may hold values from -6 to 6
- seq_lengths: int32 [8, 5], P('dp'), may hold values from 1 to 768, 1536 in all within a row
- ln1_gain: bfloat16 [1600], P('row'), may hold values from 0.5 to 1.5
- ln1_bias: bfloat16 [1600], P('row'), may hold values from -3 to 3
- qkv_weight: bfloat16 [3, 1600, 1600], P(None, 'row', 'col'), may hold values from -1 to 1
- qv_bias: bfloat16 [2, 1600], P(None, 'col'), may hold values from -3 to 3
- out_weight: bfloat16 [1600, 1600], P('col', 'row'), may hold values from -1.25 to 1.25
- out_bias: bfloat16 [1600], P('row'), may hold values from -3 to 3
- ln2_gain: bfloat16 [1600], P('row'), may hold values from 0.5 to 1.5
- ln2_bias: bfloat16 [1600], P('row'), may hold values from -3 to 3
- fc_weight: bfloat16 [1600, 6400], P('row', 'col'), may hold values from -1 to 1
- fc_bias: bfloat16 [6400], P('col'), may hold values from -3 to 3
- proj_weight: bfloat16 [6400, 1600], P('col', 'row'), may hold values from -0.078125 to 0.078125
- proj_bias: bfloat16 [1600], P('row'), may hold values from -3 to 3
Outputs:
- block_out: bfloat16 [12288, 1600], P(('dp', 'col'), 'row')
- x_grad: float32 [12288, 1600], P(('dp', 'col'), 'row')
- ln1_gain_grad: float32 [1600], P('row')
- ln1_bias_grad: float32 [1600], P('row')
- qkv_weight_grad: float32 [3, 1600, 1600], P(None, 'row', 'col')
- qv_bias_grad: float32 [2, 1600], P(None, 'col')
- out_weight_grad: float32 [1600, 1600], P('col', 'row')
- out_bias_grad: float32 [1600], P('row')
- ln2_gain_grad: float32 [1600], P('row')
- ln2_bias_grad: float32 [1600], P('row')
- fc_weight_grad: float32 [1600, 6400], P('row', 'col')
- fc_bias_grad: float32 [6400], P('col')
- proj_weight_grad: float32 [6400, 1600], P('col', 'row')
- proj_bias_grad: float32 [1600], P('row')
Inputs may be any that keep to these rules, and one draw needn't show every extreme that they name: `seq_lengths`: row g gives the lengths of the 5 sequences of data shard g, in the order in which their tokens lie among that shard's 1536 tokens; each row sums to 1536, and the longest sequence of each row has exactly 768 tokens.
All inputs are finite; a program needn't handle non-finite values.
Results may differ from a plain program's by a relative error of at most 0.015.
Values may be sent and summed in bfloat16 or wider, within the bound.
No kernel may reach another device: no remote copies, remote signals or barrier semaphores. Data moves between devices by JAX's collectives and lax.ppermute only.
A program may use at most 256 MiB of HBM per device.

v0:
```python
import math

import jax
import jax.numpy as jnp
from jax import lax
from jax.sharding import PartitionSpec as P

D = 1600
HEADS = 25
HEAD_DIM = 64
SEQ_CAP = 2048


gelu_root = math.sqrt(2.0 / math.pi)
gelu_cubic = 0.044715


def passed_along(value, axis, by):
    peers = lax.axis_size(axis)
    pairs = [(i, i + by) for i in range(peers) if 0 <= i + by < peers]
    return lax.ppermute(value, axis, pairs)


def gelu_tanh(values):
    return (
        0.5
        * values
        * (1.0 + jnp.tanh(gelu_root * (values + gelu_cubic * values * values * values)))
    )


def times_transposed(left, weight):
    return lax.dot_general(
        left, weight, (((1,), (1,)), ((), ())), preferred_element_type=jnp.float32
    )


def contract_rows(left, right):
    return lax.dot_general(
        left, right, (((0,), (0,)), ((), ())), preferred_element_type=jnp.float32
    )


def across_cols(values):
    return lax.all_gather(values, "col", axis=0, tiled=True)


def across_rows(values):
    return lax.all_gather(values, "row", axis=0, tiled=True)


def sum_rows_of(func, own_rows):
    return lax.psum_scatter(
        func(jnp.int32(0), lax.axis_size("row") * own_rows), "row", scatter_dimension=0, tiled=True
    )


def sum_cols_of(func, own_rows):
    return lax.psum_scatter(
        func(jnp.int32(0), lax.axis_size("col") * own_rows), "col", scatter_dimension=0, tiled=True
    )


def to_heads(values):
    return lax.all_to_all(values, "col", split_axis=0, concat_axis=2, tiled=True)


def from_heads(values):
    return lax.all_to_all(values, "col", split_axis=2, concat_axis=0, tiled=True)


def feature_totals(first_terms, second_terms):
    return lax.psum((jnp.sum(first_terms, axis=1), jnp.sum(second_terms, axis=1)), "row")


def norm_forward(values, norm_gain, norm_bias):
    row_totals = feature_totals(values, values * values)
    center = row_totals[0] / D
    spread = row_totals[1] / D - center * center
    inverse = lax.rsqrt(spread + 1e-05)
    normed = (values - center[:, None]) * inverse[:, None]
    scaled_out = normed * norm_gain.astype(jnp.float32) + norm_bias.astype(jnp.float32)
    return (normed, inverse, scaled_out.astype(jnp.bfloat16))


def norm_backward(incoming, normed, inverse, norm_gain):
    scaled = incoming * norm_gain.astype(jnp.float32)
    row_totals = feature_totals(scaled, scaled * normed)
    result = inverse[:, None] * (
        scaled - row_totals[0][:, None] / D - normed * row_totals[1][:, None] / D
    )
    return (result, jnp.sum(incoming * normed, axis=0), jnp.sum(incoming, axis=0))


def split_heads(values):
    row_count = values.shape[0]
    return values.reshape(row_count, HEADS, HEAD_DIM).transpose(1, 0, 2)


def join_heads(values):
    head_count, row_count, head_width = values.shape
    return values.transpose(1, 0, 2).reshape(row_count, head_count * head_width)


def attend(query_heads, key_heads, value_heads, allowed):
    scale = HEAD_DIM ** (-0.5)

    def one_head(carried, members):
        query_rows, key_rows, value_rows = members
        scores = scale * jnp.einsum(
            "qe,ke->qk", query_rows, key_rows, preferred_element_type=jnp.float32
        )
        scores = jnp.where(allowed, scores, -1e30)
        highest = jnp.max(scores, axis=1, keepdims=True)
        weights = jnp.exp(scores - highest)
        totals = jnp.sum(weights, axis=1, keepdims=True)
        probs_low = (weights / totals).astype(jnp.bfloat16)
        mixed_out = jnp.dot(probs_low, value_rows, preferred_element_type=jnp.float32)
        return (carried, (mixed_out, (highest + jnp.log(totals))[:, 0]))

    unused, outputs = lax.scan(
        one_head, jnp.zeros((), jnp.float32), (query_heads, key_heads, value_heads)
    )
    return outputs


def attend_backward(query_heads, key_heads, value_heads, grad_heads, log_totals, allowed):
    scale = HEAD_DIM ** (-0.5)

    def one_head(carried, members):
        query_rows, key_rows, value_rows, grad_rows, log_total = members
        scores = scale * jnp.einsum(
            "qe,ke->qk", query_rows, key_rows, preferred_element_type=jnp.float32
        )
        scores = jnp.where(allowed, scores, -1e30)
        prob_full = jnp.exp(scores - log_total[:, None])
        probs_low = prob_full.astype(jnp.bfloat16)
        prob_grad = jnp.einsum(
            "qe,ke->qk", grad_rows, value_rows, preferred_element_type=jnp.float32
        )
        centre = jnp.sum(prob_full * prob_grad, axis=1, keepdims=True)
        score_grad = (prob_full * (prob_grad - centre)).astype(jnp.bfloat16)
        query_grad = scale * jnp.dot(score_grad, key_rows, preferred_element_type=jnp.float32)
        key_grad = scale * jnp.einsum(
            "qk,qe->ke", score_grad, query_rows, preferred_element_type=jnp.float32
        )
        value_grad = jnp.einsum(
            "qk,qe->ke", probs_low, grad_rows, preferred_element_type=jnp.float32
        )
        return (carried, (query_grad, key_grad, value_grad))

    unused, outputs = lax.scan(
        one_head,
        jnp.zeros((), jnp.float32),
        (query_heads, key_heads, value_heads, grad_heads, log_totals),
    )
    return outputs


def per_device(
    block_in,
    out_grad,
    seq_lengths,
    ln1_gain,
    ln1_bias,
    qkv_weight,
    qv_bias,
    out_weight,
    out_bias,
    ln2_gain,
    ln2_bias,
    fc_weight,
    fc_bias,
    proj_weight,
    proj_bias,
):
    n_row = lax.axis_size("row")
    n_col = lax.axis_size("col")
    col_rows = block_in.shape[0]
    group_rows = col_rows * n_col
    row_rows = group_rows // n_row
    tok_dev = group_rows // (n_row * n_col)
    max_len = min(SEQ_CAP, group_rows // 2)
    reach_back = (max_len - 2) // tok_dev + 1
    x_float = block_in.astype(jnp.float32)
    normed_one, inverse_one, low_one = norm_forward(x_float, ln1_gain, ln1_bias)
    gathered_one = across_cols(low_one)

    def qkv_term(first_row, row_count):
        return jnp.einsum(
            "td,kde->tke", gathered_one, qkv_weight, preferred_element_type=jnp.float32
        )

    qkv_sum = sum_rows_of(qkv_term, row_rows)
    bias_three = jnp.stack([qv_bias[0], jnp.zeros_like(qv_bias[0]), qv_bias[1]]).astype(jnp.float32)
    projected = (qkv_sum + bias_three[None]).astype(jnp.bfloat16)
    heads_in = to_heads(projected)
    block_index = lax.axis_index("row") * n_col + lax.axis_index("col")
    positions = block_index * tok_dev + jnp.arange(tok_dev, dtype=jnp.int32)
    lengths_row = seq_lengths[0]
    seq_ends = jnp.cumsum(lengths_row, dtype=jnp.int32)
    starts = jnp.sum(
        jnp.where(seq_ends[None, :] <= positions[:, None], lengths_row[None, :], 0),
        axis=1,
        dtype=jnp.int32,
    )
    key_places = (block_index - reach_back) * tok_dev + jnp.arange(
        (reach_back + 1) * tok_dev, dtype=jnp.int32
    )
    allowed = (key_places[None, :] >= starts[:, None]) & (key_places[None, :] <= positions[:, None])
    key_values = heads_in[:, 1:, :]
    earlier = [
        passed_along(key_values, ("row", "col"), offset) for offset in range(reach_back, 0, -1)
    ]
    window = jnp.concatenate(earlier + [key_values], axis=0)
    query_heads = split_heads(heads_in[:, 0, :])
    key_heads = split_heads(window[:, 0, :])
    value_heads = split_heads(window[:, 1, :])
    attended_heads, log_totals = attend(query_heads, key_heads, value_heads, allowed)
    attended = join_heads(attended_heads).astype(jnp.bfloat16)
    back_rows = from_heads(attended[:, None, :])[:, 0, :]
    gathered_att = across_rows(back_rows)

    def out_term(first_row, row_count):
        return jnp.dot(gathered_att, out_weight, preferred_element_type=jnp.float32)

    branch = sum_cols_of(out_term, col_rows) + out_bias.astype(jnp.float32)
    x_mid = x_float + branch
    normed_two, inverse_two, low_two = norm_forward(x_mid, ln2_gain, ln2_bias)
    gathered_two = across_cols(low_two)

    def fc_term(first_row, row_count):
        return jnp.dot(gathered_two, fc_weight, preferred_element_type=jnp.float32)

    pre_act = sum_rows_of(fc_term, row_rows) + fc_bias.astype(jnp.float32)
    activated = gelu_tanh(pre_act).astype(jnp.bfloat16)
    gathered_act = across_rows(activated)

    def proj_term(first_row, row_count):
        return jnp.dot(gathered_act, proj_weight, preferred_element_type=jnp.float32)

    proj_sum = sum_cols_of(proj_term, col_rows)
    block_out = (x_mid + proj_sum + proj_bias.astype(jnp.float32)).astype(jnp.bfloat16)
    one_again, two_again = (gathered_one, gathered_two)
    att_again, act_again = (gathered_att, gathered_act)
    grad_gathered = across_cols(out_grad)

    def act_grad_term(first_row, row_count):
        return times_transposed(grad_gathered, proj_weight)

    act_grad = sum_rows_of(act_grad_term, row_rows)
    proj_weight_grad = contract_rows(act_again, grad_gathered)
    proj_bias_grad = jnp.sum(grad_gathered, axis=0, dtype=jnp.float32)
    gelu_value, gelu_pull = jax.vjp(gelu_tanh, pre_act)
    pre_grad = gelu_pull(act_grad)[0].astype(jnp.bfloat16)
    pre_gathered = across_rows(pre_grad)
    fc_weight_grad = contract_rows(two_again, pre_gathered)
    fc_bias_grad = jnp.sum(pre_gathered, axis=0, dtype=jnp.float32)

    def h2_grad_term(first_row, row_count):
        return times_transposed(pre_gathered, fc_weight)

    h2_grad = sum_cols_of(h2_grad_term, col_rows)
    mid_part, ln2_gain_grad, ln2_bias_grad = norm_backward(
        h2_grad, normed_two, inverse_two, ln2_gain
    )
    mid_grad = mid_part + out_grad.astype(jnp.float32)
    branch_grad = mid_grad.astype(jnp.bfloat16)
    branch_gathered = across_cols(branch_grad)
    out_weight_grad = contract_rows(att_again, branch_gathered)
    out_bias_grad = jnp.sum(branch_gathered, axis=0, dtype=jnp.float32)

    def att_grad_term(first_row, row_count):
        return times_transposed(branch_gathered, out_weight)

    att_grad = sum_rows_of(att_grad_term, row_rows).astype(jnp.bfloat16)
    att_heads = to_heads(att_grad[:, None, :])[:, 0, :]
    query_grad, key_grad, value_grad = attend_backward(
        query_heads, key_heads, value_heads, split_heads(att_heads), log_totals, allowed
    )
    window_grad = jnp.stack([join_heads(key_grad), join_heads(value_grad)], axis=1)
    own_grad = window_grad[reach_back * tok_dev :]
    for offset in range(1, reach_back + 1):
        returned_piece = window_grad[
            (reach_back - offset) * tok_dev : (reach_back - offset + 1) * tok_dev
        ]
        own_grad = own_grad + passed_along(
            returned_piece.astype(jnp.bfloat16), ("row", "col"), -offset
        ).astype(returned_piece.dtype)
    heads_grad = jnp.concatenate([join_heads(query_grad)[:, None, :], own_grad], axis=1).astype(
        jnp.bfloat16
    )
    projected_grad = from_heads(heads_grad)
    qkv_gathered = across_rows(projected_grad)
    qkv_weight_grad = jnp.einsum(
        "td,tke->kde", one_again, qkv_gathered, preferred_element_type=jnp.float32
    )
    qv_bias_grad = jnp.sum(qkv_gathered[:, 0::2, :], axis=0, dtype=jnp.float32)

    def h1_grad_term(first_row, row_count):
        return jnp.einsum(
            "tke,kde->td", qkv_gathered, qkv_weight, preferred_element_type=jnp.float32
        )

    h1_grad = sum_cols_of(h1_grad_term, col_rows)
    in_part, ln1_gain_grad, ln1_bias_grad = norm_backward(
        h1_grad, normed_one, inverse_one, ln1_gain
    )
    x_grad = mid_grad + in_part
    ln1_gain_grad, ln1_bias_grad, ln2_gain_grad, ln2_bias_grad = lax.psum(
        (ln1_gain_grad, ln1_bias_grad, ln2_gain_grad, ln2_bias_grad), ("dp", "col")
    )
    (
        qkv_weight_grad,
        qv_bias_grad,
        out_weight_grad,
        out_bias_grad,
        fc_weight_grad,
        fc_bias_grad,
        proj_weight_grad,
        proj_bias_grad,
    ) = (
        lax.psum(qkv_weight_grad.astype(jnp.bfloat16), "dp").astype(jnp.float32),
        lax.psum(qv_bias_grad.astype(jnp.bfloat16), "dp").astype(jnp.float32),
        lax.psum(out_weight_grad.astype(jnp.bfloat16), "dp").astype(jnp.float32),
        lax.psum(out_bias_grad.astype(jnp.bfloat16), "dp").astype(jnp.float32),
        lax.psum(fc_weight_grad.astype(jnp.bfloat16), "dp").astype(jnp.float32),
        lax.psum(fc_bias_grad.astype(jnp.bfloat16), "dp").astype(jnp.float32),
        lax.psum(proj_weight_grad.astype(jnp.bfloat16), "dp").astype(jnp.float32),
        lax.psum(proj_bias_grad.astype(jnp.bfloat16), "dp").astype(jnp.float32),
    )
    return (
        block_out,
        x_grad,
        ln1_gain_grad,
        ln1_bias_grad,
        qkv_weight_grad,
        qv_bias_grad,
        out_weight_grad,
        out_bias_grad,
        ln2_gain_grad,
        ln2_bias_grad,
        fc_weight_grad,
        fc_bias_grad,
        proj_weight_grad,
        proj_bias_grad,
    )


def solution(mesh):
    placed = (
        P(("dp", "col"), "row"),
        P(("dp", "col"), "row"),
        P("dp", None),
        P("row"),
        P("row"),
        P(None, "row", "col"),
        P(None, "col"),
        P("col", "row"),
        P("row"),
        P("row"),
        P("row"),
        P("row", "col"),
        P("col"),
        P("col", "row"),
        P("row"),
    )
    return jax.shard_map(
        per_device,
        mesh=mesh,
        in_specs=placed,
        out_specs=(
            P(("dp", "col"), "row"),
            P(("dp", "col"), "row"),
            P("row"),
            P("row"),
            P(None, "row", "col"),
            P(None, "col"),
            P("col", "row"),
            P("row"),
            P("row"),
            P("row"),
            P("row", "col"),
            P("col"),
            P("col", "row"),
            P("row"),
        ),
        check_vma=False,
    )
```

profile of v0, /device:TPU:0, one launch (start us, length us, event | category | flops | bytes accessed | tf_op | source)
XLA Modules:
  0.0 2492.2 jit_solution(14884697243471976543)
XLA Ops:
  10.4 5.9 all-reduce.4
  19.7 13.0 all-gather.9.cloned.1.call-done
  32.7 13.9 fusion.72
  47.4 168.3 %reduce-scatter.9.cloned.1.call-done = f32[768,3,800]{0,2,1:T(8,128)} async-done(((f32[1536,3,800]{0,2,1:T(8,128)}), f32[768,3,800]{0,2,1:T(8,128)}) %reduce-scatter.9.cloned.1.call-update) | async-done | bytes 7372816 | tf_op jit(solution)/shard_map/reduce_scatter | solution.py:53
  215.8 5.4 add_convert_fusion
  221.2 10.9 copy.91
  232.1 13.9 all_to_all.66
  246.0 14.6 copy.111
  265.7 3.7 collective-permute-start
  277.3 44.6 %collective-permute-done = bf16[384,2,1600]{0,2,1:T(8,128)(2,1)} collective-permute-done((bf16[384,2,1600]{0,2,1:T(8,128)(2,1)}, bf16[384,2,1600]{0,2,1:T(8,128)(2,1)}, u32[]{:S(2)}, u32[]{:S(2)}) %collective-permute-start) | collective-permute-done | bytes 2457632 | tf_op jit(solution)/shard_map/ppermute | solution.py:21
  322.0 3.9 pad_maximum_fusion.1
  329.5 8.7 copy.95
  338.3 8.8 copy.96
  348.3 108.8 %while.28 = (s32[]{:T(128)}, bf16[25,384,64]{1,2,0:T(8,128)(2,1)}, f32[25,384]{1,0:T(8,128)S(1)}, bf16[25,384,64]{2,1,0:T(8,128)(2,1)}, bf16[25,1152,64]{2,1,0:T...) while((s32[]{:T(128)}, bf16[25,384,64]{1,2,0:T(8,128)(2,1)}, ...), condition=%wide.region_10.11_spmd.clone, body=%wide.region_7.10_spmd.clone.sunk | while | flops 118111872 | bytes 6123121 | solution.py:121
  457.1 8.2 copy.119
  465.8 10.4 reduce.6
  477.5 31.0 %all_to_all.67 = bf16[2,2,153600]{2,1,0:T(2,128)(2,1)S(1)} all-to-all(bf16[2,2,153600]{2,1,0:T(2,128)(2,1)} %reshape.144), channel_id=1, replica_groups=mesh['dp'=8,'row'=2,'col'=2] {'col'}, dimensions={0} | all-to-all | bytes 2457600 | tf_op jit(solution)/shard_map/all_to_all | solution.py:69
  514.7 39.8 %all-gather.11.cloned.1.call-done = bf16[1536,800]{0,1:T(8,128)(2,1)} async-done(((bf16[768,800]{0,1:T(8,128)(2,1)}), bf16[1536,800]{0,1:T(8,128)(2,1)}) %all-gather.11.cloned.1.call-update) | async-done | bytes 2457616 | tf_op jit(solution)/shard_map/all_gather | solution.py:49
  554.6 6.7 fusion.80
  562.2 12.1 reduce-scatter.11.cloned.1.call-done
  574.3 3.8 fusion.75
  578.1 5.0 all-reduce.3
  588.1 17.7 fusion.83
  605.9 17.5 fusion.81
  624.1 203.1 %reduce-scatter.17.cloned.1.call-done = f32[768,3200]{1,0:T(8,128)} async-done(((f32[1536,3200]{1,0:T(8,128)}), f32[768,3200]{1,0:T(8,128)}) %reduce-scatter.17.cloned.1.call-update) | async-done | bytes 9830416 | tf_op jit(solution)/shard_map/reduce_scatter | solution.py:53
  827.2 222.6 %reduce-scatter.13.cloned.1.call-done = f32[768,3200]{1,0:T(8,128)} async-done(((f32[1536,3200]{1,0:T(8,128)}), f32[768,3200]{1,0:T(8,128)}) %reduce-scatter.13.cloned.1.call-update) | async-done | bytes 9830416 | tf_op jit(solution)/shard_map/reduce_scatter | solution.py:53
  1049.8 14.9 fusion.50
  1064.8 122.4 %all-gather.19.cloned.1.call-done = bf16[1536,3200]{1,0:T(8,128)(2,1)} async-done(((bf16[768,3200]{1,0:T(8,128)(2,1)}), bf16[1536,3200]{1,0:T(8,128)(2,1)}) %all-gather.19.cloned.1.call-update) | async-done | bytes 9830416 | tf_op jit(solution)/shard_map/all_gather | solution.py:49
  1187.2 14.0 fusion.84
  1201.3 13.0 reduce-scatter.19.cloned.1.call-done
  1214.3 4.0 multiply_reduce_fusion.1
  1218.3 5.0 all-reduce.2
  1223.8 4.4 fusion.74
  1228.3 12.4 all-gather.21.cloned.1.call-done
  1240.7 6.1 fusion.85
  1246.9 63.4 %reduce-scatter.21.cloned.1.call-done = f32[768,800]{0,1:T(8,128)} async-done(((f32[1536,800]{0,1:T(8,128)}), f32[768,800]{0,1:T(8,128)}) %reduce-scatter.21.cloned.1.call-update) | async-done | bytes 2457616 | tf_op jit(solution)/shard_map/reduce_scatter | solution.py:53
  1316.6 5.1 all_to_all.68
  1321.7 3.6 reshape.147
  1331.7 217.3 %while.29 = (s32[]{:T(128)}, bf16[25,384,64]{1,2,0:T(8,128)(2,1)S(1)}, f32[25,1152,64]{1,2,0:T(8,128)}, f32[25,1152,64]{1,2,0:T(8,128)}, bf16[25,384,64]{2,1,0:T...) while((s32[]{:T(128)}, ...), condition=%wide.region_27.28_spmd.clone, body=%wide.region_25.27_spmd.clone.sunk | while | flops 288521856 | bytes 15159425 | solution.py:152
  1548.9 11.2 stack_reshape.6
  1560.1 11.2 stack_reshape.7
  1571.3 15.2 fusion.46
  1592.8 23.9 copy.106
  1616.7 57.5 %collective-permute-done.3 = bf16[384,2,1600]{0,1,2:T(2,128)(2,1)S(1)} collective-permute-done((bf16[384,2,1600]{0,1,2:T(2,128)(2,1)S(1)}, bf16[384,2,1600]{0,1,2:T(2,128)(2,1)S(1)}, u32[]{:S(2)}, u32[]{:S(2)}) %collective-permute-start.3) | collective-permute-done | bytes 2457632 | tf_op jit(solution)/shard_map/ppermute | solution.py:21
  1674.2 7.6 fusion.56
  1681.8 5.2 pad_maximum_fusion.2
  1687.0 7.7 all_to_all.69
  1698.0 92.1 %all-gather.23.cloned.1.call-done = bf16[1536,3,800]{0,2,1:T(8,128)(2,1)} async-done(((bf16[768,3,800]{0,2,1:T(8,128)(2,1)}), bf16[1536,3,800]{0,2,1:T(8,128)(2,1)}) %all-gather.23.cloned.1.call-update) | async-done | bytes 7372816 | tf_op jit(solution)/shard_map/all_gather | solution.py:49
  1790.1 11.7 convolution_bitcast_fusion.2
  1801.9 112.0 %all-gather.15.cloned.1.call-done = bf16[1536,3200]{1,0:T(8,128)(2,1)} async-done(((bf16[768,3200]{1,0:T(8,128)(2,1)}), bf16[1536,3200]{1,0:T(8,128)(2,1)}) %all-gather.15.cloned.1.call-update) | async-done | bytes 9830416 | tf_op jit(solution)/shard_map/all_gather | solution.py:49
  1913.9 14.0 fusion.82
  1928.3 14.7 convolution_convert_fusion.1
  1943.0 14.4 convolution_convert_fusion
  1957.4 3.8 convolution_convert_fusion.2
  1961.2 9.3 convert_bitcast_fusion
  1973.4 5.5 reduce_sum.198
  1984.3 39.8 %all-reduce.5 = (bf16[2,800]{1,0:T(2,128)(2,1)S(1)}, bf16[800]{0:T(1024)(128)(2,1)S(1)}, bf16[3200]{0:T(1024)(128)(2,1)S(1)}, bf16[800]{0:T(1024)(128)(2,1)S(1)}) all-reduce(bf16[2,800]{1,0:T(2,128)(2,1)S(1)} %slice_reduce_fusion, bf16[800]{0:T(1024)(128)(2,1)S(1)} %reduce_sum.195, ...), channel_id=1, replica_groups=mesh['dp'=8,'row'=2,'col'=2] {'dp'}, use_global_device_ids=true, to_apply=%region_39.40 | all-reduce | flops 6400 | bytes 25600 | tf_op jit(solution)/shard_map/psum | solution.py:324
  2029.2 61.9 %all-reduce = (f32[800]{0:T(1024)}, f32[800]{0:T(1024)}, f32[800]{0:T(1024)}, f32[800]{0:T(1024)}) all-reduce(f32[800]{0:T(1024)S(1)} %get-tuple-element.354, f32[800]{0:T(1024)S(1)} %get-tuple-element.359, f32[800]{0:T(1024)S(1)} %copy-done.28, f32[800]{0:T(1024)S(1)} %copy-done.29), channel_id=1, replica_groups=mesh['dp'=8,'row'=2,'col'=2] {'dp','col'}, use_global_device_ids=true, to_apply=%region_34.35 | all-reduce | flops 3200 | bytes 25600 | tf_op jit(solution)/shard_map/psum | solution.py:310
  2091.1 5.0 all-reduce.1
  2096.2 6.6 fusion.68
  2102.7 361.2 %all-reduce.9.cloned.1.call-done = (bf16[3,800,800]{1,2,0:T(8,128)(2,1)}, bf16[800,800]{1,0:T(8,128)(2,1)}, bf16[800,3200]{1,0:T(8,128)(2,1)}, bf16[3200,800]{0,1:T(8,128)(2,1)}) async-done(((bf16[3,800,800]{1,2,0:T(8,128)(2,1)}, bf16[800,800]{1,0:T(8,128)(2,1)}, bf16[800,3200]{1,0:T(8,128)(2,1)}, bf16[3200,800]{0,1:T(8,128)(2,1)}), (bf16[3,800,800]{1,2,0:T(8,128)(2,1)}, bf16[800,800]{1,0:T(8,128)(2,1)}, ...) | async-done | bytes 15360016 | tf_op jit(solution)/shard_map/psum | solution.py:323
  2463.9 7.3 convert_element_type.172
  2471.2 4.7 convert_element_type.175
  2475.9 7.8 copy.109
  (507 shorter events, 403.1 us)
Async XLA Ops:
  7.2 547.4 %copy-start = (bf16[800,800]{1,0:T(8,128)(2,1)S(1)}, bf16[800,800]{1,0:T(8,128)(2,1)}, u32[]{:S(2)}) copy-start(bf16[800,800]{1,0:T(8,128)(2,1)} %param.26) | copy-start | bytes 3840004
  7.2 25.5 %all-gather.9.cloned.1.call-start = ((), (), s32[]{:S(2)}) async-start(), calls=%async_computation.12 | async-start | bytes 3686400 | tf_op jit(solution)/shard_map/all_gather | solution.py:45
  9.7 37.0 %copy-start.18 = (f32[800]{0:T(1024)}, f32[800]{0:T(1024)S(1)}, u32[]{:S(2)}) copy-start(f32[800]{0:T(1024)S(1)} %convert_element_type.142) | copy-start | bytes 9604
  16.3 0.6 copy-start.20
  16.3 0.6 copy-start.22
  19.7 196.1 %reduce-scatter.9.cloned.1.call-start = ((), (), s32[]{:S(2)}) async-start(), calls=%async_computation.13 | async-start | bytes 22118400 | tf_op jit(solution)/shard_map/reduce_scatter | solution.py:53
  46.7 0.7 copy-start.30
  46.7 507.9 %all-gather.11.cloned.1.call-start = ((), (), s32[]{:S(2)}) async-start(), calls=%async_computation.14 | async-start | bytes 3686400 | tf_op jit(solution)/shard_map/all_gather | solution.py:49
  263.1 2.7 copy-start.5
  263.1 10.0 copy-start.36
  265.7 56.2 %collective-permute-start = (bf16[384,2,1600]{0,2,1:T(8,128)(2,1)}, bf16[384,2,1600]{0,2,1:T(8,128)(2,1)}, u32[]{:S(2)}, u32[]{:S(2)}) collective-permute-start(bf16[384,2,1600]{0,2,1:T(8,128)(2,1)} %slice.43), channel_id=1, source_target_pairs={{0,2},{1,3},{4,6},{5,7},{8,10},{9,11},{12,14},{13,15},{16,18},{17,... | collective-permute-start | bytes 7372808 | tf_op jit(solution)/shard_map/ppermute | solution.py:21
  269.4 52.6 %collective-permute-start.1 = (bf16[384,2,1600]{0,2,1:T(8,128)(2,1)}, bf16[384,2,1600]{0,2,1:T(8,128)(2,1)}, u32[]{:S(2)}, u32[]{:S(2)}) collective-permute-start(bf16[384,2,1600]{0,2,1:T(8,128)(2,1)} %slice.43), channel_id=1, source_target_pairs={{0,1},{1,2},{2,3},{4,5},{5,6},{6,7},{8,9},{9,10},{10,11},{12,13},{... | collective-permute-start | bytes 7372808 | tf_op jit(solution)/shard_map/ppermute | solution.py:21
  514.7 59.6 %reduce-scatter.11.cloned.1.call-start = ((), (), s32[]{:S(2)}) async-start(), calls=%async_computation.15 | async-start | bytes 7372800 | tf_op jit(solution)/shard_map/reduce_scatter | solution.py:59
  561.3 0.8 copy-start.32
  561.3 0.9 copy-start.33
  561.3 0.9 copy-start.34
  561.3 13.0 copy-start.3
  561.3 26.8 %all-gather.17.cloned.1.call-start = ((), (), s32[]{:S(2)}) async-start(), calls=%async_computation.20 | async-start | bytes 3686400 | tf_op jit(solution)/shard_map/all_gather | solution.py:45
  561.9 43.9 %all-gather.13.cloned.1.call-start = ((), (), s32[]{:S(2)}) async-start(), calls=%async_computation.16 | async-start | bytes 3686400 | tf_op jit(solution)/shard_map/all_gather | solution.py:45
  562.2 661.1 %copy-start.12 = (f32[800]{0:T(1024)}, f32[800]{0:T(1024)S(1)}, u32[]{:S(2)}) copy-start(f32[800]{0:T(1024)S(1)} %convert_element_type.151) | copy-start | bytes 9604
  583.0 640.2 %copy-start.14 = (f32[768]{0:T(1024)}, f32[768]{0:T(1024)S(1)}, u32[]{:S(2)}) copy-start(f32[768]{0:T(1024)S(1)} %get-tuple-element.439) | copy-start | bytes 9220
  583.0 640.2 %copy-start.16 = (f32[768]{0:T(1024)}, f32[768]{0:T(1024)S(1)}, u32[]{:S(2)}) copy-start(f32[768]{0:T(1024)S(1)} %get-tuple-element.440) | copy-start | bytes 9220
  586.5 240.7 %reduce-scatter.17.cloned.1.call-start = ((), (), s32[]{:S(2)}) async-start(), calls=%async_computation.21 | async-start | bytes 29491200 | tf_op jit(solution)/shard_map/reduce_scatter | solution.py:53
  605.8 444.0 %reduce-scatter.13.cloned.1.call-start = ((), (), s32[]{:S(2)}) async-start(), calls=%async_computation.17 | async-start | bytes 29491200 | tf_op jit(solution)/shard_map/reduce_scatter | solution.py:53
  623.4 0.7 copy-start.31
  623.4 563.8 %all-gather.19.cloned.1.call-start = ((), (), s32[]{:S(2)}) async-start(), calls=%async_computation.22 | async-start | bytes 14745600 | tf_op jit(solution)/shard_map/all_gather | solution.py:49
  1064.7 149.5 %reduce-scatter.19.cloned.1.call-start = ((), (), s32[]{:S(2)}) async-start(), calls=%async_computation.23 | async-start | bytes 7372800 | tf_op jit(solution)/shard_map/reduce_scatter | solution.py:59
  1201.3 22.6 copy-start.6
  1201.3 39.4 %all-gather.21.cloned.1.call-start = ((), (), s32[]{:S(2)}) async-start(), calls=%async_computation.24 | async-start | bytes 3686400 | tf_op jit(solution)/shard_map/all_gather | solution.py:45
  1223.2 5.0 copy-start.26
  1223.2 0.6 copy-start.24
  1228.2 82.0 %reduce-scatter.21.cloned.1.call-start = ((), (), s32[]{:S(2)}) async-start(), calls=%async_computation.25 | async-start | bytes 7372800 | tf_op jit(solution)/shard_map/reduce_scatter | solution.py:53
  1246.8 543.3 %all-gather.23.cloned.1.call-start = ((), (), s32[]{:S(2)}) async-start(), calls=%async_computation.26 | async-start | bytes 11059200 | tf_op jit(solution)/shard_map/all_gather | solution.py:49
  1586.6 87.7 %copy-start.2 = (f32[1152,1,1600]{0,1,2:T(1,128)S(1)}, f32[1152,1,1600]{0,1,2:T(1,128)}, u32[]{:S(2)}) copy-start(f32[1152,1,1600]{0,1,2:T(1,128)} %stack_reshape.7) | copy-start | bytes 22118404
  1590.0 26.6 %collective-permute-start.2 = (bf16[384,2,1600]{0,1,2:T(2,128)(2,1)S(1)}, bf16[384,2,1600]{0,1,2:T(2,128)(2,1)S(1)}, u32[]{:S(2)}, u32[]{:S(2)}) collective-permute-start(bf16[384,2,1600]{0,1,2:T(2,128)(2,1)S(1)} %get-tuple-element.433), channel_id=1, source_target_pairs={{1,0},{2,1},{3,2},{5,4},{6,5},{7,6},{9,8},{10,9},{11,10},{13,12},{... | collective-permute-start | bytes 7372808 | tf_op jit(solution)/shard_map/ppermute | solution.py:21
  1591.3 82.9 %collective-permute-start.3 = (bf16[384,2,1600]{0,1,2:T(2,128)(2,1)S(1)}, bf16[384,2,1600]{0,1,2:T(2,128)(2,1)S(1)}, u32[]{:S(2)}, u32[]{:S(2)}) collective-permute-start(bf16[384,2,1600]{0,1,2:T(2,128)(2,1)S(1)} %get-tuple-element.434), channel_id=1, source_target_pairs={{2,0},{3,1},{6,4},{7,5},{10,8},{11,9},{14,12},{15,13},{18,16},{19,... | collective-permute-start | bytes 7372808 | tf_op jit(solution)/shard_map/ppermute | solution.py:21
  1697.4 216.5 %all-gather.15.cloned.1.call-start = ((), (), s32[]{:S(2)}) async-start(), calls=%async_computation.18 | async-start | bytes 14745600 | tf_op jit(solution)/shard_map/all_gather | solution.py:49
  1698.0 328.5 %reduce-scatter.23.cloned.1.call-start = ((), (), s32[]{:S(2)}) async-start(), calls=%async_computation.27 | async-start | bytes 7372800 | tf_op jit(solution)/shard_map/reduce_scatter | solution.py:59
  1801.9 294.2 %reduce-scatter.15.cloned.1.call-start = ((), (), s32[]{:S(2)}) async-start(), calls=%async_computation.19 | async-start | bytes 7372800 | tf_op jit(solution)/shard_map/reduce_scatter | solution.py:59
  1928.0 535.9 %all-reduce.9.cloned.1.call-start = ((), (), s32[]{:S(2)}) async-start(), calls=%async_computation.28 | async-start | bytes 31948800 | tf_op jit(solution)/shard_map/psum | solution.py:323
  1928.2 14.8 copy-start.9
  1928.2 33.0 %slice-start = ((s8[7372800]{0:T(1024)(128)(4,1)}), s8[4194304]{0:T(1024)(128)(4,1)S(1)}, s32[]{:S(2)}) async-start(s8[7372800]{0:T(1024)(128)(4,1)} %bitcast.190), calls=%async_computation.29 | async-start | bytes 8388608
  1943.0 14.4 copy-start.10
  1943.0 14.4 copy-start.38
  1943.0 18.2 slice-start.1
  1957.4 3.8 copy-start.37
  1970.6 0.7 copy-start.35
  1981.0 45.5 %copy-start.4 = (bf16[768,800]{0,1:T(8,128)(2,1)S(1)}, bf16[768,800]{0,1:T(8,128)(2,1)}, u32[]{:S(2)}) copy-start(bf16[768,800]{0,1:T(8,128)(2,1)} %param.19) | copy-start | bytes 3686404
  1981.0 45.5 %copy-start.19 = (f32[800]{0:T(1024)S(1)}, f32[800]{0:T(1024)}, u32[]{:S(2)}) copy-start(f32[800]{0:T(1024)} %copy-done.18) | copy-start | bytes 9604
  1981.0 45.5 %copy-start.21 = (f32[768]{0:T(1024)S(1)}, f32[768]{0:T(1024)}, u32[]{:S(2)}) copy-start(f32[768]{0:T(1024)} %copy-done.20) | copy-start | bytes 9220
  1981.0 45.5 %copy-start.23 = (f32[768]{0:T(1024)S(1)}, f32[768]{0:T(1024)}, u32[]{:S(2)}) copy-start(f32[768]{0:T(1024)} %copy-done.22) | copy-start | bytes 9220
  1984.2 45.0 %copy-start.28 = (f32[800]{0:T(1024)S(1)}, f32[800]{0:T(1024)}, u32[]{:S(2)}) copy-start(f32[800]{0:T(1024)} %get-tuple-element.352) | copy-start | bytes 9604
  1984.3 45.0 %copy-start.29 = (f32[800]{0:T(1024)S(1)}, f32[800]{0:T(1024)}, u32[]{:S(2)}) copy-start(f32[800]{0:T(1024)} %get-tuple-element.358) | copy-start | bytes 9604
  1984.3 111.8 %copy-start.7 = (bf16[768,800]{0,1:T(8,128)(2,1)S(1)}, bf16[768,800]{0,1:T(8,128)(2,1)}, u32[]{:S(2)}) copy-start(bf16[768,800]{0,1:T(8,128)(2,1)} %param.20) | copy-start | bytes 3686404
  1984.3 111.8 %copy-start.13 = (f32[800]{0:T(1024)S(1)}, f32[800]{0:T(1024)}, u32[]{:S(2)}) copy-start(f32[800]{0:T(1024)} %copy-done.12) | copy-start | bytes 9604
  1984.3 111.8 %copy-start.15 = (f32[768]{0:T(1024)S(1)}, f32[768]{0:T(1024)}, u32[]{:S(2)}) copy-start(f32[768]{0:T(1024)} %copy-done.14) | copy-start | bytes 9220
  1984.3 111.8 %copy-start.17 = (f32[768]{0:T(1024)S(1)}, f32[768]{0:T(1024)}, u32[]{:S(2)}) copy-start(f32[768]{0:T(1024)} %copy-done.16) | copy-start | bytes 9220
  1984.3 111.8 %copy-start.25 = (f32[768]{0:T(1024)S(1)}, f32[768]{0:T(1024)}, u32[]{:S(2)}) copy-start(f32[768]{0:T(1024)} %copy-done.24) | copy-start | bytes 9220
  1984.3 111.8 %copy-start.27 = (f32[768]{0:T(1024)S(1)}, f32[768]{0:T(1024)}, u32[]{:S(2)}) copy-start(f32[768]{0:T(1024)} %copy-done.26) | copy-start | bytes 9220
  2463.9 7.3 copy-start.8
  2475.9 7.8 copy-start.11
  2475.9 9.5 copy-start.1
Sparse Core Ops, SparseCore 0:
  19.8 12.9 all-gather.8
  46.8 168.9 reduce-scatter.8
  514.8 39.7 all-gather.10
  561.4 12.8 reduce-scatter.10
  575.7 12.3 all-gather.16
  590.0 12.2 all-gather.12
  605.9 221.2 reduce-scatter.16
  829.6 220.1 reduce-scatter.12
  1064.9 122.3 all-gather.18
  1201.4 12.8 reduce-scatter.18
  1228.3 12.3 all-gather.20
  1246.9 63.2 reduce-scatter.20
  1697.5 92.5 all-gather.22
  1791.5 122.3 all-gather.14
  1916.6 12.8 reduce-scatter.22
  1931.7 14.0 reduce-scatter.14
  1970.7 493.1 all-reduce.8
where the time goes:
time: 2510 us; the launch traced here: 2490 us
  waiting for transfers between devices  1540 us (61%)
  matrix products  450 us (18%)
  blocking collectives  180 us (7%)
  local copies, waits for them, and re-layouts  151 us (6%)
  other arithmetic  143 us (6%)
    reduce_scatter x4, waiting for transfers between devices, sum_rows_of(): lax.psum_scatter(func(jnp.int32(0), lax.axis_size('row') * own_rows), 'ro...  657 us
    all_gather x4, waiting for transfers between devices, across_rows(): return lax.all_gather(values, 'row', axis=0, tiled=True)  366 us
    psum x1, waiting for transfers between devices, per_device(): lax.psum(qkv_weight_grad.astype(jnp.bfloat16), 'dp').astype(jnp.float32)  361 us
    ppermute x4, waiting for transfers between devices, passed_along(): return lax.ppermute(value, axis, pairs)  102 us
    dot_general x50, matrix products, one_head(): jnp.einsum('qe,ke->qk', query_rows, key_rows, preferred_element_type=jnp....  89.1 us
    psum x1, blocking collectives, per_device(): lax.psum((ln1_gain_grad, ln1_bias_grad, ln2_gain_grad, ln2_bias_grad), ('...  61.9 us
    dot_general x25, matrix products, one_head(): jnp.dot(probs_low, value_rows, preferred_element_type=jnp.float32)  54.4 us
  transfers between devices with their start and end apart: 21, of which 16 were waited for; matrix products, arithmetic and copies ran while one was open for 7% of the time, Pallas kernels for 0%

commit v1 on v0

v1 whole, which is shorter than its diff:
```python
import functools
import math

import jax
import jax.numpy as jnp
from jax import lax
from jax.experimental import pallas as pl
from jax.experimental.pallas import tpu as pltpu
from jax.sharding import PartitionSpec as P

HEAD_DIM = 64
BLK=256
NEG=-1e30

def nt(a,b):
    return lax.dot_general(a,b,(((1,),(1,)),((),())),preferred_element_type=jnp.float32)
def nn(a,b):
    return lax.dot_general(a,b,(((1,),(0,)),((),())),preferred_element_type=jnp.float32)

def lane_masked(x, h):
    lanes = lax.broadcasted_iota(jnp.int32, x.shape, 1)
    return jnp.where((lanes // HEAD_DIM) == h, x, jnp.zeros_like(x))

def allowed_tile(i, j, first):
    keys = j * BLK + lax.broadcasted_iota(jnp.int32, (BLK, BLK), 0)
    queries = i * BLK + lax.broadcasted_iota(jnp.int32, (BLK, BLK), 1)
    return (keys >= first) & (keys <= queries)

def attend_kernel(heads, blocks, info_ref, q_ref, k_ref, v_ref, first_ref, o_ref, lse_ref, vt_ref):
    pair = pl.program_id(0)
    shift = info_ref[0]
    vt_ref[...] = jnp.transpose(v_ref[...].astype(jnp.float32)).astype(jnp.bfloat16)
    def place(b):
        return pl.multiple_of(lax.rem(b + shift, blocks) * BLK, BLK)
    def one_block(i, members):
        rows = pl.ds(place(i), BLK)
        query = q_ref[rows, :] * jnp.bfloat16(HEAD_DIM ** -0.5)
        queries = [lane_masked(query, h) for h in members]
        first = first_ref[pl.ds(i, 1), :]
        def step(j, carry):
            cols = pl.ds(place(j), BLK)
            keys = k_ref[cols, :]
            ok = allowed_tile(i, j, first)
            out = []
            for h in members:
                top, total, acc = carry[h]
                scores = jnp.where(ok, nt(keys, queries[h]), NEG)
                new_top = jnp.maximum(top, jnp.max(scores, axis=0, keepdims=True))
                probs = jnp.exp(scores - new_top)
                shrink = jnp.exp(top - new_top)
                total = total * shrink + jnp.sum(probs, axis=0, keepdims=True)
                acc = acc * shrink + nn(vt_ref[h * HEAD_DIM:(h + 1) * HEAD_DIM, cols], probs.astype(jnp.bfloat16))
                out.append((new_top, total, acc))
            return tuple(out)
        start = tuple((jnp.full((1, BLK), NEG, jnp.float32), jnp.zeros((1, BLK), jnp.float32),
                       jnp.zeros((HEAD_DIM, BLK), jnp.float32)) for h in members)
        done = lax.fori_loop(info_ref[1 + i], i + 1, step, start)
        parts = []
        for h in range(2):
            if h < len(members):
                top, total, acc = done[h]
                parts.append(acc / total)
                lse_ref[0, h:h + 1, pl.ds(i * BLK, BLK)] = top + jnp.log(total)
            else:
                parts.append(jnp.zeros((HEAD_DIM, BLK), jnp.float32))
                lse_ref[0, h:h + 1, pl.ds(i * BLK, BLK)] = jnp.zeros((1, BLK), jnp.float32)
        o_ref[rows, :] = jnp.transpose(jnp.concatenate(parts, axis=0)).astype(jnp.bfloat16)
    full = heads // 2
    @pl.when(pair < full)
    def _():
        for i in range(blocks):
            one_block(i, (0, 1))
    if heads % 2:
        @pl.when(pair == full)
        def _():
            for i in range(blocks):
                one_block(i, (0,))

def attend(info, proj, first, heads):
    tokens, width = proj.shape[0], proj.shape[1] // 3
    pairs = width // 128
    blocks = tokens // BLK
    spec = lambda at: pl.BlockSpec((tokens, 128), lambda p, s, at=at: (0, at * pairs + p))
    return pl.pallas_call(
        functools.partial(attend_kernel, heads, blocks),
        grid_spec=pltpu.PrefetchScalarGridSpec(
            num_scalar_prefetch=1, grid=(pairs,),
            in_specs=[spec(0), spec(1), spec(2), pl.BlockSpec((blocks, BLK), lambda p, s: (0, 0))],
            out_specs=[pl.BlockSpec((tokens, 128), lambda p, s: (0, p)),
                       pl.BlockSpec((1, 2, tokens), lambda p, s: (p, 0, 0))],
            scratch_shapes=[pltpu.VMEM((128, tokens), jnp.bfloat16)]),
        out_shape=[jax.ShapeDtypeStruct((tokens, width), jnp.bfloat16),
                   jax.ShapeDtypeStruct((pairs, 2, tokens), jnp.float32)],
        compiler_params=pltpu.CompilerParams(vmem_limit_bytes=48 * 2 ** 20),
        cost_estimate=pl.CostEstimate(flops=7 * 12 * 4 * 65536 * 64 * 8, bytes_accessed=8 * tokens * width, transcendentals=0),
        name="attend",
    )(info, proj, proj, proj, first)

def attend_back_kernel(heads, blocks, info_ref, q_ref, k_ref, v_ref, o_ref, g_ref, lse_ref, first_ref,
                       dq_ref, dk_ref, dv_ref, kt_ref, dk_acc, dv_acc):
    pair = pl.program_id(0)
    shift = info_ref[0]
    kt_ref[...] = jnp.transpose(k_ref[...].astype(jnp.float32)).astype(jnp.bfloat16)
    dk_acc[...] = jnp.zeros_like(dk_acc)
    dv_acc[...] = jnp.zeros_like(dv_acc)
    scale = jnp.bfloat16(HEAD_DIM ** -0.5)
    def place(b):
        return pl.multiple_of(lax.rem(b + shift, blocks) * BLK, BLK)
    def one_block(i, members):
        rows = pl.ds(place(i), BLK)
        query = q_ref[rows, :] * scale
        grad = g_ref[rows, :]
        queries = [lane_masked(query, h) for h in members]
        grads = [lane_masked(grad, h) for h in members]
        spread = jnp.transpose(grad.astype(jnp.float32) * o_ref[rows, :].astype(jnp.float32))
        centre = [jnp.sum(spread[h * HEAD_DIM:(h + 1) * HEAD_DIM], axis=0, keepdims=True) for h in members]
        lse = [lse_ref[0, h:h + 1, pl.ds(i * BLK, BLK)] for h in members]
        first = first_ref[pl.ds(i, 1), :]
        def step(j, carry):
            cols = pl.ds(place(j), BLK)
            keys = k_ref[cols, :]
            values = v_ref[cols, :]
            ok = allowed_tile(i, j, first)
            out = []
            dk = dv = None
            for h in members:
                scores = jnp.where(ok, nt(keys, queries[h]), NEG)
                probs = jnp.exp(scores - lse[h])
                prob_grad = nt(values, grads[h])
                score_grad = (probs * (prob_grad - centre[h])).astype(jnp.bfloat16)
                dv_h = nn(probs.astype(jnp.bfloat16), grads[h])
                dk_h = nn(score_grad, queries[h])
                dk, dv = (dk_h, dv_h) if dk is None else (dk + dk_h, dv + dv_h)
                out.append(carry[h] + nn(kt_ref[h * HEAD_DIM:(h + 1) * HEAD_DIM, cols], score_grad))
            dk_acc[cols, :] += dk
            dv_acc[cols, :] += dv
            return tuple(out)
        start = tuple(jnp.zeros((HEAD_DIM, BLK), jnp.float32) for h in members)
        done = list(lax.fori_loop(info_ref[1 + i], i + 1, step, start))
        if len(done) < 2:
            done.append(jnp.zeros((HEAD_DIM, BLK), jnp.float32))
        dq = jnp.transpose(jnp.concatenate(done, axis=0)) * (HEAD_DIM ** -0.5)
        dq_ref[rows, :] = dq.astype(jnp.bfloat16)
    full = heads // 2
    @pl.when(pair < full)
    def _():
        for i in range(blocks):
            one_block(i, (0, 1))
    if heads % 2:
        @pl.when(pair == full)
        def _():
            for i in range(blocks):
                one_block(i, (0,))
    dk_ref[...] = dk_acc[...].astype(jnp.bfloat16)
    dv_ref[...] = dv_acc[...].astype(jnp.bfloat16)

def attend_back(info, proj, att, grad, lse, first, heads):
    tokens, width = att.shape
    pairs = width // 128
    blocks = tokens // BLK
    spec = lambda at: pl.BlockSpec((tokens, 128), lambda p, s, at=at: (0, at * pairs + p))
    out = jax.ShapeDtypeStruct((tokens, width), jnp.bfloat16)
    return pl.pallas_call(
        functools.partial(attend_back_kernel, heads, blocks),
        grid_spec=pltpu.PrefetchScalarGridSpec(
            num_scalar_prefetch=1, grid=(pairs,),
            in_specs=[spec(0), spec(1), spec(2), spec(0), spec(0),
                      pl.BlockSpec((1, 2, tokens), lambda p, s: (p, 0, 0)),
                      pl.BlockSpec((blocks, BLK), lambda p, s: (0, 0))],
            out_specs=[spec(0), spec(0), spec(0)],
            scratch_shapes=[pltpu.VMEM((128, tokens), jnp.bfloat16), pltpu.VMEM((tokens, 128), jnp.float32),
                            pltpu.VMEM((tokens, 128), jnp.float32)]),
        out_shape=[out, out, out],
        compiler_params=pltpu.CompilerParams(vmem_limit_bytes=48 * 2 ** 20),
        cost_estimate=pl.CostEstimate(flops=7 * 12 * 10 * 65536 * 64 * 8, bytes_accessed=16 * tokens * width, transcendentals=0),
        name="attend_back",
    )(info, proj, proj, proj, att, grad, lse, first)


D = 1600
SWAP = ((0, 1), (1, 0))
gelu_root = math.sqrt(2.0 / math.pi)
gelu_cubic = 0.044715
f32 = jnp.float32
bf16 = jnp.bfloat16


def tn(a, b):
    return lax.dot_general(a, b, (((0,), (0,)), ((), ())), preferred_element_type=f32)


def row_swap(value):
    return lax.ppermute(value, "row", SWAP)


def col_swap(value):
    return lax.ppermute(value, "col", SWAP)


def dp_xor(value, mask):
    return lax.ppermute(value, "dp", [(i, i ^ mask) for i in range(lax.axis_size("dp"))])


def ordered(at, first, second, axis):
    return jnp.where(
        at == 0,
        jnp.concatenate([first, second], axis=axis),
        jnp.concatenate([second, first], axis=axis),
    )


def half_of(at, value, axis):
    size = value.shape[axis] // 2
    return jnp.where(
        at == 0,
        lax.slice_in_dim(value, 0, size, axis=axis),
        lax.slice_in_dim(value, size, 2 * size, axis=axis),
    )


def pad_to(value, size, axis):
    widths = [(0, 0)] * value.ndim
    widths[axis] = (0, size - value.shape[axis])
    return jnp.pad(value, widths)


def head_slots(c, value, axis, most, spare):
    cut = lambda low, high: lax.slice_in_dim(value, low, high, axis=axis)
    size = value.shape[axis]
    tail = col_swap(cut(0, spare))
    less = most - HEAD_DIM
    first = jnp.where(c == 0, cut(0, most), pad_to(cut(spare, spare + less), most, axis))
    second = jnp.where(
        c == 0,
        pad_to(jnp.concatenate([cut(most, size), tail], axis=axis), most, axis),
        pad_to(cut(spare + less, size), most, axis),
    )
    return first, second


def from_slots(c, first, second, axis, spare):
    cut = lambda value, low, high: lax.slice_in_dim(value, low, high, axis=axis)
    most = first.shape[axis]
    less = most - HEAD_DIM
    tail = col_swap(cut(second, less - spare, less))
    return jnp.where(
        c == 0,
        jnp.concatenate([first, cut(second, 0, less - spare)], axis=axis),
        jnp.concatenate([tail, cut(first, 0, less), cut(second, 0, less)], axis=axis),
    )


def put(buffer, piece, places):
    start = [jnp.int32(p) for p in places] + [jnp.int32(0)] * (buffer.ndim - len(places))
    return lax.dynamic_update_slice(buffer, piece, start)


def gather_quarters(other, k):
    rows, width = other.shape
    if lax.axis_size("dp") % 4:
        return row_swap(other)
    at = k % 4
    quarters = other.reshape(4, rows // 4, width)
    got = {0: row_swap(lax.dynamic_index_in_dim(quarters, at, 0, keepdims=False))}
    got[2] = dp_xor(got[0], 2)
    got[1] = dp_xor(got[0], 1)
    got[3] = dp_xor(got[2], 1)
    buffer = jnp.zeros_like(quarters)
    for d in range(4):
        buffer = put(buffer, got[d][None], (at ^ d,))
    return buffer.reshape(rows, width)


def scattered(grad, y, z):
    send = lax.dynamic_index_in_dim(grad, 1 - y, 0, keepdims=False)
    keep = lax.dynamic_index_in_dim(grad, y, 0, keepdims=False)
    part = (keep.astype(f32) + dp_xor(send, 1).astype(f32)).astype(bf16)
    total = lax.dynamic_index_in_dim(part, z, 0, keepdims=False).astype(f32)
    for d in (1, 2, 3):
        piece = lax.dynamic_index_in_dim(part, z ^ d, 0, keepdims=False)
        total = total + dp_xor(piece, 2 * d).astype(f32)
    return total.astype(bf16)


def gathered(piece, y, z):
    own = [piece] + [dp_xor(piece, 2 * d) for d in (1, 2, 3)]
    buffer = jnp.zeros((4,) + piece.shape, piece.dtype)
    for d in range(4):
        buffer = put(buffer, own[d][None], (z ^ d,))
    return buffer, dp_xor(buffer, 1)


def reduce_rows(grad, r, k):
    rows, width = grad.shape
    if lax.axis_size("dp") != 8:
        halves = grad.reshape(2, rows // 2, width)
        keep = lax.dynamic_index_in_dim(halves, r, 0, keepdims=False)
        got = row_swap(lax.dynamic_index_in_dim(halves, 1 - r, 0, keepdims=False))
        both = lax.psum(jnp.where(r == 0, jnp.stack([keep, got]), jnp.stack([got, keep])), "dp")
        return both[0], both[1]
    y, z = k % 2, k // 2
    piece = scattered(grad.reshape(2, 4, rows // 8, width), y, z)
    cross = [
        (2 * i + j, 2 * (i ^ 1) + (j ^ 1))
        for i in range(lax.axis_size("dp"))
        for j in range(2)
        if i % 2 != j
    ]
    piece = jnp.where(y == r, piece, lax.ppermute(piece, ("dp", "row"), cross))
    mine, other = gathered(piece, y, z)
    mine, other = mine.reshape(rows // 2, width), other.reshape(rows // 2, width)
    return jnp.where(y == 0, mine, other), jnp.where(y == 0, other, mine)


def reduce_cols(grad, r, k):
    rows, width = grad.shape
    if lax.axis_size("dp") != 8:
        keep, send = half_of(r, grad, 1), half_of(1 - r, grad, 1)
        got = row_swap(send)
        both = lax.psum(jnp.where(r == 0, jnp.stack([keep, got]), jnp.stack([got, keep])), "dp")
        return both[0], both[1]
    y, z = k % 2, k // 2
    piece = scattered(grad.reshape(2, 4, rows // 8, width), y, z)
    keep, got = half_of(r, piece, 1), row_swap(half_of(1 - r, piece, 1))
    piece = jnp.where(r == 0, jnp.stack([keep, got]), jnp.stack([got, keep]))
    mine, other = gathered(piece, y, z)
    both = jnp.where(y == 0, jnp.stack([mine, other]), jnp.stack([other, mine]))
    both = both.transpose(2, 0, 1, 3, 4).reshape(2, rows, width // 2)
    return both[0], both[1]


def norm(values):
    center = jnp.mean(values, axis=1, keepdims=True)
    shifted = values - center
    inverse = lax.rsqrt(jnp.mean(shifted * shifted, axis=1, keepdims=True) + 1e-05)
    return shifted * inverse, inverse


def core_sum(left, product, rows):
    other = product(left[rows:]).astype(bf16)
    return product(left[:rows]) + col_swap(other).astype(f32)


def full_sum(left, product, rows):
    low = core_sum(left, product, rows).astype(bf16)
    return low.astype(f32) + row_swap(low).astype(f32)


def half_sum(left, product, rows, r):
    part = core_sum(left, product, rows)
    return half_of(r, part, 1) + row_swap(half_of(1 - r, part, 1).astype(bf16)).astype(f32)


def per_device(
    block_in,
    out_grad,
    seq_lengths,
    ln1_gain,
    ln1_bias,
    qkv_weight,
    qv_bias,
    out_weight,
    out_bias,
    ln2_gain,
    ln2_bias,
    fc_weight,
    fc_bias,
    proj_weight,
    proj_bias,
):
    n_dp = lax.axis_size("dp")
    r, c, k = lax.axis_index("row"), lax.axis_index("col"), lax.axis_index("dp")
    tokens, half = block_in.shape
    heads = 7
    most = heads * HEAD_DIM
    wide = 8 * HEAD_DIM
    spare = 32

    qkv_first, qkv_second = head_slots(c, qkv_weight, 2, most, spare)
    qkv_mine = jnp.where(r == 0, qkv_first, qkv_second)
    qkv_other = jnp.where(r == 0, qkv_second, qkv_first)
    y = k % 2
    parts = qkv_other.reshape(3, 2, half // 2, most)
    got_one = row_swap(lax.dynamic_index_in_dim(parts, y, 1, keepdims=False))
    x_peer = row_swap(block_in)
    got_two = dp_xor(got_one, 1)
    buffer = jnp.zeros((3, 4, half // 2, wide), bf16)
    buffer = put(buffer, pad_to(qkv_mine.reshape(3, 2, half // 2, most), wide, 3), (0, 2 * r))
    buffer = put(buffer, pad_to(got_one, wide, 2)[:, None], (0, 2 * (1 - r) + y))
    buffer = put(buffer, pad_to(got_two, wide, 2)[:, None], (0, 2 * (1 - r) + 1 - y))
    qkv_full = buffer.reshape(3, 2 * half, wide)

    vectors = jnp.stack([ln1_gain, ln1_bias, out_bias, ln2_gain, ln2_bias, proj_bias])
    vectors = ordered(r, vectors, row_swap(vectors), 1).astype(f32)
    gain_one, bias_one, bias_out, gain_two, bias_two = [vectors[i][None] for i in range(5)]

    bias_first, bias_second = head_slots(c, qv_bias, 1, most, spare)
    bias_mine = pad_to(jnp.where(r == 0, bias_first, bias_second).astype(f32), wide, 1)

    out_first, out_second = head_slots(c, out_weight, 0, most, spare)
    out_mine = jnp.where(r == 0, out_first, out_second)
    out_got = row_swap(jnp.where(r == 0, out_second, out_first))
    out_full = pad_to(ordered(r, out_mine, out_got, 1), wide, 0)

    fc_mine, fc_other = half_of(r, fc_weight, 1), half_of(1 - r, fc_weight, 1)
    fc_full = ordered(r, fc_mine, gather_quarters(fc_other, k), 0)
    proj_halves = proj_weight.reshape(2, proj_weight.shape[0] // 2, half)
    proj_mine = lax.dynamic_index_in_dim(proj_halves, r, 0, keepdims=False)
    proj_other = lax.dynamic_index_in_dim(proj_halves, 1 - r, 0, keepdims=False)
    proj_full = ordered(r, proj_mine, gather_quarters(proj_other, k), 1)
    fc_bias_mine = half_of(r, fc_bias, 0).astype(f32)[None]

    lengths = seq_lengths[0]
    group = 2 * tokens
    places = jnp.arange(group, dtype=jnp.int32)
    ends = jnp.cumsum(lengths, dtype=jnp.int32)
    first = jnp.sum(
        jnp.where(ends[None, :] <= places[:, None], lengths[None, :], 0), axis=1, dtype=jnp.int32
    ).reshape(group // BLK, BLK)
    info = jnp.concatenate([(c * (tokens // BLK))[None].astype(jnp.int32), first[:, 0] // BLK])

    x_full = ordered(r, block_in, x_peer, 1).astype(f32)
    normed_one, inverse_one = norm(x_full)
    h_one = (normed_one * gain_one + bias_one).astype(bf16)
    h_one_all = jnp.concatenate([h_one, col_swap(h_one)], axis=0)
    zero_bias = jnp.zeros((1, wide), f32)
    projected = jnp.concatenate(
        [
            (nn(h_one_all, qkv_full[i]) + bias).astype(bf16)
            for i, bias in enumerate((bias_mine[:1], zero_bias, bias_mine[1:]))
        ],
        axis=1,
    )
    attended, log_totals = attend(info, projected, first, heads)
    x_mid = x_full + full_sum(attended, lambda rows: nn(rows, out_full), tokens) + bias_out
    normed_two, inverse_two = norm(x_mid)
    h_two = (normed_two * gain_two + bias_two).astype(bf16)
    h_two_all = jnp.concatenate([h_two, col_swap(h_two)], axis=0)
    pre_act = nn(h_two_all, fc_full) + fc_bias_mine
    cube = pre_act * pre_act
    bend = jnp.tanh(gelu_root * (pre_act + gelu_cubic * cube * pre_act))
    activated = (0.5 * pre_act * (1.0 + bend)).astype(bf16)
    slope = 0.5 * (1.0 + bend) + 0.5 * pre_act * (1.0 - bend * bend) * gelu_root * (
        1.0 + 3.0 * gelu_cubic * cube
    )

    out_grad_full = ordered(r, out_grad, row_swap(out_grad), 1)
    out_grad_all = jnp.concatenate([out_grad_full, col_swap(out_grad_full)], axis=0)
    proj_first, proj_second = reduce_cols(tn(activated, out_grad_all).astype(bf16), r, k)
    pre_grad = (nt(out_grad_all, proj_full) * slope).astype(bf16)
    fc_first, fc_second = reduce_rows(tn(h_two_all, pre_grad).astype(bf16), r, k)
    proj_part = half_sum(activated, lambda rows: nn(rows, proj_full), tokens, r)
    block_out = (half_of(r, x_mid, 1) + proj_part + proj_bias.astype(f32)).astype(bf16)

    h_two_grad = full_sum(pre_grad, lambda rows: nt(rows, fc_full), tokens)
    scaled = h_two_grad * gain_two
    mid_grad = out_grad_full.astype(f32) + inverse_two * (
        scaled
        - jnp.mean(scaled, axis=1, keepdims=True)
        - normed_two * jnp.mean(scaled * normed_two, axis=1, keepdims=True)
    )
    branch_grad = mid_grad.astype(bf16)
    branch_all = jnp.concatenate([branch_grad, col_swap(branch_grad)], axis=0)
    out_first, out_second = reduce_cols(tn(attended, branch_all).astype(bf16)[:most], r, k)

    attended_grad = nt(branch_all, out_full).astype(bf16)
    parts_grad = attend_back(info, projected, attended, attended_grad, log_totals, first, heads)
    qkv_parts = [reduce_rows(tn(h_one_all, part).astype(bf16)[:, :most], r, k) for part in parts_grad]

    def h_one_product(rows):
        return sum(nt(part, qkv_full[i]) for i, part in enumerate(rows))

    other = h_one_product([part[tokens:] for part in parts_grad]).astype(bf16)
    mine = h_one_product([part[:tokens] for part in parts_grad]) + col_swap(other).astype(f32)
    h_one_grad = half_of(r, mine, 1) + row_swap(half_of(1 - r, mine, 1).astype(bf16)).astype(f32)
    normed_half = half_of(r, normed_one, 1)
    scaled = h_one_grad * ln1_gain.astype(f32)[None]
    sums = jnp.stack([jnp.sum(scaled, axis=1), jnp.sum(scaled * normed_half, axis=1)])
    sums = (sums + row_swap(sums)) / D
    x_grad = half_of(r, mid_grad, 1) + inverse_one * (
        scaled - sums[0][:, None] - normed_half * sums[1][:, None]
    )

    h_two_half = half_of(r, h_two_grad, 1)
    own = jnp.stack(
        [
            jnp.sum(h_one_grad * normed_half, axis=0),
            jnp.sum(h_one_grad, axis=0),
            jnp.sum(h_two_half * half_of(r, normed_two, 1), axis=0),
            jnp.sum(h_two_half, axis=0),
            jnp.sum(half_of(r, branch_grad, 1).astype(f32), axis=0),
            jnp.sum(out_grad.astype(f32), axis=0),
        ]
    )
    own = own + col_swap(own)
    fc_bias_grad = jnp.sum(pre_grad.astype(f32), axis=0)
    qv = jnp.stack([jnp.sum(parts_grad[i].astype(f32), axis=0)[:most] for i in (0, 2)])
    pack = jnp.concatenate([own.reshape(-1), fc_bias_grad, qv.reshape(-1)])
    pack = pad_to(pack, -(-pack.shape[0] // 1024) * 1024, 0).reshape(-1, 128)
    if n_dp & (n_dp - 1):
        pack = lax.psum(pack, "dp")
    else:
        mask = 1
        while mask < n_dp:
            pack = pack + dp_xor(pack, mask)
            mask *= 2
    peer = row_swap(pack).reshape(-1)
    pack = pack.reshape(-1)
    own = pack[: 6 * half].reshape(6, half)
    low, high = 6 * half, 6 * half + fc_bias_grad.shape[0]
    fc_bias_grad = ordered(r, pack[low:high], peer[low:high], 0)
    qv_mine, qv_peer = [v[high : high + 2 * most].reshape(2, most) for v in (pack, peer)]
    qv_bias_grad = from_slots(
        c, jnp.where(r == 0, qv_mine, qv_peer), jnp.where(r == 0, qv_peer, qv_mine), 1, spare
    )

    qkv_weight_grad = jnp.stack([from_slots(c, a, b, 1, spare).astype(f32) for a, b in qkv_parts])
    out_weight_grad = from_slots(c, out_first, out_second, 0, spare).astype(f32)
    fc_weight_grad = jnp.concatenate([fc_first, fc_second], axis=1).astype(f32)
    proj_weight_grad = jnp.concatenate([proj_first, proj_second], axis=0).astype(f32)
    return (
        block_out,
        x_grad,
        own[0],
        own[1],
        qkv_weight_grad,
        qv_bias_grad,
        out_weight_grad,
        own[4],
        own[2],
        own[3],
        fc_weight_grad,
        fc_bias_grad,
        proj_weight_grad,
        own[5],
    )


def solution(mesh):
    placed = (
        P(("dp", "col"), "row"),
        P(("dp", "col"), "row"),
        P("dp", None),
        P("row"),
        P("row"),
        P(None, "row", "col"),
        P(None, "col"),
        P("col", "row"),
        P("row"),
        P("row"),
        P("row"),
        P("row", "col"),
        P("col"),
        P("col", "row"),
        P("row"),
    )
    return jax.shard_map(
        per_device,
        mesh=mesh,
        in_specs=placed,
        out_specs=(
            P(("dp", "col"), "row"),
            P(("dp", "col"), "row"),
            P("row"),
            P("row"),
            P(None, "row", "col"),
            P(None, "col"),
            P("col", "row"),
            P("row"),
            P("row"),
            P("row"),
            P("row", "col"),
            P("col"),
            P("col", "row"),
            P("row"),
        ),
        check_vma=False,
    )
```

time: 2510 us -> 1240 us (0.49)
  waiting for transfers between devices: 1540 us -> 566 us
  matrix products: 450 us -> 177 us
  blocking collectives: 180 us -> 0 us
  starting transfers between devices: 11.4 us -> 184 us
  Pallas kernels: 0 us -> 85.8 us
  local copies, waits for them, and re-layouts: 151 us -> 102 us
  other arithmetic: 143 us -> 98.9 us
    reduce_scatter x8 -> x0, waiting for transfers between devices: 683 us -> none  [the longest x4 657 us: sum_rows_of(): lax.psum_scatter(func(jnp.int32(0), lax.axis_size('row') * own_rows), 'ro...]
    ppermute x4 -> x94, waiting for transfers between devices: 102 us -> 566 us  [the longest x58 433 us: dp_xor(): lax.ppermute(value, 'dp', [(i, i ^ mask) for i in range(lax.axis_size('dp...]
    all_gather x8 -> x0, waiting for transfers between devices: 393 us -> none  [the longest x4 366 us: across_rows(): return lax.all_gather(values, 'row', axis=0, tiled=True)]
    psum x1 -> x0, waiting for transfers between devices: 361 us -> none  [per_device(): lax.psum(qkv_weight_grad.astype(jnp.bfloat16), 'dp').astype(jnp.float32)]
    dot_general x187 -> x24, matrix products: 450 us -> 177 us  [the longest x8 70.9 us: nn(): lax.dot_general(a, b, (((1,), (0,)), ((), ())), preferred_element_type=jn...]
    ppermute x4 -> x94, starting transfers between devices: 10.1 us -> 184 us  [the longest x58 159 us: dp_xor(): lax.ppermute(value, 'dp', [(i, i ^ mask) for i in range(lax.axis_size('dp...]
    psum x6 -> x0, blocking collectives: 122 us -> none  [the longest x1 61.9 us: per_device(): lax.psum((ln1_gain_grad, ln1_bias_grad, ln2_gain_grad, ln2_bias_grad), ('...]
    pallas_call x0 -> x2, Pallas kernels: none -> 85.8 us  [the longest x1 43.8 us: attend_back(): pl.pallas_call(functools.partial(attend_back_kernel, heads, blocks), grid...]
  transfers between devices with their start and end apart: 21 -> 94, of which waited for: 16 -> 39; matrix products, arithmetic and copies ran while one was open for 7% -> 26% of each run, Pallas kernels for 0% -> 0%
where the time goes in v1:
time: 1240 us; the launch traced here: 1220 us
  waiting for transfers between devices  566 us (46%)
  starting transfers between devices  184 us (15%)
  matrix products  177 us (14%)
  local copies, waits for them, and re-layouts  102 us (8%)
  other arithmetic  98.9 us (8%)
  Pallas kernels  85.8 us (7%)
    ppermute x58, waiting for transfers between devices, dp_xor(): lax.ppermute(value, 'dp', [(i, i ^ mask) for i in range(lax.axis_size('dp...  433 us
    ppermute x58, starting transfers between devices, dp_xor(): lax.ppermute(value, 'dp', [(i, i ^ mask) for i in range(lax.axis_size('dp...  159 us
    ppermute x15, waiting for transfers between devices, row_swap(): return lax.ppermute(value, 'row', SWAP)  126 us
    dot_general x8, matrix products, nn(): lax.dot_general(a, b, (((1,), (0,)), ((), ())), preferred_element_type=jn...  70.9 us
    dot_general x10, matrix products, nt(): lax.dot_general(a, b, (((1,), (1,)), ((), ())), preferred_element_type=jn...  59.8 us
    dot_general x6, matrix products, tn(): lax.dot_general(a, b, (((0,), (0,)), ((), ())), preferred_element_type=f32)  46.8 us
    pallas_call x1, Pallas kernels, attend_back(): pl.pallas_call(functools.partial(attend_back_kernel, heads, blocks), grid...  43.8 us
    pallas_call x1, Pallas kernels, attend(): pl.pallas_call(functools.partial(attend_kernel, heads, blocks), grid_spec...  42 us
  transfers between devices with their start and end apart: 94, of which 39 were waited for; matrix products, arithmetic and copies ran while one was open for 26% of the time, Pallas kernels for 0%

profile of v1, /device:TPU:0, one launch (start us, length us, event | category | flops | bytes accessed | tf_op | source)
XLA Modules:
  0.0 1217.3 jit_solution(1532621578842788315)
XLA Ops:
  12.0 5.8 fusion.109
  31.5 10.5 collective-permute-done
  53.8 14.6 %collective-permute-done.4 = bf16[3,400,448]{2,1,0:T(8,128)(2,1)} collective-permute-done((bf16[3,400,448]{2,1,0:T(8,128)(2,1)}, bf16[3,400,448]{2,1,0:T(8,128)(2,1)}, u32[]{:S(2)}, u32[]{:S(2)}) %collective-permute-start.4) | collective-permute-done | bytes 1075232 | tf_op jit(solution)/shard_map/ppermute | solution.py:193
  70.9 14.1 %collective-permute-done.8 = bf16[448,800]{1,0:T(8,128)(2,1)S(1)} collective-permute-done((bf16[448,800]{1,0:T(8,128)(2,1)S(1)}, bf16[448,800]{1,0:T(8,128)(2,1)S(1)}, u32[]{:S(2)}, u32[]{:S(2)}) %collective-permute-start.8) | collective-permute-done | bytes 716832 | tf_op jit(solution)/shard_map/ppermute | solution.py:193
  88.1 8.7 collective-permute-done.5
  97.3 7.2 convolution_convert_fusion.5
  104.6 5.5 fusion.16
  110.1 5.5 fusion.15
  118.0 42.0 %attend.1 = (bf16[1536,512]{1,0:T(8,128)(2,1)S(1)}, f32[4,2,1536]{2,1,0:T(2,128)S(1)}) custom-call(s32[7]{0:T(128)S(1)} %pad_add_fusion.info_ref, bf16[1536,1536]{1,0:T(8,128)(2,1)} %pad_maximum_fusion.4.q_ref.k_ref.v_ref, bf16[1536,1536]{1,0:T(8,128)(2,1)} %pad_maximum_fusion.4.q_ref.k_ref.v_ref, bf16[1536,1536]{1,0:T(8,128)(2,1)} %pad_maximum_fusion.4.q_ref.k_ref.v_ref, ...), custom_call_target="tpu_custom_call" | custom-call | flops 11274289152 | bytes 6291456 | tf_op jit(solution)/shard_map/attend/pallas_call | solution.py:84
  163.0 5.0 collective-permute-done.9
  168.0 5.1 add_convert_fusion.3
  173.6 5.2 broadcast_select_fusion.3
  180.4 8.6 copy.102
  199.5 44.3 %collective-permute-done.12 = bf16[200,1600]{1,0:T(8,128)(2,1)S(1)} collective-permute-done((bf16[200,1600]{1,0:T(8,128)(2,1)S(1)}, bf16[200,1600]{1,0:T(8,128)(2,1)S(1)}, u32[]{:S(2)}, u32[]{:S(2)}) %collective-permute-start.12) | collective-permute-done | bytes 640032 | tf_op jit(solution)/shard_map/ppermute | solution.py:193
  245.3 13.9 %collective-permute-done.16 = bf16[400,800]{1,0:T(8,128)(2,1)} collective-permute-done((bf16[400,800]{1,0:T(8,128)(2,1)S(1)}, bf16[400,800]{1,0:T(8,128)(2,1)}, u32[]{:S(2)}, u32[]{:S(2)}) %collective-permute-start.16) | collective-permute-done | bytes 640032 | tf_op jit(solution)/shard_map/ppermute | solution.py:193
  267.4 7.6 fusion.105
  278.9 5.9 collective-permute-done.22
  293.8 26.6 %collective-permute-done.19 = bf16[400,800]{1,0:T(8,128)(2,1)S(1)} collective-permute-done((bf16[400,800]{1,0:T(8,128)(2,1)S(1)}, bf16[400,800]{1,0:T(8,128)(2,1)S(1)}, u32[]{:S(2)}, u32[]{:S(2)}) %collective-permute-start.19) | collective-permute-done | bytes 640032 | tf_op jit(solution)/shard_map/ppermute | solution.py:201
  323.7 20.5 %multiply_convert_fusion.1 = (bf16[1536,1600]{0,1:T(8,128)(2,1)}, f32[1536,1600]{0,1:T(8,128)}) fusion(f32[1600]{0:T(1024)S(1)} %select_convert_fusion.2, bf16[800,1600]{1,0:T(8,128)(2,1)} %bitcast.22, bf16[800,1600]{1,0:T(8,128)(2,1)} %get-tuple-element.105, pred[]{:T(512)S(6)} %eq.20, bf16[768,1600]{0,1:T(8,128)(2,1)} %copy-done.55, ...), kind=kOutput, calls=%fused_computation.5 | convolution fusion | flops 7921766400 | bytes 24787200 | tf_op jit(solution)/shard_map/dot_general | solution.py:18
  344.2 13.0 %convolution_convert_fusion.4 = bf16[768,1600]{0,1:T(8,128)(2,1)} fusion(bf16[1536,1600]{0,1:T(8,128)(2,1)} %get-tuple-element.163, bf16[1600,800]{1,0:T(8,128)(2,1)} %bitcast.31, bf16[1600,800]{1,0:T(8,128)(2,1)} %get-tuple-element.101, pred[]{:T(512)S(6)} %eq.20), kind=kOutput, calls=%fused_computation.49 | convolution fusion | flops 3956428800 | bytes 10649601 | tf_op jit(solution)/shard_map/dot_general | solution.py:18
  357.2 21.3 %convert_reduce_fusion = (f32[1600]{0:T(1024)}, bf16[1536,1600]{0,1:T(8,128)(2,1)}) fusion(f32[1536,1600]{0,1:T(8,128)} %get-tuple-element.164, f32[1600]{0:T(1024)S(1)} %copy-done.50, bf16[768,1600]{0,1:T(8,128)(2,1)} %collective-permute-done.23, bf16[768,1600]{0,1:T(8,128)(2,1)S(1)} %maximum_select_fusion.4, bf16[1600,800]{1,0:T(8,128)(2,1)} %bitcast.31, ...), kind=kOutput, calls=%fused_computation.3 | convolution fusion | flops 7948798464 | bytes 24793600 | tf_op jit(solution)/shard_map/dot_general | solution.py:16
  378.5 11.0 convolution_convert_fusion.3
  390.0 12.1 convolution_convert_fusion.1
  405.5 11.7 convolution_convert_fusion
  421.1 11.1 convert_add_fusion.5
  434.5 8.4 add_convert_fusion.1
  444.0 76.9 %collective-permute-done.85 = bf16[4,200,1600]{2,1,0:T(8,128)(2,1)S(1)} collective-permute-done((bf16[4,200,1600]{2,1,0:T(8,128)(2,1)}, bf16[4,200,1600]{2,1,0:T(8,128)(2,1)S(1)}, u32[]{:S(2)}, u32[]{:S(2)}) %collective-permute-start.85) | collective-permute-done | bytes 2560032 | tf_op jit(solution)/shard_map/ppermute | solution.py:201
  523.7 6.2 collective-permute-start.88
  534.0 11.9 collective-permute-done.88
  549.7 49.5 %collective-permute-done.87 = bf16[200,1600]{1,0:T(8,128)(2,1)S(1)} collective-permute-done((bf16[200,1600]{1,0:T(8,128)(2,1)S(1)}, bf16[200,1600]{1,0:T(8,128)(2,1)S(1)}, u32[]{:S(2)}, u32[]{:S(2)}) %collective-permute-start.87) | collective-permute-done | bytes 640032 | tf_op jit(solution)/shard_map/ppermute | solution.py:201
  599.3 15.2 %collective-permute-start.77 = (bf16[200,1600]{1,0:T(8,128)(2,1)S(1)}, bf16[200,1600]{1,0:T(8,128)(2,1)S(1)}, u32[]{:S(2)}, u32[]{:S(2)}) collective-permute-start(bf16[200,1600]{1,0:T(8,128)(2,1)S(1)} %get-tuple-element.118), channel_id=1, source_target_pairs={{0,8},{4,12},{8,0},{12,4},{16,24},{20,28},{24,16},{28,20},{1,9},{5... | collective-permute-start | bytes 1920008 | tf_op jit(solution)/shard_map/ppermute | solution.py:201
  615.6 24.9 %collective-permute-done.78 = bf16[200,1600]{1,0:T(8,128)(2,1)S(1)} collective-permute-done((bf16[200,1600]{1,0:T(8,128)(2,1)S(1)}, bf16[200,1600]{1,0:T(8,128)(2,1)S(1)}, u32[]{:S(2)}, u32[]{:S(2)}) %collective-permute-start.78) | collective-permute-done | bytes 640032 | tf_op jit(solution)/shard_map/ppermute | solution.py:201
  651.2 24.4 %collective-permute-done.90 = bf16[2,200,800]{2,1,0:T(8,128)(2,1)S(1)} collective-permute-done((bf16[2,200,800]{2,1,0:T(8,128)(2,1)S(1)}, bf16[2,200,800]{2,1,0:T(8,128)(2,1)S(1)}, u32[]{:S(2)}, u32[]{:S(2)}) %collective-permute-start.90) | collective-permute-done | bytes 640032 | tf_op jit(solution)/shard_map/ppermute | solution.py:201
  675.7 17.9 %collective-permute-done.91 = bf16[2,200,800]{2,1,0:T(8,128)(2,1)S(1)} collective-permute-done((bf16[2,200,800]{2,1,0:T(8,128)(2,1)S(1)}, bf16[2,200,800]{2,1,0:T(8,128)(2,1)S(1)}, u32[]{:S(2)}, u32[]{:S(2)}) %collective-permute-start.91) | collective-permute-done | bytes 640032 | tf_op jit(solution)/shard_map/ppermute | solution.py:201
  698.8 5.5 collective-permute-done.81
  704.3 47.4 %collective-permute-done.82 = bf16[200,1600]{1,0:T(8,128)(2,1)S(1)} collective-permute-done((bf16[200,1600]{1,0:T(8,128)(2,1)S(1)}, bf16[200,1600]{1,0:T(8,128)(2,1)S(1)}, u32[]{:S(2)}, u32[]{:S(2)}) %collective-permute-start.82) | collective-permute-done | bytes 640032 | tf_op jit(solution)/shard_map/ppermute | solution.py:201
  766.8 5.0 maximum_convert_fusion
  771.8 12.2 %copy.113 = f32[3200,800]{0,1:T(8,128)} copy(f32[3200,800]{1,0:T(8,128)} %maximum_convert_fusion) | data formatting | bytes 20480000
  784.0 25.7 %collective-permute-done.84 = bf16[4,200,1600]{2,1,0:T(8,128)(2,1)} collective-permute-done((bf16[4,200,1600]{2,1,0:T(8,128)(2,1)S(1)}, bf16[4,200,1600]{2,1,0:T(8,128)(2,1)}, u32[]{:S(2)}, u32[]{:S(2)}) %collective-permute-start.84) | collective-permute-done | bytes 2560032 | tf_op jit(solution)/shard_map/ppermute | solution.py:201
  811.9 5.4 maximum_convert_fusion.1
  817.4 6.7 fusion.14.g_ref
  824.1 43.8 %attend_back.1 = (bf16[1536,512]{1,0:T(8,128)(2,1)S(1)}, bf16[1536,512]{1,0:T(8,128)(2,1)S(1)}, bf16[1536,512]{1,0:T(8,128)(2,1)S(1)}) custom-call(s32[7]{0:T(128)S(1)} %copy-done.5, bf16[1536,1536]{1,0:T(8,128)(2,1)} %pad_maximum_fusion.4.q_ref.k_ref.v_ref, bf16[1536,1536]{1,0:T(8,128)(2,1)} %pad_maximum_fusion.4.q_ref.k_ref.v_ref, ...), custom_call_target="tpu_custom_call" | custom-call | flops 28185722880 | bytes 12582912 | tf_op jit(solution)/shard_map/attend_back/pallas_call | solution.py:163
  875.8 5.5 fusion.101
  890.0 6.0 fusion.102
  903.4 5.5 fusion.103
  916.7 6.0 fusion.11
  932.1 18.4 %collective-permute-start.56 = (bf16[200,448]{1,0:T(8,128)(2,1)S(1)}, bf16[200,448]{1,0:T(8,128)(2,1)S(1)}, u32[]{:S(2)}, u32[]{:S(2)}) collective-permute-start(bf16[200,448]{1,0:T(8,128)(2,1)S(1)} %get-tuple-element.141), channel_id=1, source_target_pairs={{0,16},{4,20},{8,24},{12,28},{16,0},{20,4},{24,8},{28,12},{1,17},{... | collective-permute-start | bytes 537608 | tf_op jit(solution)/shard_map/ppermute | solution.py:201
  951.9 5.7 collective-permute-start.55
  960.3 7.6 collective-permute-start.47
  968.2 14.1 %collective-permute-start.46 = (bf16[200,448]{1,0:T(8,128)(2,1)S(1)}, bf16[200,448]{1,0:T(8,128)(2,1)S(1)}, u32[]{:S(2)}, u32[]{:S(2)}) collective-permute-start(bf16[200,448]{1,0:T(8,128)(2,1)S(1)} %get-tuple-element.138), channel_id=1, source_target_pairs={{0,16},{4,20},{8,24},{12,28},{16,0},{20,4},{24,8},{28,12},{1,17},{... | collective-permute-start | bytes 537608 | tf_op jit(solution)/shard_map/ppermute | solution.py:201
  986.9 18.0 %collective-permute-done.46 = bf16[200,448]{1,0:T(8,128)(2,1)S(1)} collective-permute-done((bf16[200,448]{1,0:T(8,128)(2,1)S(1)}, bf16[200,448]{1,0:T(8,128)(2,1)S(1)}, u32[]{:S(2)}, u32[]{:S(2)}) %collective-permute-start.46) | collective-permute-done | bytes 179232 | tf_op jit(solution)/shard_map/ppermute | solution.py:201
  1008.6 10.8 collective-permute-start.36
  1019.4 6.3 collective-permute-done.68
  1029.5 6.4 collective-permute-start.70
  1053.3 8.9 collective-permute-done.72
  1064.7 9.0 collective-permute-start.49
  1084.3 6.9 collective-permute-start.39
  1100.4 9.6 collective-permute-done.40
  1110.1 5.9 collective-permute-done.74
  1119.7 13.8 %collective-permute-done.62 = bf16[4,200,448]{2,1,0:T(8,128)(2,1)S(1)} collective-permute-done((bf16[4,200,448]{2,1,0:T(8,128)(2,1)S(1)}, bf16[4,200,448]{2,1,0:T(8,128)(2,1)S(1)}, u32[]{:S(2)}, u32[]{:S(2)}) %collective-permute-start.62) | collective-permute-done | bytes 716832 | tf_op jit(solution)/shard_map/ppermute | solution.py:201
  1133.8 17.2 %collective-permute-done.52 = bf16[4,200,448]{2,1,0:T(8,128)(2,1)S(1)} collective-permute-done((bf16[4,200,448]{2,1,0:T(8,128)(2,1)S(1)}, bf16[4,200,448]{2,1,0:T(8,128)(2,1)S(1)}, u32[]{:S(2)}, u32[]{:S(2)}) %collective-permute-start.52) | collective-permute-done | bytes 716832 | tf_op jit(solution)/shard_map/ppermute | solution.py:201
  1151.4 11.6 collective-permute-done.42
  1177.2 15.8 %collective-permute-done.28 = bf16[768,800]{0,1:T(8,128)(2,1)S(1)} collective-permute-done((bf16[768,800]{0,1:T(8,128)(2,1)S(1)}, bf16[768,800]{0,1:T(8,128)(2,1)S(1)}, u32[]{:S(2)}, u32[]{:S(2)}) %collective-permute-start.28) | collective-permute-done | bytes 1228832 | tf_op jit(solution)/shard_map/ppermute | solution.py:193
  1205.8 5.3 fusion.21
  (487 shorter events, 276.4 us)
Async XLA Ops:
  9.3 42.6 %collective-permute-start.7 = (bf16[32,800]{1,0:T(8,128)(2,1)}, bf16[32,800]{1,0:T(8,128)(2,1)}, u32[]{:S(2)}, u32[]{:S(2)}) collective-permute-start(bf16[32,800]{1,0:T(8,128)(2,1)} %slice.372), channel_id=1, source_target_pairs={{0,1},{1,0},{2,3},{3,2},{4,5},{5,4},{6,7},{7,6},{8,9},{9,8},{10,11... | collective-permute-start | bytes 153608 | tf_op jit(solution)/shard_map/ppermute | solution.py:197
  11.9 58.1 %collective-permute-start.6 = (bf16[2,32]{1,0:T(2,128)(2,1)S(1)}, bf16[2,32]{1,0:T(2,128)(2,1)S(1)}, u32[]{:S(2)}, u32[]{:S(2)}) collective-permute-start(bf16[2,32]{1,0:T(2,128)(2,1)S(1)} %slice.362), channel_id=1, source_target_pairs={{0,1},{1,0},{2,3},{3,2},{4,5},{5,4},{6,7},{7,6},{8,9},{9,8},{10,11... | collective-permute-start | bytes 392 | tf_op jit(solution)/shard_map/ppermute | solution.py:197
  11.9 30.1 %collective-permute-start = (bf16[768,800]{0,1:T(8,128)(2,1)}, bf16[768,800]{0,1:T(8,128)(2,1)S(1)}, u32[]{:S(2)}, u32[]{:S(2)}) collective-permute-start(bf16[768,800]{0,1:T(8,128)(2,1)} %param.15), channel_id=1, source_target_pairs={{0,2},{2,0},{1,3},{3,1},{4,6},{6,4},{5,7},{7,5},{8,10},{10,8},{9,1... | collective-permute-start | bytes 3686408 | tf_op jit(solution)/shard_map/ppermute | solution.py:193
  29.5 38.9 %collective-permute-start.4 = (bf16[3,400,448]{2,1,0:T(8,128)(2,1)}, bf16[3,400,448]{2,1,0:T(8,128)(2,1)}, u32[]{:S(2)}, u32[]{:S(2)}) collective-permute-start(bf16[3,400,448]{2,1,0:T(8,128)(2,1)} %dynamic-slice_bitcast_fusion.3), channel_id=1, source_target_pairs={{0,2},{2,0},{1,3},{3,1},{4,6},{6,4},{5,7},{7,5},{8,10},{10,8},{9,1... | collective-permute-start | bytes 3225608 | tf_op jit(solution)/shard_map/ppermute | solution.py:193
  48.9 48.4 %collective-permute-start.2 = (bf16[768,1600]{0,1:T(8,128)(2,1)}, bf16[768,1600]{0,1:T(8,128)(2,1)}, u32[]{:S(2)}, u32[]{:S(2)}) collective-permute-start(bf16[768,1600]{0,1:T(8,128)(2,1)} %get-tuple-element.122), channel_id=1, source_target_pairs={{0,1},{1,0},{2,3},{3,2},{4,5},{5,4},{6,7},{7,6},{8,9},{9,8},{10,11... | collective-permute-start | bytes 7372808 | tf_op jit(solution)/shard_map/ppermute | solution.py:197
  53.6 31.4 %collective-permute-start.8 = (bf16[448,800]{1,0:T(8,128)(2,1)S(1)}, bf16[448,800]{1,0:T(8,128)(2,1)S(1)}, u32[]{:S(2)}, u32[]{:S(2)}) collective-permute-start(bf16[448,800]{1,0:T(8,128)(2,1)S(1)} %get-tuple-element.114), channel_id=1, source_target_pairs={{0,2},{2,0},{1,3},{3,1},{4,6},{6,4},{5,7},{7,5},{8,10},{10,8},{9,1... | collective-permute-start | bytes 2150408 | tf_op jit(solution)/shard_map/ppermute | solution.py:193
  68.4 28.3 %collective-permute-start.5 = (bf16[3,400,448]{2,1,0:T(8,128)(2,1)}, bf16[3,400,448]{2,1,0:T(8,128)(2,1)S(1)}, u32[]{:S(2)}, u32[]{:S(2)}) collective-permute-start(bf16[3,400,448]{2,1,0:T(8,128)(2,1)} %collective-permute-done.4), channel_id=1, source_target_pairs={{0,4},{4,0},{8,12},{12,8},{16,20},{20,16},{24,28},{28,24},{1,5},{5... | collective-permute-start | bytes 3225608 | tf_op jit(solution)/shard_map/ppermute | solution.py:201
  173.1 94.2 %collective-permute-start.10 = (bf16[768,1600]{0,1:T(8,128)(2,1)}, bf16[768,1600]{0,1:T(8,128)(2,1)}, u32[]{:S(2)}, u32[]{:S(2)}) collective-permute-start(bf16[768,1600]{0,1:T(8,128)(2,1)} %add_convert_fusion.3), channel_id=1, source_target_pairs={{0,2},{2,0},{1,3},{3,1},{4,6},{6,4},{5,7},{7,5},{8,10},{10,8},{9,1... | collective-permute-start | bytes 7372808 | tf_op jit(solution)/shard_map/ppermute | solution.py:193
  178.8 65.0 %collective-permute-start.12 = (bf16[200,1600]{1,0:T(8,128)(2,1)S(1)}, bf16[200,1600]{1,0:T(8,128)(2,1)S(1)}, u32[]{:S(2)}, u32[]{:S(2)}) collective-permute-start(bf16[200,1600]{1,0:T(8,128)(2,1)S(1)} %dynamic-slice_bitcast_fusion.15), channel_id=1, source_target_pairs={{0,2},{2,0},{1,3},{3,1},{4,6},{6,4},{5,7},{7,5},{8,10},{10,8},{9,1... | collective-permute-start | bytes 1920008 | tf_op jit(solution)/shard_map/ppermute | solution.py:193
  194.0 65.3 %collective-permute-start.16 = (bf16[400,800]{1,0:T(8,128)(2,1)S(1)}, bf16[400,800]{1,0:T(8,128)(2,1)}, u32[]{:S(2)}, u32[]{:S(2)}) collective-permute-start(bf16[400,800]{1,0:T(8,128)(2,1)S(1)} %dynamic-slice_bitcast_fusion.8), channel_id=1, source_target_pairs={{0,2},{2,0},{1,3},{3,1},{4,6},{6,4},{5,7},{7,5},{8,10},{10,8},{9,1... | collective-permute-start | bytes 1920008 | tf_op jit(solution)/shard_map/ppermute | solution.py:193
  194.5 90.3 %collective-permute-start.22 = (bf16[768,800]{0,1:T(8,128)(2,1)}, bf16[768,800]{0,1:T(8,128)(2,1)}, u32[]{:S(2)}, u32[]{:S(2)}) collective-permute-start(bf16[768,800]{0,1:T(8,128)(2,1)} %param.16), channel_id=1, source_target_pairs={{0,2},{2,0},{1,3},{3,1},{4,6},{6,4},{5,7},{7,5},{8,10},{10,8},{9,1... | collective-permute-start | bytes 3686408 | tf_op jit(solution)/shard_map/ppermute | solution.py:193
  243.8 47.2 %collective-permute-start.13 = (bf16[200,1600]{1,0:T(8,128)(2,1)S(1)}, bf16[200,1600]{1,0:T(8,128)(2,1)S(1)}, u32[]{:S(2)}, u32[]{:S(2)}) collective-permute-start(bf16[200,1600]{1,0:T(8,128)(2,1)S(1)} %collective-permute-done.12), channel_id=1, source_target_pairs={{0,4},{4,0},{8,12},{12,8},{16,20},{20,16},{24,28},{28,24},{1,5},{5... | collective-permute-start | bytes 1920008 | tf_op jit(solution)/shard_map/ppermute | solution.py:201
  245.3 42.2 %collective-permute-start.14 = (bf16[200,1600]{1,0:T(8,128)(2,1)S(1)}, bf16[200,1600]{1,0:T(8,128)(2,1)S(1)}, u32[]{:S(2)}, u32[]{:S(2)}) collective-permute-start(bf16[200,1600]{1,0:T(8,128)(2,1)S(1)} %collective-permute-done.12), channel_id=1, source_target_pairs={{0,8},{4,12},{8,0},{12,4},{16,24},{20,28},{24,16},{28,20},{1,9},{5... | collective-permute-start | bytes 1920008 | tf_op jit(solution)/shard_map/ppermute | solution.py:201
  259.3 28.8 %collective-permute-start.17 = (bf16[400,800]{1,0:T(8,128)(2,1)}, bf16[400,800]{1,0:T(8,128)(2,1)S(1)}, u32[]{:S(2)}, u32[]{:S(2)}) collective-permute-start(bf16[400,800]{1,0:T(8,128)(2,1)} %collective-permute-done.16), channel_id=1, source_target_pairs={{0,4},{4,0},{8,12},{12,8},{16,20},{20,16},{24,28},{28,24},{1,5},{5... | collective-permute-start | bytes 1920008 | tf_op jit(solution)/shard_map/ppermute | solution.py:201
  267.4 22.2 %collective-permute-start.18 = (bf16[400,800]{1,0:T(8,128)(2,1)}, bf16[400,800]{1,0:T(8,128)(2,1)S(1)}, u32[]{:S(2)}, u32[]{:S(2)}) collective-permute-start(bf16[400,800]{1,0:T(8,128)(2,1)} %collective-permute-done.16), channel_id=1, source_target_pairs={{0,8},{4,12},{8,0},{12,4},{16,24},{20,28},{24,16},{28,20},{1,9},{5... | collective-permute-start | bytes 1920008 | tf_op jit(solution)/shard_map/ppermute | solution.py:201
  284.8 37.4 %collective-permute-start.11 = (bf16[768,1600]{0,1:T(8,128)(2,1)S(1)}, bf16[768,1600]{0,1:T(8,128)(2,1)S(1)}, u32[]{:S(2)}, u32[]{:S(2)}) collective-permute-start(bf16[768,1600]{0,1:T(8,128)(2,1)S(1)} %get-tuple-element.93), channel_id=1, source_target_pairs={{0,1},{1,0},{2,3},{3,2},{4,5},{5,4},{6,7},{7,6},{8,9},{9,8},{10,11... | collective-permute-start | bytes 7372808 | tf_op jit(solution)/shard_map/ppermute | solution.py:197
  287.5 69.7 %collective-permute-start.23 = (bf16[768,1600]{0,1:T(8,128)(2,1)S(1)}, bf16[768,1600]{0,1:T(8,128)(2,1)}, u32[]{:S(2)}, u32[]{:S(2)}) collective-permute-start(bf16[768,1600]{0,1:T(8,128)(2,1)S(1)} %maximum_select_fusion.4), channel_id=1, source_target_pairs={{0,1},{1,0},{2,3},{3,2},{4,5},{5,4},{6,7},{7,6},{8,9},{9,8},{10,11... | collective-permute-start | bytes 7372808 | tf_op jit(solution)/shard_map/ppermute | solution.py:197
  288.1 33.2 %collective-permute-start.15 = (bf16[200,1600]{1,0:T(8,128)(2,1)S(1)}, bf16[200,1600]{1,0:T(8,128)(2,1)S(1)}, u32[]{:S(2)}, u32[]{:S(2)}) collective-permute-start(bf16[200,1600]{1,0:T(8,128)(2,1)S(1)} %collective-permute-done.14), channel_id=1, source_target_pairs={{0,4},{4,0},{8,12},{12,8},{16,20},{20,16},{24,28},{28,24},{1,5},{5... | collective-permute-start | bytes 1920008 | tf_op jit(solution)/shard_map/ppermute | solution.py:201
  289.6 30.8 %collective-permute-start.19 = (bf16[400,800]{1,0:T(8,128)(2,1)S(1)}, bf16[400,800]{1,0:T(8,128)(2,1)S(1)}, u32[]{:S(2)}, u32[]{:S(2)}) collective-permute-start(bf16[400,800]{1,0:T(8,128)(2,1)S(1)} %collective-permute-done.18), channel_id=1, source_target_pairs={{0,4},{4,0},{8,12},{12,8},{16,20},{20,16},{24,28},{28,24},{1,5},{5... | collective-permute-start | bytes 1920008 | tf_op jit(solution)/shard_map/ppermute | solution.py:201
  357.2 63.7 %collective-permute-start.20 = (bf16[768,1600]{0,1:T(8,128)(2,1)}, bf16[768,1600]{0,1:T(8,128)(2,1)}, u32[]{:S(2)}, u32[]{:S(2)}) collective-permute-start(bf16[768,1600]{0,1:T(8,128)(2,1)} %convolution_convert_fusion.4), channel_id=1, source_target_pairs={{0,1},{1,0},{2,3},{3,2},{4,5},{5,4},{6,7},{7,6},{8,9},{9,8},{10,11... | collective-permute-start | bytes 7372808 | tf_op jit(solution)/shard_map/ppermute | solution.py:197
  389.5 44.6 %collective-permute-start.24 = (bf16[768,1600]{0,1:T(8,128)(2,1)}, bf16[768,1600]{0,1:T(8,128)(2,1)S(1)}, u32[]{:S(2)}, u32[]{:S(2)}) collective-permute-start(bf16[768,1600]{0,1:T(8,128)(2,1)} %convolution_convert_fusion.3), channel_id=1, source_target_pairs={{0,1},{1,0},{2,3},{3,2},{4,5},{5,4},{6,7},{7,6},{8,9},{9,8},{10,11... | collective-permute-start | bytes 7372808 | tf_op jit(solution)/shard_map/ppermute | solution.py:197
  404.0 126.0 %collective-permute-start.76 = (bf16[4,200,1600]{2,1,0:T(8,128)(2,1)}, bf16[4,200,1600]{2,1,0:T(8,128)(2,1)}, u32[]{:S(2)}, u32[]{:S(2)}) collective-permute-start(bf16[4,200,1600]{2,1,0:T(8,128)(2,1)} %dynamic-slice_bitcast_fusion.2), channel_id=1, source_target_pairs={{0,4},{4,0},{8,12},{12,8},{16,20},{20,16},{24,28},{28,24},{1,5},{5... | collective-permute-start | bytes 7680008 | tf_op jit(solution)/shard_map/ppermute | solution.py:201
  418.9 102.0 %collective-permute-start.85 = (bf16[4,200,1600]{2,1,0:T(8,128)(2,1)}, bf16[4,200,1600]{2,1,0:T(8,128)(2,1)S(1)}, u32[]{:S(2)}, u32[]{:S(2)}) collective-permute-start(bf16[4,200,1600]{2,1,0:T(8,128)(2,1)} %dynamic-slice_bitcast_fusion.1), channel_id=1, source_target_pairs={{0,4},{4,0},{8,12},{12,8},{16,20},{20,16},{24,28},{28,24},{1,5},{5... | collective-permute-start | bytes 7680008 | tf_op jit(solution)/shard_map/ppermute | solution.py:201
  433.5 212.7 %collective-permute-start.21 = (bf16[768,800]{0,1:T(8,128)(2,1)}, bf16[768,800]{0,1:T(8,128)(2,1)}, u32[]{:S(2)}, u32[]{:S(2)}) collective-permute-start(bf16[768,800]{0,1:T(8,128)(2,1)} %select_convert_fusion.1), channel_id=1, source_target_pairs={{0,2},{2,0},{1,3},{3,1},{4,6},{6,4},{5,7},{7,5},{8,10},{10,8},{9,1... | collective-permute-start | bytes 3686408 | tf_op jit(solution)/shard_map/ppermute | solution.py:193
  442.8 311.6 %collective-permute-start.25 = (bf16[768,1600]{0,1:T(8,128)(2,1)S(1)}, bf16[768,1600]{0,1:T(8,128)(2,1)S(1)}, u32[]{:S(2)}, u32[]{:S(2)}) collective-permute-start(bf16[768,1600]{0,1:T(8,128)(2,1)S(1)} %add_convert_fusion.1), channel_id=1, source_target_pairs={{0,2},{2,0},{1,3},{3,1},{4,6},{6,4},{5,7},{7,5},{8,10},{10,8},{9,1... | collective-permute-start | bytes 7372808 | tf_op jit(solution)/shard_map/ppermute | solution.py:193
  523.7 22.2 %collective-permute-start.88 = (bf16[200,1600]{1,0:T(8,128)(2,1)S(1)}, bf16[200,1600]{1,0:T(8,128)(2,1)S(1)}, u32[]{:S(2)}, u32[]{:S(2)}) collective-permute-start(bf16[200,1600]{1,0:T(8,128)(2,1)S(1)} %get-tuple-element.116), channel_id=1, source_target_pairs={{0,24},{4,28},{8,16},{12,20},{16,8},{20,12},{24,0},{28,4},{1,25},{... | collective-permute-start | bytes 1920008 | tf_op jit(solution)/shard_map/ppermute | solution.py:201
  529.9 69.3 %collective-permute-start.87 = (bf16[200,1600]{1,0:T(8,128)(2,1)S(1)}, bf16[200,1600]{1,0:T(8,128)(2,1)S(1)}, u32[]{:S(2)}, u32[]{:S(2)}) collective-permute-start(bf16[200,1600]{1,0:T(8,128)(2,1)S(1)} %get-tuple-element.117), channel_id=1, source_target_pairs={{0,16},{4,20},{8,24},{12,28},{16,0},{20,4},{24,8},{28,12},{1,17},{... | collective-permute-start | bytes 1920008 | tf_op jit(solution)/shard_map/ppermute | solution.py:201
  529.9 69.3 %collective-permute-start.86 = (bf16[200,1600]{1,0:T(8,128)(2,1)S(1)}, bf16[200,1600]{1,0:T(8,128)(2,1)S(1)}, u32[]{:S(2)}, u32[]{:S(2)}) collective-permute-start(bf16[200,1600]{1,0:T(8,128)(2,1)S(1)} %get-tuple-element.115), channel_id=1, source_target_pairs={{0,8},{4,12},{8,0},{12,4},{16,24},{20,28},{24,16},{28,20},{1,9},{5... | collective-permute-start | bytes 1920008 | tf_op jit(solution)/shard_map/ppermute | solution.py:201
  545.9 69.1 %collective-permute-start.79 = (bf16[200,1600]{1,0:T(8,128)(2,1)S(1)}, bf16[200,1600]{1,0:T(8,128)(2,1)S(1)}, u32[]{:S(2)}, u32[]{:S(2)}) collective-permute-start(bf16[200,1600]{1,0:T(8,128)(2,1)S(1)} %get-tuple-element.119), channel_id=1, source_target_pairs={{0,24},{4,28},{8,16},{12,20},{16,8},{20,12},{24,0},{28,4},{1,25},{... | collective-permute-start | bytes 1920008 | tf_op jit(solution)/shard_map/ppermute | solution.py:201
  599.3 41.2 %collective-permute-start.78 = (bf16[200,1600]{1,0:T(8,128)(2,1)S(1)}, bf16[200,1600]{1,0:T(8,128)(2,1)S(1)}, u32[]{:S(2)}, u32[]{:S(2)}) collective-permute-start(bf16[200,1600]{1,0:T(8,128)(2,1)S(1)} %get-tuple-element.120), channel_id=1, source_target_pairs={{0,16},{4,20},{8,24},{12,28},{16,0},{20,4},{24,8},{28,12},{1,17},{... | collective-permute-start | bytes 1920008 | tf_op jit(solution)/shard_map/ppermute | solution.py:201
  599.3 41.2 %collective-permute-start.77 = (bf16[200,1600]{1,0:T(8,128)(2,1)S(1)}, bf16[200,1600]{1,0:T(8,128)(2,1)S(1)}, u32[]{:S(2)}, u32[]{:S(2)}) collective-permute-start(bf16[200,1600]{1,0:T(8,128)(2,1)S(1)} %get-tuple-element.118), channel_id=1, source_target_pairs={{0,8},{4,12},{8,0},{12,4},{16,24},{20,28},{24,16},{28,20},{1,9},{5... | collective-permute-start | bytes 1920008 | tf_op jit(solution)/shard_map/ppermute | solution.py:201
  615.0 27.3 %collective-permute-start.89 = (bf16[200,800]{1,0:T(8,128)(2,1)S(1)}, bf16[200,800]{1,0:T(8,128)(2,1)S(1)}, u32[]{:S(2)}, u32[]{:S(2)}) collective-permute-start(bf16[200,800]{1,0:T(8,128)(2,1)S(1)} %get-tuple-element.147), channel_id=1, source_target_pairs={{0,2},{2,0},{1,3},{3,1},{4,6},{6,4},{5,7},{7,5},{8,10},{10,8},{9,1... | collective-permute-start | bytes 960008 | tf_op jit(solution)/shard_map/ppermute | solution.py:193
  642.6 33.0 %collective-permute-start.90 = (bf16[2,200,800]{2,1,0:T(8,128)(2,1)S(1)}, bf16[2,200,800]{2,1,0:T(8,128)(2,1)S(1)}, u32[]{:S(2)}, u32[]{:S(2)}) collective-permute-start(bf16[2,200,800]{2,1,0:T(8,128)(2,1)S(1)} %maximum_select_fusion.12), channel_id=1, source_target_pairs={{0,8},{4,12},{8,0},{12,4},{16,24},{20,28},{24,16},{28,20},{1,9},{5... | collective-permute-start | bytes 1920008 | tf_op jit(solution)/shard_map/ppermute | solution.py:201
  642.7 50.9 %collective-permute-start.91 = (bf16[2,200,800]{2,1,0:T(8,128)(2,1)S(1)}, bf16[2,200,800]{2,1,0:T(8,128)(2,1)S(1)}, u32[]{:S(2)}, u32[]{:S(2)}) collective-permute-start(bf16[2,200,800]{2,1,0:T(8,128)(2,1)S(1)} %maximum_select_fusion.12), channel_id=1, source_target_pairs={{0,16},{4,20},{8,24},{12,28},{16,0},{20,4},{24,8},{28,12},{1,17},{... | collective-permute-start | bytes 1920008 | tf_op jit(solution)/shard_map/ppermute | solution.py:201
  646.3 49.8 %collective-permute-start.92 = (bf16[2,200,800]{2,1,0:T(8,128)(2,1)S(1)}, bf16[2,200,800]{2,1,0:T(8,128)(2,1)S(1)}, u32[]{:S(2)}, u32[]{:S(2)}) collective-permute-start(bf16[2,200,800]{2,1,0:T(8,128)(2,1)S(1)} %maximum_select_fusion.12), channel_id=1, source_target_pairs={{0,24},{4,28},{8,16},{12,20},{16,8},{20,12},{24,0},{28,4},{1,25},{... | collective-permute-start | bytes 1920008 | tf_op jit(solution)/shard_map/ppermute | solution.py:201
  651.1 53.1 %collective-permute-start.81 = (bf16[200,1600]{1,0:T(8,128)(2,1)S(1)}, bf16[200,1600]{1,0:T(8,128)(2,1)S(1)}, u32[]{:S(2)}, u32[]{:S(2)}) collective-permute-start(bf16[200,1600]{1,0:T(8,128)(2,1)S(1)} %get-tuple-element.82), channel_id=1, source_target_pairs={{0,8},{4,12},{8,0},{12,4},{16,24},{20,28},{24,16},{28,20},{1,9},{5... | collective-permute-start | bytes 1920008 | tf_op jit(solution)/shard_map/ppermute | solution.py:201
  675.6 76.2 %collective-permute-start.82 = (bf16[200,1600]{1,0:T(8,128)(2,1)S(1)}, bf16[200,1600]{1,0:T(8,128)(2,1)S(1)}, u32[]{:S(2)}, u32[]{:S(2)}) collective-permute-start(bf16[200,1600]{1,0:T(8,128)(2,1)S(1)} %get-tuple-element.82), channel_id=1, source_target_pairs={{0,16},{4,20},{8,24},{12,28},{16,0},{20,4},{24,8},{28,12},{1,17},{... | collective-permute-start | bytes 1920008 | tf_op jit(solution)/shard_map/ppermute | solution.py:201
  693.6 58.2 %collective-permute-start.83 = (bf16[200,1600]{1,0:T(8,128)(2,1)S(1)}, bf16[200,1600]{1,0:T(8,128)(2,1)S(1)}, u32[]{:S(2)}, u32[]{:S(2)}) collective-permute-start(bf16[200,1600]{1,0:T(8,128)(2,1)S(1)} %get-tuple-element.82), channel_id=1, source_target_pairs={{0,24},{4,28},{8,16},{12,20},{16,8},{20,12},{24,0},{28,4},{1,25},{... | collective-permute-start | bytes 1920008 | tf_op jit(solution)/shard_map/ppermute | solution.py:201
  696.3 68.7 %collective-permute-start.93 = (bf16[4,2,200,800]{3,2,0,1:T(8,128)(2,1)S(1)}, bf16[4,2,200,800]{3,2,0,1:T(8,128)(2,1)S(1)}, u32[]{:S(2)}, u32[]{:S(2)}) collective-permute-start(bf16[4,2,200,800]{3,2,0,1:T(8,128)(2,1)S(1)} %bitcast_dynamic-update-slice_fusion.4), channel_id=1, source_target_pairs={{0,4},{4,0},{8,12},{12,8},{16,20},{20,16},{24,28},{28,24},{1,5},{5... | collective-permute-start | bytes 7680008 | tf_op jit(solution)/shard_map/ppermute | solution.py:201
  751.9 57.8 %collective-permute-start.84 = (bf16[4,200,1600]{2,1,0:T(8,128)(2,1)S(1)}, bf16[4,200,1600]{2,1,0:T(8,128)(2,1)}, u32[]{:S(2)}, u32[]{:S(2)}) collective-permute-start(bf16[4,200,1600]{2,1,0:T(8,128)(2,1)S(1)} %bitcast_dynamic-update-slice_fusion.9), channel_id=1, source_target_pairs={{0,4},{4,0},{8,12},{12,8},{16,20},{20,16},{24,28},{28,24},{1,5},{5... | collective-permute-start | bytes 7680008 | tf_op jit(solution)/shard_map/ppermute | solution.py:201
  760.3 57.0 %collective-permute-start.26 = (bf16[768,1600]{0,1:T(8,128)(2,1)}, bf16[768,1600]{0,1:T(8,128)(2,1)}, u32[]{:S(2)}, u32[]{:S(2)}) collective-permute-start(bf16[768,1600]{0,1:T(8,128)(2,1)} %get-tuple-element.91), channel_id=1, source_target_pairs={{0,1},{1,0},{2,3},{3,2},{4,5},{5,4},{6,7},{7,6},{8,9},{9,8},{10,11... | collective-permute-start | bytes 7372808 | tf_op jit(solution)/shard_map/ppermute | solution.py:197
  875.8 287.8 %collective-permute-start.27 = (bf16[768,1600]{0,1:T(8,128)(2,1)}, bf16[768,1600]{0,1:T(8,128)(2,1)}, u32[]{:S(2)}, u32[]{:S(2)}) collective-permute-start(bf16[768,1600]{0,1:T(8,128)(2,1)} %add_convert_fusion), channel_id=1, source_target_pairs={{0,1},{1,0},{2,3},{3,2},{4,5},{5,4},{6,7},{7,6},{8,9},{9,8},{10,11... | collective-permute-start | bytes 7372808 | tf_op jit(solution)/shard_map/ppermute | solution.py:197
  888.3 38.8 %collective-permute-start.54 = (bf16[4,200,448]{2,1,0:T(8,128)(2,1)}, bf16[4,200,448]{2,1,0:T(8,128)(2,1)}, u32[]{:S(2)}, u32[]{:S(2)}) collective-permute-start(bf16[4,200,448]{2,1,0:T(8,128)(2,1)} %dynamic-slice_bitcast_fusion.4), channel_id=1, source_target_pairs={{0,4},{4,0},{8,12},{12,8},{16,20},{20,16},{24,28},{28,24},{1,5},{5... | collective-permute-start | bytes 2150408 | tf_op jit(solution)/shard_map/ppermute | solution.py:201
  903.1 29.0 %collective-permute-start.44 = (bf16[4,200,448]{2,1,0:T(8,128)(2,1)}, bf16[4,200,448]{2,1,0:T(8,128)(2,1)}, u32[]{:S(2)}, u32[]{:S(2)}) collective-permute-start(bf16[4,200,448]{2,1,0:T(8,128)(2,1)} %dynamic-slice_bitcast_fusion.5), channel_id=1, source_target_pairs={{0,4},{4,0},{8,12},{12,8},{16,20},{20,16},{24,28},{28,24},{1,5},{5... | collective-permute-start | bytes 2150408 | tf_op jit(solution)/shard_map/ppermute | solution.py:201
  914.9 37.0 %collective-permute-start.34 = (bf16[4,200,448]{2,1,0:T(8,128)(2,1)S(1)}, bf16[4,200,448]{2,1,0:T(8,128)(2,1)S(1)}, u32[]{:S(2)}, u32[]{:S(2)}) collective-permute-start(bf16[4,200,448]{2,1,0:T(8,128)(2,1)S(1)} %dynamic-slice_bitcast_fusion.6), channel_id=1, source_target_pairs={{0,4},{4,0},{8,12},{12,8},{16,20},{20,16},{24,28},{28,24},{1,5},{5... | collective-permute-start | bytes 2150408 | tf_op jit(solution)/shard_map/ppermute | solution.py:201
  922.9 37.4 %collective-permute-start.66 = (bf16[4,56,1600]{2,1,0:T(8,128)(2,1)S(1)}, bf16[4,56,1600]{2,1,0:T(8,128)(2,1)S(1)}, u32[]{:S(2)}, u32[]{:S(2)}) collective-permute-start(bf16[4,56,1600]{2,1,0:T(8,128)(2,1)S(1)} %dynamic-slice_bitcast_fusion.7), channel_id=1, source_target_pairs={{0,4},{4,0},{8,12},{12,8},{16,20},{20,16},{24,28},{28,24},{1,5},{5... | collective-permute-start | bytes 2150408 | tf_op jit(solution)/shard_map/ppermute | solution.py:201
  928.7 39.5 %collective-permute-start.57 = (bf16[200,448]{1,0:T(8,128)(2,1)S(1)}, bf16[200,448]{1,0:T(8,128)(2,1)S(1)}, u32[]{:S(2)}, u32[]{:S(2)}) collective-permute-start(bf16[200,448]{1,0:T(8,128)(2,1)S(1)} %get-tuple-element.140), channel_id=1, source_target_pairs={{0,24},{4,28},{8,16},{12,20},{16,8},{20,12},{24,0},{28,4},{1,25},{... | collective-permute-start | bytes 537608 | tf_op jit(solution)/shard_map/ppermute | solution.py:201
  932.1 50.1 %collective-permute-start.56 = (bf16[200,448]{1,0:T(8,128)(2,1)S(1)}, bf16[200,448]{1,0:T(8,128)(2,1)S(1)}, u32[]{:S(2)}, u32[]{:S(2)}) collective-permute-start(bf16[200,448]{1,0:T(8,128)(2,1)S(1)} %get-tuple-element.141), channel_id=1, source_target_pairs={{0,16},{4,20},{8,24},{12,28},{16,0},{20,4},{24,8},{28,12},{1,17},{... | collective-permute-start | bytes 537608 | tf_op jit(solution)/shard_map/ppermute | solution.py:201
  951.9 31.0 %collective-permute-start.55 = (bf16[200,448]{1,0:T(8,128)(2,1)S(1)}, bf16[200,448]{1,0:T(8,128)(2,1)S(1)}, u32[]{:S(2)}, u32[]{:S(2)}) collective-permute-start(bf16[200,448]{1,0:T(8,128)(2,1)S(1)} %get-tuple-element.139), channel_id=1, source_target_pairs={{0,8},{4,12},{8,0},{12,4},{16,24},{20,28},{24,16},{28,20},{1,9},{5... | collective-permute-start | bytes 537608 | tf_op jit(solution)/shard_map/ppermute | solution.py:201
  960.3 25.1 %collective-permute-start.47 = (bf16[200,448]{1,0:T(8,128)(2,1)S(1)}, bf16[200,448]{1,0:T(8,128)(2,1)S(1)}, u32[]{:S(2)}, u32[]{:S(2)}) collective-permute-start(bf16[200,448]{1,0:T(8,128)(2,1)S(1)} %get-tuple-element.137), channel_id=1, source_target_pairs={{0,24},{4,28},{8,16},{12,20},{16,8},{20,12},{24,0},{28,4},{1,25},{... | collective-permute-start | bytes 537608 | tf_op jit(solution)/shard_map/ppermute | solution.py:201
  968.2 36.7 %collective-permute-start.46 = (bf16[200,448]{1,0:T(8,128)(2,1)S(1)}, bf16[200,448]{1,0:T(8,128)(2,1)S(1)}, u32[]{:S(2)}, u32[]{:S(2)}) collective-permute-start(bf16[200,448]{1,0:T(8,128)(2,1)S(1)} %get-tuple-element.138), channel_id=1, source_target_pairs={{0,16},{4,20},{8,24},{12,28},{16,0},{20,4},{24,8},{28,12},{1,17},{... | collective-permute-start | bytes 537608 | tf_op jit(solution)/shard_map/ppermute | solution.py:201
  982.3 22.7 %collective-permute-start.45 = (bf16[200,448]{1,0:T(8,128)(2,1)S(1)}, bf16[200,448]{1,0:T(8,128)(2,1)S(1)}, u32[]{:S(2)}, u32[]{:S(2)}) collective-permute-start(bf16[200,448]{1,0:T(8,128)(2,1)S(1)} %get-tuple-element.136), channel_id=1, source_target_pairs={{0,8},{4,12},{8,0},{12,4},{16,24},{20,28},{24,16},{28,20},{1,9},{5... | collective-permute-start | bytes 537608 | tf_op jit(solution)/shard_map/ppermute | solution.py:201
  982.9 43.8 %collective-permute-start.37 = (bf16[200,448]{1,0:T(8,128)(2,1)S(1)}, bf16[200,448]{1,0:T(8,128)(2,1)S(1)}, u32[]{:S(2)}, u32[]{:S(2)}) collective-permute-start(bf16[200,448]{1,0:T(8,128)(2,1)S(1)} %get-tuple-element.134), channel_id=1, source_target_pairs={{0,24},{4,28},{8,16},{12,20},{16,8},{20,12},{24,0},{28,4},{1,25},{... | collective-permute-start | bytes 537608 | tf_op jit(solution)/shard_map/ppermute | solution.py:201
  985.4 23.2 %collective-permute-start.69 = (bf16[56,1600]{1,0:T(8,128)(2,1)S(1)}, bf16[56,1600]{1,0:T(8,128)(2,1)S(1)}, u32[]{:S(2)}, u32[]{:S(2)}) collective-permute-start(bf16[56,1600]{1,0:T(8,128)(2,1)S(1)} %get-tuple-element.143), channel_id=1, source_target_pairs={{0,24},{4,28},{8,16},{12,20},{16,8},{20,12},{24,0},{28,4},{1,25},{... | collective-permute-start | bytes 537608 | tf_op jit(solution)/shard_map/ppermute | solution.py:201
  1047.4 26.3 %collective-permute-start.59 = (bf16[200,448]{1,0:T(8,128)(2,1)S(1)}, bf16[200,448]{1,0:T(8,128)(2,1)S(1)}, u32[]{:S(2)}, u32[]{:S(2)}) collective-permute-start(bf16[200,448]{1,0:T(8,128)(2,1)S(1)} %get-tuple-element.88), channel_id=1, source_target_pairs={{0,8},{4,12},{8,0},{12,4},{16,24},{20,28},{24,16},{28,20},{1,9},{5... | collective-permute-start | bytes 537608 | tf_op jit(solution)/shard_map/ppermute | solution.py:201
  1052.9 26.6 %collective-permute-start.60 = (bf16[200,448]{1,0:T(8,128)(2,1)S(1)}, bf16[200,448]{1,0:T(8,128)(2,1)S(1)}, u32[]{:S(2)}, u32[]{:S(2)}) collective-permute-start(bf16[200,448]{1,0:T(8,128)(2,1)S(1)} %get-tuple-element.88), channel_id=1, source_target_pairs={{0,16},{4,20},{8,24},{12,28},{16,0},{20,4},{24,8},{28,12},{1,17},{... | collective-permute-start | bytes 537608 | tf_op jit(solution)/shard_map/ppermute | solution.py:201
  1062.2 22.1 %collective-permute-start.61 = (bf16[200,448]{1,0:T(8,128)(2,1)S(1)}, bf16[200,448]{1,0:T(8,128)(2,1)S(1)}, u32[]{:S(2)}, u32[]{:S(2)}) collective-permute-start(bf16[200,448]{1,0:T(8,128)(2,1)S(1)} %get-tuple-element.88), channel_id=1, source_target_pairs={{0,24},{4,28},{8,16},{12,20},{16,8},{20,12},{24,0},{28,4},{1,25},{... | collective-permute-start | bytes 537608 | tf_op jit(solution)/shard_map/ppermute | solution.py:201
  1064.7 26.6 %collective-permute-start.49 = (bf16[200,448]{1,0:T(8,128)(2,1)S(1)}, bf16[200,448]{1,0:T(8,128)(2,1)S(1)}, u32[]{:S(2)}, u32[]{:S(2)}) collective-permute-start(bf16[200,448]{1,0:T(8,128)(2,1)S(1)} %get-tuple-element.86), channel_id=1, source_target_pairs={{0,8},{4,12},{8,0},{12,4},{16,24},{20,28},{24,16},{28,20},{1,9},{5... | collective-permute-start | bytes 537608 | tf_op jit(solution)/shard_map/ppermute | solution.py:201
  1073.7 21.4 %collective-permute-start.50 = (bf16[200,448]{1,0:T(8,128)(2,1)S(1)}, bf16[200,448]{1,0:T(8,128)(2,1)S(1)}, u32[]{:S(2)}, u32[]{:S(2)}) collective-permute-start(bf16[200,448]{1,0:T(8,128)(2,1)S(1)} %get-tuple-element.86), channel_id=1, source_target_pairs={{0,16},{4,20},{8,24},{12,28},{16,0},{20,4},{24,8},{28,12},{1,17},{... | collective-permute-start | bytes 537608 | tf_op jit(solution)/shard_map/ppermute | solution.py:201
  1099.3 34.2 %collective-permute-start.62 = (bf16[4,200,448]{2,1,0:T(8,128)(2,1)S(1)}, bf16[4,200,448]{2,1,0:T(8,128)(2,1)S(1)}, u32[]{:S(2)}, u32[]{:S(2)}) collective-permute-start(bf16[4,200,448]{2,1,0:T(8,128)(2,1)S(1)} %bitcast_dynamic-update-slice_fusion.17), channel_id=1, source_target_pairs={{0,4},{4,0},{8,12},{12,8},{16,20},{20,16},{24,28},{28,24},{1,5},{5... | collective-permute-start | bytes 2150408 | tf_op jit(solution)/shard_map/ppermute | solution.py:201
  1110.0 41.1 %collective-permute-start.52 = (bf16[4,200,448]{2,1,0:T(8,128)(2,1)S(1)}, bf16[4,200,448]{2,1,0:T(8,128)(2,1)S(1)}, u32[]{:S(2)}, u32[]{:S(2)}) collective-permute-start(bf16[4,200,448]{2,1,0:T(8,128)(2,1)S(1)} %bitcast_dynamic-update-slice_fusion.21), channel_id=1, source_target_pairs={{0,4},{4,0},{8,12},{12,8},{16,20},{20,16},{24,28},{28,24},{1,5},{5... | collective-permute-start | bytes 2150408 | tf_op jit(solution)/shard_map/ppermute | solution.py:201
  1116.6 46.4 %collective-permute-start.42 = (bf16[4,200,448]{2,1,0:T(8,128)(2,1)S(1)}, bf16[4,200,448]{2,1,0:T(8,128)(2,1)S(1)}, u32[]{:S(2)}, u32[]{:S(2)}) collective-permute-start(bf16[4,200,448]{2,1,0:T(8,128)(2,1)S(1)} %bitcast_dynamic-update-slice_fusion.25), channel_id=1, source_target_pairs={{0,4},{4,0},{8,12},{12,8},{16,20},{20,16},{24,28},{28,24},{1,5},{5... | collective-permute-start | bytes 2150408 | tf_op jit(solution)/shard_map/ppermute | solution.py:201
  1133.8 35.2 %collective-permute-start.63 = (bf16[800,32]{1,0:T(8,128)(2,1)S(1)}, bf16[800,32]{1,0:T(8,128)(2,1)S(1)}, u32[]{:S(2)}, u32[]{:S(2)}) collective-permute-start(bf16[800,32]{1,0:T(8,128)(2,1)S(1)} %slice.501), channel_id=1, source_target_pairs={{0,1},{1,0},{2,3},{3,2},{4,5},{5,4},{6,7},{7,6},{8,9},{9,8},{10,11... | collective-permute-start | bytes 153608 | tf_op jit(solution)/shard_map/ppermute | solution.py:197
  1168.6 24.5 %collective-permute-start.28 = (bf16[768,800]{0,1:T(8,128)(2,1)S(1)}, bf16[768,800]{0,1:T(8,128)(2,1)S(1)}, u32[]{:S(2)}, u32[]{:S(2)}) collective-permute-start(bf16[768,800]{0,1:T(8,128)(2,1)S(1)} %select_convert_fusion), channel_id=1, source_target_pairs={{0,2},{2,0},{1,3},{3,1},{4,6},{6,4},{5,7},{7,5},{8,10},{10,8},{9,1... | collective-permute-start | bytes 3686408 | tf_op jit(solution)/shard_map/ppermute | solution.py:193
  (94 other events, 1949.6 us)

commit v2 on v1

v2 whole, which is shorter than its diff:
```python
import functools
import math

import jax
import jax.numpy as jnp
from jax import lax
from jax.experimental import pallas as pl
from jax.experimental.pallas import tpu as pltpu
from jax.sharding import PartitionSpec as P

HEAD_DIM = 64
gelu_root = math.sqrt(2.0 / math.pi)
gelu_cubic = 0.044715
BLK = 256
NEG = -1e30
KERNEL_VMEM = 40 * 2**20


def dot_over(dims, a, b):
    return lax.dot_general(a, b, (dims, ((), ())), preferred_element_type=jnp.float32)


def nn(a, b):
    return dot_over(((1,), (0,)), a, b)


def nt(a, b):
    return dot_over(((1,), (1,)), a, b)


def tn(a, b):
    return dot_over(((0,), (0,)), a, b)


def head_rows(h):
    return slice(h * HEAD_DIM, (h + 1) * HEAD_DIM)


def allowed_tile(i, j, first):
    keys = j * BLK + lax.broadcasted_iota(jnp.int32, (BLK, BLK), 0)
    queries = i * BLK + lax.broadcasted_iota(jnp.int32, (BLK, BLK), 1)
    return (keys >= first) & (keys <= queries)


def turned(x):
    return jnp.transpose(x.astype(jnp.float32)).astype(jnp.bfloat16)


def attend_kernel(heads, blocks, info_ref, q_ref, k_ref, v_ref, first_ref, o_ref, lse_ref, keys_ref):
    i = pl.program_id(0)
    shift = info_ref[0]

    @pl.when(i == 0)
    def _():
        for h in range(heads):
            keys_ref[h] = turned(k_ref[head_rows(h), :])

    first = first_ref[pl.ds(i, 1), :]
    scale = jnp.bfloat16(HEAD_DIM**-0.5)

    def step(j, carry):
        place = pl.ds(pl.multiple_of(lax.rem(j + shift, blocks) * BLK, BLK), BLK)
        allowed = allowed_tile(i, j, first)
        out = []
        for h in range(heads):
            top, total, acc = carry[h]
            scores = nn(keys_ref[h, place, :], q_ref[head_rows(h), :] * scale)
            scores = jnp.where(allowed, scores, NEG)
            new_top = jnp.maximum(top, jnp.max(scores, axis=0, keepdims=True))
            probs = jnp.exp(scores - new_top)
            shrink = jnp.exp(top - new_top)
            total = total * shrink + jnp.sum(probs, axis=0, keepdims=True)
            acc = acc * shrink + nn(v_ref[head_rows(h), place], probs.astype(jnp.bfloat16))
            out.append((new_top, total, acc))
        return tuple(out)

    row = lambda value: jnp.full((1, BLK), value, jnp.float32)
    start = tuple((row(NEG), row(0.0), jnp.zeros((HEAD_DIM, BLK), jnp.float32)) for h in range(heads))
    done = lax.fori_loop(info_ref[1 + i], i + 1, step, start)
    for h, (top, total, acc) in enumerate(done):
        o_ref[head_rows(h), :] = (acc / total).astype(jnp.bfloat16)
        lse_ref[h : h + 1, :] = top + jnp.log(total)


def attend(info, projected, first, heads):
    tokens = projected.shape[1]
    wide, blocks = heads * HEAD_DIM, tokens // BLK
    at = lambda i, s: lax.rem(i + s[0], blocks)
    return pl.pallas_call(
        functools.partial(attend_kernel, heads, blocks),
        grid_spec=pltpu.PrefetchScalarGridSpec(
            num_scalar_prefetch=1,
            grid=(blocks,),
            in_specs=[
                pl.BlockSpec((wide, BLK), lambda i, s: (0, at(i, s))),
                pl.BlockSpec((wide, tokens), lambda i, s: (1, 0)),
                pl.BlockSpec((wide, tokens), lambda i, s: (2, 0)),
                pl.BlockSpec((blocks, BLK), lambda i, s: (0, 0)),
            ],
            out_specs=[
                pl.BlockSpec((wide, BLK), lambda i, s: (0, at(i, s))),
                pl.BlockSpec((8, BLK), lambda i, s: (0, i)),
            ],
            scratch_shapes=[pltpu.VMEM((heads, tokens, HEAD_DIM), jnp.bfloat16)],
        ),
        out_shape=[
            jax.ShapeDtypeStruct((wide, tokens), jnp.bfloat16),
            jax.ShapeDtypeStruct((8, tokens), jnp.float32),
        ],
        compiler_params=pltpu.CompilerParams(vmem_limit_bytes=KERNEL_VMEM),
        cost_estimate=pl.CostEstimate(flops=0, bytes_accessed=2 * tokens * wide, transcendentals=0),
        name="attend",
    )(info, projected, projected, projected, first)


def attend_back_kernel(
    heads, blocks, info_ref, q_ref, k_ref, v_ref, o_ref, g_ref, lse_ref, first_ref,
    d_ref, keys_ref, values_ref, dk_acc, dv_acc,
):
    i = pl.program_id(0)
    shift = info_ref[0]

    @pl.when(i == 0)
    def _():
        for h in range(heads):
            keys_ref[h] = turned(k_ref[head_rows(h), :])
            values_ref[h] = turned(v_ref[head_rows(h), :])
        dk_acc[...] = jnp.zeros_like(dk_acc)
        dv_acc[...] = jnp.zeros_like(dv_acc)

    first = first_ref[pl.ds(i, 1), :]
    scale = jnp.bfloat16(HEAD_DIM**-0.5)
    centre = [
        jnp.sum(
            g_ref[head_rows(h), :].astype(jnp.float32) * o_ref[head_rows(h), :].astype(jnp.float32),
            axis=0,
            keepdims=True,
        )
        for h in range(heads)
    ]

    def step(j, carry):
        place = pl.ds(pl.multiple_of(lax.rem(j + shift, blocks) * BLK, BLK), BLK)
        allowed = allowed_tile(i, j, first)
        out = []
        for h in range(heads):
            rows = head_rows(h)
            query = q_ref[rows, :] * scale
            grad = g_ref[rows, :]
            scores = jnp.where(allowed, nn(keys_ref[h, place, :], query), NEG)
            probs = jnp.exp(scores - lse_ref[h : h + 1, :])
            prob_grad = nn(values_ref[h, place, :], grad)
            score_grad = (probs * (prob_grad - centre[h])).astype(jnp.bfloat16)
            dv_acc[rows, place] += nt(grad, probs.astype(jnp.bfloat16))
            dk_acc[rows, place] += nt(query, score_grad)
            out.append(carry[h] + nn(k_ref[rows, place], score_grad))
        return tuple(out)

    start = tuple(jnp.zeros((HEAD_DIM, BLK), jnp.float32) for h in range(heads))
    done = lax.fori_loop(info_ref[1 + i], i + 1, step, start)
    mine = pl.ds(pl.multiple_of(lax.rem(i + shift, blocks) * BLK, BLK), BLK)
    for h in range(heads):
        d_ref[head_rows(2 * heads + h), mine] = (done[h] * HEAD_DIM**-0.5).astype(jnp.bfloat16)

    @pl.when(i == blocks - 1)
    def _():
        d_ref[: heads * HEAD_DIM, :] = dk_acc[...].astype(jnp.bfloat16)
        d_ref[heads * HEAD_DIM : 2 * heads * HEAD_DIM, :] = dv_acc[...].astype(jnp.bfloat16)


def attend_back(info, projected, attended, grad, log_totals, first, heads):
    tokens = projected.shape[1]
    wide, blocks = heads * HEAD_DIM, tokens // BLK
    at = lambda i, s: lax.rem(i + s[0], blocks)
    block = pl.BlockSpec((wide, BLK), lambda i, s: (0, at(i, s)))
    whole = lambda part: pl.BlockSpec((wide, tokens), lambda i, s: (part, 0))
    return pl.pallas_call(
        functools.partial(attend_back_kernel, heads, blocks),
        grid_spec=pltpu.PrefetchScalarGridSpec(
            num_scalar_prefetch=1,
            grid=(blocks,),
            in_specs=[
                block,
                whole(1),
                whole(2),
                block,
                block,
                pl.BlockSpec((8, BLK), lambda i, s: (0, i)),
                pl.BlockSpec((blocks, BLK), lambda i, s: (0, 0)),
            ],
            out_specs=pl.BlockSpec((3 * wide, tokens), lambda i, s: (0, 0)),
            scratch_shapes=[
                pltpu.VMEM((heads, tokens, HEAD_DIM), jnp.bfloat16),
                pltpu.VMEM((heads, tokens, HEAD_DIM), jnp.bfloat16),
                pltpu.VMEM((wide, tokens), jnp.float32),
                pltpu.VMEM((wide, tokens), jnp.float32),
            ],
        ),
        out_shape=jax.ShapeDtypeStruct((3 * wide, tokens), jnp.bfloat16),
        compiler_params=pltpu.CompilerParams(vmem_limit_bytes=KERNEL_VMEM),
        cost_estimate=pl.CostEstimate(flops=0, bytes_accessed=2 * tokens * wide, transcendentals=0),
        name="attend_back",
    )(info, projected, projected, projected, attended, grad, log_totals, first)


def call(body, name, grid, specs, args, out_specs, out_shapes, scalars=None, scratch=()):
    return pl.pallas_call(
        body,
        grid_spec=pltpu.PrefetchScalarGridSpec(
            num_scalar_prefetch=1, grid=grid, in_specs=specs, out_specs=out_specs, scratch_shapes=scratch
        ),
        out_shape=out_shapes,
        compiler_params=pltpu.CompilerParams(vmem_limit_bytes=KERNEL_VMEM),
        cost_estimate=pl.CostEstimate(flops=0, bytes_accessed=0, transcendentals=0),
        name=name,
    )(jnp.zeros((1,), jnp.int32) if scalars is None else scalars, *args)


def shape(*dims, dtype=jnp.bfloat16):
    return jax.ShapeDtypeStruct(dims, dtype)


def whole_spec(value):
    zeros = (0,) * value.ndim
    return pl.BlockSpec(value.shape, lambda *_: zeros)


def chunks(size, step):
    return [slice(i, min(i + step, size)) for i in range(0, size, step)]


def project(weight, own, other, bias):
    parts, depth, width = weight.shape
    count = own.shape[1]

    def body(_, w_ref, own_ref, other_ref, b_ref, o_ref):
        def run(ref):
            for cols in chunks(count, 256):
                o_ref[:, cols] = (tn(w_ref[0], ref[:, cols]) + b_ref[0]).astype(jnp.bfloat16)

        pl.when(pl.program_id(0) == 0)(lambda: run(own_ref))
        pl.when(pl.program_id(0) == 1)(lambda: run(other_ref))

    return call(
        body, "project", (2, parts),
        [
            pl.BlockSpec((1, depth, width), lambda i, j, _: (j, 0, 0)),
            whole_spec(own),
            whole_spec(other),
            pl.BlockSpec((1, width, 1), lambda i, j, _: (j, 0, 0)),
        ],
        (weight, own, other, bias),
        pl.BlockSpec((width, count), lambda i, j, _: (j, i)),
        shape(parts * width, 2 * count),
    )


def hidden(weight, own, other, bias):
    depth, width = weight.shape
    count = own.shape[1]
    block = 256
    half = count // block

    def body(_, w_ref, own_ref, other_ref, b_ref, act_ref, slope_ref):
        tokens = jnp.where(pl.program_id(0) < half, own_ref[...], other_ref[...])
        for rows in chunks(width, 256):
            pre = tn(w_ref[:, rows], tokens) + b_ref[rows, :]
            square = pre * pre
            bend = jnp.tanh(pre * (gelu_root + (gelu_root * gelu_cubic) * square))
            lift = 0.5 * (1.0 + bend)
            act_ref[rows, :] = (pre * lift).astype(jnp.bfloat16)
            slope_ref[rows, :] = lift + (pre * lift) * (1.0 - bend) * (
                gelu_root + (3.0 * gelu_root * gelu_cubic) * square
            )

    tile = pl.BlockSpec((width, block), lambda i, _: (0, i))
    return call(
        body, "hidden", (2 * half,),
        [
            whole_spec(weight),
            pl.BlockSpec((depth, block), lambda i, _: (0, jnp.minimum(i, half - 1))),
            pl.BlockSpec((depth, block), lambda i, _: (0, jnp.maximum(i - half, 0))),
            whole_spec(bias),
        ],
        (weight, own, other, bias),
        [tile, tile],
        [shape(width, 2 * count), shape(width, 2 * count, dtype=jnp.float32)],
    )


def hidden_back(weight, own, other, slope):
    depth, width = weight.shape
    count = own.shape[1]
    block = 256
    half = count // block

    def body(_, w_ref, own_ref, other_ref, s_ref, o_ref, sum_ref):
        tokens = jnp.where(pl.program_id(0) < half, own_ref[...], other_ref[...])

        @pl.when(pl.program_id(0) == 0)
        def _():
            sum_ref[...] = jnp.zeros_like(sum_ref)

        for rows in chunks(width, 256):
            grad = (tn(w_ref[:, rows], tokens) * s_ref[rows, :]).astype(jnp.bfloat16)
            o_ref[rows, :] = grad
            grad = grad.astype(jnp.float32)
            sum_ref[rows, :] += grad[:, :128] + grad[:, 128:]

    tile = pl.BlockSpec((width, block), lambda i, _: (0, i))
    return call(
        body, "hidden_back", (2 * half,),
        [
            whole_spec(weight),
            pl.BlockSpec((depth, block), lambda i, _: (0, jnp.minimum(i, half - 1))),
            pl.BlockSpec((depth, block), lambda i, _: (0, jnp.maximum(i - half, 0))),
            tile,
        ],
        (weight, own, other, slope),
        [tile, pl.BlockSpec((width, 128), lambda i, _: (0, 0))],
        [shape(width, 2 * count), shape(width, 128, dtype=jnp.float32)],
    )


def mapped(weight, tokens, part, turn, received=None):
    depth, count = weight.shape[0 if turn else 1], tokens.shape[1] // 2
    rows = weight.shape[1 if turn else 0]
    block = rows if turn else 400
    step = 256 if turn else block

    def body(_, w_ref, t_ref, *refs):
        o_ref = refs[-1]
        for cut in chunks(block, step):
            part = tn(w_ref[:, cut], t_ref[...]) if turn else nn(w_ref[cut, :], t_ref[...])
            if received is not None:
                part = part + refs[0][cut, :].astype(jnp.float32)
            o_ref[cut, :] = part.astype(jnp.bfloat16)

    extra = () if received is None else (received,)
    if turn:
        cols = 256
        grid = (count // cols,)
        tile = pl.BlockSpec((rows, cols), lambda i, _: (0, i))
        specs = [
            whole_spec(weight),
            pl.BlockSpec((depth, cols), lambda i, _: (0, part * (count // cols) + i)),
        ] + [tile] * len(extra)
    else:
        grid = (rows // block,)
        tile = pl.BlockSpec((block, count), lambda i, _: (i, 0))
        specs = [
            pl.BlockSpec((block, depth), lambda i, _: (i, 0)),
            pl.BlockSpec((depth, count), lambda i, _: (0, part)),
        ] + [tile] * len(extra)
    return call(body, "mapped", grid, specs, (weight, tokens) + extra, tile, shape(rows, count))


def mapped_three(weight, parts, part, received=None):
    count = parts.shape[1] // 2
    _, rows, width = weight.shape
    block = 400

    def body(_, w_ref, p_ref, *refs):
        total = sum(nn(w_ref[(i + 1) % 3], p_ref[i * width : (i + 1) * width, :]) for i in range(3))
        if received is not None:
            total = total + refs[0][...].astype(jnp.float32)
        refs[-1][...] = total.astype(refs[-1].dtype)

    tile = pl.BlockSpec((block, count), lambda i, _: (i, 0))
    extra = () if received is None else (received,)
    return call(
        body, "mapped_three", (rows // block,),
        [
            pl.BlockSpec((3, block, width), lambda i, _: (0, i, 0)),
            pl.BlockSpec((3 * width, count), lambda i, _: (0, part)),
        ] + [tile] * len(extra),
        (weight, parts) + extra,
        tile,
        shape(rows, count, dtype=jnp.bfloat16 if received is None else jnp.float32),
    )


def attended_back(weight, own, other):
    width, depth = weight.shape
    count = own.shape[1]

    def body(_, w_ref, own_ref, other_ref, o_ref):
        def run(ref):
            for cols in chunks(count, 256):
                o_ref[:, cols] = nn(w_ref[...], ref[:, cols]).astype(jnp.bfloat16)

        pl.when(pl.program_id(0) == 0)(lambda: run(own_ref))
        pl.when(pl.program_id(0) == 1)(lambda: run(other_ref))

    return call(
        body, "attended_back", (2,),
        [whole_spec(weight), whole_spec(own), whole_spec(other)],
        (weight, own, other),
        pl.BlockSpec((width, count), lambda i, _: (0, i)),
        shape(width, 2 * count),
    )


def weight_grad(own, other, right, order, parts, part):
    rows, count = own.shape
    (place, width), size = part, rows // parts

    def body(_, own_ref, other_ref, r_ref, o_ref):
        o_ref[0] = (nt(own_ref[0], r_ref[:, :count]) + nt(other_ref[0], r_ref[:, count:])).astype(jnp.bfloat16)

    tile = pl.BlockSpec((1, size, count), lambda i, s: (s[i], 0, 0))
    return call(
        body, "weight_grad", order.shape,
        [tile, tile, pl.BlockSpec((width, 2 * count), lambda i, s: (place, 0))],
        (own.reshape(parts, size, count), other.reshape(parts, size, count), right),
        pl.BlockSpec((1, size, width), lambda i, s: (i, 0, 0)),
        shape(order.shape[0], size, width),
        scalars=order,
    )


SWAP = ((0, 1), (1, 0))
f32 = jnp.float32
bf16 = jnp.bfloat16


def row_swap(value):
    return lax.ppermute(value, "row", SWAP)


def col_swap(value):
    return lax.ppermute(value, "col", SWAP)


def dp_xor(value, mask):
    return lax.ppermute(value, "dp", [(i, i ^ mask) for i in range(lax.axis_size("dp"))])


def after(value, *marks):
    return lax.optimization_barrier((value,) + marks)[0] if marks else value


def ordered(at, first, second, axis):
    return jnp.where(
        at == 0,
        jnp.concatenate([first, second], axis=axis),
        jnp.concatenate([second, first], axis=axis),
    )


def paired(at, first, second, axis):
    return ordered(at, jnp.expand_dims(first, axis), jnp.expand_dims(second, axis), axis)


def half_of(at, value, axis):
    size = value.shape[axis] // 2
    return jnp.where(
        at == 0,
        lax.slice_in_dim(value, 0, size, axis=axis),
        lax.slice_in_dim(value, size, 2 * size, axis=axis),
    )


def pick(value, at, axis):
    return lax.dynamic_index_in_dim(value, at, axis, keepdims=False)


def plus(a, b):
    return a.astype(f32) + b.astype(f32)


def pad_to(value, size, axis):
    widths = [(0, 0)] * value.ndim
    widths[axis] = (0, size - value.shape[axis])
    return jnp.pad(value, widths)


def head_slots(c, value, tail, axis, most):
    cut = lambda low, high: lax.slice_in_dim(value, low, high, axis=axis)
    size, spare = value.shape[axis], tail.shape[axis]
    less = most - HEAD_DIM
    first = jnp.where(c == 0, cut(0, most), pad_to(cut(spare, spare + less), most, axis))
    second = jnp.where(
        c == 0,
        pad_to(jnp.concatenate([cut(most, size), tail], axis=axis), most, axis),
        pad_to(cut(spare + less, size), most, axis),
    )
    return first, second


def from_slots(c, first, second, axis, spare):
    cut = lambda value, low, high: lax.slice_in_dim(value, low, high, axis=axis)
    most = first.shape[axis]
    less = most - HEAD_DIM
    tail = col_swap(cut(second, less - spare, less))
    return jnp.where(
        c == 0,
        jnp.concatenate([first, cut(second, 0, less - spare)], axis=axis),
        jnp.concatenate([tail, cut(first, 0, less), cut(second, 0, less)], axis=axis),
    )


def pack(qkv, tail, fc, proj, c, r, at, most):
    rows, size = qkv.shape[1] // 4, qkv.shape[2]
    spare, less, wide = tail.shape[2], most - HEAD_DIM, fc.shape[1] // 2
    scalars = jnp.stack([at, c, r]).astype(jnp.int32)

    def body(s_ref, q_ref, t_ref, f_ref, p_ref, qo_ref, fo_ref, po_ref):
        core, row = s_ref[1], s_ref[2]

        @pl.when((core == 0) & (row == 1))
        def _():
            qo_ref[...] = q_ref[:, 0, :, :most]

        @pl.when((core == 0) & (row == 0))
        def _():
            qo_ref[...] = jnp.zeros_like(qo_ref)
            qo_ref[:, :, : size - most] = q_ref[:, 0, :, most:]
            qo_ref[:, :, size - most : size - most + spare] = t_ref[:, 0]

        @pl.when((core == 1) & (row == 1))
        def _():
            qo_ref[...] = jnp.zeros_like(qo_ref)
            qo_ref[:, :, :less] = q_ref[:, 0, :, spare : spare + less]

        @pl.when((core == 1) & (row == 0))
        def _():
            qo_ref[...] = jnp.zeros_like(qo_ref)
            qo_ref[:, :, :less] = q_ref[:, 0, :, spare + less :]

        @pl.when(row == 0)
        def _():
            fo_ref[...] = f_ref[0, :, wide:]
            po_ref[...] = p_ref[0, :, wide:]

        @pl.when(row == 1)
        def _():
            fo_ref[...] = f_ref[0, :, :wide]
            po_ref[...] = p_ref[0, :, :wide]

    quarter = lambda v: v.reshape(v.shape[:-2] + (4, rows, v.shape[-1]))
    return call(
        body, "pack", (1,),
        [
            pl.BlockSpec((3, 1, rows, size), lambda i, s: (0, s[0], 0, 0)),
            pl.BlockSpec((3, 1, rows, spare), lambda i, s: (0, s[0], 0, 0)),
            pl.BlockSpec((1, rows, 2 * wide), lambda i, s: (s[0], 0, 0)),
            pl.BlockSpec((1, rows, 2 * wide), lambda i, s: (s[0], 0, 0)),
        ],
        tuple(quarter(v) for v in (qkv, tail, fc, proj)),
        [pl.BlockSpec((3, rows, most), lambda i, s: (0, 0, 0))] + [pl.BlockSpec((rows, wide), lambda i, s: (0, 0))] * 2,
        [shape(3, rows, most), shape(rows, wide), shape(rows, wide)],
        scalars=scalars,
    )


class Fetch:
    def __init__(self, sent, k):
        self.y, self.z = k % 2, (k // 2) % 2
        self.got = row_swap(sent)

    def second(self, *marks):
        self.got = after(self.got, *marks)
        self.got = paired(self.z, self.got, dp_xor(self.got, 2), 1)
        return self.got

    def third(self, *marks):
        self.got = after(self.got, *marks)
        self.peer = dp_xor(self.got, 1)

    def result(self, *marks):
        both = paired(self.y, after(self.got, *marks), self.peer, 2)
        return both.reshape(both.shape[0], -1, both.shape[-1])


class Total:
    def __init__(self, own, other, right, part, r, k, y_first, *marks):
        self.rows, self.width = own.shape[0], part[1]
        self.r, self.k, self.y_first = r, k, y_first
        self.fast = lax.axis_size("dp") == 8
        right = after(right, *marks)
        if not self.fast:
            self.grad = weight_grad(own, other, right, jnp.arange(4, dtype=jnp.int32), 4, part)
            return
        self.y, self.lo, self.hi = k % 2, (k // 2) % 2, k // 4
        if y_first:
            send, parts, mask = 2 * (1 - self.y) + jnp.arange(2), 4, 1
            keep = 2 * self.y + jnp.arange(2)
        else:
            send, parts, mask = (1 - self.lo) + 2 * jnp.arange(4), 8, 2
            keep = self.lo + 2 * jnp.arange(4)
        shaped = lambda v: v.reshape(2, 2, self.rows // 8, self.width)
        sent = weight_grad(own, other, right, send.astype(jnp.int32), parts, part)
        self.got = dp_xor(shaped(sent), mask)
        self.keep = shaped(weight_grad(own, other, after(right, sent), keep.astype(jnp.int32), parts, part))

    def marks(self):
        return [self.keep] if self.fast else []

    def sum_one(self, *marks):
        if self.fast:
            part = plus(after(self.keep, *marks), self.got).astype(bf16)
            axis, at, mask = (1, self.lo, 2) if self.y_first else (0, self.y, 1)
            self.keep, self.got = pick(part, at, axis), dp_xor(pick(part, 1 - at, axis), mask)
            return [self.keep]
        return []

    def sum_two(self, *marks):
        if self.fast:
            part = plus(after(self.keep, *marks), self.got).astype(bf16)
            self.keep, self.got = pick(part, self.hi, 0), dp_xor(pick(part, 1 - self.hi, 0), 4)
            return [self.keep]
        return []

    def sum_three(self, *marks):
        if self.fast:
            cross = [
                (2 * i + j, 2 * (i ^ 1) + (j ^ 1))
                for i in range(lax.axis_size("dp"))
                for j in range(2)
                if i % 2 != j
            ]
            self.keep = plus(after(self.keep, *marks), self.got).astype(bf16)
            self.got = lax.ppermute(self.keep, ("dp", "row"), cross)
            return [self.keep]
        return []

    def spread_one(self, *marks):
        if self.fast:
            self.keep = jnp.where(self.y == self.r, after(self.keep, *marks), self.got)
            self.got = dp_xor(self.keep, 4)
            return [self.keep]
        return []

    def spread_two(self, *marks):
        if self.fast:
            self.keep = paired(self.hi, after(self.keep, *marks), self.got, 0)
            self.got = dp_xor(self.keep, 2 if self.y_first else 1)
            return [self.keep]
        return []

    def spread_three(self, *marks):
        if self.fast:
            if self.y_first:
                self.keep = paired(self.lo, after(self.keep, *marks), self.got, 1)
                self.got = dp_xor(self.keep, 1)
            else:
                self.keep = paired(self.y, after(self.keep, *marks), self.got, 0)
                self.got = dp_xor(self.keep, 2)
            return [self.keep]
        return []

    def result(self, *marks):
        if not self.fast:
            halves = self.grad.reshape(2, self.rows // 2, self.width)
            keep, got = pick(halves, self.r, 0), row_swap(pick(halves, 1 - self.r, 0))
            both = lax.psum(paired(self.r, keep, got, 0), "dp")
            return both[0], both[1]
        keep, got = after(self.keep, *marks), self.got
        if self.y_first:
            both = paired(self.y, keep, got, 0)
        else:
            both = paired(self.lo, keep, got, 2)
        both = both.reshape(2, self.rows // 2, self.width)
        return both[0], both[1]


def norm(values):
    center = jnp.mean(values, axis=0, keepdims=True)
    shifted = values - center
    inverse = lax.rsqrt(jnp.mean(shifted * shifted, axis=0, keepdims=True) + 1e-05)
    return shifted * inverse, inverse


def per_device(
    block_in,
    out_grad,
    seq_lengths,
    ln1_gain,
    ln1_bias,
    qkv_weight,
    qv_bias,
    out_weight,
    out_bias,
    ln2_gain,
    ln2_bias,
    fc_weight,
    fc_bias,
    proj_weight,
    proj_bias,
):
    n_dp = lax.axis_size("dp")
    r, c, k = lax.axis_index("row"), lax.axis_index("col"), lax.axis_index("dp")
    x_own, grad_own = block_in.T, out_grad.T
    half, tokens = x_own.shape
    heads = 7
    most = heads * HEAD_DIM
    spare = 32
    column = lambda v: v.astype(f32)[:, None]

    qkv_tail = col_swap(qkv_weight[:, :, :spare])
    proj_turned = proj_weight.T
    qkv_sent, fc_sent, proj_sent = pack(
        qkv_weight, qkv_tail, fc_weight, proj_turned, c, r, 2 * ((k // 2) % 2) + k % 2, most
    )
    qkv_fetch = Fetch(qkv_sent, k)
    x_peer = row_swap(after(x_own, qkv_sent))
    fc_fetch = Fetch(fc_sent[None], k)
    proj_fetch = Fetch(proj_sent[None], k)
    vectors = jnp.stack([ln1_gain, ln1_bias, out_bias, ln2_gain, ln2_bias])
    vectors = ordered(r, vectors, row_swap(vectors), 1).astype(f32)
    gain_one, bias_one, bias_out, gain_two, bias_two = [vectors[i][:, None] for i in range(5)]

    bias_first, bias_second = head_slots(c, qv_bias, col_swap(qv_bias[:, :spare]), 1, most)
    bias_mine = jnp.where(r == 0, bias_first, bias_second).astype(f32)
    bias_mine = jnp.stack([bias_mine[0], jnp.zeros_like(bias_mine[0]), bias_mine[1]])[:, :, None]

    out_first, out_second = head_slots(c, after(out_weight, qkv_sent), col_swap(out_weight[:spare]), 0, most)
    out_mine = jnp.where(r == 0, out_first, out_second)
    out_got = row_swap(jnp.where(r == 0, out_second, out_first))

    qkv_first, qkv_second = head_slots(c, after(qkv_weight, out_mine), qkv_tail, 2, most)
    qkv_mine = jnp.where(r == 0, qkv_first, qkv_second)
    mark = qkv_fetch.second(qkv_mine)
    qkv_fetch.third()
    fc_mine = half_of(r, after(fc_weight, mark), 1)
    proj_mine = half_of(r, after(proj_turned, mark), 1)
    fc_bias_mine = column(half_of(r, fc_bias, 0))

    lengths = seq_lengths[0]
    group = 2 * tokens
    places = jnp.arange(group, dtype=jnp.int32)
    ends = jnp.cumsum(lengths, dtype=jnp.int32)
    first = jnp.sum(
        jnp.where(ends[None, :] <= places[:, None], lengths[None, :], 0), axis=1, dtype=jnp.int32
    ).reshape(group // BLK, BLK)
    info = jnp.concatenate([(c * (tokens // BLK))[None].astype(jnp.int32), first[:, 0] // BLK])

    x_full = ordered(r, x_own, x_peer, 0).astype(f32)
    normed_one, inverse_one = norm(x_full)
    h_one = (normed_one * gain_one + bias_one).astype(bf16)
    h_one_peer = col_swap(h_one)
    mark = fc_fetch.second(h_one)
    qkv_full = ordered(r, qkv_mine, qkv_fetch.result(mark), 1)
    projected = project(qkv_full, h_one, h_one_peer, bias_mine)
    fc_fetch.third(projected)
    mark = proj_fetch.second(fc_fetch.got)
    attended, log_totals = attend(info, after(projected, mark), first, heads)
    proj_fetch.third(attended)
    out_full = ordered(r, out_mine, out_got, 1)
    other = mapped(out_full, attended, 1, True)
    low = mapped(out_full, attended, 0, True, col_swap(other))
    branch_other = row_swap(low)
    fc_full = ordered(r, after(fc_mine, low), fc_fetch.result(low)[0], 0)
    proj_full = ordered(r, after(proj_mine, fc_full), proj_fetch.result(fc_full)[0], 0)
    x_mid = after(x_full, proj_full) + plus(low, branch_other) + bias_out
    normed_two, inverse_two = norm(x_mid)
    h_two = (normed_two * gain_two + bias_two).astype(bf16)
    h_two_peer = col_swap(h_two)
    grad_full = ordered(r, after(grad_own, h_two), row_swap(after(grad_own, low)), 0)
    grad_peer = col_swap(grad_full)
    activated, slope = hidden(fc_full, h_two, h_two_peer, fc_bias_mine)

    ff = (0, activated.shape[0])
    proj_total = Total(grad_full, grad_peer, activated, ff, r, k, True)
    pre_grad, fc_bias_grad = hidden_back(proj_full, after(grad_full, *proj_total.marks()), grad_peer, slope)
    other = mapped(fc_full, pre_grad, 1, False)
    low = mapped(fc_full, pre_grad, 0, False, col_swap(other))
    h_two_grad = plus(low, row_swap(low))
    fc_total = Total(h_two, h_two_peer, pre_grad, ff, r, k, True, low)
    mark = proj_total.sum_one(*fc_total.marks())
    other = mapped(proj_full, after(activated, *mark), 1, False)
    proj_part = mapped(proj_full, activated, 0, False, col_swap(other))
    block_other = row_swap(half_of(1 - r, proj_part, 0))
    mark = proj_total.sum_two(proj_part)

    scaled = after(h_two_grad, proj_part, *mark) * gain_two
    mid_grad = grad_full.astype(f32) + inverse_two * (
        scaled
        - jnp.mean(scaled, axis=0, keepdims=True)
        - normed_two * jnp.mean(scaled * normed_two, axis=0, keepdims=True)
    )
    branch_grad = mid_grad.astype(bf16)
    branch_peer = col_swap(branch_grad)
    mark = proj_total.sum_three(branch_grad)
    mark = fc_total.sum_one(*mark)

    out_total = Total(branch_grad, branch_peer, attended, (0, most), r, k, False, *mark)
    mark = proj_total.spread_one(*out_total.marks())
    attended_grad = attended_back(out_full, after(branch_grad, *mark), branch_peer)
    parts = attend_back(info, projected, attended, attended_grad, log_totals, first, heads)
    mark = fc_total.sum_two(parts)
    mark = out_total.sum_one(*mark)
    mark = proj_total.spread_two(*mark)
    q_total = Total(h_one, h_one_peer, parts, (2, most), r, k, False, *mark)
    kv_total = Total(h_one, h_one_peer, parts, (0, 2 * most), r, k, True, *q_total.marks())
    other = mapped_three(qkv_full, after(parts, *kv_total.marks()), 1)
    mark = out_total.sum_two(other)
    mark = fc_total.sum_three(*mark)
    mine = mapped_three(qkv_full, after(parts, *mark), 0, col_swap(other))
    one_other = row_swap(half_of(1 - r, mine, 0).astype(bf16))
    mark = out_total.sum_three(mine)
    mark = proj_total.spread_three(*mark)
    mark = fc_total.spread_one(*mark)
    mark = kv_total.sum_one(*mark)
    mark = out_total.spread_one(*mark)

    normed_half = half_of(r, normed_one, 0)
    h_one_grad = after(half_of(r, mine, 0), *mark) + one_other.astype(f32)
    scaled = h_one_grad * column(ln1_gain)
    sums = jnp.stack([jnp.sum(scaled, axis=0), jnp.sum(scaled * normed_half, axis=0)])
    sums_peer = row_swap(sums)

    mark = q_total.sum_one(sums)
    mark = fc_total.spread_two(*mark)
    sums = (after(sums, *mark) + sums_peer) / (2 * half)
    x_grad = half_of(r, mid_grad, 0) + inverse_one * (
        scaled - sums[0][None] - normed_half * sums[1][None]
    )
    mark = out_total.spread_two(x_grad)
    mark = kv_total.sum_two(*mark)
    block_out = after(half_of(r, x_mid, 0), *mark) + plus(half_of(r, proj_part, 0), block_other)
    block_out = (block_out + column(proj_bias)).astype(bf16)

    h_two_half = half_of(r, h_two_grad, 0)
    own = jnp.stack(
        [
            jnp.sum(h_one_grad * normed_half, axis=1),
            jnp.sum(h_one_grad, axis=1),
            jnp.sum(h_two_half * half_of(r, normed_two, 0), axis=1),
            jnp.sum(h_two_half, axis=1),
            jnp.sum(half_of(r, branch_grad, 0).astype(f32), axis=1),
            jnp.sum(grad_own.astype(f32), axis=1),
        ]
    )
    own_peer = col_swap(own)
    fc_bias_grad = jnp.sum(fc_bias_grad, axis=1)
    qv = jnp.stack([jnp.sum(parts[i * most : (i + 1) * most].astype(f32), axis=1) for i in (2, 1)])

    proj_weight_grad = jnp.concatenate(proj_total.result(block_out), axis=1).astype(f32).T
    mark = q_total.sum_two(proj_weight_grad)
    mark = kv_total.sum_three(*mark)
    own = after(own, *mark) + own_peer
    pack_sums = jnp.concatenate([own.reshape(-1), fc_bias_grad, qv.reshape(-1)])
    pack_sums = pad_to(pack_sums, -(-pack_sums.shape[0] // 1024) * 1024, 0).reshape(-1, 128)
    steps = [
        [out_total.spread_three, q_total.sum_three],
        [kv_total.spread_one, fc_total.spread_three],
        [q_total.spread_one],
    ]
    if n_dp & (n_dp - 1):
        pack_sums = lax.psum(pack_sums, "dp")
    else:
        mask = 1
        while mask < n_dp:
            peer = dp_xor(pack_sums, mask)
            for step in steps[:1]:
                for one in step:
                    mark = one(*mark)
            steps = steps[1:]
            pack_sums = after(pack_sums, *mark) + peer
            mask *= 2
    peer = row_swap(pack_sums).reshape(-1)
    mark = kv_total.spread_two(*mark)
    mark = q_total.spread_two(*mark)
    peer = after(peer, *mark)
    pack_sums = pack_sums.reshape(-1)
    own = pack_sums[: 6 * half].reshape(6, half)
    low, high = 6 * half, 6 * half + fc_bias_grad.shape[0]
    fc_bias_grad = ordered(r, pack_sums[low:high], peer[low:high], 0)
    qv_mine, qv_peer = [v[high : high + 2 * most].reshape(2, most) for v in (pack_sums, peer)]
    qv_bias_grad = from_slots(
        c, jnp.where(r == 0, qv_mine, qv_peer), jnp.where(r == 0, qv_peer, qv_mine), 1, spare
    )
    out_weight_grad = from_slots(c, *out_total.result(*mark), 1, spare).T.astype(f32)
    fc_weight_grad = jnp.concatenate(fc_total.result(out_weight_grad), axis=1).astype(f32)
    mark = kv_total.spread_three(fc_weight_grad)
    mark = q_total.spread_three(*mark)
    q_both = q_total.result(*mark)
    kv_both = kv_total.result(q_both[0])
    pairs = [q_both] + [[v[:, i * most : (i + 1) * most] for v in kv_both] for i in range(2)]
    qkv_weight_grad = jnp.stack([from_slots(c, *pair, 1, spare).astype(f32) for pair in pairs])
    return (
        block_out.T,
        x_grad.T,
        own[0],
        own[1],
        qkv_weight_grad,
        qv_bias_grad,
        out_weight_grad,
        own[4],
        own[2],
        own[3],
        fc_weight_grad,
        fc_bias_grad,
        proj_weight_grad,
        own[5],
    )


def solution(mesh):
    placed = (
        P(("dp", "col"), "row"),
        P(("dp", "col"), "row"),
        P("dp", None),
        P("row"),
        P("row"),
        P(None, "row", "col"),
        P(None, "col"),
        P("col", "row"),
        P("row"),
        P("row"),
        P("row"),
        P("row", "col"),
        P("col"),
        P("col", "row"),
        P("row"),
    )
    return jax.shard_map(
        per_device,
        mesh=mesh,
        in_specs=placed,
        out_specs=(
            P(("dp", "col"), "row"),
            P(("dp", "col"), "row"),
            P("row"),
            P("row"),
            P(None, "row", "col"),
            P(None, "col"),
            P("col", "row"),
            P("row"),
            P("row"),
            P("row"),
            P("row", "col"),
            P("col"),
            P("col", "row"),
            P("row"),
        ),
        check_vma=False,
    )
```

time: 1240 us -> 903 us (0.73); the launches traced: 1220 us -> 897 us
  waiting for transfers between devices: 566 us -> 373 us
  matrix products: 177 us -> 0 us
  Pallas kernels: 85.8 us -> 200 us
  starting transfers between devices: 184 us -> 109 us
  other arithmetic: 98.9 us -> 159 us
  local copies, waits for them, and re-layouts: 102 us -> 53.4 us
    ppermute x58 -> x39, waiting for transfers between devices: 433 us -> 249 us  [dp_xor(): lax.ppermute(value, 'dp', [(i, i ^ mask) for i in range(lax.axis_size('dp...]
    dot_general x24 -> x0, matrix products: 177 us -> none  [the longest x8 70.9 us: nn(): lax.dot_general(a, b, (((1,), (0,)), ((), ())), preferred_element_type=jn...]
    pallas_call x0 -> x23, Pallas kernels: none -> 149 us  [call(): pl.pallas_call(body, grid_spec=pltpu.PrefetchScalarGridSpec(num_scalar_pr...]
    ppermute x58 -> x39, starting transfers between devices: 159 us -> 76.6 us  [dp_xor(): lax.ppermute(value, 'dp', [(i, i ^ mask) for i in range(lax.axis_size('dp...]
    select_n x3 -> x27, other arithmetic: 4.36 us -> 63.6 us  [ordered(): jnp.where(at == 0, jnp.concatenate([first, second], axis=axis), jnp.conca...]
    pallas_call x1, Pallas kernels: 43.8 us -> 24.9 us  [attend_back(): pl.pallas_call(functools.partial(attend_back_kernel, heads, blocks), grid...]
    pallas_call x1, Pallas kernels: 42 us -> 25.5 us  [attend(): pl.pallas_call(functools.partial(attend_kernel, heads, blocks), grid_spec...]
    ppermute x15 -> x13, waiting for transfers between devices: 126 us -> 116 us  [row_swap(): return lax.ppermute(value, 'row', SWAP)]
  transfers between devices with their start and end apart: 94 -> 74, of which waited for: 39 -> 34; matrix products, arithmetic and copies ran while one was open for 26% -> 19% of each run, Pallas kernels for 0% -> 16%
where the time goes in v2:
time: 903 us; the launch traced here: 897 us
  waiting for transfers between devices  373 us (41%)
  Pallas kernels  200 us (22%)
  other arithmetic  159 us (18%)
  starting transfers between devices  109 us (12%)
  local copies, waits for them, and re-layouts  53.4 us (6%)
    ppermute x39, waiting for transfers between devices, dp_xor(): lax.ppermute(value, 'dp', [(i, i ^ mask) for i in range(lax.axis_size('dp...  249 us
    pallas_call x23, Pallas kernels, call(): pl.pallas_call(body, grid_spec=pltpu.PrefetchScalarGridSpec(num_scalar_pr...  149 us
    ppermute x13, waiting for transfers between devices, row_swap(): return lax.ppermute(value, 'row', SWAP)  116 us
    ppermute x39, starting transfers between devices, dp_xor(): lax.ppermute(value, 'dp', [(i, i ^ mask) for i in range(lax.axis_size('dp...  76.6 us
    select_n x27, other arithmetic, ordered(): jnp.where(at == 0, jnp.concatenate([first, second], axis=axis), jnp.conca...  63.6 us
    ppermute x13, starting transfers between devices, row_swap(): return lax.ppermute(value, 'row', SWAP)  26.6 us
    unnamed x170, local copies, waits for them, and re-layouts  26.2 us
    pallas_call x1, Pallas kernels, attend(): pl.pallas_call(functools.partial(attend_kernel, heads, blocks), grid_spec...  25.5 us
  transfers between devices with their start and end apart: 74, of which 34 were waited for; matrix products, arithmetic and copies ran while one was open for 19% of the time, Pallas kernels for 16%

profile of v2, /device:TPU:0, one launch (start us, length us, event | category | flops | bytes accessed | tf_op | source)
XLA Modules:
  0.0 897.1 jit_solution(13678822244260751018)
XLA Ops:
  29.0 6.5 collective-permute-done.2
  37.1 38.3 %collective-permute-done.1 = bf16[800,768]{1,0:T(8,128)(2,1)S(1)} collective-permute-done((bf16[800,768]{1,0:T(8,128)(2,1)S(1)}, bf16[800,768]{1,0:T(8,128)(2,1)S(1)}, u32[]{:S(2)}, u32[]{:S(2)}) %collective-permute-start.1) | collective-permute-done | bytes 1228832 | tf_op jit(solution)/shard_map/ppermute | solution.py:428
  77.3 4.8 subtract_multiply_fusion.1
  91.8 12.9 %collective-permute-done.8 = bf16[1,200,1600]{2,1,0:T(8,128)(2,1)} collective-permute-done((bf16[1,200,1600]{2,1,0:T(8,128)(2,1)}, bf16[1,200,1600]{2,1,0:T(8,128)(2,1)}, u32[]{:S(2)}, u32[]{:S(2)}) %collective-permute-start.8) | collective-permute-done | bytes 640032 | tf_op jit(solution)/shard_map/ppermute | solution.py:436
  107.7 7.7 collective-permute-done.9
  123.6 13.3 %project.1.q_ref.k_ref.v_ref = bf16[1344,1536]{1,0:T(8,128)(2,1)S(1)} custom-call(s32[1]{0:T(128)} %constant.194.clone.1._, bf16[3,1600,448]{2,1,0:T(8,128)(2,1)} %maximum_select_fusion.4.w_ref, bf16[1600,768]{1,0:T(8,128)(2,1)} %get-tuple-element.281.own_ref, bf16[1600,768]{1,0:T(8,128)(2,1)S(1)} %collective-permute-done.10.other_ref, ...), custom_call_target="tpu_custom_call" | custom-call | tf_op jit(solution)/shard_map/project/pallas_call | solution.py:207
  143.7 11.5 %collective-permute-done.13 = bf16[1,200,1600]{2,1,0:T(8,128)(2,1)S(1)} collective-permute-done((bf16[1,200,1600]{2,1,0:T(8,128)(2,1)}, bf16[1,200,1600]{2,1,0:T(8,128)(2,1)S(1)}, u32[]{:S(2)}, u32[]{:S(2)}) %collective-permute-start.13) | collective-permute-done | bytes 640032 | tf_op jit(solution)/shard_map/ppermute | solution.py:436
  158.1 25.5 %attend.1 = (bf16[448,1536]{1,0:T(8,128)(2,1)S(1)}, f32[8,1536]{1,0:T(8,128)S(1)}) custom-call(s32[7]{0:T(128)S(1)} %pad_add_fusion.1.info_ref, bf16[1344,1536]{1,0:T(8,128)(2,1)S(1)} %copy-done.4, bf16[1344,1536]{1,0:T(8,128)(2,1)S(1)} %copy-done.4, bf16[1344,1536]{1,0:T(8,128)(2,1)S(1)} %copy-done.4, s32[6,256]{1,0:T(8,128)S(1)} %reshape.690.first_ref), custom_call_target="tpu_custom_call" | custom-call | bytes 1376256 | tf_op jit(solution)/shard_map/attend/pallas_call | solution.py:89
  186.0 7.7 collective-permute-start.15
  193.7 3.5 slice_select_fusion
  203.6 20.2 %collective-permute-done.15 = bf16[1,2,200,1600]{3,2,1,0:T(8,128)(2,1)S(1)} collective-permute-done((bf16[1,2,200,1600]{3,2,1,0:T(8,128)(2,1)S(1)}, bf16[1,2,200,1600]{3,2,1,0:T(8,128)(2,1)S(1)}, u32[]{:S(2)}, u32[]{:S(2)}) %collective-permute-start.15) | collective-permute-done | bytes 1280032 | tf_op jit(solution)/shard_map/ppermute | solution.py:436
  226.3 7.9 maximum_select_fusion.w_ref
  234.2 17.9 %collective-permute-done.16 = bf16[1,2,200,1600]{3,2,1,0:T(8,128)(2,1)} collective-permute-done((bf16[1,2,200,1600]{3,2,1,0:T(8,128)(2,1)}, bf16[1,2,200,1600]{3,2,1,0:T(8,128)(2,1)}, u32[]{:S(2)}, u32[]{:S(2)}) %collective-permute-start.16) | collective-permute-done | bytes 1280032 | tf_op jit(solution)/shard_map/ppermute | solution.py:436
  257.0 7.9 maximum_select_fusion.1.w_ref
  265.1 4.8 fusion.23
  272.1 3.6 add_convert_fusion.3
  275.8 17.8 %collective-permute-done.18 = bf16[800,768]{1,0:T(8,128)(2,1)S(1)} collective-permute-done((bf16[800,768]{1,0:T(8,128)(2,1)S(1)}, bf16[800,768]{1,0:T(8,128)(2,1)S(1)}, u32[]{:S(2)}, u32[]{:S(2)}) %collective-permute-start.18) | collective-permute-done | bytes 1228832 | tf_op jit(solution)/shard_map/ppermute | solution.py:428
  295.0 19.2 %hidden.1 = (bf16[1600,1536]{1,0:T(8,128)(2,1)S(1)}, f32[1600,1536]{1,0:T(8,128)}) custom-call(s32[1]{0:T(128)} %constant.194.clone.1._, bf16[1600,1600]{1,0:T(8,128)(2,1)} %maximum_select_fusion.w_ref, bf16[1600,768]{1,0:T(8,128)(2,1)} %get-tuple-element.262.own_ref, bf16[1600,768]{1,0:T(8,128)(2,1)} %collective-permute-done.20.other_ref, ...), custom_call_target="tpu_custom_call" | custom-call | tf_op jit(solution)/shard_map/hidden/pallas_call | solution.py:207
  314.2 8.0 weight_grad.10
  323.8 6.8 weight_grad.11
  332.1 15.3 %hidden_back.1 = (bf16[1600,1536]{1,0:T(8,128)(2,1)S(1)}, f32[1600,128]{1,0:T(8,128)S(1)}) custom-call(s32[1]{0:T(128)} %constant.194.clone.1._, bf16[1600,1600]{1,0:T(8,128)(2,1)} %maximum_select_fusion.1.w_ref, bf16[1600,768]{1,0:T(8,128)(2,1)S(1)} %maximum_select_fusion.12.own_ref, bf16[1600,768]{1,0:T(8,128)(2,1)} %collective-permute-done.19.other_ref, ...), custom_call_target="tpu_custom_call" | custom-call | tf_op jit(solution)/shard_map/hidden_back/pallas_call | solution.py:207
  347.4 5.4 mapped.8
  352.9 4.8 collective-permute-done.21.refs_0_
  360.1 8.1 mapped.9
  368.5 7.6 weight_grad.12
  377.7 7.0 weight_grad.13
  390.0 5.4 mapped.10
  397.5 26.5 %collective-permute-done.22 = bf16[1600,768]{1,0:T(8,128)(2,1)} collective-permute-done((bf16[1600,768]{1,0:T(8,128)(2,1)}, bf16[1600,768]{1,0:T(8,128)(2,1)}, u32[]{:S(2)}, u32[]{:S(2)}) %collective-permute-start.22) | collective-permute-done | bytes 2457632 | tf_op jit(solution)/shard_map/ppermute | solution.py:428
  427.0 4.2 copy-done.7
  431.1 7.0 mapped.11
  450.3 23.1 %collective-permute-done.26 = bf16[200,1600]{1,0:T(8,128)(2,1)} collective-permute-done((bf16[200,1600]{1,0:T(8,128)(2,1)}, bf16[200,1600]{1,0:T(8,128)(2,1)}, u32[]{:S(2)}, u32[]{:S(2)}) %collective-permute-start.26) | collective-permute-done | bytes 640032 | tf_op jit(solution)/shard_map/ppermute | solution.py:436
  482.7 4.2 weight_grad.14
  487.0 4.2 weight_grad.15
  494.3 4.6 attended_back.1.g_ref
  498.9 24.9 %attend_back.1.r_ref.p_ref = bf16[1344,1536]{1,0:T(8,128)(2,1)S(1)} custom-call(s32[7]{0:T(128)S(1)} %pad_add_fusion.1.info_ref, bf16[1344,1536]{1,0:T(8,128)(2,1)S(1)} %copy-done.5, bf16[1344,1536]{1,0:T(8,128)(2,1)S(1)} %copy-done.5, bf16[1344,1536]{1,0:T(8,128)(2,1)S(1)} %copy-done.5, bf16[448,1536]{1,0:T(8,128)(2,1)S(1)} %copy-done.18, ...), custom_call_target="tpu_custom_call" | custom-call | bytes 1376256 | tf_op jit(solution)/shard_map/attend_back/pallas_call | solution.py:177
  523.8 6.3 collective-permute-start.31
  533.0 14.7 %collective-permute-done.31 = bf16[2,2,200,448]{3,2,1,0:T(8,128)(2,1)S(1)} collective-permute-done((bf16[2,2,200,448]{3,2,1,0:T(8,128)(2,1)S(1)}, bf16[2,2,200,448]{3,2,1,0:T(8,128)(2,1)S(1)}, u32[]{:S(2)}, u32[]{:S(2)}) %collective-permute-start.31) | collective-permute-done | bytes 716832 | tf_op jit(solution)/shard_map/ppermute | solution.py:436
  556.1 3.5 weight_grad.18
  559.7 3.5 weight_grad.19
  564.4 5.8 mapped_three.2
  570.3 4.3 collective-permute-start.33
  574.6 4.2 slice_select_fusion.6
  586.8 24.4 %collective-permute-done.34 = bf16[200,1600]{1,0:T(8,128)(2,1)S(1)} collective-permute-done((bf16[200,1600]{1,0:T(8,128)(2,1)S(1)}, bf16[200,1600]{1,0:T(8,128)(2,1)S(1)}, u32[]{:S(2)}, u32[]{:S(2)}) %collective-permute-start.34) | collective-permute-done | bytes 640032 | tf_op jit(solution)/shard_map/ppermute | solution.py:436
  613.4 6.4 mapped_three.3
  619.8 7.8 collective-permute-done.36
  633.6 17.2 %collective-permute-start.41 = (bf16[800,768]{1,0:T(8,128)(2,1)S(1)}, bf16[800,768]{1,0:T(8,128)(2,1)S(1)}, u32[]{:S(2)}, u32[]{:S(2)}) collective-permute-start(bf16[800,768]{1,0:T(8,128)(2,1)S(1)} %select_convert_fusion), channel_id=1, source_target_pairs={{0,2},{2,0},{1,3},{3,1},{4,6},{6,4},{5,7},{7,5},{8,10},{10,8},{9,1... | collective-permute-start | bytes 3686408 | tf_op jit(solution)/shard_map/ppermute | solution.py:428
  656.4 20.7 %collective-permute-done.41 = bf16[800,768]{1,0:T(8,128)(2,1)S(1)} collective-permute-done((bf16[800,768]{1,0:T(8,128)(2,1)S(1)}, bf16[800,768]{1,0:T(8,128)(2,1)S(1)}, u32[]{:S(2)}, u32[]{:S(2)}) %collective-permute-start.41) | collective-permute-done | bytes 1228832 | tf_op jit(solution)/shard_map/ppermute | solution.py:428
  691.7 10.0 %collective-permute-done.45 = bf16[200,448]{1,0:T(8,128)(2,1)S(1)} collective-permute-done((bf16[200,448]{1,0:T(8,128)(2,1)S(1)}, bf16[200,448]{1,0:T(8,128)(2,1)S(1)}, u32[]{:S(2)}, u32[]{:S(2)}) %collective-permute-start.45) | collective-permute-done | bytes 179232 | tf_op jit(solution)/shard_map/ppermute | solution.py:436
  710.5 6.6 collective-permute-done.48
  717.2 3.9 maximum_select_fusion.2
  721.4 5.4 convert_bitcast_fusion
  727.1 10.5 %collective-permute-done.50 = bf16[200,896]{1,0:T(8,128)(2,1)S(1)} collective-permute-done((bf16[200,896]{1,0:T(8,128)(2,1)S(1)}, bf16[200,896]{1,0:T(8,128)(2,1)S(1)}, u32[]{:S(2)}, u32[]{:S(2)}) %collective-permute-start.50) | collective-permute-done | bytes 358432 | tf_op jit(solution)/shard_map/ppermute | solution.py:436
  739.4 4.2 collective-permute-done.53
  750.3 4.7 fusion.12
  756.2 4.0 collective-permute-start.62
  765.0 16.6 %collective-permute-done.60 = bf16[200,896]{1,0:T(8,128)(2,1)S(1)} collective-permute-done((bf16[200,896]{1,0:T(8,128)(2,1)}, bf16[200,896]{1,0:T(8,128)(2,1)S(1)}, u32[]{:S(2)}, u32[]{:S(2)}) %collective-permute-start.60) | collective-permute-done | bytes 358432 | tf_op jit(solution)/shard_map/ppermute | solution.py:436
  788.1 18.6 %collective-permute-done.54 = f32[64,128]{1,0:T(8,128)S(1)} collective-permute-done((f32[64,128]{1,0:T(8,128)S(1)}, f32[64,128]{1,0:T(8,128)S(1)}, u32[]{:S(2)}, u32[]{:S(2)}) %collective-permute-start.54) | collective-permute-done | bytes 32800 | tf_op jit(solution)/shard_map/ppermute | solution.py:436
  806.7 7.6 collective-permute-start.57
  819.9 5.1 maximum_select_fusion.3
  825.9 5.4 maximum_convert_fusion
  835.1 10.1 %collective-permute-done.59 = f32[64,128]{1,0:T(8,128)S(1)} collective-permute-done((f32[64,128]{1,0:T(8,128)S(1)}, f32[64,128]{1,0:T(8,128)S(1)}, u32[]{:S(2)}, u32[]{:S(2)}) %collective-permute-start.59) | collective-permute-done | bytes 32800 | tf_op jit(solution)/shard_map/ppermute | solution.py:436
  851.2 4.1 copy.108
  858.9 25.4 %collective-permute-done.69 = bf16[2,2,200,896]{3,2,1,0:T(8,128)(2,1)} collective-permute-done((bf16[2,2,200,896]{3,2,1,0:T(8,128)(2,1)}, bf16[2,2,200,896]{3,2,1,0:T(8,128)(2,1)}, u32[]{:S(2)}, u32[]{:S(2)}) %collective-permute-start.69) | collective-permute-done | bytes 1433632 | tf_op jit(solution)/shard_map/ppermute | solution.py:436
  893.1 3.9 maximum_convert_fusion.1
  (490 shorter events, 231.3 us)
Async XLA Ops:
  4.1 5.9 collective-permute-start.7
  7.9 13.1 %collective-permute-start.3 = (bf16[32,800]{1,0:T(8,128)(2,1)S(1)}, bf16[32,800]{1,0:T(8,128)(2,1)S(1)}, u32[]{:S(2)}, u32[]{:S(2)}) collective-permute-start(bf16[32,800]{1,0:T(8,128)(2,1)S(1)} %slice.315), channel_id=1, source_target_pairs={{0,1},{1,0},{2,3},{3,2},{4,5},{5,4},{6,7},{7,6},{8,9},{9,8},{10,11... | collective-permute-start | bytes 153608 | tf_op jit(solution)/shard_map/ppermute | solution.py:432
  18.7 16.9 %collective-permute-start.2 = (bf16[3,200,448]{2,1,0:T(8,128)(2,1)S(1)}, bf16[3,200,448]{2,1,0:T(8,128)(2,1)}, u32[]{:S(2)}, u32[]{:S(2)}) collective-permute-start(bf16[3,200,448]{2,1,0:T(8,128)(2,1)S(1)} %get-tuple-element.100), channel_id=1, source_target_pairs={{0,2},{2,0},{1,3},{3,1},{4,6},{6,4},{5,7},{7,5},{8,10},{10,8},{9,1... | collective-permute-start | bytes 1612808 | tf_op jit(solution)/shard_map/ppermute | solution.py:428
  18.9 68.8 %collective-permute-start.6 = (bf16[1,200,1600]{2,1,0:T(8,128)(2,1)S(1)}, bf16[1,200,1600]{2,1,0:T(8,128)(2,1)}, u32[]{:S(2)}, u32[]{:S(2)}) collective-permute-start(bf16[1,200,1600]{2,1,0:T(8,128)(2,1)S(1)} %bitcast.205), channel_id=1, source_target_pairs={{0,2},{2,0},{1,3},{3,1},{4,6},{6,4},{5,7},{7,5},{8,10},{10,8},{9,1... | collective-permute-start | bytes 1920008 | tf_op jit(solution)/shard_map/ppermute | solution.py:428
  21.0 54.4 %collective-permute-start.1 = (bf16[800,768]{1,0:T(8,128)(2,1)S(1)}, bf16[800,768]{1,0:T(8,128)(2,1)S(1)}, u32[]{:S(2)}, u32[]{:S(2)}) collective-permute-start(bf16[800,768]{1,0:T(8,128)(2,1)S(1)} %bitcast.220), channel_id=1, source_target_pairs={{0,2},{2,0},{1,3},{3,1},{4,6},{6,4},{5,7},{7,5},{8,10},{10,8},{9,1... | collective-permute-start | bytes 3686408 | tf_op jit(solution)/shard_map/ppermute | solution.py:428
  35.5 47.5 %collective-permute-start.4 = (bf16[3,200,448]{2,1,0:T(8,128)(2,1)}, bf16[3,200,448]{2,1,0:T(8,128)(2,1)}, u32[]{:S(2)}, u32[]{:S(2)}) collective-permute-start(bf16[3,200,448]{2,1,0:T(8,128)(2,1)} %collective-permute-done.2), channel_id=1, source_target_pairs={{0,8},{4,12},{8,0},{12,4},{16,24},{20,28},{24,16},{28,20},{1,9},{5... | collective-permute-start | bytes 1612808 | tf_op jit(solution)/shard_map/ppermute | solution.py:436
  82.1 41.5 %collective-permute-start.10 = (bf16[1600,768]{1,0:T(8,128)(2,1)}, bf16[1600,768]{1,0:T(8,128)(2,1)S(1)}, u32[]{:S(2)}, u32[]{:S(2)}) collective-permute-start(bf16[1600,768]{1,0:T(8,128)(2,1)} %get-tuple-element.281.own_ref), channel_id=1, source_target_pairs={{0,1},{1,0},{2,3},{3,2},{4,5},{5,4},{6,7},{7,6},{8,9},{9,8},{10,11... | collective-permute-start | bytes 7372808 | tf_op jit(solution)/shard_map/ppermute | solution.py:432
  82.1 7.1 collective-permute-start.11
  86.1 29.3 %collective-permute-start.9 = (bf16[3,2,200,448]{3,2,0,1:T(8,128)(2,1)}, bf16[3,2,200,448]{3,2,0,1:T(8,128)(2,1)}, u32[]{:S(2)}, u32[]{:S(2)}) collective-permute-start(bf16[3,2,200,448]{3,2,0,1:T(8,128)(2,1)} %maximum_select_fusion.25), channel_id=1, source_target_pairs={{0,4},{4,0},{8,12},{12,8},{16,20},{20,16},{24,28},{28,24},{1,5},{5... | collective-permute-start | bytes 3225608 | tf_op jit(solution)/shard_map/ppermute | solution.py:436
  87.7 17.0 %collective-permute-start.8 = (bf16[1,200,1600]{2,1,0:T(8,128)(2,1)}, bf16[1,200,1600]{2,1,0:T(8,128)(2,1)}, u32[]{:S(2)}, u32[]{:S(2)}) collective-permute-start(bf16[1,200,1600]{2,1,0:T(8,128)(2,1)} %collective-permute-done.6), channel_id=1, source_target_pairs={{0,8},{4,12},{8,0},{12,4},{16,24},{20,28},{24,16},{28,20},{1,9},{5... | collective-permute-start | bytes 1920008 | tf_op jit(solution)/shard_map/ppermute | solution.py:436
  89.7 49.2 %collective-permute-start.12 = (bf16[1,200,1600]{2,1,0:T(8,128)(2,1)}, bf16[1,200,1600]{2,1,0:T(8,128)(2,1)}, u32[]{:S(2)}, u32[]{:S(2)}) collective-permute-start(bf16[1,200,1600]{2,1,0:T(8,128)(2,1)} %bitcast.204), channel_id=1, source_target_pairs={{0,2},{2,0},{1,3},{3,1},{4,6},{6,4},{5,7},{7,5},{8,10},{10,8},{9,1... | collective-permute-start | bytes 1920008 | tf_op jit(solution)/shard_map/ppermute | solution.py:428
  90.0 50.6 %collective-permute-start.5 = (bf16[448,800]{1,0:T(8,128)(2,1)}, bf16[448,800]{1,0:T(8,128)(2,1)}, u32[]{:S(2)}, u32[]{:S(2)}) collective-permute-start(bf16[448,800]{1,0:T(8,128)(2,1)} %get-tuple-element.272), channel_id=1, source_target_pairs={{0,2},{2,0},{1,3},{3,1},{4,6},{6,4},{5,7},{7,5},{8,10},{10,8},{9,1... | collective-permute-start | bytes 2150408 | tf_op jit(solution)/shard_map/ppermute | solution.py:428
  138.9 16.3 %collective-permute-start.13 = (bf16[1,200,1600]{2,1,0:T(8,128)(2,1)}, bf16[1,200,1600]{2,1,0:T(8,128)(2,1)S(1)}, u32[]{:S(2)}, u32[]{:S(2)}) collective-permute-start(bf16[1,200,1600]{2,1,0:T(8,128)(2,1)} %collective-permute-done.12), channel_id=1, source_target_pairs={{0,8},{4,12},{8,0},{12,4},{16,24},{20,28},{24,16},{28,20},{1,9},{5... | collective-permute-start | bytes 1920008 | tf_op jit(solution)/shard_map/ppermute | solution.py:436
  185.9 11.4 %collective-permute-start.14 = (bf16[1600,768]{1,0:T(8,128)(2,1)S(1)}, bf16[1600,768]{1,0:T(8,128)(2,1)S(1)}, u32[]{:S(2)}, u32[]{:S(2)}) collective-permute-start(bf16[1600,768]{1,0:T(8,128)(2,1)S(1)} %mapped.6), channel_id=1, source_target_pairs={{0,1},{1,0},{2,3},{3,2},{4,5},{5,4},{6,7},{7,6},{8,9},{9,8},{10,11... | collective-permute-start | bytes 7372808 | tf_op jit(solution)/shard_map/ppermute | solution.py:432
  186.0 37.8 %collective-permute-start.15 = (bf16[1,2,200,1600]{3,2,1,0:T(8,128)(2,1)S(1)}, bf16[1,2,200,1600]{3,2,1,0:T(8,128)(2,1)S(1)}, u32[]{:S(2)}, u32[]{:S(2)}) collective-permute-start(bf16[1,2,200,1600]{3,2,1,0:T(8,128)(2,1)S(1)} %copy-done.48), channel_id=1, source_target_pairs={{0,4},{4,0},{8,12},{12,8},{16,20},{20,16},{24,28},{28,24},{1,5},{5... | collective-permute-start | bytes 3840008 | tf_op jit(solution)/shard_map/ppermute | solution.py:436
  197.2 54.9 %collective-permute-start.16 = (bf16[1,2,200,1600]{3,2,1,0:T(8,128)(2,1)}, bf16[1,2,200,1600]{3,2,1,0:T(8,128)(2,1)}, u32[]{:S(2)}, u32[]{:S(2)}) collective-permute-start(bf16[1,2,200,1600]{3,2,1,0:T(8,128)(2,1)} %maximum_select_fusion.22), channel_id=1, source_target_pairs={{0,4},{4,0},{8,12},{12,8},{16,20},{20,16},{24,28},{28,24},{1,5},{5... | collective-permute-start | bytes 3840008 | tf_op jit(solution)/shard_map/ppermute | solution.py:436
  200.6 64.5 %collective-permute-start.17 = (bf16[1600,768]{1,0:T(8,128)(2,1)}, bf16[1600,768]{1,0:T(8,128)(2,1)}, u32[]{:S(2)}, u32[]{:S(2)}) collective-permute-start(bf16[1600,768]{1,0:T(8,128)(2,1)} %mapped.7), channel_id=1, source_target_pairs={{0,2},{2,0},{1,3},{3,1},{4,6},{6,4},{5,7},{7,5},{8,10},{10,8},{9,1... | collective-permute-start | bytes 7372808 | tf_op jit(solution)/shard_map/ppermute | solution.py:428
  264.8 28.8 %collective-permute-start.18 = (bf16[800,768]{1,0:T(8,128)(2,1)S(1)}, bf16[800,768]{1,0:T(8,128)(2,1)S(1)}, u32[]{:S(2)}, u32[]{:S(2)}) collective-permute-start(bf16[800,768]{1,0:T(8,128)(2,1)S(1)} %bitcast.251), channel_id=1, source_target_pairs={{0,2},{2,0},{1,3},{3,1},{4,6},{6,4},{5,7},{7,5},{8,10},{10,8},{9,1... | collective-permute-start | bytes 3686408 | tf_op jit(solution)/shard_map/ppermute | solution.py:428
  275.7 19.3 %collective-permute-start.20 = (bf16[1600,768]{1,0:T(8,128)(2,1)}, bf16[1600,768]{1,0:T(8,128)(2,1)}, u32[]{:S(2)}, u32[]{:S(2)}) collective-permute-start(bf16[1600,768]{1,0:T(8,128)(2,1)} %get-tuple-element.262.own_ref), channel_id=1, source_target_pairs={{0,1},{1,0},{2,3},{3,2},{4,5},{5,4},{6,7},{7,6},{8,9},{9,8},{10,11... | collective-permute-start | bytes 7372808 | tf_op jit(solution)/shard_map/ppermute | solution.py:432
  294.5 19.7 %collective-permute-start.19 = (bf16[1600,768]{1,0:T(8,128)(2,1)S(1)}, bf16[1600,768]{1,0:T(8,128)(2,1)}, u32[]{:S(2)}, u32[]{:S(2)}) collective-permute-start(bf16[1600,768]{1,0:T(8,128)(2,1)S(1)} %maximum_select_fusion.12.own_ref), channel_id=1, source_target_pairs={{0,1},{1,0},{2,3},{3,2},{4,5},{5,4},{6,7},{7,6},{8,9},{9,8},{10,11... | collective-permute-start | bytes 7372808 | tf_op jit(solution)/shard_map/ppermute | solution.py:432
  322.2 62.5 %collective-permute-start.23 = (bf16[2,2,200,1600]{3,2,1,0:T(8,128)(2,1)}, bf16[2,2,200,1600]{3,2,1,0:T(8,128)(2,1)}, u32[]{:S(2)}, u32[]{:S(2)}) collective-permute-start(bf16[2,2,200,1600]{3,2,1,0:T(8,128)(2,1)} %bitcast.40), channel_id=1, source_target_pairs={{0,4},{4,0},{8,12},{12,8},{16,20},{20,16},{24,28},{28,24},{1,5},{5... | collective-permute-start | bytes 7680008 | tf_op jit(solution)/shard_map/ppermute | solution.py:436
  368.3 55.7 %collective-permute-start.22 = (bf16[1600,768]{1,0:T(8,128)(2,1)}, bf16[1600,768]{1,0:T(8,128)(2,1)}, u32[]{:S(2)}, u32[]{:S(2)}) collective-permute-start(bf16[1600,768]{1,0:T(8,128)(2,1)} %mapped.9), channel_id=1, source_target_pairs={{0,2},{2,0},{1,3},{3,1},{4,6},{6,4},{5,7},{7,5},{8,10},{10,8},{9,1... | collective-permute-start | bytes 7372808 | tf_op jit(solution)/shard_map/ppermute | solution.py:428
  395.4 31.5 %collective-permute-start.24 = (bf16[1600,768]{1,0:T(8,128)(2,1)S(1)}, bf16[1600,768]{1,0:T(8,128)(2,1)}, u32[]{:S(2)}, u32[]{:S(2)}) collective-permute-start(bf16[1600,768]{1,0:T(8,128)(2,1)S(1)} %mapped.10), channel_id=1, source_target_pairs={{0,1},{1,0},{2,3},{3,2},{4,5},{5,4},{6,7},{7,6},{8,9},{9,8},{10,11... | collective-permute-start | bytes 7372808 | tf_op jit(solution)/shard_map/ppermute | solution.py:432
  395.5 42.7 %collective-permute-start.25 = (bf16[2,200,1600]{2,1,0:T(8,128)(2,1)}, bf16[2,200,1600]{2,1,0:T(8,128)(2,1)}, u32[]{:S(2)}, u32[]{:S(2)}) collective-permute-start(bf16[2,200,1600]{2,1,0:T(8,128)(2,1)} %get-tuple-element.278), channel_id=1, source_target_pairs={{0,8},{4,12},{8,0},{12,4},{16,24},{20,28},{24,16},{28,20},{1,9},{5... | collective-permute-start | bytes 3840008 | tf_op jit(solution)/shard_map/ppermute | solution.py:436
  397.0 78.6 %collective-permute-start.28 = (bf16[2,2,200,1600]{3,2,1,0:T(8,128)(2,1)}, bf16[2,2,200,1600]{3,2,1,0:T(8,128)(2,1)}, u32[]{:S(2)}, u32[]{:S(2)}) collective-permute-start(bf16[2,2,200,1600]{3,2,1,0:T(8,128)(2,1)} %bitcast.200), channel_id=1, source_target_pairs={{0,4},{4,0},{8,12},{12,8},{16,20},{20,16},{24,28},{28,24},{1,5},{5... | collective-permute-start | bytes 7680008 | tf_op jit(solution)/shard_map/ppermute | solution.py:436
  441.7 31.6 %collective-permute-start.26 = (bf16[200,1600]{1,0:T(8,128)(2,1)}, bf16[200,1600]{1,0:T(8,128)(2,1)}, u32[]{:S(2)}, u32[]{:S(2)}) collective-permute-start(bf16[200,1600]{1,0:T(8,128)(2,1)} %get-tuple-element.302), channel_id=1, source_target_pairs={{0,16},{4,20},{8,24},{12,28},{16,0},{20,4},{24,8},{28,12},{1,17},{... | collective-permute-start | bytes 1920008 | tf_op jit(solution)/shard_map/ppermute | solution.py:436
  449.9 32.3 %collective-permute-start.27 = (bf16[1600,768]{1,0:T(8,128)(2,1)S(1)}, bf16[1600,768]{1,0:T(8,128)(2,1)}, u32[]{:S(2)}, u32[]{:S(2)}) collective-permute-start(bf16[1600,768]{1,0:T(8,128)(2,1)S(1)} %get-tuple-element.139.own_ref), channel_id=1, source_target_pairs={{0,1},{1,0},{2,3},{3,2},{4,5},{5,4},{6,7},{7,6},{8,9},{9,8},{10,11... | collective-permute-start | bytes 7372808 | tf_op jit(solution)/shard_map/ppermute | solution.py:432
  474.8 16.4 %collective-permute-start.29 = (bf16[200,1600]{1,0:T(8,128)(2,1)S(1)}, bf16[200,1600]{1,0:T(8,128)(2,1)S(1)}, u32[]{:S(2)}, u32[]{:S(2)}) collective-permute-start(bf16[200,1600]{1,0:T(8,128)(2,1)S(1)} %add_convert_fusion.14), channel_id=1, source_target_pairs={{2,4},{4,2},{10,12},{12,10},{18,20},{20,18},{26,28},{28,26},{3,5},... | collective-permute-start | bytes 1920008 | tf_op jit(solution)/shard_map/ppermute | solution.py:624
  480.3 49.8 %collective-permute-start.30 = (bf16[2,200,1600]{2,1,0:T(8,128)(2,1)}, bf16[2,200,1600]{2,1,0:T(8,128)(2,1)}, u32[]{:S(2)}, u32[]{:S(2)}) collective-permute-start(bf16[2,200,1600]{2,1,0:T(8,128)(2,1)} %get-tuple-element.276), channel_id=1, source_target_pairs={{0,8},{4,12},{8,0},{12,4},{16,24},{20,28},{24,16},{28,20},{1,9},{5... | collective-permute-start | bytes 3840008 | tf_op jit(solution)/shard_map/ppermute | solution.py:436
  491.3 57.6 %collective-permute-start.32 = (bf16[200,1600]{1,0:T(8,128)(2,1)S(1)}, bf16[200,1600]{1,0:T(8,128)(2,1)S(1)}, u32[]{:S(2)}, u32[]{:S(2)}) collective-permute-start(bf16[200,1600]{1,0:T(8,128)(2,1)S(1)} %broadcast_select_fusion.4), channel_id=1, source_target_pairs={{0,16},{4,20},{8,24},{12,28},{16,0},{20,4},{24,8},{28,12},{1,17},{... | collective-permute-start | bytes 1920008 | tf_op jit(solution)/shard_map/ppermute | solution.py:436
  523.8 23.9 %collective-permute-start.31 = (bf16[2,2,200,448]{3,2,1,0:T(8,128)(2,1)S(1)}, bf16[2,2,200,448]{3,2,1,0:T(8,128)(2,1)S(1)}, u32[]{:S(2)}, u32[]{:S(2)}) collective-permute-start(bf16[2,2,200,448]{3,2,1,0:T(8,128)(2,1)S(1)} %bitcast.203), channel_id=1, source_target_pairs={{0,8},{4,12},{8,0},{12,4},{16,24},{20,28},{24,16},{28,20},{1,9},{5... | collective-permute-start | bytes 2150408 | tf_op jit(solution)/shard_map/ppermute | solution.py:436
  570.2 41.2 %collective-permute-start.35 = (bf16[1600,768]{1,0:T(8,128)(2,1)}, bf16[1600,768]{1,0:T(8,128)(2,1)}, u32[]{:S(2)}, u32[]{:S(2)}) collective-permute-start(bf16[1600,768]{1,0:T(8,128)(2,1)} %mapped_three.2), channel_id=1, source_target_pairs={{0,1},{1,0},{2,3},{3,2},{4,5},{5,4},{6,7},{7,6},{8,9},{9,8},{10,11... | collective-permute-start | bytes 7372808 | tf_op jit(solution)/shard_map/ppermute | solution.py:432
  570.3 14.6 %collective-permute-start.33 = (bf16[2,200,448]{2,1,0:T(8,128)(2,1)}, bf16[2,200,448]{2,1,0:T(8,128)(2,1)S(1)}, u32[]{:S(2)}, u32[]{:S(2)}) collective-permute-start(bf16[2,200,448]{2,1,0:T(8,128)(2,1)} %get-tuple-element.306), channel_id=1, source_target_pairs={{0,4},{4,0},{8,12},{12,8},{16,20},{20,16},{24,28},{28,24},{1,5},{5... | collective-permute-start | bytes 1075208 | tf_op jit(solution)/shard_map/ppermute | solution.py:436
  578.8 32.4 %collective-permute-start.34 = (bf16[200,1600]{1,0:T(8,128)(2,1)S(1)}, bf16[200,1600]{1,0:T(8,128)(2,1)S(1)}, u32[]{:S(2)}, u32[]{:S(2)}) collective-permute-start(bf16[200,1600]{1,0:T(8,128)(2,1)S(1)} %copy-done.58), channel_id=1, source_target_pairs={{0,16},{4,20},{8,24},{12,28},{16,0},{20,4},{24,8},{28,12},{1,17},{... | collective-permute-start | bytes 1920008 | tf_op jit(solution)/shard_map/ppermute | solution.py:436
  579.3 50.6 %collective-permute-start.37 = (bf16[2,200,1600]{2,1,0:T(8,128)(2,1)S(1)}, bf16[2,200,1600]{2,1,0:T(8,128)(2,1)}, u32[]{:S(2)}, u32[]{:S(2)}) collective-permute-start(bf16[2,200,1600]{2,1,0:T(8,128)(2,1)S(1)} %copy-done.47), channel_id=1, source_target_pairs={{0,8},{4,12},{8,0},{12,4},{16,24},{20,28},{24,16},{28,20},{1,9},{5... | collective-permute-start | bytes 3840008 | tf_op jit(solution)/shard_map/ppermute | solution.py:436
  582.2 121.9 %collective-permute-start.47 = (bf16[800,768]{1,0:T(8,128)(2,1)}, bf16[800,768]{1,0:T(8,128)(2,1)}, u32[]{:S(2)}, u32[]{:S(2)}) collective-permute-start(bf16[800,768]{1,0:T(8,128)(2,1)} %broadcast_select_fusion), channel_id=1, source_target_pairs={{0,2},{2,0},{1,3},{3,1},{4,6},{6,4},{5,7},{7,5},{8,10},{10,8},{9,1... | collective-permute-start | bytes 3686408 | tf_op jit(solution)/shard_map/ppermute | solution.py:428
  584.9 66.0 %collective-permute-start.39 = (bf16[2,2,200,896]{3,2,1,0:T(8,128)(2,1)S(1)}, bf16[2,2,200,896]{3,2,1,0:T(8,128)(2,1)S(1)}, u32[]{:S(2)}, u32[]{:S(2)}) collective-permute-start(bf16[2,2,200,896]{3,2,1,0:T(8,128)(2,1)S(1)} %bitcast.201), channel_id=1, source_target_pairs={{0,4},{4,0},{8,12},{12,8},{16,20},{20,16},{24,28},{28,24},{1,5},{5... | collective-permute-start | bytes 4300808 | tf_op jit(solution)/shard_map/ppermute | solution.py:436
  611.2 16.4 %collective-permute-start.36 = (bf16[200,448]{1,0:T(8,128)(2,1)S(1)}, bf16[200,448]{1,0:T(8,128)(2,1)S(1)}, u32[]{:S(2)}, u32[]{:S(2)}) collective-permute-start(bf16[200,448]{1,0:T(8,128)(2,1)S(1)} %get-tuple-element.312), channel_id=1, source_target_pairs={{0,16},{4,20},{8,24},{12,28},{16,0},{20,4},{24,8},{28,12},{1,17},{... | collective-permute-start | bytes 537608 | tf_op jit(solution)/shard_map/ppermute | solution.py:436
  611.4 70.5 %collective-permute-start.42 = (bf16[2,2,200,448]{3,2,1,0:T(8,128)(2,1)S(1)}, bf16[2,2,200,448]{3,2,1,0:T(8,128)(2,1)}, u32[]{:S(2)}, u32[]{:S(2)}) collective-permute-start(bf16[2,2,200,448]{3,2,1,0:T(8,128)(2,1)S(1)} %bitcast.202), channel_id=1, source_target_pairs={{0,8},{4,12},{8,0},{12,4},{16,24},{20,28},{24,16},{28,20},{1,9},{5... | collective-permute-start | bytes 2150408 | tf_op jit(solution)/shard_map/ppermute | solution.py:436
  627.6 6.1 collective-permute-start.38
  629.9 26.4 %collective-permute-start.40 = (bf16[200,448]{1,0:T(8,128)(2,1)S(1)}, bf16[200,448]{1,0:T(8,128)(2,1)S(1)}, u32[]{:S(2)}, u32[]{:S(2)}) collective-permute-start(bf16[200,448]{1,0:T(8,128)(2,1)S(1)} %add_convert_fusion.19), channel_id=1, source_target_pairs={{2,4},{4,2},{10,12},{12,10},{18,20},{20,18},{26,28},{28,26},{3,5},... | collective-permute-start | bytes 537608 | tf_op jit(solution)/shard_map/ppermute | solution.py:624
  633.6 43.5 %collective-permute-start.41 = (bf16[800,768]{1,0:T(8,128)(2,1)S(1)}, bf16[800,768]{1,0:T(8,128)(2,1)S(1)}, u32[]{:S(2)}, u32[]{:S(2)}) collective-permute-start(bf16[800,768]{1,0:T(8,128)(2,1)S(1)} %select_convert_fusion), channel_id=1, source_target_pairs={{0,2},{2,0},{1,3},{3,1},{4,6},{6,4},{5,7},{7,5},{8,10},{10,8},{9,1... | collective-permute-start | bytes 3686408 | tf_op jit(solution)/shard_map/ppermute | solution.py:428
  650.9 32.6 %collective-permute-start.43 = (bf16[200,1600]{1,0:T(8,128)(2,1)S(1)}, bf16[200,1600]{1,0:T(8,128)(2,1)S(1)}, u32[]{:S(2)}, u32[]{:S(2)}) collective-permute-start(bf16[200,1600]{1,0:T(8,128)(2,1)S(1)} %broadcast_select_fusion.3), channel_id=1, source_target_pairs={{0,16},{4,20},{8,24},{12,28},{16,0},{20,4},{24,8},{28,12},{1,17},{... | collective-permute-start | bytes 1920008 | tf_op jit(solution)/shard_map/ppermute | solution.py:436
  656.3 60.8 %collective-permute-start.48 = (bf16[2,2,200,1600]{3,2,1,0:T(8,128)(2,1)S(1)}, bf16[2,2,200,1600]{3,2,1,0:T(8,128)(2,1)}, u32[]{:S(2)}, u32[]{:S(2)}) collective-permute-start(bf16[2,2,200,1600]{3,2,1,0:T(8,128)(2,1)S(1)} %maximum_select_fusion.8), channel_id=1, source_target_pairs={{0,4},{4,0},{8,12},{12,8},{16,20},{20,16},{24,28},{28,24},{1,5},{5... | collective-permute-start | bytes 7680008 | tf_op jit(solution)/shard_map/ppermute | solution.py:436
  677.2 24.9 %collective-permute-start.46 = (bf16[2,200,896]{2,1,0:T(8,128)(2,1)}, bf16[2,200,896]{2,1,0:T(8,128)(2,1)S(1)}, u32[]{:S(2)}, u32[]{:S(2)}) collective-permute-start(bf16[2,200,896]{2,1,0:T(8,128)(2,1)} %get-tuple-element.297), channel_id=1, source_target_pairs={{0,8},{4,12},{8,0},{12,4},{16,24},{20,28},{24,16},{28,20},{1,9},{5... | collective-permute-start | bytes 2150408 | tf_op jit(solution)/shard_map/ppermute | solution.py:436
  681.9 19.7 %collective-permute-start.45 = (bf16[200,448]{1,0:T(8,128)(2,1)S(1)}, bf16[200,448]{1,0:T(8,128)(2,1)S(1)}, u32[]{:S(2)}, u32[]{:S(2)}) collective-permute-start(bf16[200,448]{1,0:T(8,128)(2,1)S(1)} %broadcast_select_fusion.7), channel_id=1, source_target_pairs={{0,16},{4,20},{8,24},{12,28},{16,0},{20,4},{24,8},{28,12},{1,17},{... | collective-permute-start | bytes 537608 | tf_op jit(solution)/shard_map/ppermute | solution.py:436
  687.2 57.4 %collective-permute-start.56 = (bf16[2,200,1600]{2,1,0:T(8,128)(2,1)S(1)}, bf16[2,200,1600]{2,1,0:T(8,128)(2,1)S(1)}, u32[]{:S(2)}, u32[]{:S(2)}) collective-permute-start(bf16[2,200,1600]{2,1,0:T(8,128)(2,1)S(1)} %maximum_select_fusion.24), channel_id=1, source_target_pairs={{0,8},{4,12},{8,0},{12,4},{16,24},{20,28},{24,16},{28,20},{1,9},{5... | collective-permute-start | bytes 3840008 | tf_op jit(solution)/shard_map/ppermute | solution.py:436
  701.6 25.2 %collective-permute-start.49 = (bf16[2,200,448]{2,1,0:T(8,128)(2,1)S(1)}, bf16[2,200,448]{2,1,0:T(8,128)(2,1)S(1)}, u32[]{:S(2)}, u32[]{:S(2)}) collective-permute-start(bf16[2,200,448]{2,1,0:T(8,128)(2,1)S(1)} %get-tuple-element.304), channel_id=1, source_target_pairs={{0,4},{4,0},{8,12},{12,8},{16,20},{20,16},{24,28},{28,24},{1,5},{5... | collective-permute-start | bytes 1075208 | tf_op jit(solution)/shard_map/ppermute | solution.py:436
  702.1 36.2 %collective-permute-start.52 = (bf16[2,200,448]{2,1,0:T(8,128)(2,1)S(1)}, bf16[2,200,448]{2,1,0:T(8,128)(2,1)S(1)}, u32[]{:S(2)}, u32[]{:S(2)}) collective-permute-start(bf16[2,200,448]{2,1,0:T(8,128)(2,1)S(1)} %maximum_select_fusion.29), channel_id=1, source_target_pairs={{0,4},{4,0},{8,12},{12,8},{16,20},{20,16},{24,28},{28,24},{1,5},{5... | collective-permute-start | bytes 1075208 | tf_op jit(solution)/shard_map/ppermute | solution.py:436
  707.1 30.4 %collective-permute-start.50 = (bf16[200,896]{1,0:T(8,128)(2,1)S(1)}, bf16[200,896]{1,0:T(8,128)(2,1)S(1)}, u32[]{:S(2)}, u32[]{:S(2)}) collective-permute-start(bf16[200,896]{1,0:T(8,128)(2,1)S(1)} %get-tuple-element.308), channel_id=1, source_target_pairs={{0,16},{4,20},{8,24},{12,28},{16,0},{20,4},{24,8},{28,12},{1,17},{... | collective-permute-start | bytes 1075208 | tf_op jit(solution)/shard_map/ppermute | solution.py:436
  727.0 16.7 %collective-permute-start.53 = (bf16[200,448]{1,0:T(8,128)(2,1)S(1)}, bf16[200,448]{1,0:T(8,128)(2,1)S(1)}, u32[]{:S(2)}, u32[]{:S(2)}) collective-permute-start(bf16[200,448]{1,0:T(8,128)(2,1)S(1)} %get-tuple-element.310), channel_id=1, source_target_pairs={{0,16},{4,20},{8,24},{12,28},{16,0},{20,4},{24,8},{28,12},{1,17},{... | collective-permute-start | bytes 537608 | tf_op jit(solution)/shard_map/ppermute | solution.py:436
  737.6 6.1 collective-permute-start.55
  746.5 73.4 %collective-permute-start.64 = (bf16[2,2,200,1600]{3,2,0,1:T(8,128)(2,1)}, bf16[2,2,200,1600]{3,2,0,1:T(8,128)(2,1)}, u32[]{:S(2)}, u32[]{:S(2)}) collective-permute-start(bf16[2,2,200,1600]{3,2,0,1:T(8,128)(2,1)} %maximum_select_fusion.9), channel_id=1, source_target_pairs={{0,4},{4,0},{8,12},{12,8},{16,20},{20,16},{24,28},{28,24},{1,5},{5... | collective-permute-start | bytes 7680008 | tf_op jit(solution)/shard_map/ppermute | solution.py:436
  756.2 30.0 %collective-permute-start.62 = (bf16[2,2,200,448]{3,2,1,0:T(8,128)(2,1)S(1)}, bf16[2,2,200,448]{3,2,1,0:T(8,128)(2,1)S(1)}, u32[]{:S(2)}, u32[]{:S(2)}) collective-permute-start(bf16[2,2,200,448]{3,2,1,0:T(8,128)(2,1)S(1)} %copy-done.54), channel_id=1, source_target_pairs={{0,8},{4,12},{8,0},{12,4},{16,24},{20,28},{24,16},{28,20},{1,9},{5... | collective-permute-start | bytes 2150408 | tf_op jit(solution)/shard_map/ppermute | solution.py:436
  761.0 20.5 %collective-permute-start.60 = (bf16[200,896]{1,0:T(8,128)(2,1)}, bf16[200,896]{1,0:T(8,128)(2,1)S(1)}, u32[]{:S(2)}, u32[]{:S(2)}) collective-permute-start(bf16[200,896]{1,0:T(8,128)(2,1)} %broadcast_select_fusion.5), channel_id=1, source_target_pairs={{0,16},{4,20},{8,24},{12,28},{16,0},{20,4},{24,8},{28,12},{1,17},{... | collective-permute-start | bytes 1075208 | tf_op jit(solution)/shard_map/ppermute | solution.py:436
  761.8 24.3 %collective-permute-start.61 = (bf16[200,448]{1,0:T(8,128)(2,1)S(1)}, bf16[200,448]{1,0:T(8,128)(2,1)S(1)}, u32[]{:S(2)}, u32[]{:S(2)}) collective-permute-start(bf16[200,448]{1,0:T(8,128)(2,1)S(1)} %broadcast_select_fusion.6), channel_id=1, source_target_pairs={{0,16},{4,20},{8,24},{12,28},{16,0},{20,4},{24,8},{28,12},{1,17},{... | collective-permute-start | bytes 537608 | tf_op jit(solution)/shard_map/ppermute | solution.py:436
  786.9 30.3 %collective-permute-start.63 = (bf16[800,32]{1,0:T(8,128)(2,1)S(1)}, bf16[800,32]{1,0:T(8,128)(2,1)S(1)}, u32[]{:S(2)}, u32[]{:S(2)}) collective-permute-start(bf16[800,32]{1,0:T(8,128)(2,1)S(1)} %slice.437), channel_id=1, source_target_pairs={{0,1},{1,0},{2,3},{3,2},{4,5},{5,4},{6,7},{7,6},{8,9},{9,8},{10,11... | collective-permute-start | bytes 153608 | tf_op jit(solution)/shard_map/ppermute | solution.py:432
  786.9 19.7 %collective-permute-start.54 = (f32[64,128]{1,0:T(8,128)S(1)}, f32[64,128]{1,0:T(8,128)S(1)}, u32[]{:S(2)}, u32[]{:S(2)}) collective-permute-start(f32[64,128]{1,0:T(8,128)S(1)} %pad_bitcast_fusion), channel_id=1, source_target_pairs={{0,4},{4,0},{8,12},{12,8},{16,20},{20,16},{24,28},{28,24},{1,5},{5... | collective-permute-start | bytes 98312 | tf_op jit(solution)/shard_map/ppermute | solution.py:436
  806.7 28.4 %collective-permute-start.57 = (f32[64,128]{1,0:T(8,128)S(1)}, f32[64,128]{1,0:T(8,128)S(1)}, u32[]{:S(2)}, u32[]{:S(2)}) collective-permute-start(f32[64,128]{1,0:T(8,128)S(1)} %add.339), channel_id=1, source_target_pairs={{0,8},{4,12},{8,0},{12,4},{16,24},{20,28},{24,16},{28,20},{1,9},{5... | collective-permute-start | bytes 98312 | tf_op jit(solution)/shard_map/ppermute | solution.py:436
  814.3 18.6 %collective-permute-start.66 = (bf16[2,200,448]{2,1,0:T(8,128)(2,1)S(1)}, bf16[2,200,448]{2,1,0:T(8,128)(2,1)S(1)}, u32[]{:S(2)}, u32[]{:S(2)}) collective-permute-start(bf16[2,200,448]{2,1,0:T(8,128)(2,1)S(1)} %maximum_select_fusion.30), channel_id=1, source_target_pairs={{0,4},{4,0},{8,12},{12,8},{16,20},{20,16},{24,28},{28,24},{1,5},{5... | collective-permute-start | bytes 1075208 | tf_op jit(solution)/shard_map/ppermute | solution.py:436
  816.8 14.5 %collective-permute-start.65 = (bf16[2,200,896]{2,1,0:T(8,128)(2,1)S(1)}, bf16[2,200,896]{2,1,0:T(8,128)(2,1)S(1)}, u32[]{:S(2)}, u32[]{:S(2)}) collective-permute-start(bf16[2,200,896]{2,1,0:T(8,128)(2,1)S(1)} %maximum_select_fusion.28), channel_id=1, source_target_pairs={{0,8},{4,12},{8,0},{12,4},{16,24},{20,28},{24,16},{28,20},{1,9},{5... | collective-permute-start | bytes 2150408 | tf_op jit(solution)/shard_map/ppermute | solution.py:436
  833.1 22.3 %collective-permute-start.67 = (bf16[2,2,200,448]{3,2,1,0:T(8,128)(2,1)S(1)}, bf16[2,2,200,448]{3,2,1,0:T(8,128)(2,1)S(1)}, u32[]{:S(2)}, u32[]{:S(2)}) collective-permute-start(bf16[2,2,200,448]{3,2,1,0:T(8,128)(2,1)S(1)} %maximum_select_fusion.27), channel_id=1, source_target_pairs={{0,8},{4,12},{8,0},{12,4},{16,24},{20,28},{24,16},{28,20},{1,9},{5... | collective-permute-start | bytes 2150408 | tf_op jit(solution)/shard_map/ppermute | solution.py:436
  835.1 10.2 %collective-permute-start.59 = (f32[64,128]{1,0:T(8,128)S(1)}, f32[64,128]{1,0:T(8,128)S(1)}, u32[]{:S(2)}, u32[]{:S(2)}) collective-permute-start(f32[64,128]{1,0:T(8,128)S(1)} %add.340), channel_id=1, source_target_pairs={{0,16},{4,20},{8,24},{12,28},{16,0},{20,4},{24,8},{28,12},{1,17},{... | collective-permute-start | bytes 98312 | tf_op jit(solution)/shard_map/ppermute | solution.py:436
  850.1 34.1 %collective-permute-start.69 = (bf16[2,2,200,896]{3,2,1,0:T(8,128)(2,1)}, bf16[2,2,200,896]{3,2,1,0:T(8,128)(2,1)}, u32[]{:S(2)}, u32[]{:S(2)}) collective-permute-start(bf16[2,2,200,896]{3,2,1,0:T(8,128)(2,1)} %maximum_select_fusion.17), channel_id=1, source_target_pairs={{0,4},{4,0},{8,12},{12,8},{16,20},{20,16},{24,28},{28,24},{1,5},{5... | collective-permute-start | bytes 4300808 | tf_op jit(solution)/shard_map/ppermute | solution.py:436
  (95 other events, 979.0 us)

commit v3 on v2

--- a/solution.py
+++ b/solution.py
@@ -14,6 +14,7 @@
 BLK = 256
 NEG = -1e30
 KERNEL_VMEM = 40 * 2**20
+WIDE_VMEM = 58 * 2**20
 
 
 def dot_over(dims, a, b):
@@ -108,7 +109,7 @@
             jax.ShapeDtypeStruct((8, tokens), jnp.float32),
         ],
         compiler_params=pltpu.CompilerParams(vmem_limit_bytes=KERNEL_VMEM),
-        cost_estimate=pl.CostEstimate(flops=0, bytes_accessed=2 * tokens * wide, transcendentals=0),
+        cost_estimate=pl.CostEstimate(flops=0, bytes_accessed=0, transcendentals=0),
         name="attend",
     )(info, projected, projected, projected, first)
 
@@ -198,22 +199,26 @@
         ),
         out_shape=jax.ShapeDtypeStruct((3 * wide, tokens), jnp.bfloat16),
         compiler_params=pltpu.CompilerParams(vmem_limit_bytes=KERNEL_VMEM),
-        cost_estimate=pl.CostEstimate(flops=0, bytes_accessed=2 * tokens * wide, transcendentals=0),
+        cost_estimate=pl.CostEstimate(flops=0, bytes_accessed=0, transcendentals=0),
         name="attend_back",
     )(info, projected, projected, projected, attended, grad, log_totals, first)
 
 
-def call(body, name, grid, specs, args, out_specs, out_shapes, scalars=None, scratch=()):
+def call(body, name, grid, specs, args, out_specs, out_shapes, scalars=None, vmem=KERNEL_VMEM):
     return pl.pallas_call(
         body,
         grid_spec=pltpu.PrefetchScalarGridSpec(
-            num_scalar_prefetch=1, grid=grid, in_specs=specs, out_specs=out_specs, scratch_shapes=scratch
+            num_scalar_prefetch=1, grid=grid, in_specs=specs, out_specs=out_specs
         ),
         out_shape=out_shapes,
-        compiler_params=pltpu.CompilerParams(vmem_limit_bytes=KERNEL_VMEM),
+        compiler_params=pltpu.CompilerParams(vmem_limit_bytes=vmem),
         cost_estimate=pl.CostEstimate(flops=0, bytes_accessed=0, transcendentals=0),
         name=name,
     )(jnp.zeros((1,), jnp.int32) if scalars is None else scalars, *args)
+
+
+f32 = jnp.float32
+bf16 = jnp.bfloat16
 
 
 def shape(*dims, dtype=jnp.bfloat16):
@@ -401,20 +406,28 @@
     )
 
 
-def weight_grad(own, other, right, order, parts, part):
-    rows, count = own.shape
-    (place, width), size = part, rows // parts
-
-    def body(_, own_ref, other_ref, r_ref, o_ref):
-        o_ref[0] = (nt(own_ref[0], r_ref[:, :count]) + nt(other_ref[0], r_ref[:, count:])).astype(jnp.bfloat16)
+def weight_grad(sources, order, parts):
+    rows, count = sources[0][0].shape
+    size = rows // parts
+    widths = [part[1] for _, _, _, part in sources]
+
+    def body(_, *refs):
+        o_ref, at = refs[-1], 0
+        for i, width in enumerate(widths):
+            own_ref, other_ref, r_ref = refs[3 * i : 3 * i + 3]
+            grad = nt(own_ref[0], r_ref[:, :count]) + nt(other_ref[0], r_ref[:, count:])
+            o_ref[0, :, at : at + width] = grad.astype(bf16)
+            at += width
 
     tile = pl.BlockSpec((1, size, count), lambda i, s: (s[i], 0, 0))
-    return call(
-        body, "weight_grad", order.shape,
-        [tile, tile, pl.BlockSpec((width, 2 * count), lambda i, s: (place, 0))],
-        (own.reshape(parts, size, count), other.reshape(parts, size, count), right),
-        pl.BlockSpec((1, size, width), lambda i, s: (i, 0, 0)),
-        shape(order.shape[0], size, width),
+    specs, args = [], []
+    for own, other, right, (place, width) in sources:
+        specs += [tile, tile, pl.BlockSpec((width, 2 * count), lambda i, s, place=place: (place, 0))]
+        args += [own.reshape(parts, size, count), other.reshape(parts, size, count), right]
+    return call(
+        body, "weight_grad", order.shape, specs, tuple(args),
+        pl.BlockSpec((1, size, sum(widths)), lambda i, s: (i, 0, 0)),
+        shape(order.shape[0], size, sum(widths)),
         scalars=order,
     )
 
@@ -446,10 +459,6 @@
         jnp.concatenate([first, second], axis=axis),
         jnp.concatenate([second, first], axis=axis),
     )
-
-
-def paired(at, first, second, axis):
-    return ordered(at, jnp.expand_dims(first, axis), jnp.expand_dims(second, axis), axis)
 
 
 def half_of(at, value, axis):
@@ -500,45 +509,56 @@
     )
 
 
+def put_slots(o_ref, q_ref, t_ref, core, second, most):
+    size, spare = q_ref.shape[-1], t_ref.shape[-1]
+    less = most - HEAD_DIM
+
+    @pl.when((core == 0) & (second == 0))
+    def _():
+        o_ref[...] = q_ref[:, 0, :, :most]
+
+    @pl.when((core == 0) & (second == 1))
+    def _():
+        o_ref[...] = jnp.zeros_like(o_ref)
+        o_ref[:, :, : size - most] = q_ref[:, 0, :, most:]
+        o_ref[:, :, size - most : size - most + spare] = t_ref[:, 0]
+
+    @pl.when((core == 1) & (second == 0))
+    def _():
+        o_ref[...] = jnp.zeros_like(o_ref)
+        o_ref[:, :, :less] = q_ref[:, 0, :, spare : spare + less]
+
+    @pl.when((core == 1) & (second == 1))
+    def _():
+        o_ref[...] = jnp.zeros_like(o_ref)
+        o_ref[:, :, :less] = q_ref[:, 0, :, spare + less :]
+
+
+def put_half(o_ref, f_ref, second):
+    wide = f_ref.shape[-1] // 2
+
+    @pl.when(second == 0)
+    def _():
+        o_ref[...] = f_ref[0, :, :wide]
+
+    @pl.when(second == 1)
+    def _():
+        o_ref[...] = f_ref[0, :, wide:]
+
+
+def quarters(value):
+    return value.reshape(value.shape[:-2] + (4, value.shape[-2] // 4, value.shape[-1]))
+
+
 def pack(qkv, tail, fc, proj, c, r, at, most):
-    rows, size = qkv.shape[1] // 4, qkv.shape[2]
-    spare, less, wide = tail.shape[2], most - HEAD_DIM, fc.shape[1] // 2
+    rows, size, spare, wide = qkv.shape[1] // 4, qkv.shape[2], tail.shape[2], fc.shape[1] // 2
     scalars = jnp.stack([at, c, r]).astype(jnp.int32)
 
     def body(s_ref, q_ref, t_ref, f_ref, p_ref, qo_ref, fo_ref, po_ref):
-        core, row = s_ref[1], s_ref[2]
-
-        @pl.when((core == 0) & (row == 1))
-        def _():
-            qo_ref[...] = q_ref[:, 0, :, :most]
-
-        @pl.when((core == 0) & (row == 0))
-        def _():
-            qo_ref[...] = jnp.zeros_like(qo_ref)
-            qo_ref[:, :, : size - most] = q_ref[:, 0, :, most:]
-            qo_ref[:, :, size - most : size - most + spare] = t_ref[:, 0]
-
-        @pl.when((core == 1) & (row == 1))
-        def _():
-            qo_ref[...] = jnp.zeros_like(qo_ref)
-            qo_ref[:, :, :less] = q_ref[:, 0, :, spare : spare + less]
-
-        @pl.when((core == 1) & (row == 0))
-        def _():
-            qo_ref[...] = jnp.zeros_like(qo_ref)
-            qo_ref[:, :, :less] = q_ref[:, 0, :, spare + less :]
-
-        @pl.when(row == 0)
-        def _():
-            fo_ref[...] = f_ref[0, :, wide:]
-            po_ref[...] = p_ref[0, :, wide:]
-
-        @pl.when(row == 1)
-        def _():
-            fo_ref[...] = f_ref[0, :, :wide]
-            po_ref[...] = p_ref[0, :, :wide]
-
-    quarter = lambda v: v.reshape(v.shape[:-2] + (4, rows, v.shape[-1]))
+        put_slots(qo_ref, q_ref, t_ref, s_ref[1], 1 - s_ref[2], most)
+        put_half(fo_ref, f_ref, 1 - s_ref[2])
+        put_half(po_ref, p_ref, 1 - s_ref[2])
+
     return call(
         body, "pack", (1,),
         [
@@ -547,40 +567,488 @@
             pl.BlockSpec((1, rows, 2 * wide), lambda i, s: (s[0], 0, 0)),
             pl.BlockSpec((1, rows, 2 * wide), lambda i, s: (s[0], 0, 0)),
         ],
-        tuple(quarter(v) for v in (qkv, tail, fc, proj)),
+        tuple(quarters(v) for v in (qkv, tail, fc, proj)),
         [pl.BlockSpec((3, rows, most), lambda i, s: (0, 0, 0))] + [pl.BlockSpec((rows, wide), lambda i, s: (0, 0))] * 2,
         [shape(3, rows, most), shape(rows, wide), shape(rows, wide)],
-        scalars=scalars,
+        scalars=scalars, vmem=WIDE_VMEM,
+    )
+
+
+def own_rows(mine, tail, c, r, width):
+    three = mine.ndim == 3
+    rows, size = mine.shape[-2] // 4, mine.shape[-1]
+
+    def body(s_ref, m_ref, *refs):
+        t_ref, o_ref = refs if three else (None,) + refs
+        if three:
+            put_slots(o_ref.at[:, 0], m_ref, t_ref, s_ref[1], s_ref[0], width)
+        else:
+            put_half(o_ref.at[0], m_ref, s_ref[0])
+
+    lead, zero = ((3,), (0,)) if three else ((), ())
+    block = lambda width, at: pl.BlockSpec(lead + (1, rows, width), lambda i, s: zero + (at(i, s), 0, 0))
+    own = lambda i, s: i
+    return call(
+        body, "own_rows", (4,),
+        [block(size, own)] + ([block(tail.shape[-1], own)] if three else []),
+        tuple([quarters(mine)] + ([quarters(tail)] if three else [])),
+        block(width, lambda i, s: 4 * s[0] + i), shape(*lead, 8, rows, width),
+        scalars=jnp.stack([r, c]).astype(jnp.int32), vmem=WIDE_VMEM,
+    )
+
+
+def all_rows(held, got, r, y, z):
+    lead, tile = held.shape[:-3], held.shape[-2:]
+    zero = (0,) * len(lead)
+
+    def body(s_ref, h_ref, *refs):
+        o_ref = refs[-1]
+        place = (pl.program_id(0) // 2 != s_ref[2]) * 2 + (pl.program_id(0) % 2 != s_ref[1])
+        for i in range(4):
+
+            @pl.when(place == i)
+            def _(i=i):
+                o_ref[...] = refs[i][...].reshape(o_ref.shape)
+
+    fetched = pl.BlockSpec(lead + tile, lambda i, s: zero + (0, 0))
+    out = pl.pallas_call(
+        body,
+        grid_spec=pltpu.PrefetchScalarGridSpec(
+            num_scalar_prefetch=1,
+            grid=(4,),
+            in_specs=[pl.BlockSpec(memory_space=pl.ANY)] + [fetched] * 4,
+            out_specs=pl.BlockSpec(lead + (1,) + tile, lambda i, s: zero + (4 * (1 - s[0]) + i, 0, 0)),
+        ),
+        out_shape=shape(*held.shape),
+        input_output_aliases={1: 0},
+        compiler_params=pltpu.CompilerParams(vmem_limit_bytes=KERNEL_VMEM),
+        cost_estimate=pl.CostEstimate(flops=0, bytes_accessed=0, transcendentals=0),
+        name="all_rows",
+    )(jnp.stack([r, y, z]).astype(jnp.int32), held, *got)
+    return out.reshape(lead + (8 * tile[0], tile[1]))
+
+
+def half_rows(value, at):
+    rows, count = value.shape[0] // 2, value.shape[1]
+
+    def body(_, a_ref, o_ref):
+        o_ref[...] = a_ref[...].astype(bf16)
+
+    return call(
+        body, "half_rows", (count // 256,),
+        [pl.BlockSpec((rows, 256), lambda i, s: (s[0], i))], (value,),
+        pl.BlockSpec((rows, 256), lambda i, s: (0, i)), shape(rows, count), scalars=at[None].astype(jnp.int32),
+    )
+
+
+def packed_sums(sums_two, sums_one, grad_own, hidden_sums, parts, most):
+    width, half = sums_two.shape[1], sums_one.shape[1]
+
+    def body(_, two_ref, one_ref, grad_ref, hid_ref, p_ref, o_ref):
+        def over(value):
+            ones = jnp.ones((8, value.shape[1]), value.dtype)
+            exact = lax.Precision.HIGHEST if value.dtype == f32 else None
+            return lax.dot_general(
+                ones, value, (((1,), (1,)), ((), ())), preferred_element_type=f32, precision=exact
+            )[0:1]
+
+        o_ref[...] = jnp.zeros_like(o_ref)
+        for i in range(3):
+            o_ref[i : i + 1, :] = over(two_ref[i])
+        o_ref[3:4, :half] = over(one_ref[0])
+        o_ref[3:4, half:] = over(one_ref[1])
+        o_ref[4:5, :half] = over(grad_ref[...])
+        o_ref[8:9, :] = over(hid_ref[...])
+        o_ref[9:10, :most] = over(p_ref[2 * most :, :])
+        o_ref[10:11, :most] = over(p_ref[most : 2 * most, :])
+
+    args = (sums_two, sums_one, grad_own, hidden_sums, parts)
+    return call(
+        body, "packed_sums", (1,), [whole_spec(v) for v in args], args,
+        pl.BlockSpec((16, width), lambda i, s: (0, 0)), shape(16, width, dtype=f32),
+    )
+
+
+def sums_added(a, b, rows):
+    def body(_, a_ref, b_ref, o_ref):
+        at = lax.broadcasted_iota(jnp.int32, a_ref.shape, 0)
+        o_ref[...] = a_ref[...] + jnp.where(at < rows, b_ref[...], 0.0)
+
+    spec = whole_spec(a)
+    return call(body, "sums_added", (1,), [spec, spec], (a, b), spec, shape(*a.shape, dtype=f32))
+
+
+def spread_index(sizes, axis, step, value):
+    places = []
+    for size in reversed(sizes):
+        places.insert(0, step % size)
+        step = step // size
+    places.insert(axis, value)
+    return tuple(places) + (0, 0)
+
+
+def halved(keep, got, axis, at):
+    lead, tile = keep.shape[:-2], keep.shape[-2:]
+    rest = lead[:axis] + lead[axis + 1 :]
+
+    def body(_, a_ref, b_ref, c_ref, d_ref, keep_ref, send_ref):
+        keep_ref[...] = (a_ref[...].astype(f32) + b_ref[...].astype(f32)).astype(bf16).reshape(keep_ref.shape)
+        send_ref[...] = (c_ref[...].astype(f32) + d_ref[...].astype(f32)).astype(bf16).reshape(send_ref.shape)
+
+    ones = (1,) * len(lead)
+    mine = pl.BlockSpec(ones + tile, lambda i, s: spread_index(rest, axis, i, s[0]))
+    theirs = pl.BlockSpec(ones + tile, lambda i, s: spread_index(rest, axis, i, 1 - s[0]))
+    steps = math.prod(rest)
+    out = pl.BlockSpec((1,) + tile, lambda i, s: (i, 0, 0))
+    first, second = call(
+        body, "halved", (steps,), [mine, mine, theirs, theirs], (keep, got, keep, got),
+        [out, out], [shape(steps, *tile)] * 2, scalars=at[None].astype(jnp.int32),
+    )
+    return first.reshape(rest + tile), second.reshape(rest + tile)
+
+
+def added(a, b):
+    def body(_, a_ref, b_ref, o_ref):
+        o_ref[...] = (a_ref[...].astype(f32) + b_ref[...].astype(f32)).astype(bf16)
+
+    spec = whole_spec(a)
+    return call(body, "added", (1,), [spec, spec], (a, b), spec, shape(*a.shape))
+
+
+def chosen(flag, a, b):
+    def body(s_ref, a_ref, b_ref, o_ref):
+        o_ref[...] = jnp.where(s_ref[0] == 1, a_ref[...], b_ref[...])
+
+    spec = whole_spec(a)
+    return call(body, "chosen", (1,), [spec, spec], (a, b), spec, shape(*a.shape), scalars=flag[None].astype(jnp.int32))
+
+
+def paired(at, first, second, axis):
+    lead, tile = first.shape[:-2], first.shape[-2:]
+    ones = (1,) * len(lead)
+    steps = math.prod(lead)
+
+    def body(_, a_ref, b_ref, o_ref):
+        @pl.when(pl.program_id(0) == 0)
+        def _():
+            o_ref[...] = a_ref[...].reshape(o_ref.shape)
+
+        @pl.when(pl.program_id(0) == 1)
+        def _():
+            o_ref[...] = b_ref[...].reshape(o_ref.shape)
+
+    def place(step):
+        return spread_index(lead, len(lead), step, 0)[: len(lead)] + (0, 0)
+
+    out = lambda i, j, s: spread_index(lead, axis, j, jnp.where(i == 0, s[0], 1 - s[0]))
+    return call(
+        body, "paired", (2, steps),
+        [
+            pl.BlockSpec(ones + tile, lambda i, j, s: place(jnp.where(i == 0, j, steps - 1))),
+            pl.BlockSpec(ones + tile, lambda i, j, s: place(jnp.where(i == 1, j, 0))),
+        ],
+        (first, second),
+        pl.BlockSpec(ones + (1,) + tile, out),
+        shape(*lead[:axis], 2, *lead[axis:], *tile),
+        scalars=at[None].astype(jnp.int32),
+    )
+
+
+def widened(keep, got, at, y_last):
+    rows, width = keep.shape[-2:]
+
+    def body(s_ref, a_ref, b_ref, c_ref, d_ref, o_ref):
+        if y_last:
+            swap = s_ref[0] == 1
+            o_ref[:, :width] = jnp.where(swap, b_ref[0, 0], a_ref[0, 0]).astype(f32)
+            o_ref[:, width:] = jnp.where(swap, a_ref[0, 0], b_ref[0, 0]).astype(f32)
+        else:
+            other = pl.program_id(0) % 2 != s_ref[0]
+            o_ref[:, :width] = jnp.where(other, b_ref[0, 0], a_ref[0, 0]).astype(f32)
+            o_ref[:, width:] = jnp.where(other, d_ref[0, 0], c_ref[0, 0]).astype(f32)
+
+    tile = (1, 1, rows, width)
+    if y_last:
+        one = pl.BlockSpec(tile, lambda i, s: (i // 2, i % 2, 0, 0))
+        none = pl.BlockSpec(tile, lambda i, s: (0, 0, 0, 0))
+        specs = [one, one, none, none]
+    else:
+        specs = [pl.BlockSpec(tile, lambda i, s, f=f: (f, i // 2, 0, 0)) for f in (0, 0, 1, 1)]
+    return call(
+        body, "widened", (4,), specs, (keep, got, keep, got),
+        pl.BlockSpec((rows, 2 * width), lambda i, s: (i, 0)),
+        shape(4 * rows, 2 * width, dtype=f32), scalars=at[None].astype(jnp.int32),
+    )
+
+
+def tails_of(keep, got, at, y_last, most, low, high):
+    rows, width = keep.shape[-2:]
+    count = width // most
+
+    def body(s_ref, a_ref, b_ref, o_ref):
+        second = jnp.where((s_ref[0] == 1) if y_last else (pl.program_id(0) % 2 == s_ref[0]), a_ref[0, 0], b_ref[0, 0])
+        for i in range(count):
+            o_ref[i, 0] = second[:, i * most + low : i * most + high]
+
+    tile = (1, 1, rows, width)
+    where = (lambda i, s: (i // 2, i % 2, 0, 0)) if y_last else (lambda i, s: (1, i // 2, 0, 0))
+    return call(
+        body, "tails_of", (4,), [pl.BlockSpec(tile, where)] * 2, (keep, got),
+        pl.BlockSpec((count, 1, rows, high - low), lambda i, s: (0, i, 0, 0)),
+        shape(count, 4, rows, high - low), scalars=at[None].astype(jnp.int32),
+    )
+
+
+def unslotted(keep, got, tails, at, y_last, c, most, size):
+    rows, width = keep.shape[-2:]
+    count, spare, less = width // most, tails.shape[-1], most - HEAD_DIM
+
+    def body(s_ref, a_ref, b_ref, c_ref, d_ref, t_ref, o_ref):
+        if y_last:
+            swap = s_ref[0] == 1
+            first = jnp.where(swap, b_ref[0, 0], a_ref[0, 0])
+            second = jnp.where(swap, a_ref[0, 0], b_ref[0, 0])
+        else:
+            other = pl.program_id(0) % 2 != s_ref[0]
+            first = jnp.where(other, b_ref[0, 0], a_ref[0, 0])
+            second = jnp.where(other, d_ref[0, 0], c_ref[0, 0])
+        first, second = first.astype(f32), second.astype(f32)
+
+        @pl.when(s_ref[1] == 0)
+        def _():
+            for i in range(count):
+                o_ref[i, :, :most] = first[:, i * most : (i + 1) * most]
+                o_ref[i, :, most:] = second[:, i * most : i * most + size - most]
+
+        @pl.when(s_ref[1] == 1)
+        def _():
+            for i in range(count):
+                o_ref[i, :, :spare] = t_ref[i, 0].astype(f32)
+                o_ref[i, :, spare : spare + less] = first[:, i * most : i * most + less]
+                o_ref[i, :, spare + less :] = second[:, i * most : i * most + less]
+
+    tile = (1, 1, rows, width)
+    if y_last:
+        one = pl.BlockSpec(tile, lambda i, s: (i // 2, i % 2, 0, 0))
+        none = pl.BlockSpec(tile, lambda i, s: (0, 0, 0, 0))
+        specs = [one, one, none, none]
+    else:
+        specs = [pl.BlockSpec(tile, lambda i, s, f=f: (f, i // 2, 0, 0)) for f in (0, 0, 1, 1)]
+    return call(
+        body, "unslotted", (4,),
+        specs + [pl.BlockSpec((count, 1, rows, spare), lambda i, s: (0, i, 0, 0))],
+        (keep, got, keep, got, tails),
+        pl.BlockSpec((count, rows, size), lambda i, s: (0, i, 0)),
+        shape(count, 4 * rows, size, dtype=f32), scalars=jnp.stack([at, c]).astype(jnp.int32),
+    )
+
+
+def side_by_side(own, got, r):
+    rows, width = own.shape
+    size = rows // 4
+
+    def body(s_ref, a_ref, b_ref, o_ref):
+        swap = s_ref[0] == 1
+        o_ref[:, :width] = jnp.where(swap, b_ref[...], a_ref[...]).astype(f32)
+        o_ref[:, width:] = jnp.where(swap, a_ref[...], b_ref[...]).astype(f32)
+
+    return call(
+        body, "side_by_side", (4,),
+        [pl.BlockSpec((size, width), lambda i, s: (i, 0))] * 2,
+        (own, got),
+        pl.BlockSpec((size, 2 * width), lambda i, s: (i, 0)),
+        shape(rows, 2 * width, dtype=f32), scalars=r[None].astype(jnp.int32),
+    )
+
+
+TOKENS = 256
+
+
+def tile_of(rows, at=None):
+    if at is None:
+        return pl.BlockSpec((rows, TOKENS), lambda i, s: (0, i))
+    return pl.BlockSpec((rows, TOKENS), lambda i, s: (at(s), i))
+
+
+def norm_stats(parts):
+    count = sum(part.shape[0] for part in parts)
+    center = sum(jnp.sum(part, axis=0, keepdims=True) for part in parts) / count
+    spread = sum(jnp.sum((part - center) * (part - center), axis=0, keepdims=True) for part in parts) / count
+    return center, lax.rsqrt(spread + 1e-05)
+
+
+def norm_one(x_own, x_peer, gain, bias, r):
+    half, count = x_own.shape
+
+    def body(s_ref, own_ref, peer_ref, g_ref, b_ref, h_ref, stat_ref):
+        own, peer = own_ref[...].astype(f32), peer_ref[...].astype(f32)
+        parts = [jnp.where(s_ref[0] == 0, own, peer), jnp.where(s_ref[0] == 0, peer, own)]
+        center, inverse = norm_stats(parts)
+        stat_ref[0:1, :] = center
+        stat_ref[1:2, :] = inverse
+        for i, part in enumerate(parts):
+            rows = slice(i * half, (i + 1) * half)
+            h_ref[rows, :] = ((part - center) * inverse * g_ref[rows, :] + b_ref[rows, :]).astype(bf16)
+
+    return call(
+        body, "norm_one", (count // TOKENS,),
+        [tile_of(half), tile_of(half), whole_spec(gain), whole_spec(bias)],
+        (x_own, x_peer, gain, bias),
+        [tile_of(2 * half), tile_of(8)],
+        [shape(2 * half, count), shape(8, count, dtype=f32)],
+        scalars=r[None].astype(jnp.int32),
+    )
+
+
+def norm_two(x_own, x_peer, low, other, out_bias, gain, bias, r):
+    half, count = x_own.shape
+
+    def body(s_ref, own_ref, peer_ref, low_ref, other_ref, ob_ref, g_ref, b_ref, x_ref, h_ref, stat_ref):
+        own, peer = own_ref[...].astype(f32), peer_ref[...].astype(f32)
+        parts = [jnp.where(s_ref[0] == 0, own, peer), jnp.where(s_ref[0] == 0, peer, own)]
+        for i in range(2):
+            rows = slice(i * half, (i + 1) * half)
+            branch = low_ref[rows, :].astype(f32) + other_ref[rows, :].astype(f32) + ob_ref[rows, :]
+            parts[i] = parts[i] + branch
+            x_ref[rows, :] = parts[i]
+        center, inverse = norm_stats(parts)
+        stat_ref[0:1, :] = center
+        stat_ref[1:2, :] = inverse
+        for i, part in enumerate(parts):
+            rows = slice(i * half, (i + 1) * half)
+            h_ref[rows, :] = ((part - center) * inverse * g_ref[rows, :] + b_ref[rows, :]).astype(bf16)
+
+    full = tile_of(2 * half)
+    return call(
+        body, "norm_two", (count // TOKENS,),
+        [tile_of(half), tile_of(half), full, full, whole_spec(out_bias), whole_spec(gain), whole_spec(bias)],
+        (x_own, x_peer, low, other, out_bias, gain, bias),
+        [full, full, tile_of(8)],
+        [shape(2 * half, count, dtype=f32), shape(2 * half, count), shape(8, count, dtype=f32)],
+        scalars=r[None].astype(jnp.int32),
+    )
+
+
+def lanes_summed(ref, at, value, first):
+    total = sum(value[:, i : i + 128] for i in range(0, value.shape[1], 128))
+
+    @pl.when(first)
+    def _():
+        ref[at] = total
+
+    @pl.when(jnp.logical_not(first))
+    def _():
+        ref[at] += total
+
+
+def norm_two_back(low, other, grad, x_mid, stats, gain):
+    width, count = low.shape
+
+    def body(_, low_ref, other_ref, g_ref, x_ref, stat_ref, gain_ref, mid_ref, branch_ref, sum_ref):
+        first = pl.program_id(0) == 0
+        incoming = low_ref[...].astype(f32) + other_ref[...].astype(f32)
+        inverse = stat_ref[1:2, :]
+        normed = (x_ref[...] - stat_ref[0:1, :]) * inverse
+        scaled = incoming * gain_ref[...]
+        mean = jnp.sum(scaled, axis=0, keepdims=True) / width
+        along = jnp.sum(scaled * normed, axis=0, keepdims=True) / width
+        mid = g_ref[...].astype(f32) + inverse * (scaled - mean - normed * along)
+        mid_ref[...] = mid
+        branch = mid.astype(bf16)
+        branch_ref[...] = branch
+        lanes_summed(sum_ref, 0, incoming * normed, first)
+        lanes_summed(sum_ref, 1, incoming, first)
+        lanes_summed(sum_ref, 2, branch.astype(f32), first)
+
+    full = tile_of(width)
+    return call(
+        body, "norm_two_back", (count // TOKENS,),
+        [full, full, full, full, tile_of(8), whole_spec(gain)],
+        (low, other, grad, x_mid, stats, gain),
+        [full, full, pl.BlockSpec((3, width, 128), lambda i, s: (0, 0, 0))],
+        [shape(width, count, dtype=f32), shape(width, count), shape(3, width, 128, dtype=f32)],
+    )
+
+
+def norm_one_sums(mine, other, x_own, stats, gain, r):
+    half, count = x_own.shape
+
+    def body(_, m_ref, o_ref, x_ref, stat_ref, gain_ref, row_ref, sum_ref):
+        first = pl.program_id(0) == 0
+        incoming = m_ref[...] + o_ref[...].astype(f32)
+        normed = (x_ref[...].astype(f32) - stat_ref[0:1, :]) * stat_ref[1:2, :]
+        scaled = incoming * gain_ref[...]
+        row_ref[...] = jnp.zeros_like(row_ref)
+        row_ref[0:1, :] = jnp.sum(scaled, axis=0, keepdims=True)
+        row_ref[1:2, :] = jnp.sum(scaled * normed, axis=0, keepdims=True)
+        lanes_summed(sum_ref, 0, incoming * normed, first)
+        lanes_summed(sum_ref, 1, incoming, first)
+
+    return call(
+        body, "norm_one_sums", (count // TOKENS,),
+        [tile_of(half, lambda s: s[0]), tile_of(half), tile_of(half), tile_of(8), whole_spec(gain)],
+        (mine, other, x_own, stats, gain),
+        [tile_of(8), pl.BlockSpec((2, half, 128), lambda i, s: (0, 0, 0))],
+        [shape(8, count, dtype=f32), shape(2, half, 128, dtype=f32)],
+        scalars=r[None].astype(jnp.int32),
+    )
+
+
+def norm_one_back(mine, other, x_own, stats, gain, mid_grad, sums, sums_peer, r):
+    half, count = x_own.shape
+
+    def body(_, m_ref, o_ref, x_ref, stat_ref, gain_ref, mid_ref, a_ref, b_ref, out_ref):
+        inverse = stat_ref[1:2, :]
+        normed = (x_ref[...].astype(f32) - stat_ref[0:1, :]) * inverse
+        scaled = (m_ref[...] + o_ref[...].astype(f32)) * gain_ref[...]
+        means = (a_ref[...] + b_ref[...]) / (2 * half)
+        out_ref[...] = mid_ref[...] + inverse * (scaled - means[0:1, :] - normed * means[1:2, :])
+
+    mine_tile = tile_of(half, lambda s: s[0])
+    return call(
+        body, "norm_one_back", (count // TOKENS,),
+        [mine_tile, tile_of(half), tile_of(half), tile_of(8), whole_spec(gain), mine_tile, tile_of(8), tile_of(8)],
+        (mine, other, x_own, stats, gain, mid_grad, sums, sums_peer),
+        tile_of(half), shape(half, count, dtype=f32), scalars=r[None].astype(jnp.int32),
+    )
+
+
+def block_result(x_mid, part, other, bias, r):
+    half, count = other.shape
+
+    def body(_, x_ref, p_ref, o_ref, b_ref, out_ref):
+        out_ref[...] = (x_ref[...] + (p_ref[...].astype(f32) + o_ref[...].astype(f32)) + b_ref[...]).astype(bf16)
+
+    mine_tile = tile_of(half, lambda s: s[0])
+    return call(
+        body, "block_result", (count // TOKENS,),
+        [mine_tile, mine_tile, tile_of(half), whole_spec(bias)],
+        (x_mid, part, other, bias),
+        tile_of(half), shape(half, count), scalars=r[None].astype(jnp.int32),
     )
 
 
 class Fetch:
-    def __init__(self, sent, k):
-        self.y, self.z = k % 2, (k // 2) % 2
-        self.got = row_swap(sent)
-
-    def second(self, *marks):
-        self.got = after(self.got, *marks)
-        self.got = paired(self.z, self.got, dp_xor(self.got, 2), 1)
+    def __init__(self, sent):
+        self.got = [row_swap(sent)]
+
+    def more(self, *marks):
+        first = after(self.got[0], *marks)
+        self.got = [first, dp_xor(first, 1), dp_xor(first, 2)]
+
+    def rest(self, *marks):
+        self.got.append(dp_xor(after(self.got[2], *marks), 1))
         return self.got
 
-    def third(self, *marks):
-        self.got = after(self.got, *marks)
-        self.peer = dp_xor(self.got, 1)
-
-    def result(self, *marks):
-        both = paired(self.y, after(self.got, *marks), self.peer, 2)
-        return both.reshape(both.shape[0], -1, both.shape[-1])
-
 
 class Total:
-    def __init__(self, own, other, right, part, r, k, y_first, *marks):
-        self.rows, self.width = own.shape[0], part[1]
-        self.r, self.k, self.y_first = r, k, y_first
+    def __init__(self, sources, r, k, y_first, y_last, *marks):
+        self.rows, self.width = sources[0][0].shape[0], sum(part[1] for _, _, _, part in sources)
+        self.r, self.k, self.y_first, self.y_last = r, k, y_first, y_last
         self.fast = lax.axis_size("dp") == 8
-        right = after(right, *marks)
+        tied = lambda marks: [(own, other, after(right, *marks), part) for own, other, right, part in sources]
         if not self.fast:
-            self.grad = weight_grad(own, other, right, jnp.arange(4, dtype=jnp.int32), 4, part)
+            self.grad = weight_grad(tied(marks), jnp.arange(4, dtype=jnp.int32), 4)
             return
         self.y, self.lo, self.hi = k % 2, (k // 2) % 2, k // 4
         if y_first:
@@ -590,25 +1058,33 @@
             send, parts, mask = (1 - self.lo) + 2 * jnp.arange(4), 8, 2
             keep = self.lo + 2 * jnp.arange(4)
         shaped = lambda v: v.reshape(2, 2, self.rows // 8, self.width)
-        sent = weight_grad(own, other, right, send.astype(jnp.int32), parts, part)
-        self.got = dp_xor(shaped(sent), mask)
-        self.keep = shaped(weight_grad(own, other, after(right, sent), keep.astype(jnp.int32), parts, part))
+        sent = weight_grad(tied(marks), send.astype(jnp.int32), parts)
+        self.got, self.sent = dp_xor(shaped(sent), mask), [sent]
+        self.kept = lambda *marks: shaped(weight_grad(tied(marks), keep.astype(jnp.int32), parts))
+
+    def hold(self, *marks):
+        if self.fast:
+            self.keep = self.kept(*marks)
+        return self.marks()
 
     def marks(self):
         return [self.keep] if self.fast else []
 
+    def sent_marks(self):
+        return self.sent if self.fast else []
+
     def sum_one(self, *marks):
         if self.fast:
-            part = plus(after(self.keep, *marks), self.got).astype(bf16)
             axis, at, mask = (1, self.lo, 2) if self.y_first else (0, self.y, 1)
-            self.keep, self.got = pick(part, at, axis), dp_xor(pick(part, 1 - at, axis), mask)
+            self.keep, send = halved(after(self.keep, *marks), self.got, axis, at)
+            self.got = dp_xor(send, mask)
             return [self.keep]
         return []
 
     def sum_two(self, *marks):
         if self.fast:
-            part = plus(after(self.keep, *marks), self.got).astype(bf16)
-            self.keep, self.got = pick(part, self.hi, 0), dp_xor(pick(part, 1 - self.hi, 0), 4)
+            self.keep, send = halved(after(self.keep, *marks), self.got, 0, self.hi)
+            self.got = dp_xor(send, 4)
             return [self.keep]
         return []
 
@@ -620,14 +1096,14 @@
                 for j in range(2)
                 if i % 2 != j
             ]
-            self.keep = plus(after(self.keep, *marks), self.got).astype(bf16)
+            self.keep = added(after(self.keep, *marks), self.got)
             self.got = lax.ppermute(self.keep, ("dp", "row"), cross)
             return [self.keep]
         return []
 
     def spread_one(self, *marks):
         if self.fast:
-            self.keep = jnp.where(self.y == self.r, after(self.keep, *marks), self.got)
+            self.keep = chosen(self.y == self.r, after(self.keep, *marks), self.got)
             self.got = dp_xor(self.keep, 4)
             return [self.keep]
         return []
@@ -635,13 +1111,13 @@
     def spread_two(self, *marks):
         if self.fast:
             self.keep = paired(self.hi, after(self.keep, *marks), self.got, 0)
-            self.got = dp_xor(self.keep, 2 if self.y_first else 1)
+            self.got = dp_xor(self.keep, 2 if self.y_last else 1)
             return [self.keep]
         return []
 
     def spread_three(self, *marks):
         if self.fast:
-            if self.y_first:
+            if self.y_last:
                 self.keep = paired(self.lo, after(self.keep, *marks), self.got, 1)
                 self.got = dp_xor(self.keep, 1)
             else:
@@ -650,26 +1126,71 @@
             return [self.keep]
         return []
 
+    def tail(self, most, spare, *marks):
+        if not self.fast:
+            return list(marks)
+        less = most - HEAD_DIM
+        at = self.y if self.y_last else self.lo
+        self.keep = after(self.keep, *marks)
+        tails = tails_of(self.keep, self.got, at, self.y_last, most, less - spare, less)
+        self.tails = col_swap(tails)
+        return [tails]
+
+    def slots(self, c, most, spare, *marks):
+        less = most - HEAD_DIM
+        size = 2 * less + spare
+        if not self.fast:
+            both = self.result()
+            cut = lambda i: [v[:, i * most : (i + 1) * most] for v in both]
+            return jnp.stack([from_slots(c, *cut(i), 1, spare).astype(f32) for i in range(self.width // most)])
+        at = self.y if self.y_last else self.lo
+        keep = after(self.keep, *marks)
+        return unslotted(keep, self.got, self.tails, at, self.y_last, c, most, size)
+
+    def wide(self, *marks):
+        if self.fast:
+            return widened(after(self.keep, *marks), self.got, self.y if self.y_last else self.lo, self.y_last)
+        return jnp.concatenate(self.result(*marks), axis=1).astype(f32)
+
     def result(self, *marks):
         if not self.fast:
             halves = self.grad.reshape(2, self.rows // 2, self.width)
             keep, got = pick(halves, self.r, 0), row_swap(pick(halves, 1 - self.r, 0))
-            both = lax.psum(paired(self.r, keep, got, 0), "dp")
+            both = lax.psum(ordered(self.r, keep[None], got[None], 0), "dp")
             return both[0], both[1]
         keep, got = after(self.keep, *marks), self.got
-        if self.y_first:
-            both = paired(self.y, keep, got, 0)
-        else:
-            both = paired(self.lo, keep, got, 2)
-        both = both.reshape(2, self.rows // 2, self.width)
+        if self.y_last:
+            keep, got = [v.reshape(self.rows // 2, self.width) for v in (keep, got)]
+            return jnp.where(self.y == 0, keep, got), jnp.where(self.y == 0, got, keep)
+        both = paired(self.lo, keep, got, 2).reshape(2, self.rows // 2, self.width)
         return both[0], both[1]
 
 
-def norm(values):
-    center = jnp.mean(values, axis=0, keepdims=True)
-    shifted = values - center
-    inverse = lax.rsqrt(jnp.mean(shifted * shifted, axis=0, keepdims=True) + 1e-05)
-    return shifted * inverse, inverse
+class Whole:
+    def __init__(self, source, r):
+        self.source, self.r, self.sums = source, r, {}
+
+    def part(self, mine, *marks):
+        own, other, right, part = self.source
+        first = 2 * (self.r if mine else 1 - self.r)
+        order = (first + jnp.arange(2)).astype(jnp.int32)
+        grad = weight_grad([(own, other, after(right, *marks), part)], order, 4)
+        self.sums[mine] = lax.psum(grad.reshape(-1, grad.shape[-1]), "dp")
+        return [grad]
+
+    def swap(self, *marks):
+        self.got = row_swap(after(self.sums[False], *marks))
+
+    def wide(self, *marks):
+        return side_by_side(after(self.sums[True], *marks), self.got, self.r)
+
+
+def hop(value, mask):
+    return dp_xor(value, mask) if lax.axis_size("dp") == 8 else None
+
+
+def hop_added(value, peer, *marks):
+    return value if peer is None else sums_added(after(value, *marks), peer, 16)
 
 
 def per_device(
@@ -698,15 +1219,12 @@
     spare = 32
     column = lambda v: v.astype(f32)[:, None]
 
+    y, z = k % 2, (k // 2) % 2
     qkv_tail = col_swap(qkv_weight[:, :, :spare])
     proj_turned = proj_weight.T
-    qkv_sent, fc_sent, proj_sent = pack(
-        qkv_weight, qkv_tail, fc_weight, proj_turned, c, r, 2 * ((k // 2) % 2) + k % 2, most
-    )
-    qkv_fetch = Fetch(qkv_sent, k)
+    qkv_sent, fc_sent, proj_sent = pack(qkv_weight, qkv_tail, fc_weight, proj_turned, c, r, 2 * z + y, most)
+    qkv_fetch = Fetch(qkv_sent)
     x_peer = row_swap(after(x_own, qkv_sent))
-    fc_fetch = Fetch(fc_sent[None], k)
-    proj_fetch = Fetch(proj_sent[None], k)
     vectors = jnp.stack([ln1_gain, ln1_bias, out_bias, ln2_gain, ln2_bias])
     vectors = ordered(r, vectors, row_swap(vectors), 1).astype(f32)
     gain_one, bias_one, bias_out, gain_two, bias_two = [vectors[i][:, None] for i in range(5)]
@@ -717,15 +1235,15 @@
 
     out_first, out_second = head_slots(c, after(out_weight, qkv_sent), col_swap(out_weight[:spare]), 0, most)
     out_mine = jnp.where(r == 0, out_first, out_second)
-    out_got = row_swap(jnp.where(r == 0, out_second, out_first))
-
-    qkv_first, qkv_second = head_slots(c, after(qkv_weight, out_mine), qkv_tail, 2, most)
-    qkv_mine = jnp.where(r == 0, qkv_first, qkv_second)
-    mark = qkv_fetch.second(qkv_mine)
-    qkv_fetch.third()
-    fc_mine = half_of(r, after(fc_weight, mark), 1)
-    proj_mine = half_of(r, after(proj_turned, mark), 1)
+    out_sent = jnp.where(r == 0, out_second, out_first)
     fc_bias_mine = column(half_of(r, fc_bias, 0))
+    gain_half, proj_bias_half = column(ln1_gain), column(proj_bias)
+    ff_size = fc_weight.shape[1] // 2
+    qkv_full = own_rows(after(qkv_weight, out_sent), qkv_tail, c, r, most)
+    qkv_fetch.more(qkv_full)
+    fc_full = own_rows(after(fc_weight, qkv_fetch.got[0]), None, c, r, ff_size)
+    qkv_fetch.rest(fc_full)
+    proj_full = own_rows(after(proj_turned, fc_full, *qkv_fetch.got[1:3]), None, c, r, ff_size)
 
     lengths = seq_lengths[0]
     group = 2 * tokens
@@ -736,165 +1254,155 @@
     ).reshape(group // BLK, BLK)
     info = jnp.concatenate([(c * (tokens // BLK))[None].astype(jnp.int32), first[:, 0] // BLK])
 
-    x_full = ordered(r, x_own, x_peer, 0).astype(f32)
-    normed_one, inverse_one = norm(x_full)
-    h_one = (normed_one * gain_one + bias_one).astype(bf16)
+    columns = [gain_one, bias_one, bias_out, gain_two, bias_two, bias_mine, fc_bias_mine, gain_half, proj_bias_half]
+    h_one, stats_one = norm_one(after(x_own, proj_full, info, *columns), x_peer, gain_one, bias_one, r)
     h_one_peer = col_swap(h_one)
-    mark = fc_fetch.second(h_one)
-    qkv_full = ordered(r, qkv_mine, qkv_fetch.result(mark), 1)
+    fc_fetch = Fetch(after(fc_sent, h_one))
+    proj_fetch = Fetch(after(proj_sent, h_one))
+    out_got = row_swap(after(out_sent, h_one))
+    grad_got = row_swap(after(grad_own, h_one))
+    qkv_full = all_rows(after(qkv_full, h_one), qkv_fetch.got, r, y, z)
     projected = project(qkv_full, h_one, h_one_peer, bias_mine)
-    fc_fetch.third(projected)
-    mark = proj_fetch.second(fc_fetch.got)
-    attended, log_totals = attend(info, after(projected, mark), first, heads)
-    proj_fetch.third(attended)
-    out_full = ordered(r, out_mine, out_got, 1)
-    other = mapped(out_full, attended, 1, True)
+    fc_fetch.more(projected)
+    proj_fetch.more(projected)
+    out_full = ordered(r, after(out_mine, projected), out_got, 1)
+    mark = [out_full, fc_fetch.got[0], proj_fetch.got[0]]
+    attended, log_totals = attend(info, after(projected, *mark), first, heads)
+    fc_fetch.rest(attended)
+    proj_fetch.rest(attended)
+    other = mapped(out_full, after(attended, *fc_fetch.got[1:3], *proj_fetch.got[1:3]), 1, True)
     low = mapped(out_full, attended, 0, True, col_swap(other))
     branch_other = row_swap(low)
-    fc_full = ordered(r, after(fc_mine, low), fc_fetch.result(low)[0], 0)
-    proj_full = ordered(r, after(proj_mine, fc_full), proj_fetch.result(fc_full)[0], 0)
-    x_mid = after(x_full, proj_full) + plus(low, branch_other) + bias_out
-    normed_two, inverse_two = norm(x_mid)
-    h_two = (normed_two * gain_two + bias_two).astype(bf16)
+    fc_full = all_rows(after(fc_full, low), fc_fetch.got, r, y, z)
+    proj_full = all_rows(after(proj_full, fc_full), proj_fetch.got, r, y, z)
+    x_mid, h_two, stats_two = norm_two(x_own, x_peer, after(low, proj_full), branch_other, bias_out, gain_two, bias_two, r)
     h_two_peer = col_swap(h_two)
-    grad_full = ordered(r, after(grad_own, h_two), row_swap(after(grad_own, low)), 0)
+    activated, slope = hidden(fc_full, h_two, h_two_peer, fc_bias_mine)
+    grad_full = paired(r, after(grad_own, activated), grad_got, 0).reshape(2 * half, tokens)
     grad_peer = col_swap(grad_full)
-    activated, slope = hidden(fc_full, h_two, h_two_peer, fc_bias_mine)
-
-    ff = (0, activated.shape[0])
-    proj_total = Total(grad_full, grad_peer, activated, ff, r, k, True)
-    pre_grad, fc_bias_grad = hidden_back(proj_full, after(grad_full, *proj_total.marks()), grad_peer, slope)
-    other = mapped(fc_full, pre_grad, 1, False)
-    low = mapped(fc_full, pre_grad, 0, False, col_swap(other))
-    h_two_grad = plus(low, row_swap(low))
-    fc_total = Total(h_two, h_two_peer, pre_grad, ff, r, k, True, low)
-    mark = proj_total.sum_one(*fc_total.marks())
-    other = mapped(proj_full, after(activated, *mark), 1, False)
-    proj_part = mapped(proj_full, activated, 0, False, col_swap(other))
-    block_other = row_swap(half_of(1 - r, proj_part, 0))
-    mark = proj_total.sum_two(proj_part)
-
-    scaled = after(h_two_grad, proj_part, *mark) * gain_two
-    mid_grad = grad_full.astype(f32) + inverse_two * (
-        scaled
-        - jnp.mean(scaled, axis=0, keepdims=True)
-        - normed_two * jnp.mean(scaled * normed_two, axis=0, keepdims=True)
-    )
-    branch_grad = mid_grad.astype(bf16)
-    branch_peer = col_swap(branch_grad)
-    mark = proj_total.sum_three(branch_grad)
+
+    mark = [grad_peer]
+    pre_grad, hidden_sums = hidden_back(proj_full, grad_full, grad_peer, slope)
+    mark = [pre_grad]
+    h_two_other = mapped(fc_full, after(pre_grad, *mark), 1, False)
+    mark = [h_two_other]
+    proj_total = Total([(grad_full, grad_peer, activated, (0, ff_size))], r, k, True, False, *mark)
+    mark = proj_total.sent_marks()
+    low = mapped(fc_full, after(pre_grad, *mark), 0, False, col_swap(h_two_other))
+    low_other, mark = row_swap(low), [low]
+    fc_total = Total([(h_two, h_two_peer, pre_grad, (0, ff_size))], r, k, False, True, *mark)
+    mark = fc_total.sent_marks()
+    mark = fc_total.hold(*mark)
+    mark = proj_total.hold(*mark)
+    mark = proj_total.sum_one(*mark)
+    mid_grad, branch_grad, sums_two = norm_two_back(
+        after(low, *mark), low_other, grad_full, x_mid, stats_two, gain_two
+    )
+    branch_peer, mark = col_swap(branch_grad), [branch_grad]
     mark = fc_total.sum_one(*mark)
-
-    out_total = Total(branch_grad, branch_peer, attended, (0, most), r, k, False, *mark)
-    mark = proj_total.spread_one(*out_total.marks())
     attended_grad = attended_back(out_full, after(branch_grad, *mark), branch_peer)
-    parts = attend_back(info, projected, attended, attended_grad, log_totals, first, heads)
-    mark = fc_total.sum_two(parts)
-    mark = out_total.sum_one(*mark)
+    mark = [attended_grad]
+    parts = attend_back(info, projected, attended, after(attended_grad, *mark), log_totals, first, heads)
+    mark = [parts]
+    kv_total = Total([(h_one, h_one_peer, parts, (0, 2 * most))], r, k, True, False, *mark)
+    mark = kv_total.sent_marks()
+    three_other = mapped_three(qkv_full, after(parts, *mark), 1)
+    mark = [three_other]
+    mark = proj_total.sum_two(*mark)
+    mark = fc_total.sum_two(*mark)
+    oq_total = Total([(branch_grad, branch_peer, attended, (0, most)), (h_one, h_one_peer, parts, (2, most))], r, k, True, True, *mark)
+    mark = oq_total.sent_marks()
+    mark = oq_total.hold(*mark)
+    mine = mapped_three(qkv_full, after(parts, *mark), 0, col_swap(three_other))
+    mark = [mine]
+    mark = kv_total.hold(*mark)
+    send = half_rows(after(mine, *mark), 1 - r)
+    one_other, mark = row_swap(send), [send]
+    mark = kv_total.sum_one(*mark)
+    mark = proj_total.sum_three(*mark)
+    mark = oq_total.sum_one(*mark)
+    mark = fc_total.sum_three(*mark)
+    mark = kv_total.sum_two(*mark)
+    mark = proj_total.spread_one(*mark)
+    mark = oq_total.sum_two(*mark)
+    mark = kv_total.sum_three(*mark)
+    sums, sums_one = norm_one_sums(after(mine, *mark), one_other, x_own, stats_one, gain_half, r)
+    sums_peer, mark = row_swap(sums), [sums]
+    packed = packed_sums(sums_two, after(sums_one, *mark), grad_own, hidden_sums, parts, most)
+    packed_peer, mark = col_swap(packed), [packed]
+    mark = fc_total.spread_one(*mark)
+    mark = oq_total.sum_three(*mark)
+    packed = sums_added(after(packed, *mark), packed_peer, 8)
+    packed_peer, mark = hop(packed, 2), [packed]
+    x_grad = norm_one_back(after(mine, *mark), one_other, x_own, stats_one, gain_half, mid_grad, sums, sums_peer, r)
+    mark = [x_grad]
+    mark = oq_total.spread_one(*mark)
+    packed = hop_added(packed, packed_peer, *mark)
+    packed_peer, mark = hop(packed, 1), [packed]
     mark = proj_total.spread_two(*mark)
-    q_total = Total(h_one, h_one_peer, parts, (2, most), r, k, False, *mark)
-    kv_total = Total(h_one, h_one_peer, parts, (0, 2 * most), r, k, True, *q_total.marks())
-    other = mapped_three(qkv_full, after(parts, *kv_total.marks()), 1)
-    mark = out_total.sum_two(other)
-    mark = fc_total.sum_three(*mark)
-    mine = mapped_three(qkv_full, after(parts, *mark), 0, col_swap(other))
-    one_other = row_swap(half_of(1 - r, mine, 0).astype(bf16))
-    mark = out_total.sum_three(mine)
+    mark = kv_total.spread_one(*mark)
+    mark = fc_total.spread_two(*mark)
+    part_other = mapped(proj_full, after(activated, *mark), 1, False)
+    mark = [part_other]
+    packed = hop_added(packed, packed_peer, *mark)
+    packed_peer, mark = hop(packed, 4), [packed]
+    mark = kv_total.spread_two(*mark)
+    mark = oq_total.spread_two(*mark)
     mark = proj_total.spread_three(*mark)
-    mark = fc_total.spread_one(*mark)
-    mark = kv_total.sum_one(*mark)
-    mark = out_total.spread_one(*mark)
-
-    normed_half = half_of(r, normed_one, 0)
-    h_one_grad = after(half_of(r, mine, 0), *mark) + one_other.astype(f32)
-    scaled = h_one_grad * column(ln1_gain)
-    sums = jnp.stack([jnp.sum(scaled, axis=0), jnp.sum(scaled * normed_half, axis=0)])
-    sums_peer = row_swap(sums)
-
-    mark = q_total.sum_one(sums)
-    mark = fc_total.spread_two(*mark)
-    sums = (after(sums, *mark) + sums_peer) / (2 * half)
-    x_grad = half_of(r, mid_grad, 0) + inverse_one * (
-        scaled - sums[0][None] - normed_half * sums[1][None]
-    )
-    mark = out_total.spread_two(x_grad)
-    mark = kv_total.sum_two(*mark)
-    block_out = after(half_of(r, x_mid, 0), *mark) + plus(half_of(r, proj_part, 0), block_other)
-    block_out = (block_out + column(proj_bias)).astype(bf16)
-
-    h_two_half = half_of(r, h_two_grad, 0)
-    own = jnp.stack(
-        [
-            jnp.sum(h_one_grad * normed_half, axis=1),
-            jnp.sum(h_one_grad, axis=1),
-            jnp.sum(h_two_half * half_of(r, normed_two, 0), axis=1),
-            jnp.sum(h_two_half, axis=1),
-            jnp.sum(half_of(r, branch_grad, 0).astype(f32), axis=1),
-            jnp.sum(grad_own.astype(f32), axis=1),
-        ]
-    )
-    own_peer = col_swap(own)
-    fc_bias_grad = jnp.sum(fc_bias_grad, axis=1)
-    qv = jnp.stack([jnp.sum(parts[i * most : (i + 1) * most].astype(f32), axis=1) for i in (2, 1)])
-
-    proj_weight_grad = jnp.concatenate(proj_total.result(block_out), axis=1).astype(f32).T
-    mark = q_total.sum_two(proj_weight_grad)
-    mark = kv_total.sum_three(*mark)
-    own = after(own, *mark) + own_peer
-    pack_sums = jnp.concatenate([own.reshape(-1), fc_bias_grad, qv.reshape(-1)])
-    pack_sums = pad_to(pack_sums, -(-pack_sums.shape[0] // 1024) * 1024, 0).reshape(-1, 128)
-    steps = [
-        [out_total.spread_three, q_total.sum_three],
-        [kv_total.spread_one, fc_total.spread_three],
-        [q_total.spread_one],
-    ]
-    if n_dp & (n_dp - 1):
-        pack_sums = lax.psum(pack_sums, "dp")
-    else:
-        mask = 1
-        while mask < n_dp:
-            peer = dp_xor(pack_sums, mask)
-            for step in steps[:1]:
-                for one in step:
-                    mark = one(*mark)
-            steps = steps[1:]
-            pack_sums = after(pack_sums, *mark) + peer
-            mask *= 2
-    peer = row_swap(pack_sums).reshape(-1)
-    mark = kv_total.spread_two(*mark)
-    mark = q_total.spread_two(*mark)
-    peer = after(peer, *mark)
-    pack_sums = pack_sums.reshape(-1)
-    own = pack_sums[: 6 * half].reshape(6, half)
-    low, high = 6 * half, 6 * half + fc_bias_grad.shape[0]
-    fc_bias_grad = ordered(r, pack_sums[low:high], peer[low:high], 0)
-    qv_mine, qv_peer = [v[high : high + 2 * most].reshape(2, most) for v in (pack_sums, peer)]
+    mark = kv_total.spread_three(*mark)
+    mark = oq_total.spread_three(*mark)
+    packed = hop_added(packed, packed_peer, *mark)
+    if n_dp != 8:
+        for i in range(n_dp.bit_length() - 1):
+            packed = sums_added(packed, dp_xor(packed, 1 << i), 16)
+    packed_peer, mark = row_swap(packed), [packed]
+    mark = fc_total.spread_three(*mark)
+    packed_peer = after(packed_peer, *mark)
+    mark = [packed_peer]
+    proj_part = mapped(proj_full, after(activated, *mark), 0, False, col_swap(part_other))
+    mark = [proj_part]
+    mark = kv_total.tail(most, spare, *mark)
+    mark = oq_total.tail(most, spare, *mark)
+    send = half_rows(after(proj_part, *mark), 1 - r)
+    block_other, mark = row_swap(send), [send]
+    whole = oq_total.slots(c, most, spare, *mark)
+    out_weight_grad = whole[0]
+    q_weight_grad = whole[1]
+    mark = [whole]
+    whole = kv_total.slots(c, most, spare, *mark)
+    k_weight_grad = whole[0]
+    v_weight_grad = whole[1]
+    mark = [whole]
+    block_out = block_result(after(x_mid, *mark), proj_part, block_other, proj_bias_half, r)
+    mark = [block_out]
+    proj_weight_grad = proj_total.wide(*mark).T
+    mark = [proj_weight_grad]
+    fc_weight_grad = fc_total.wide(*mark)
+    mark = [fc_weight_grad]
+
+    own = half_of(r, packed, 1)
+    fc_bias_grad = ordered(r, packed[8], packed_peer[8], 0)
+    qv_mine, qv_peer = packed[9:11, :most], packed_peer[9:11, :most]
     qv_bias_grad = from_slots(
         c, jnp.where(r == 0, qv_mine, qv_peer), jnp.where(r == 0, qv_peer, qv_mine), 1, spare
     )
-    out_weight_grad = from_slots(c, *out_total.result(*mark), 1, spare).T.astype(f32)
-    fc_weight_grad = jnp.concatenate(fc_total.result(out_weight_grad), axis=1).astype(f32)
-    mark = kv_total.spread_three(fc_weight_grad)
-    mark = q_total.spread_three(*mark)
-    q_both = q_total.result(*mark)
-    kv_both = kv_total.result(q_both[0])
-    pairs = [q_both] + [[v[:, i * most : (i + 1) * most] for v in kv_both] for i in range(2)]
-    qkv_weight_grad = jnp.stack([from_slots(c, *pair, 1, spare).astype(f32) for pair in pairs])
+    qkv_weight_grad = jnp.stack([q_weight_grad, k_weight_grad, v_weight_grad])
+    out_weight_grad = out_weight_grad.T
     return (
         block_out.T,
         x_grad.T,
-        own[0],
-        own[1],
+        packed[3, :half],
+        packed[3, half:],
         qkv_weight_grad,
         qv_bias_grad,
         out_weight_grad,
-        own[4],
         own[2],
-        own[3],
+        own[0],
+        own[1],
         fc_weight_grad,
         fc_bias_grad,
         proj_weight_grad,
-        own[5],
+        packed[4, :half],
     )
 
 

time: 903 us -> 805 us (0.89)
  other arithmetic: 159 us -> 18.1 us
  Pallas kernels: 200 us -> 326 us
  waiting for transfers between devices: 373 us -> 287 us
  local copies, waits for them, and re-layouts: 53.4 us -> 81.7 us
  starting transfers between devices: 109 us -> 83.9 us
    pallas_call x23 -> x68, Pallas kernels: 149 us -> 269 us  [call(): pl.pallas_call(body, grid_spec=pltpu.PrefetchScalarGridSpec(num_scalar_pr...]
    ppermute x13, waiting for transfers between devices: 116 us -> 52.1 us  [row_swap(): return lax.ppermute(value, 'row', SWAP)]
    select_n x27 -> x2, other arithmetic: 63.6 us -> 3.17 us  [ordered(): jnp.where(at == 0, jnp.concatenate([first, second], axis=axis), jnp.conca...]
    convert_element_type x26 -> x0, other arithmetic: 37.8 us -> none  [the longest x5 8.59 us: sum_one(): part = plus(after(self.keep, *marks), self.got).astype(bf16)]
    unnamed x170 -> x184, local copies, waits for them, and re-layouts: 26.2 us -> 61.1 us
    ppermute x39 -> x36, waiting for transfers between devices: 249 us -> 221 us  [dp_xor(): lax.ppermute(value, 'dp', [(i, i ^ mask) for i in range(lax.axis_size('dp...]
    ppermute x39 -> x36, starting transfers between devices: 76.6 us -> 57.6 us  [dp_xor(): lax.ppermute(value, 'dp', [(i, i ^ mask) for i in range(lax.axis_size('dp...]
    reduce_sum x11 -> x0, other arithmetic: 17.9 us -> none  [the longest x2 5.64 us: norm(): center = jnp.mean(values, axis=0, keepdims=True)]
  transfers between devices with their start and end apart: 74 -> 68, of which waited for: 34 -> 34; matrix products, arithmetic and copies ran while one was open for 19% -> 5% of each run, Pallas kernels for 16% -> 35%
where the time goes in v3:
time: 805 us; the launch traced here: 799 us
  Pallas kernels  326 us (40%)
  waiting for transfers between devices  287 us (36%)
  starting transfers between devices  83.9 us (10%)
  local copies, waits for them, and re-layouts  81.7 us (10%)
  other arithmetic  18.1 us (2%)
    pallas_call x68, Pallas kernels, call(): pl.pallas_call(body, grid_spec=pltpu.PrefetchScalarGridSpec(num_scalar_pr...  269 us
    ppermute x36, waiting for transfers between devices, dp_xor(): lax.ppermute(value, 'dp', [(i, i ^ mask) for i in range(lax.axis_size('dp...  221 us
    unnamed x184, local copies, waits for them, and re-layouts  61.1 us
    ppermute x36, starting transfers between devices, dp_xor(): lax.ppermute(value, 'dp', [(i, i ^ mask) for i in range(lax.axis_size('dp...  57.6 us
    ppermute x13, waiting for transfers between devices, row_swap(): return lax.ppermute(value, 'row', SWAP)  52.1 us
    pallas_call x1, Pallas kernels, attend(): pl.pallas_call(functools.partial(attend_kernel, heads, blocks), grid_spec...  25.3 us
    pallas_call x1, Pallas kernels, attend_back(): pl.pallas_call(functools.partial(attend_back_kernel, heads, blocks), grid...  25.3 us
    ppermute x13, starting transfers between devices, row_swap(): return lax.ppermute(value, 'row', SWAP)  19.7 us
  transfers between devices with their start and end apart: 68, of which 34 were waited for; matrix products, arithmetic and copies ran while one was open for 5% of the time, Pallas kernels for 35%

profile of v3, /device:TPU:0, one launch (start us, length us, event | category | flops | bytes accessed | tf_op | source)
XLA Modules:
  0.0 799.0 jit_solution(3038372005260803101)
XLA Ops:
  19.4 5.0 pack.1
  28.1 5.5 own_rows.3.h_ref
  33.6 7.7 collective-permute-done.3.refs_0_
  46.1 5.2 own_rows.4.h_ref
  51.3 4.6 collective-permute-done.5.refs_2_
  57.2 5.3 own_rows.5.h_ref
  62.5 4.2 collective-permute-done.1.peer_ref
  78.0 13.9 %collective-permute-done.8.refs_3_ = bf16[3,200,448]{2,1,0:T(8,128)(2,1)} collective-permute-done((bf16[3,200,448]{2,1,0:T(8,128)(2,1)}, bf16[3,200,448]{2,1,0:T(8,128)(2,1)}, u32[]{:S(2)}, u32[]{:S(2)}) %collective-permute-start.8) | collective-permute-done | bytes 537632 | tf_op jit(solution)/shard_map/ppermute | solution.py:449
  99.1 12.5 %project.1.q_ref.k_ref.v_ref = bf16[1344,1536]{1,0:T(8,128)(2,1)S(1)} custom-call(s32[1]{0:T(128)} %constant.100.clone.1._, bf16[3,1600,448]{2,1,0:T(8,128)(2,1)} %bitcast.83, bf16[1600,768]{1,0:T(8,128)(2,1)S(1)} %get-tuple-element.139.own_ref, bf16[1600,768]{1,0:T(8,128)(2,1)} %collective-permute-done.9.other_ref, f32[3,448,1]{2,1,0:T(8,128)S(1)} %copy.64.b_ref), custom_call_target="tpu_custom_call" | custom-call | tf_op jit(solution)/shard_map/project/pallas_call | solution.py:208
  115.9 7.1 collective-permute-done.10
  125.5 25.3 %attend.1 = (bf16[448,1536]{1,0:T(8,128)(2,1)S(1)}, f32[8,1536]{1,0:T(8,128)S(1)}) custom-call(s32[7]{0:T(128)S(1)} %pad_add_fusion.3.info_ref, bf16[1344,1536]{1,0:T(8,128)(2,1)S(1)} %project.1.q_ref.k_ref.v_ref, bf16[1344,1536]{1,0:T(8,128)(2,1)S(1)} %project.1.q_ref.k_ref.v_ref, bf16[1344,1536]{1,0:T(8,128)(2,1)S(1)} %project.1.q_ref.k_ref.v_ref, ...), custom_call_target="tpu_custom_call" | custom-call | tf_op jit(solution)/shard_map/attend/pallas_call | solution.py:90
  153.2 4.7 collective-permute-done.17.refs_0_
  157.8 3.4 mapped.7.low_ref
  161.6 9.7 %collective-permute-start.18 = (bf16[200,1600]{1,0:T(8,128)(2,1)S(1)}, bf16[200,1600]{1,0:T(8,128)(2,1)}, u32[]{:S(2)}, u32[]{:S(2)}) collective-permute-start(bf16[200,1600]{1,0:T(8,128)(2,1)S(1)} %collective-permute-done.14.refs_2_), channel_id=1, source_target_pairs={{0,4},{4,0},{8,12},{12,8},{16,20},{20,16},{24,28},{28,24},{1,5},{5... | collective-permute-start | bytes 1920008 | tf_op jit(solution)/shard_map/ppermute | solution.py:449
  174.1 13.1 %collective-permute-done.18.refs_3_ = bf16[200,1600]{1,0:T(8,128)(2,1)} collective-permute-done((bf16[200,1600]{1,0:T(8,128)(2,1)S(1)}, bf16[200,1600]{1,0:T(8,128)(2,1)}, u32[]{:S(2)}, u32[]{:S(2)}) %collective-permute-start.18) | collective-permute-done | bytes 640032 | tf_op jit(solution)/shard_map/ppermute | solution.py:449
  193.0 7.7 collective-permute-done.19.refs_3_
  203.1 13.8 %collective-permute-done.20.other_ref = bf16[1600,768]{1,0:T(8,128)(2,1)} collective-permute-done((bf16[1600,768]{1,0:T(8,128)(2,1)}, bf16[1600,768]{1,0:T(8,128)(2,1)}, u32[]{:S(2)}, u32[]{:S(2)}) %collective-permute-start.20) | collective-permute-done | bytes 2457632 | tf_op jit(solution)/shard_map/ppermute | solution.py:441
  217.0 7.2 norm_two.1
  230.3 19.5 %hidden.1 = (bf16[1600,1536]{1,0:T(8,128)(2,1)S(1)}, f32[1600,1536]{1,0:T(8,128)}) custom-call(s32[1]{0:T(128)} %constant.100.clone.1._, bf16[1600,1600]{1,0:T(8,128)(2,1)} %bitcast.78, bf16[1600,768]{1,0:T(8,128)(2,1)} %get-tuple-element.159.own_ref, bf16[1600,768]{1,0:T(8,128)(2,1)S(1)} %collective-permute-done.21.other_ref, f32[1600,1]{1,0:T(8,128)S(1)} %copy-done.61), custom_call_target="tpu_custom_call" | custom-call | tf_op jit(solution)/shard_map/hidden/pallas_call | solution.py:208
  249.8 4.2 collective-permute-done.22.b_ref
  256.1 4.7 collective-permute-done.23.other_ref
  260.8 15.9 %hidden_back.1 = (bf16[1600,1536]{1,0:T(8,128)(2,1)S(1)}, f32[1600,128]{1,0:T(8,128)S(1)}) custom-call(s32[1]{0:T(128)} %constant.100.clone.1._, bf16[1600,1600]{1,0:T(8,128)(2,1)} %bitcast.73, bf16[1600,768]{1,0:T(8,128)(2,1)S(1)} %bitcast.91, bf16[1600,768]{1,0:T(8,128)(2,1)S(1)} %collective-permute-done.23.other_ref, f32[1600,1536]{1,0:T(8,128)} %get-tuple-element.163.s_ref), custom_call_target="tpu_custom_call" | custom-call | tf_op jit(solution)/shard_map/hidden_back/pallas_call | solution.py:208
  277.7 6.2 mapped.8
  288.1 6.5 weight_grad.8
  294.7 9.7 %collective-permute-start.25 = (bf16[2,2,200,1600]{3,2,1,0:T(8,128)(2,1)}, bf16[2,2,200,1600]{3,2,1,0:T(8,128)(2,1)}, u32[]{:S(2)}, u32[]{:S(2)}) collective-permute-start(bf16[2,2,200,1600]{3,2,1,0:T(8,128)(2,1)} %bitcast.39), channel_id=1, source_target_pairs={{0,4},{4,0},{8,12},{12,8},{16,20},{20,16},{24,28},{28,24},{1,5},{5... | collective-permute-start | bytes 7680008 | tf_op jit(solution)/shard_map/ppermute | solution.py:449
  304.4 8.0 %mapped.9.low_ref = bf16[1600,768]{1,0:T(8,128)(2,1)} custom-call(s32[1]{0:T(128)} %constant.100.clone.1._, bf16[1600,1600]{1,0:T(8,128)(2,1)} %bitcast.79, bf16[1600,1536]{1,0:T(8,128)(2,1)S(1)} %copy-done.18, bf16[1600,768]{1,0:T(8,128)(2,1)} %collective-permute-done.24.refs_0_), custom_call_target="tpu_custom_call" | custom-call | tf_op jit(solution)/shard_map/mapped/pallas_call | solution.py:208
  316.8 9.2 %weight_grad.9 = bf16[4,200,1600]{2,1,0:T(8,128)(2,1)} custom-call(s32[4]{0:T(128)S(1)} %fusion.9._, bf16[8,200,768]{2,1,0:T(8,128)(2,1)} %bitcast.35.refs_0_, bf16[8,200,768]{2,1,0:T(8,128)(2,1)S(1)} %bitcast.103, bf16[1600,1536]{1,0:T(8,128)(2,1)S(1)} %copy-done.19), custom_call_target="tpu_custom_call" | custom-call | tf_op jit(solution)/shard_map/weight_grad/pallas_call | solution.py:208
  330.1 8.3 %weight_grad.10 = bf16[4,200,1600]{2,1,0:T(8,128)(2,1)S(1)} custom-call(s32[4]{0:T(128)S(1)} %fusion.10._, bf16[8,200,768]{2,1,0:T(8,128)(2,1)} %bitcast.35.refs_0_, bf16[8,200,768]{2,1,0:T(8,128)(2,1)S(1)} %bitcast.104, bf16[1600,1536]{1,0:T(8,128)(2,1)S(1)} %copy-done.20), custom_call_target="tpu_custom_call" | custom-call | tf_op jit(solution)/shard_map/weight_grad/pallas_call | solution.py:208
  340.9 5.4 weight_grad.11
  346.3 16.7 %collective-permute-done.25.b_ref.d_ref = bf16[2,2,200,1600]{3,2,1,0:T(8,128)(2,1)} collective-permute-done((bf16[2,2,200,1600]{3,2,1,0:T(8,128)(2,1)}, bf16[2,2,200,1600]{3,2,1,0:T(8,128)(2,1)}, u32[]{:S(2)}, u32[]{:S(2)}) %collective-permute-start.25) | collective-permute-done | bytes 2560032 | tf_op jit(solution)/shard_map/ppermute | solution.py:449
  368.1 9.4 %norm_two_back.1 = (f32[1600,768]{1,0:T(8,128)}, bf16[1600,768]{1,0:T(8,128)(2,1)S(1)}, f32[3,1600,128]{2,1,0:T(8,128)S(1)}) custom-call(s32[1]{0:T(128)} %constant.100.clone.1._, bf16[1600,768]{1,0:T(8,128)(2,1)} %mapped.9.low_ref, bf16[1600,768]{1,0:T(8,128)(2,1)} %collective-permute-done.26.other_ref, bf16[1600,768]{1,0:T(8,128)(2,1)S(1)} %bitcast.94, ...), custom_call_target="tpu_custom_call" | custom-call | tf_op jit(solution)/shard_map/norm_two_back/pallas_call | solution.py:208
  379.0 7.9 collective-permute-done.27.b_ref.d_ref
  394.2 25.3 %attend_back.1.refs_2_.p_ref.refs_5_ = bf16[1344,1536]{1,0:T(8,128)(2,1)S(1)} custom-call(s32[7]{0:T(128)S(1)} %pad_add_fusion.3.info_ref, bf16[1344,1536]{1,0:T(8,128)(2,1)S(1)} %copy-done.4, bf16[1344,1536]{1,0:T(8,128)(2,1)S(1)} %copy-done.4, bf16[1344,1536]{1,0:T(8,128)(2,1)S(1)} %copy-done.4, bf16[448,1536]{1,0:T(8,128)(2,1)S(1)} %copy-done.25, ...), custom_call_target="tpu_custom_call" | custom-call | tf_op jit(solution)/shard_map/attend_back/pallas_call | solution.py:178
  419.6 5.9 weight_grad.12
  425.5 5.8 mapped_three.2
  431.3 9.5 %collective-permute-start.32 = (bf16[2,2,200,896]{3,2,1,0:T(8,128)(2,1)}, bf16[2,2,200,896]{3,2,1,0:T(8,128)(2,1)}, u32[]{:S(2)}, u32[]{:S(2)}) collective-permute-start(bf16[2,2,200,896]{3,2,1,0:T(8,128)(2,1)} %bitcast.48), channel_id=1, source_target_pairs={{0,4},{4,0},{8,12},{12,8},{16,20},{20,16},{24,28},{28,24},{1,5},{5... | collective-permute-start | bytes 4300808 | tf_op jit(solution)/shard_map/ppermute | solution.py:449
  446.5 6.0 weight_grad.13
  460.2 5.4 weight_grad.14
  465.7 6.4 mapped_three.3.a_ref.m_ref
  472.1 5.0 weight_grad.15
  482.3 14.5 %collective-permute-done.33.b_ref = bf16[200,1600]{1,0:T(8,128)(2,1)} collective-permute-done((bf16[200,1600]{1,0:T(8,128)(2,1)}, bf16[200,1600]{1,0:T(8,128)(2,1)}, u32[]{:S(2)}, u32[]{:S(2)}) %collective-permute-start.33) | collective-permute-done | bytes 640032 | tf_op jit(solution)/shard_map/ppermute | solution.py:449
  498.0 6.0 collective-permute-done.34.b_ref.d_ref
  514.6 11.6 %collective-permute-done.36.b_ref.d_ref = bf16[2,200,896]{2,1,0:T(8,128)(2,1)S(1)} collective-permute-done((bf16[2,200,896]{2,1,0:T(8,128)(2,1)S(1)}, bf16[2,200,896]{2,1,0:T(8,128)(2,1)S(1)}, u32[]{:S(2)}, u32[]{:S(2)}) %collective-permute-start.36) | collective-permute-done | bytes 716832 | tf_op jit(solution)/shard_map/ppermute | solution.py:449
  530.1 19.2 %collective-permute-done.38.b_ref.d_ref = bf16[2,200,896]{2,1,0:T(8,128)(2,1)} collective-permute-done((bf16[2,200,896]{2,1,0:T(8,128)(2,1)}, bf16[2,200,896]{2,1,0:T(8,128)(2,1)}, u32[]{:S(2)}, u32[]{:S(2)}) %collective-permute-start.38) | collective-permute-done | bytes 716832 | tf_op jit(solution)/shard_map/ppermute | solution.py:449
  563.3 6.1 packed_sums.1.a_ref
  571.0 27.7 %collective-permute-done.42.b_ref = bf16[200,896]{1,0:T(8,128)(2,1)} collective-permute-done((bf16[200,896]{1,0:T(8,128)(2,1)}, bf16[200,896]{1,0:T(8,128)(2,1)}, u32[]{:S(2)}, u32[]{:S(2)}) %collective-permute-start.42) | collective-permute-done | bytes 358432 | tf_op jit(solution)/shard_map/ppermute | solution.py:449
  601.8 6.6 collective-permute-start.44
  608.4 12.6 %collective-permute-done.44.b_ref = f32[8,768]{1,0:T(8,128)S(1)} collective-permute-done((f32[8,768]{1,0:T(8,128)S(1)}, f32[8,768]{1,0:T(8,128)S(1)}, u32[]{:S(2)}, u32[]{:S(2)}) %collective-permute-start.44) | collective-permute-done | bytes 24608 | tf_op jit(solution)/shard_map/ppermute | solution.py:441
  638.4 6.2 mapped.10
  644.6 19.5 %collective-permute-done.50.b_ref = f32[16,1600]{1,0:T(8,128)S(1)} collective-permute-done((f32[16,1600]{1,0:T(8,128)S(1)}, f32[16,1600]{1,0:T(8,128)S(1)}, u32[]{:S(2)}, u32[]{:S(2)}) %collective-permute-start.50) | collective-permute-done | bytes 102432 | tf_op jit(solution)/shard_map/ppermute | solution.py:449
  664.1 5.6 collective-permute-done.51.b_ref
  670.4 6.0 collective-permute-done.52.b_ref
  680.4 5.7 collective-permute-done.54.b_ref
  689.0 8.9 %collective-permute-done.55.b_ref = bf16[2,200,896]{2,1,0:T(8,128)(2,1)S(1)} collective-permute-done((bf16[2,200,896]{2,1,0:T(8,128)(2,1)S(1)}, bf16[2,200,896]{2,1,0:T(8,128)(2,1)S(1)}, u32[]{:S(2)}, u32[]{:S(2)}) %collective-permute-start.55) | collective-permute-done | bytes 716832 | tf_op jit(solution)/shard_map/ppermute | solution.py:449
  709.9 6.9 mapped.11.a_ref.p_ref
  716.9 11.9 %collective-permute-done.60.b_ref.d_ref = bf16[2,2,200,896]{3,2,1,0:T(8,128)(2,1)} collective-permute-done((bf16[2,2,200,896]{3,2,1,0:T(8,128)(2,1)}, bf16[2,2,200,896]{3,2,1,0:T(8,128)(2,1)}, u32[]{:S(2)}, u32[]{:S(2)}) %collective-permute-start.60) | collective-permute-done | bytes 1433632 | tf_op jit(solution)/shard_map/ppermute | solution.py:449
  743.1 4.4 unslotted.2
  747.6 4.4 unslotted.3
  756.3 4.1 copy.73
  760.4 7.7 pad_maximum_fusion
  770.4 3.4 block_result.1
  773.8 10.4 %collective-permute-done.66.b_ref.d_ref = bf16[2,2,200,1600]{3,2,1,0:T(8,128)(2,1)} collective-permute-done((bf16[2,2,200,1600]{3,2,1,0:T(8,128)(2,1)S(1)}, bf16[2,2,200,1600]{3,2,1,0:T(8,128)(2,1)}, u32[]{:S(2)}, u32[]{:S(2)}) %collective-permute-start.66) | collective-permute-done | bytes 2560032 | tf_op jit(solution)/shard_map/ppermute | solution.py:449
  784.2 6.6 widened.2
  790.8 8.0 widened.3
  (398 shorter events, 215.6 us)
Async XLA Ops:
  2.0 16.2 %collective-permute-start = (bf16[3,800,32]{1,2,0:T(8,128)(2,1)S(1)}, bf16[3,800,32]{1,2,0:T(8,128)(2,1)S(1)}, u32[]{:S(2)}, u32[]{:S(2)}) collective-permute-start(bf16[3,800,32]{1,2,0:T(8,128)(2,1)S(1)} %copy.74), channel_id=1, source_target_pairs={{0,1},{1,0},{2,3},{3,2},{4,5},{5,4},{6,7},{7,6},{8,9},{9,8},{10,11... | collective-permute-start | bytes 460808 | tf_op jit(solution)/shard_map/ppermute | solution.py:445
  3.4 23.1 %collective-permute-start.2 = (bf16[32,800]{1,0:T(8,128)(2,1)S(1)}, bf16[32,800]{1,0:T(8,128)(2,1)S(1)}, u32[]{:S(2)}, u32[]{:S(2)}) collective-permute-start(bf16[32,800]{1,0:T(8,128)(2,1)S(1)} %slice.124), channel_id=1, source_target_pairs={{0,1},{1,0},{2,3},{3,2},{4,5},{5,4},{6,7},{7,6},{8,9},{9,8},{10,11... | collective-permute-start | bytes 153608 | tf_op jit(solution)/shard_map/ppermute | solution.py:445
  4.1 13.3 %collective-permute-start.7 = (bf16[2,32]{1,0:T(2,128)(2,1)S(1)}, bf16[2,32]{1,0:T(2,128)(2,1)S(1)}, u32[]{:S(2)}, u32[]{:S(2)}) collective-permute-start(bf16[2,32]{1,0:T(2,128)(2,1)S(1)} %slice.135), channel_id=1, source_target_pairs={{0,1},{1,0},{2,3},{3,2},{4,5},{5,4},{6,7},{7,6},{8,9},{9,8},{10,11... | collective-permute-start | bytes 392 | tf_op jit(solution)/shard_map/ppermute | solution.py:445
  8.0 36.4 %collective-permute-start.6 = (bf16[5,800]{1,0:T(8,128)(2,1)S(1)}, bf16[5,800]{1,0:T(8,128)(2,1)S(1)}, u32[]{:S(2)}, u32[]{:S(2)}) collective-permute-start(bf16[5,800]{1,0:T(8,128)(2,1)S(1)} %stack.86), channel_id=1, source_target_pairs={{0,2},{2,0},{1,3},{3,1},{4,6},{6,4},{5,7},{7,5},{8,10},{10,8},{9,1... | collective-permute-start | bytes 24008 | tf_op jit(solution)/shard_map/ppermute | solution.py:441
  24.3 17.0 %collective-permute-start.3 = (bf16[3,200,448]{2,1,0:T(8,128)(2,1)}, bf16[3,200,448]{2,1,0:T(8,128)(2,1)}, u32[]{:S(2)}, u32[]{:S(2)}) collective-permute-start(bf16[3,200,448]{2,1,0:T(8,128)(2,1)} %get-tuple-element.131), channel_id=1, source_target_pairs={{0,2},{2,0},{1,3},{3,1},{4,6},{6,4},{5,7},{7,5},{8,10},{10,8},{9,1... | collective-permute-start | bytes 1612808 | tf_op jit(solution)/shard_map/ppermute | solution.py:441
  24.3 42.4 %collective-permute-start.1 = (bf16[800,768]{1,0:T(8,128)(2,1)S(1)}, bf16[800,768]{1,0:T(8,128)(2,1)S(1)}, u32[]{:S(2)}, u32[]{:S(2)}) collective-permute-start(bf16[800,768]{1,0:T(8,128)(2,1)S(1)} %bitcast.111), channel_id=1, source_target_pairs={{0,2},{2,0},{1,3},{3,1},{4,6},{6,4},{5,7},{7,5},{8,10},{10,8},{9,1... | collective-permute-start | bytes 3686408 | tf_op jit(solution)/shard_map/ppermute | solution.py:441
  41.4 14.6 %collective-permute-start.5 = (bf16[3,200,448]{2,1,0:T(8,128)(2,1)}, bf16[3,200,448]{2,1,0:T(8,128)(2,1)}, u32[]{:S(2)}, u32[]{:S(2)}) collective-permute-start(bf16[3,200,448]{2,1,0:T(8,128)(2,1)} %collective-permute-done.3.refs_0_), channel_id=1, source_target_pairs={{0,8},{4,12},{8,0},{12,4},{16,24},{20,28},{24,16},{28,20},{1,9},{5... | collective-permute-start | bytes 1612808 | tf_op jit(solution)/shard_map/ppermute | solution.py:449
  42.9 14.3 %collective-permute-start.4 = (bf16[3,200,448]{2,1,0:T(8,128)(2,1)}, bf16[3,200,448]{2,1,0:T(8,128)(2,1)}, u32[]{:S(2)}, u32[]{:S(2)}) collective-permute-start(bf16[3,200,448]{2,1,0:T(8,128)(2,1)} %collective-permute-done.3.refs_0_), channel_id=1, source_target_pairs={{0,4},{4,0},{8,12},{12,8},{16,20},{20,16},{24,28},{28,24},{1,5},{5... | collective-permute-start | bytes 1612808 | tf_op jit(solution)/shard_map/ppermute | solution.py:449
  73.8 25.3 %collective-permute-start.9 = (bf16[1600,768]{1,0:T(8,128)(2,1)S(1)}, bf16[1600,768]{1,0:T(8,128)(2,1)}, u32[]{:S(2)}, u32[]{:S(2)}) collective-permute-start(bf16[1600,768]{1,0:T(8,128)(2,1)S(1)} %get-tuple-element.139.own_ref), channel_id=1, source_target_pairs={{0,1},{1,0},{2,3},{3,2},{4,5},{5,4},{6,7},{7,6},{8,9},{9,8},{10,11... | collective-permute-start | bytes 7372808 | tf_op jit(solution)/shard_map/ppermute | solution.py:445
  73.8 37.9 %collective-permute-start.12 = (bf16[200,1600]{1,0:T(8,128)(2,1)}, bf16[200,1600]{1,0:T(8,128)(2,1)}, u32[]{:S(2)}, u32[]{:S(2)}) collective-permute-start(bf16[200,1600]{1,0:T(8,128)(2,1)} %get-tuple-element.148), channel_id=1, source_target_pairs={{0,2},{2,0},{1,3},{3,1},{4,6},{6,4},{5,7},{7,5},{8,10},{10,8},{9,1... | collective-permute-start | bytes 1920008 | tf_op jit(solution)/shard_map/ppermute | solution.py:441
  74.1 37.6 %collective-permute-start.11 = (bf16[200,1600]{1,0:T(8,128)(2,1)}, bf16[200,1600]{1,0:T(8,128)(2,1)}, u32[]{:S(2)}, u32[]{:S(2)}) collective-permute-start(bf16[200,1600]{1,0:T(8,128)(2,1)} %get-tuple-element.145), channel_id=1, source_target_pairs={{0,2},{2,0},{1,3},{3,1},{4,6},{6,4},{5,7},{7,5},{8,10},{10,8},{9,1... | collective-permute-start | bytes 1920008 | tf_op jit(solution)/shard_map/ppermute | solution.py:441
  75.8 16.0 %collective-permute-start.8 = (bf16[3,200,448]{2,1,0:T(8,128)(2,1)}, bf16[3,200,448]{2,1,0:T(8,128)(2,1)}, u32[]{:S(2)}, u32[]{:S(2)}) collective-permute-start(bf16[3,200,448]{2,1,0:T(8,128)(2,1)} %collective-permute-done.5.refs_2_), channel_id=1, source_target_pairs={{0,4},{4,0},{8,12},{12,8},{16,20},{20,16},{24,28},{28,24},{1,5},{5... | collective-permute-start | bytes 1612808 | tf_op jit(solution)/shard_map/ppermute | solution.py:449
  77.4 45.6 %collective-permute-start.10 = (bf16[448,800]{1,0:T(8,128)(2,1)}, bf16[448,800]{1,0:T(8,128)(2,1)}, u32[]{:S(2)}, u32[]{:S(2)}) collective-permute-start(bf16[448,800]{1,0:T(8,128)(2,1)} %get-tuple-element.143), channel_id=1, source_target_pairs={{0,2},{2,0},{1,3},{3,1},{4,6},{6,4},{5,7},{7,5},{8,10},{10,8},{9,1... | collective-permute-start | bytes 2150408 | tf_op jit(solution)/shard_map/ppermute | solution.py:441
  111.7 39.1 %collective-permute-start.16 = (bf16[200,1600]{1,0:T(8,128)(2,1)}, bf16[200,1600]{1,0:T(8,128)(2,1)}, u32[]{:S(2)}, u32[]{:S(2)}) collective-permute-start(bf16[200,1600]{1,0:T(8,128)(2,1)} %collective-permute-done.12.refs_0_), channel_id=1, source_target_pairs={{0,8},{4,12},{8,0},{12,4},{16,24},{20,28},{24,16},{28,20},{1,9},{5... | collective-permute-start | bytes 1920008 | tf_op jit(solution)/shard_map/ppermute | solution.py:449
  113.4 37.5 %collective-permute-start.14 = (bf16[200,1600]{1,0:T(8,128)(2,1)}, bf16[200,1600]{1,0:T(8,128)(2,1)S(1)}, u32[]{:S(2)}, u32[]{:S(2)}) collective-permute-start(bf16[200,1600]{1,0:T(8,128)(2,1)} %collective-permute-done.11.refs_0_), channel_id=1, source_target_pairs={{0,8},{4,12},{8,0},{12,4},{16,24},{20,28},{24,16},{28,20},{1,9},{5... | collective-permute-start | bytes 1920008 | tf_op jit(solution)/shard_map/ppermute | solution.py:449
  113.8 37.0 %collective-permute-start.15 = (bf16[200,1600]{1,0:T(8,128)(2,1)}, bf16[200,1600]{1,0:T(8,128)(2,1)S(1)}, u32[]{:S(2)}, u32[]{:S(2)}) collective-permute-start(bf16[200,1600]{1,0:T(8,128)(2,1)} %collective-permute-done.12.refs_0_), channel_id=1, source_target_pairs={{0,4},{4,0},{8,12},{12,8},{16,20},{20,16},{24,28},{28,24},{1,5},{5... | collective-permute-start | bytes 1920008 | tf_op jit(solution)/shard_map/ppermute | solution.py:449
  115.3 35.5 %collective-permute-start.13 = (bf16[200,1600]{1,0:T(8,128)(2,1)}, bf16[200,1600]{1,0:T(8,128)(2,1)S(1)}, u32[]{:S(2)}, u32[]{:S(2)}) collective-permute-start(bf16[200,1600]{1,0:T(8,128)(2,1)} %collective-permute-done.11.refs_0_), channel_id=1, source_target_pairs={{0,4},{4,0},{8,12},{12,8},{16,20},{20,16},{24,28},{28,24},{1,5},{5... | collective-permute-start | bytes 1920008 | tf_op jit(solution)/shard_map/ppermute | solution.py:449
  153.1 4.7 collective-permute-start.17
  161.2 55.8 %collective-permute-start.20 = (bf16[1600,768]{1,0:T(8,128)(2,1)}, bf16[1600,768]{1,0:T(8,128)(2,1)}, u32[]{:S(2)}, u32[]{:S(2)}) collective-permute-start(bf16[1600,768]{1,0:T(8,128)(2,1)} %mapped.7.low_ref), channel_id=1, source_target_pairs={{0,2},{2,0},{1,3},{3,1},{4,6},{6,4},{5,7},{7,5},{8,10},{10,8},{9,1... | collective-permute-start | bytes 7372808 | tf_op jit(solution)/shard_map/ppermute | solution.py:441
  161.6 25.6 %collective-permute-start.18 = (bf16[200,1600]{1,0:T(8,128)(2,1)S(1)}, bf16[200,1600]{1,0:T(8,128)(2,1)}, u32[]{:S(2)}, u32[]{:S(2)}) collective-permute-start(bf16[200,1600]{1,0:T(8,128)(2,1)S(1)} %collective-permute-done.14.refs_2_), channel_id=1, source_target_pairs={{0,4},{4,0},{8,12},{12,8},{16,20},{20,16},{24,28},{28,24},{1,5},{5... | collective-permute-start | bytes 1920008 | tf_op jit(solution)/shard_map/ppermute | solution.py:449
  171.3 29.4 %collective-permute-start.19 = (bf16[200,1600]{1,0:T(8,128)(2,1)}, bf16[200,1600]{1,0:T(8,128)(2,1)}, u32[]{:S(2)}, u32[]{:S(2)}) collective-permute-start(bf16[200,1600]{1,0:T(8,128)(2,1)} %collective-permute-done.16.refs_2_), channel_id=1, source_target_pairs={{0,4},{4,0},{8,12},{12,8},{16,20},{20,16},{24,28},{28,24},{1,5},{5... | collective-permute-start | bytes 1920008 | tf_op jit(solution)/shard_map/ppermute | solution.py:449
  224.2 4.9 collective-permute-start.21
  224.3 29.7 %collective-permute-start.22 = (bf16[800,768]{1,0:T(8,128)(2,1)}, bf16[800,768]{1,0:T(8,128)(2,1)}, u32[]{:S(2)}, u32[]{:S(2)}) collective-permute-start(bf16[800,768]{1,0:T(8,128)(2,1)} %bitcast.31.a_ref.grad_ref), channel_id=1, source_target_pairs={{0,2},{2,0},{1,3},{3,1},{4,6},{6,4},{5,7},{7,5},{8,10},{10,8},{9,1... | collective-permute-start | bytes 3686408 | tf_op jit(solution)/shard_map/ppermute | solution.py:441
  283.9 20.5 %collective-permute-start.24 = (bf16[1600,768]{1,0:T(8,128)(2,1)}, bf16[1600,768]{1,0:T(8,128)(2,1)}, u32[]{:S(2)}, u32[]{:S(2)}) collective-permute-start(bf16[1600,768]{1,0:T(8,128)(2,1)} %mapped.8), channel_id=1, source_target_pairs={{0,1},{1,0},{2,3},{3,2},{4,5},{5,4},{6,7},{7,6},{8,9},{9,8},{10,11... | collective-permute-start | bytes 7372808 | tf_op jit(solution)/shard_map/ppermute | solution.py:445
  294.7 68.3 %collective-permute-start.25 = (bf16[2,2,200,1600]{3,2,1,0:T(8,128)(2,1)}, bf16[2,2,200,1600]{3,2,1,0:T(8,128)(2,1)}, u32[]{:S(2)}, u32[]{:S(2)}) collective-permute-start(bf16[2,2,200,1600]{3,2,1,0:T(8,128)(2,1)} %bitcast.39), channel_id=1, source_target_pairs={{0,4},{4,0},{8,12},{12,8},{16,20},{20,16},{24,28},{28,24},{1,5},{5... | collective-permute-start | bytes 7680008 | tf_op jit(solution)/shard_map/ppermute | solution.py:449
  312.4 55.6 %collective-permute-start.26 = (bf16[1600,768]{1,0:T(8,128)(2,1)}, bf16[1600,768]{1,0:T(8,128)(2,1)}, u32[]{:S(2)}, u32[]{:S(2)}) collective-permute-start(bf16[1600,768]{1,0:T(8,128)(2,1)} %mapped.9.low_ref), channel_id=1, source_target_pairs={{0,2},{2,0},{1,3},{3,1},{4,6},{6,4},{5,7},{7,5},{8,10},{10,8},{9,1... | collective-permute-start | bytes 7372808 | tf_op jit(solution)/shard_map/ppermute | solution.py:441
  326.0 61.0 %collective-permute-start.27 = (bf16[2,2,200,1600]{3,2,1,0:T(8,128)(2,1)}, bf16[2,2,200,1600]{3,2,1,0:T(8,128)(2,1)}, u32[]{:S(2)}, u32[]{:S(2)}) collective-permute-start(bf16[2,2,200,1600]{3,2,1,0:T(8,128)(2,1)} %bitcast.40), channel_id=1, source_target_pairs={{0,8},{4,12},{8,0},{12,4},{16,24},{20,28},{24,16},{28,20},{1,9},{5... | collective-permute-start | bytes 7680008 | tf_op jit(solution)/shard_map/ppermute | solution.py:449
  379.0 11.7 %collective-permute-start.28 = (bf16[1600,768]{1,0:T(8,128)(2,1)S(1)}, bf16[1600,768]{1,0:T(8,128)(2,1)S(1)}, u32[]{:S(2)}, u32[]{:S(2)}) collective-permute-start(bf16[1600,768]{1,0:T(8,128)(2,1)S(1)} %get-tuple-element.177.own_ref), channel_id=1, source_target_pairs={{0,1},{1,0},{2,3},{3,2},{4,5},{5,4},{6,7},{7,6},{8,9},{9,8},{10,11... | collective-permute-start | bytes 7372808 | tf_op jit(solution)/shard_map/ppermute | solution.py:445
  379.0 61.9 %collective-permute-start.29 = (bf16[2,200,1600]{2,1,0:T(8,128)(2,1)}, bf16[2,200,1600]{2,1,0:T(8,128)(2,1)S(1)}, u32[]{:S(2)}, u32[]{:S(2)}) collective-permute-start(bf16[2,200,1600]{2,1,0:T(8,128)(2,1)} %get-tuple-element.182), channel_id=1, source_target_pairs={{0,8},{4,12},{8,0},{12,4},{16,24},{20,28},{24,16},{28,20},{1,9},{5... | collective-permute-start | bytes 3840008 | tf_op jit(solution)/shard_map/ppermute | solution.py:449
  390.7 51.2 %collective-permute-start.30 = (bf16[2,200,1600]{2,1,0:T(8,128)(2,1)}, bf16[2,200,1600]{2,1,0:T(8,128)(2,1)}, u32[]{:S(2)}, u32[]{:S(2)}) collective-permute-start(bf16[2,200,1600]{2,1,0:T(8,128)(2,1)} %get-tuple-element.185), channel_id=1, source_target_pairs={{0,4},{4,0},{8,12},{12,8},{16,20},{20,16},{24,28},{28,24},{1,5},{5... | collective-permute-start | bytes 3840008 | tf_op jit(solution)/shard_map/ppermute | solution.py:449
  431.3 34.3 %collective-permute-start.31 = (bf16[1600,768]{1,0:T(8,128)(2,1)}, bf16[1600,768]{1,0:T(8,128)(2,1)}, u32[]{:S(2)}, u32[]{:S(2)}) collective-permute-start(bf16[1600,768]{1,0:T(8,128)(2,1)} %mapped_three.2), channel_id=1, source_target_pairs={{0,1},{1,0},{2,3},{3,2},{4,5},{5,4},{6,7},{7,6},{8,9},{9,8},{10,11... | collective-permute-start | bytes 7372808 | tf_op jit(solution)/shard_map/ppermute | solution.py:445
  431.3 49.3 %collective-permute-start.32 = (bf16[2,2,200,896]{3,2,1,0:T(8,128)(2,1)}, bf16[2,2,200,896]{3,2,1,0:T(8,128)(2,1)}, u32[]{:S(2)}, u32[]{:S(2)}) collective-permute-start(bf16[2,2,200,896]{3,2,1,0:T(8,128)(2,1)} %bitcast.48), channel_id=1, source_target_pairs={{0,4},{4,0},{8,12},{12,8},{16,20},{20,16},{24,28},{28,24},{1,5},{5... | collective-permute-start | bytes 4300808 | tf_op jit(solution)/shard_map/ppermute | solution.py:449
  452.5 51.5 %collective-permute-start.34 = (bf16[2,2,200,896]{3,2,1,0:T(8,128)(2,1)}, bf16[2,2,200,896]{3,2,1,0:T(8,128)(2,1)}, u32[]{:S(2)}, u32[]{:S(2)}) collective-permute-start(bf16[2,2,200,896]{3,2,1,0:T(8,128)(2,1)} %bitcast.50), channel_id=1, source_target_pairs={{0,4},{4,0},{8,12},{12,8},{16,20},{20,16},{24,28},{28,24},{1,5},{5... | collective-permute-start | bytes 4300808 | tf_op jit(solution)/shard_map/ppermute | solution.py:449
  452.5 44.2 %collective-permute-start.33 = (bf16[200,1600]{1,0:T(8,128)(2,1)}, bf16[200,1600]{1,0:T(8,128)(2,1)}, u32[]{:S(2)}, u32[]{:S(2)}) collective-permute-start(bf16[200,1600]{1,0:T(8,128)(2,1)} %bitcast.49), channel_id=1, source_target_pairs={{0,16},{4,20},{8,24},{12,28},{16,0},{20,4},{24,8},{28,12},{1,17},{... | collective-permute-start | bytes 1920008 | tf_op jit(solution)/shard_map/ppermute | solution.py:449
  452.6 58.4 %collective-permute-start.35 = (bf16[200,1600]{1,0:T(8,128)(2,1)}, bf16[200,1600]{1,0:T(8,128)(2,1)}, u32[]{:S(2)}, u32[]{:S(2)}) collective-permute-start(bf16[200,1600]{1,0:T(8,128)(2,1)} %bitcast.51), channel_id=1, source_target_pairs={{0,16},{4,20},{8,24},{12,28},{16,0},{20,4},{24,8},{28,12},{1,17},{... | collective-permute-start | bytes 1920008 | tf_op jit(solution)/shard_map/ppermute | solution.py:449
  478.9 78.2 %collective-permute-start.40 = (bf16[800,768]{1,0:T(8,128)(2,1)}, bf16[800,768]{1,0:T(8,128)(2,1)S(1)}, u32[]{:S(2)}, u32[]{:S(2)}) collective-permute-start(bf16[800,768]{1,0:T(8,128)(2,1)} %half_rows.2), channel_id=1, source_target_pairs={{0,2},{2,0},{1,3},{3,1},{4,6},{6,4},{5,7},{7,5},{8,10},{10,8},{9,1... | collective-permute-start | bytes 3686408 | tf_op jit(solution)/shard_map/ppermute | solution.py:441
  482.2 44.0 %collective-permute-start.36 = (bf16[2,200,896]{2,1,0:T(8,128)(2,1)S(1)}, bf16[2,200,896]{2,1,0:T(8,128)(2,1)S(1)}, u32[]{:S(2)}, u32[]{:S(2)}) collective-permute-start(bf16[2,200,896]{2,1,0:T(8,128)(2,1)S(1)} %get-tuple-element.203), channel_id=1, source_target_pairs={{0,8},{4,12},{8,0},{12,4},{16,24},{20,28},{24,16},{28,20},{1,9},{5... | collective-permute-start | bytes 2150408 | tf_op jit(solution)/shard_map/ppermute | solution.py:449
  506.2 43.1 %collective-permute-start.38 = (bf16[2,200,896]{2,1,0:T(8,128)(2,1)}, bf16[2,200,896]{2,1,0:T(8,128)(2,1)}, u32[]{:S(2)}, u32[]{:S(2)}) collective-permute-start(bf16[2,200,896]{2,1,0:T(8,128)(2,1)} %get-tuple-element.207), channel_id=1, source_target_pairs={{0,8},{4,12},{8,0},{12,4},{16,24},{20,28},{24,16},{28,20},{1,9},{5... | collective-permute-start | bytes 2150408 | tf_op jit(solution)/shard_map/ppermute | solution.py:449
  506.2 21.9 %collective-permute-start.37 = (bf16[200,1600]{1,0:T(8,128)(2,1)S(1)}, bf16[200,1600]{1,0:T(8,128)(2,1)}, u32[]{:S(2)}, u32[]{:S(2)}) collective-permute-start(bf16[200,1600]{1,0:T(8,128)(2,1)S(1)} %added.4.a_ref), channel_id=1, source_target_pairs={{2,4},{4,2},{10,12},{12,10},{18,20},{20,18},{26,28},{28,26},{3,5},... | collective-permute-start | bytes 1920008 | tf_op jit(solution)/shard_map/ppermute | solution.py:1100
  513.0 56.4 %collective-permute-start.41 = (bf16[200,1600]{1,0:T(8,128)(2,1)}, bf16[200,1600]{1,0:T(8,128)(2,1)}, u32[]{:S(2)}, u32[]{:S(2)}) collective-permute-start(bf16[200,1600]{1,0:T(8,128)(2,1)} %added.5.a_ref), channel_id=1, source_target_pairs={{2,4},{4,2},{10,12},{12,10},{18,20},{20,18},{26,28},{28,26},{3,5},... | collective-permute-start | bytes 1920008 | tf_op jit(solution)/shard_map/ppermute | solution.py:1100
  527.8 27.2 %collective-permute-start.39 = (bf16[200,896]{1,0:T(8,128)(2,1)}, bf16[200,896]{1,0:T(8,128)(2,1)}, u32[]{:S(2)}, u32[]{:S(2)}) collective-permute-start(bf16[200,896]{1,0:T(8,128)(2,1)} %bitcast.54), channel_id=1, source_target_pairs={{0,16},{4,20},{8,24},{12,28},{16,0},{20,4},{24,8},{28,12},{1,17},{... | collective-permute-start | bytes 1075208 | tf_op jit(solution)/shard_map/ppermute | solution.py:449
  551.9 46.8 %collective-permute-start.42 = (bf16[200,896]{1,0:T(8,128)(2,1)}, bf16[200,896]{1,0:T(8,128)(2,1)}, u32[]{:S(2)}, u32[]{:S(2)}) collective-permute-start(bf16[200,896]{1,0:T(8,128)(2,1)} %bitcast.55), channel_id=1, source_target_pairs={{0,16},{4,20},{8,24},{12,28},{16,0},{20,4},{24,8},{28,12},{1,17},{... | collective-permute-start | bytes 1075208 | tf_op jit(solution)/shard_map/ppermute | solution.py:449
  551.9 77.4 %collective-permute-start.47 = (bf16[200,1600]{1,0:T(8,128)(2,1)}, bf16[200,1600]{1,0:T(8,128)(2,1)S(1)}, u32[]{:S(2)}, u32[]{:S(2)}) collective-permute-start(bf16[200,1600]{1,0:T(8,128)(2,1)} %chosen.4.a_ref), channel_id=1, source_target_pairs={{0,16},{4,20},{8,24},{12,28},{16,0},{20,4},{24,8},{28,12},{1,17},{... | collective-permute-start | bytes 1920008 | tf_op jit(solution)/shard_map/ppermute | solution.py:449
  570.9 61.4 %collective-permute-start.49 = (bf16[200,1600]{1,0:T(8,128)(2,1)S(1)}, bf16[200,1600]{1,0:T(8,128)(2,1)S(1)}, u32[]{:S(2)}, u32[]{:S(2)}) collective-permute-start(bf16[200,1600]{1,0:T(8,128)(2,1)S(1)} %chosen.5.a_ref), channel_id=1, source_target_pairs={{0,16},{4,20},{8,24},{12,28},{16,0},{20,4},{24,8},{28,12},{1,17},{... | collective-permute-start | bytes 1920008 | tf_op jit(solution)/shard_map/ppermute | solution.py:449
  599.8 26.6 %collective-permute-start.45 = (bf16[200,896]{1,0:T(8,128)(2,1)S(1)}, bf16[200,896]{1,0:T(8,128)(2,1)S(1)}, u32[]{:S(2)}, u32[]{:S(2)}) collective-permute-start(bf16[200,896]{1,0:T(8,128)(2,1)S(1)} %added.7.a_ref), channel_id=1, source_target_pairs={{2,4},{4,2},{10,12},{12,10},{18,20},{20,18},{26,28},{28,26},{3,5},... | collective-permute-start | bytes 1075208 | tf_op jit(solution)/shard_map/ppermute | solution.py:1100
  600.5 31.6 %collective-permute-start.48 = (bf16[200,896]{1,0:T(8,128)(2,1)S(1)}, bf16[200,896]{1,0:T(8,128)(2,1)S(1)}, u32[]{:S(2)}, u32[]{:S(2)}) collective-permute-start(bf16[200,896]{1,0:T(8,128)(2,1)S(1)} %added.6.a_ref), channel_id=1, source_target_pairs={{2,4},{4,2},{10,12},{12,10},{18,20},{20,18},{26,28},{28,26},{3,5},... | collective-permute-start | bytes 1075208 | tf_op jit(solution)/shard_map/ppermute | solution.py:1100
  601.8 19.2 %collective-permute-start.44 = (f32[8,768]{1,0:T(8,128)S(1)}, f32[8,768]{1,0:T(8,128)S(1)}, u32[]{:S(2)}, u32[]{:S(2)}) collective-permute-start(f32[8,768]{1,0:T(8,128)S(1)} %get-tuple-element.215.a_ref), channel_id=1, source_target_pairs={{0,2},{2,0},{1,3},{3,1},{4,6},{6,4},{5,7},{7,5},{8,10},{10,8},{9,1... | collective-permute-start | bytes 73736 | tf_op jit(solution)/shard_map/ppermute | solution.py:441
  621.0 8.3 %collective-permute-start.46 = (f32[16,1600]{1,0:T(8,128)S(1)}, f32[16,1600]{1,0:T(8,128)S(1)}, u32[]{:S(2)}, u32[]{:S(2)}) collective-permute-start(f32[16,1600]{1,0:T(8,128)S(1)} %sums_added.4.a_ref), channel_id=1, source_target_pairs={{0,8},{4,12},{8,0},{12,4},{16,24},{20,28},{24,16},{28,20},{1,9},{5... | collective-permute-start | bytes 307208 | tf_op jit(solution)/shard_map/ppermute | solution.py:449
  630.6 47.3 %collective-permute-start.53 = (bf16[2,200,1600]{2,1,0:T(8,128)(2,1)S(1)}, bf16[2,200,1600]{2,1,0:T(8,128)(2,1)S(1)}, u32[]{:S(2)}, u32[]{:S(2)}) collective-permute-start(bf16[2,200,1600]{2,1,0:T(8,128)(2,1)S(1)} %paired.10.a_ref), channel_id=1, source_target_pairs={{0,4},{4,0},{8,12},{12,8},{16,20},{20,16},{24,28},{28,24},{1,5},{5... | collective-permute-start | bytes 3840008 | tf_op jit(solution)/shard_map/ppermute | solution.py:449
  632.4 69.5 %collective-permute-start.58 = (bf16[2,200,1600]{2,1,0:T(8,128)(2,1)S(1)}, bf16[2,200,1600]{2,1,0:T(8,128)(2,1)S(1)}, u32[]{:S(2)}, u32[]{:S(2)}) collective-permute-start(bf16[2,200,1600]{2,1,0:T(8,128)(2,1)S(1)} %paired.11.a_ref), channel_id=1, source_target_pairs={{0,8},{4,12},{8,0},{12,4},{16,24},{20,28},{24,16},{28,20},{1,9},{5... | collective-permute-start | bytes 3840008 | tf_op jit(solution)/shard_map/ppermute | solution.py:449
  632.5 31.6 %collective-permute-start.50 = (f32[16,1600]{1,0:T(8,128)S(1)}, f32[16,1600]{1,0:T(8,128)S(1)}, u32[]{:S(2)}, u32[]{:S(2)}) collective-permute-start(f32[16,1600]{1,0:T(8,128)S(1)} %sums_added.5.a_ref), channel_id=1, source_target_pairs={{0,4},{4,0},{8,12},{12,8},{16,20},{20,16},{24,28},{28,24},{1,5},{5... | collective-permute-start | bytes 307208 | tf_op jit(solution)/shard_map/ppermute | solution.py:449
  633.1 36.7 %collective-permute-start.51 = (bf16[200,896]{1,0:T(8,128)(2,1)S(1)}, bf16[200,896]{1,0:T(8,128)(2,1)S(1)}, u32[]{:S(2)}, u32[]{:S(2)}) collective-permute-start(bf16[200,896]{1,0:T(8,128)(2,1)S(1)} %chosen.7.a_ref), channel_id=1, source_target_pairs={{0,16},{4,20},{8,24},{12,28},{16,0},{20,4},{24,8},{28,12},{1,17},{... | collective-permute-start | bytes 1075208 | tf_op jit(solution)/shard_map/ppermute | solution.py:449
  633.8 42.6 %collective-permute-start.52 = (bf16[200,896]{1,0:T(8,128)(2,1)S(1)}, bf16[200,896]{1,0:T(8,128)(2,1)S(1)}, u32[]{:S(2)}, u32[]{:S(2)}) collective-permute-start(bf16[200,896]{1,0:T(8,128)(2,1)S(1)} %chosen.6.a_ref), channel_id=1, source_target_pairs={{0,16},{4,20},{8,24},{12,28},{16,0},{20,4},{24,8},{28,12},{1,17},{... | collective-permute-start | bytes 1075208 | tf_op jit(solution)/shard_map/ppermute | solution.py:449
  664.1 43.5 %collective-permute-start.59 = (bf16[1600,768]{1,0:T(8,128)(2,1)}, bf16[1600,768]{1,0:T(8,128)(2,1)}, u32[]{:S(2)}, u32[]{:S(2)}) collective-permute-start(bf16[1600,768]{1,0:T(8,128)(2,1)} %mapped.10), channel_id=1, source_target_pairs={{0,1},{1,0},{2,3},{3,2},{4,5},{5,4},{6,7},{7,6},{8,9},{9,8},{10,11... | collective-permute-start | bytes 7372808 | tf_op jit(solution)/shard_map/ppermute | solution.py:445
  669.8 16.3 %collective-permute-start.54 = (bf16[2,200,896]{2,1,0:T(8,128)(2,1)S(1)}, bf16[2,200,896]{2,1,0:T(8,128)(2,1)S(1)}, u32[]{:S(2)}, u32[]{:S(2)}) collective-permute-start(bf16[2,200,896]{2,1,0:T(8,128)(2,1)S(1)} %paired.12.a_ref), channel_id=1, source_target_pairs={{0,4},{4,0},{8,12},{12,8},{16,20},{20,16},{24,28},{28,24},{1,5},{5... | collective-permute-start | bytes 2150408 | tf_op jit(solution)/shard_map/ppermute | solution.py:449
  676.6 21.3 %collective-permute-start.55 = (bf16[2,200,896]{2,1,0:T(8,128)(2,1)S(1)}, bf16[2,200,896]{2,1,0:T(8,128)(2,1)S(1)}, u32[]{:S(2)}, u32[]{:S(2)}) collective-permute-start(bf16[2,200,896]{2,1,0:T(8,128)(2,1)S(1)} %paired.13.a_ref), channel_id=1, source_target_pairs={{0,8},{4,12},{8,0},{12,4},{16,24},{20,28},{24,16},{28,20},{1,9},{5... | collective-permute-start | bytes 2150408 | tf_op jit(solution)/shard_map/ppermute | solution.py:449
  677.9 22.2 %collective-permute-start.56 = (f32[16,1600]{1,0:T(8,128)S(1)}, f32[16,1600]{1,0:T(8,128)S(1)}, u32[]{:S(2)}, u32[]{:S(2)}) collective-permute-start(f32[16,1600]{1,0:T(8,128)S(1)} %sums_added.6.a_ref), channel_id=1, source_target_pairs={{0,16},{4,20},{8,24},{12,28},{16,0},{20,4},{24,8},{28,12},{1,17},{... | collective-permute-start | bytes 307208 | tf_op jit(solution)/shard_map/ppermute | solution.py:449
  687.7 41.0 %collective-permute-start.60 = (bf16[2,2,200,896]{3,2,1,0:T(8,128)(2,1)}, bf16[2,2,200,896]{3,2,1,0:T(8,128)(2,1)}, u32[]{:S(2)}, u32[]{:S(2)}) collective-permute-start(bf16[2,2,200,896]{3,2,1,0:T(8,128)(2,1)} %paired.15.a_ref.c_ref), channel_id=1, source_target_pairs={{0,8},{4,12},{8,0},{12,4},{16,24},{20,28},{24,16},{28,20},{1,9},{5... | collective-permute-start | bytes 4300808 | tf_op jit(solution)/shard_map/ppermute | solution.py:449
  699.6 34.7 %collective-permute-start.61 = (bf16[2,2,200,896]{3,2,1,0:T(8,128)(2,1)}, bf16[2,2,200,896]{3,2,1,0:T(8,128)(2,1)}, u32[]{:S(2)}, u32[]{:S(2)}) collective-permute-start(bf16[2,2,200,896]{3,2,1,0:T(8,128)(2,1)} %paired.16.a_ref.c_ref), channel_id=1, source_target_pairs={{0,4},{4,0},{8,12},{12,8},{16,20},{20,16},{24,28},{28,24},{1,5},{5... | collective-permute-start | bytes 4300808 | tf_op jit(solution)/shard_map/ppermute | solution.py:449
  700.1 5.0 collective-permute-start.57
  701.9 82.3 %collective-permute-start.66 = (bf16[2,2,200,1600]{3,2,1,0:T(8,128)(2,1)S(1)}, bf16[2,2,200,1600]{3,2,1,0:T(8,128)(2,1)}, u32[]{:S(2)}, u32[]{:S(2)}) collective-permute-start(bf16[2,2,200,1600]{3,2,1,0:T(8,128)(2,1)S(1)} %paired.14.a_ref.c_ref), channel_id=1, source_target_pairs={{0,8},{4,12},{8,0},{12,4},{16,24},{20,28},{24,16},{28,20},{1,9},{5... | collective-permute-start | bytes 7680008 | tf_op jit(solution)/shard_map/ppermute | solution.py:449
  705.2 85.7 %collective-permute-start.67 = (bf16[2,2,200,1600]{3,2,1,0:T(8,128)(2,1)}, bf16[2,2,200,1600]{3,2,1,0:T(8,128)(2,1)}, u32[]{:S(2)}, u32[]{:S(2)}) collective-permute-start(bf16[2,2,200,1600]{3,2,1,0:T(8,128)(2,1)} %paired.17.a_ref.c_ref), channel_id=1, source_target_pairs={{0,4},{4,0},{8,12},{12,8},{16,20},{20,16},{24,28},{28,24},{1,5},{5... | collective-permute-start | bytes 7680008 | tf_op jit(solution)/shard_map/ppermute | solution.py:449
  738.7 29.4 %collective-permute-start.64 = (bf16[800,768]{1,0:T(8,128)(2,1)}, bf16[800,768]{1,0:T(8,128)(2,1)}, u32[]{:S(2)}, u32[]{:S(2)}) collective-permute-start(bf16[800,768]{1,0:T(8,128)(2,1)} %half_rows.3), channel_id=1, source_target_pairs={{0,2},{2,0},{1,3},{3,1},{4,6},{6,4},{5,7},{7,5},{8,10},{10,8},{9,1... | collective-permute-start | bytes 3686408 | tf_op jit(solution)/shard_map/ppermute | solution.py:441
  741.7 5.8 collective-permute-start.63
  (96 other events, 1030.2 us)

commit v4 on v3

--- a/solution.py
+++ b/solution.py
@@ -204,7 +204,14 @@
     )(info, projected, projected, projected, attended, grad, log_totals, first)
 
 
-def call(body, name, grid, specs, args, out_specs, out_shapes, scalars=None, vmem=KERNEL_VMEM):
+ROW, COL, LOW_Y, LOW_Z, HIGH_Z, QUARTER, PEER, SAME = range(8)
+
+
+class Here:
+    places = None
+
+
+def call(body, name, grid, specs, args, out_specs, out_shapes, vmem=KERNEL_VMEM):
     return pl.pallas_call(
         body,
         grid_spec=pltpu.PrefetchScalarGridSpec(
@@ -214,7 +221,7 @@
         compiler_params=pltpu.CompilerParams(vmem_limit_bytes=vmem),
         cost_estimate=pl.CostEstimate(flops=0, bytes_accessed=0, transcendentals=0),
         name=name,
-    )(jnp.zeros((1,), jnp.int32) if scalars is None else scalars, *args)
+    )(Here.places, *args)
 
 
 f32 = jnp.float32
@@ -260,7 +267,7 @@
     )
 
 
-def hidden(weight, own, other, bias):
+def hidden(weight, own, other, columns):
     depth, width = weight.shape
     count = own.shape[1]
     block = 256
@@ -269,7 +276,7 @@
     def body(_, w_ref, own_ref, other_ref, b_ref, act_ref, slope_ref):
         tokens = jnp.where(pl.program_id(0) < half, own_ref[...], other_ref[...])
         for rows in chunks(width, 256):
-            pre = tn(w_ref[:, rows], tokens) + b_ref[rows, :]
+            pre = tn(w_ref[:, rows], tokens) + b_ref[rows, 5:6]
             square = pre * pre
             bend = jnp.tanh(pre * (gelu_root + (gelu_root * gelu_cubic) * square))
             lift = 0.5 * (1.0 + bend)
@@ -285,9 +292,9 @@
             whole_spec(weight),
             pl.BlockSpec((depth, block), lambda i, _: (0, jnp.minimum(i, half - 1))),
             pl.BlockSpec((depth, block), lambda i, _: (0, jnp.maximum(i - half, 0))),
-            whole_spec(bias),
+            whole_spec(columns),
         ],
-        (weight, own, other, bias),
+        (weight, own, other, columns),
         [tile, tile],
         [shape(width, 2 * count), shape(width, 2 * count, dtype=jnp.float32)],
     )
@@ -323,7 +330,7 @@
         ],
         (weight, own, other, slope),
         [tile, pl.BlockSpec((width, 128), lambda i, _: (0, 0))],
-        [shape(width, 2 * count), shape(width, 128, dtype=jnp.float32)],
+        [shape(width, 2 * count), shape(width, 128, dtype=jnp.float32)], vmem=WIDE_VMEM,
     )
 
 
@@ -406,7 +413,7 @@
     )
 
 
-def weight_grad(sources, order, parts):
+def weight_grad(sources, place_of, blocks, parts):
     rows, count = sources[0][0].shape
     size = rows // parts
     widths = [part[1] for _, _, _, part in sources]
@@ -419,16 +426,15 @@
             o_ref[0, :, at : at + width] = grad.astype(bf16)
             at += width
 
-    tile = pl.BlockSpec((1, size, count), lambda i, s: (s[i], 0, 0))
+    tile = pl.BlockSpec((1, size, count), lambda i, s: (place_of(i, s), 0, 0))
     specs, args = [], []
     for own, other, right, (place, width) in sources:
         specs += [tile, tile, pl.BlockSpec((width, 2 * count), lambda i, s, place=place: (place, 0))]
         args += [own.reshape(parts, size, count), other.reshape(parts, size, count), right]
     return call(
-        body, "weight_grad", order.shape, specs, tuple(args),
+        body, "weight_grad", (blocks,), specs, tuple(args),
         pl.BlockSpec((1, size, sum(widths)), lambda i, s: (i, 0, 0)),
-        shape(order.shape[0], size, sum(widths)),
-        scalars=order,
+        shape(blocks, size, sum(widths)), vmem=WIDE_VMEM,
     )
 
 
@@ -550,40 +556,51 @@
     return value.reshape(value.shape[:-2] + (4, value.shape[-2] // 4, value.shape[-1]))
 
 
-def pack(qkv, tail, fc, proj, c, r, at, most):
-    rows, size, spare, wide = qkv.shape[1] // 4, qkv.shape[2], tail.shape[2], fc.shape[1] // 2
-    scalars = jnp.stack([at, c, r]).astype(jnp.int32)
-
-    def body(s_ref, q_ref, t_ref, f_ref, p_ref, qo_ref, fo_ref, po_ref):
-        put_slots(qo_ref, q_ref, t_ref, s_ref[1], 1 - s_ref[2], most)
-        put_half(fo_ref, f_ref, 1 - s_ref[2])
-        put_half(po_ref, p_ref, 1 - s_ref[2])
+def pack_heads(qkv, tail, most):
+    rows, size, spare = qkv.shape[1] // 4, qkv.shape[2], tail.shape[2]
+
+    def body(s_ref, q_ref, t_ref, o_ref):
+        put_slots(o_ref, q_ref, t_ref, s_ref[COL], s_ref[PEER], most)
+
+    return call(
+        body, "pack_heads", (3,),
+        [
+            pl.BlockSpec((1, 1, rows, size), lambda i, s: (i, s[QUARTER], 0, 0)),
+            pl.BlockSpec((1, 1, rows, spare), lambda i, s: (i, s[QUARTER], 0, 0)),
+        ],
+        (quarters(qkv), quarters(tail)),
+        pl.BlockSpec((1, rows, most), lambda i, s: (i, 0, 0)), shape(3, rows, most),
+        vmem=WIDE_VMEM,
+    )
+
+
+def pack(fc, proj):
+    rows, wide = fc.shape[0] // 4, fc.shape[1] // 2
+
+    def body(s_ref, f_ref, p_ref, fo_ref, po_ref):
+        put_half(fo_ref, f_ref, s_ref[PEER])
+        put_half(po_ref, p_ref, s_ref[PEER])
 
     return call(
         body, "pack", (1,),
-        [
-            pl.BlockSpec((3, 1, rows, size), lambda i, s: (0, s[0], 0, 0)),
-            pl.BlockSpec((3, 1, rows, spare), lambda i, s: (0, s[0], 0, 0)),
-            pl.BlockSpec((1, rows, 2 * wide), lambda i, s: (s[0], 0, 0)),
-            pl.BlockSpec((1, rows, 2 * wide), lambda i, s: (s[0], 0, 0)),
-        ],
-        tuple(quarters(v) for v in (qkv, tail, fc, proj)),
-        [pl.BlockSpec((3, rows, most), lambda i, s: (0, 0, 0))] + [pl.BlockSpec((rows, wide), lambda i, s: (0, 0))] * 2,
-        [shape(3, rows, most), shape(rows, wide), shape(rows, wide)],
-        scalars=scalars, vmem=WIDE_VMEM,
-    )
-
-
-def own_rows(mine, tail, c, r, width):
+        [pl.BlockSpec((1, rows, 2 * wide), lambda i, s: (s[QUARTER], 0, 0))] * 2,
+        (quarters(fc), quarters(proj)),
+        [pl.BlockSpec((rows, wide), lambda i, s: (0, 0))] * 2,
+        [shape(rows, wide)] * 2,
+        vmem=WIDE_VMEM,
+    )
+
+
+def own_rows(mine, tail, width):
     three = mine.ndim == 3
     rows, size = mine.shape[-2] // 4, mine.shape[-1]
 
     def body(s_ref, m_ref, *refs):
         t_ref, o_ref = refs if three else (None,) + refs
         if three:
-            put_slots(o_ref.at[:, 0], m_ref, t_ref, s_ref[1], s_ref[0], width)
+            put_slots(o_ref.at[:, 0], m_ref, t_ref, s_ref[COL], s_ref[ROW], width)
         else:
-            put_half(o_ref.at[0], m_ref, s_ref[0])
+            put_half(o_ref.at[0], m_ref, s_ref[ROW])
 
     lead, zero = ((3,), (0,)) if three else ((), ())
     block = lambda width, at: pl.BlockSpec(lead + (1, rows, width), lambda i, s: zero + (at(i, s), 0, 0))
@@ -592,18 +609,18 @@
         body, "own_rows", (4,),
         [block(size, own)] + ([block(tail.shape[-1], own)] if three else []),
         tuple([quarters(mine)] + ([quarters(tail)] if three else [])),
-        block(width, lambda i, s: 4 * s[0] + i), shape(*lead, 8, rows, width),
-        scalars=jnp.stack([r, c]).astype(jnp.int32), vmem=WIDE_VMEM,
-    )
-
-
-def all_rows(held, got, r, y, z):
+        block(width, lambda i, s: 4 * s[ROW] + i), shape(*lead, 8, rows, width),
+        vmem=WIDE_VMEM,
+    )
+
+
+def all_rows(held, got):
     lead, tile = held.shape[:-3], held.shape[-2:]
     zero = (0,) * len(lead)
 
     def body(s_ref, h_ref, *refs):
         o_ref = refs[-1]
-        place = (pl.program_id(0) // 2 != s_ref[2]) * 2 + (pl.program_id(0) % 2 != s_ref[1])
+        place = (pl.program_id(0) // 2 != s_ref[LOW_Z]) * 2 + (pl.program_id(0) % 2 != s_ref[LOW_Y])
         for i in range(4):
 
             @pl.when(place == i)
@@ -617,14 +634,14 @@
             num_scalar_prefetch=1,
             grid=(4,),
             in_specs=[pl.BlockSpec(memory_space=pl.ANY)] + [fetched] * 4,
-            out_specs=pl.BlockSpec(lead + (1,) + tile, lambda i, s: zero + (4 * (1 - s[0]) + i, 0, 0)),
+            out_specs=pl.BlockSpec(lead + (1,) + tile, lambda i, s: zero + (4 * s[PEER] + i, 0, 0)),
         ),
         out_shape=shape(*held.shape),
         input_output_aliases={1: 0},
-        compiler_params=pltpu.CompilerParams(vmem_limit_bytes=KERNEL_VMEM),
+        compiler_params=pltpu.CompilerParams(vmem_limit_bytes=WIDE_VMEM),
         cost_estimate=pl.CostEstimate(flops=0, bytes_accessed=0, transcendentals=0),
         name="all_rows",
-    )(jnp.stack([r, y, z]).astype(jnp.int32), held, *got)
+    )(Here.places, held, *got)
     return out.reshape(lead + (8 * tile[0], tile[1]))
 
 
@@ -636,8 +653,8 @@
 
     return call(
         body, "half_rows", (count // 256,),
-        [pl.BlockSpec((rows, 256), lambda i, s: (s[0], i))], (value,),
-        pl.BlockSpec((rows, 256), lambda i, s: (0, i)), shape(rows, count), scalars=at[None].astype(jnp.int32),
+        [pl.BlockSpec((rows, 256), lambda i, s: (s[at], i))], (value,),
+        pl.BlockSpec((rows, 256), lambda i, s: (0, i)), shape(rows, count),
     )
 
 
@@ -696,13 +713,13 @@
         send_ref[...] = (c_ref[...].astype(f32) + d_ref[...].astype(f32)).astype(bf16).reshape(send_ref.shape)
 
     ones = (1,) * len(lead)
-    mine = pl.BlockSpec(ones + tile, lambda i, s: spread_index(rest, axis, i, s[0]))
-    theirs = pl.BlockSpec(ones + tile, lambda i, s: spread_index(rest, axis, i, 1 - s[0]))
+    mine = pl.BlockSpec(ones + tile, lambda i, s: spread_index(rest, axis, i, s[at]))
+    theirs = pl.BlockSpec(ones + tile, lambda i, s: spread_index(rest, axis, i, 1 - s[at]))
     steps = math.prod(rest)
     out = pl.BlockSpec((1,) + tile, lambda i, s: (i, 0, 0))
     first, second = call(
         body, "halved", (steps,), [mine, mine, theirs, theirs], (keep, got, keep, got),
-        [out, out], [shape(steps, *tile)] * 2, scalars=at[None].astype(jnp.int32),
+        [out, out], [shape(steps, *tile)] * 2,
     )
     return first.reshape(rest + tile), second.reshape(rest + tile)
 
@@ -715,12 +732,12 @@
     return call(body, "added", (1,), [spec, spec], (a, b), spec, shape(*a.shape))
 
 
-def chosen(flag, a, b):
+def chosen(a, b):
     def body(s_ref, a_ref, b_ref, o_ref):
-        o_ref[...] = jnp.where(s_ref[0] == 1, a_ref[...], b_ref[...])
+        o_ref[...] = jnp.where(s_ref[SAME] == 1, a_ref[...], b_ref[...])
 
     spec = whole_spec(a)
-    return call(body, "chosen", (1,), [spec, spec], (a, b), spec, shape(*a.shape), scalars=flag[None].astype(jnp.int32))
+    return call(body, "chosen", (1,), [spec, spec], (a, b), spec, shape(*a.shape))
 
 
 def paired(at, first, second, axis):
@@ -740,7 +757,7 @@
     def place(step):
         return spread_index(lead, len(lead), step, 0)[: len(lead)] + (0, 0)
 
-    out = lambda i, j, s: spread_index(lead, axis, j, jnp.where(i == 0, s[0], 1 - s[0]))
+    out = lambda i, j, s: spread_index(lead, axis, j, jnp.where(i == 0, s[at], 1 - s[at]))
     return call(
         body, "paired", (2, steps),
         [
@@ -750,7 +767,6 @@
         (first, second),
         pl.BlockSpec(ones + (1,) + tile, out),
         shape(*lead[:axis], 2, *lead[axis:], *tile),
-        scalars=at[None].astype(jnp.int32),
     )
 
 
@@ -759,11 +775,11 @@
 
     def body(s_ref, a_ref, b_ref, c_ref, d_ref, o_ref):
         if y_last:
-            swap = s_ref[0] == 1
+            swap = s_ref[at] == 1
             o_ref[:, :width] = jnp.where(swap, b_ref[0, 0], a_ref[0, 0]).astype(f32)
             o_ref[:, width:] = jnp.where(swap, a_ref[0, 0], b_ref[0, 0]).astype(f32)
         else:
-            other = pl.program_id(0) % 2 != s_ref[0]
+            other = pl.program_id(0) % 2 != s_ref[at]
             o_ref[:, :width] = jnp.where(other, b_ref[0, 0], a_ref[0, 0]).astype(f32)
             o_ref[:, width:] = jnp.where(other, d_ref[0, 0], c_ref[0, 0]).astype(f32)
 
@@ -777,7 +793,7 @@
     return call(
         body, "widened", (4,), specs, (keep, got, keep, got),
         pl.BlockSpec((rows, 2 * width), lambda i, s: (i, 0)),
-        shape(4 * rows, 2 * width, dtype=f32), scalars=at[None].astype(jnp.int32),
+        shape(4 * rows, 2 * width, dtype=f32),
     )
 
 
@@ -786,7 +802,7 @@
     count = width // most
 
     def body(s_ref, a_ref, b_ref, o_ref):
-        second = jnp.where((s_ref[0] == 1) if y_last else (pl.program_id(0) % 2 == s_ref[0]), a_ref[0, 0], b_ref[0, 0])
+        second = jnp.where((s_ref[at] == 1) if y_last else (pl.program_id(0) % 2 == s_ref[at]), a_ref[0, 0], b_ref[0, 0])
         for i in range(count):
             o_ref[i, 0] = second[:, i * most + low : i * most + high]
 
@@ -795,32 +811,32 @@
     return call(
         body, "tails_of", (4,), [pl.BlockSpec(tile, where)] * 2, (keep, got),
         pl.BlockSpec((count, 1, rows, high - low), lambda i, s: (0, i, 0, 0)),
-        shape(count, 4, rows, high - low), scalars=at[None].astype(jnp.int32),
-    )
-
-
-def unslotted(keep, got, tails, at, y_last, c, most, size):
+        shape(count, 4, rows, high - low),
+    )
+
+
+def unslotted(keep, got, tails, at, y_last, most, size):
     rows, width = keep.shape[-2:]
     count, spare, less = width // most, tails.shape[-1], most - HEAD_DIM
 
     def body(s_ref, a_ref, b_ref, c_ref, d_ref, t_ref, o_ref):
         if y_last:
-            swap = s_ref[0] == 1
+            swap = s_ref[at] == 1
             first = jnp.where(swap, b_ref[0, 0], a_ref[0, 0])
             second = jnp.where(swap, a_ref[0, 0], b_ref[0, 0])
         else:
-            other = pl.program_id(0) % 2 != s_ref[0]
+            other = pl.program_id(0) % 2 != s_ref[at]
             first = jnp.where(other, b_ref[0, 0], a_ref[0, 0])
             second = jnp.where(other, d_ref[0, 0], c_ref[0, 0])
         first, second = first.astype(f32), second.astype(f32)
 
-        @pl.when(s_ref[1] == 0)
+        @pl.when(s_ref[COL] == 0)
         def _():
             for i in range(count):
                 o_ref[i, :, :most] = first[:, i * most : (i + 1) * most]
                 o_ref[i, :, most:] = second[:, i * most : i * most + size - most]
 
-        @pl.when(s_ref[1] == 1)
+        @pl.when(s_ref[COL] == 1)
         def _():
             for i in range(count):
                 o_ref[i, :, :spare] = t_ref[i, 0].astype(f32)
@@ -839,25 +855,7 @@
         specs + [pl.BlockSpec((count, 1, rows, spare), lambda i, s: (0, i, 0, 0))],
         (keep, got, keep, got, tails),
         pl.BlockSpec((count, rows, size), lambda i, s: (0, i, 0)),
-        shape(count, 4 * rows, size, dtype=f32), scalars=jnp.stack([at, c]).astype(jnp.int32),
-    )
-
-
-def side_by_side(own, got, r):
-    rows, width = own.shape
-    size = rows // 4
-
-    def body(s_ref, a_ref, b_ref, o_ref):
-        swap = s_ref[0] == 1
-        o_ref[:, :width] = jnp.where(swap, b_ref[...], a_ref[...]).astype(f32)
-        o_ref[:, width:] = jnp.where(swap, a_ref[...], b_ref[...]).astype(f32)
-
-    return call(
-        body, "side_by_side", (4,),
-        [pl.BlockSpec((size, width), lambda i, s: (i, 0))] * 2,
-        (own, got),
-        pl.BlockSpec((size, 2 * width), lambda i, s: (i, 0)),
-        shape(rows, 2 * width, dtype=f32), scalars=r[None].astype(jnp.int32),
+        shape(count, 4 * rows, size, dtype=f32),
     )
 
 
@@ -877,38 +875,37 @@
     return center, lax.rsqrt(spread + 1e-05)
 
 
-def norm_one(x_own, x_peer, gain, bias, r):
+def norm_one(x_own, x_peer, columns):
     half, count = x_own.shape
 
-    def body(s_ref, own_ref, peer_ref, g_ref, b_ref, h_ref, stat_ref):
+    def body(s_ref, own_ref, peer_ref, c_ref, h_ref, stat_ref):
         own, peer = own_ref[...].astype(f32), peer_ref[...].astype(f32)
-        parts = [jnp.where(s_ref[0] == 0, own, peer), jnp.where(s_ref[0] == 0, peer, own)]
+        parts = [jnp.where(s_ref[ROW] == 0, own, peer), jnp.where(s_ref[ROW] == 0, peer, own)]
         center, inverse = norm_stats(parts)
         stat_ref[0:1, :] = center
         stat_ref[1:2, :] = inverse
         for i, part in enumerate(parts):
             rows = slice(i * half, (i + 1) * half)
-            h_ref[rows, :] = ((part - center) * inverse * g_ref[rows, :] + b_ref[rows, :]).astype(bf16)
+            h_ref[rows, :] = ((part - center) * inverse * c_ref[rows, 0:1] + c_ref[rows, 1:2]).astype(bf16)
 
     return call(
         body, "norm_one", (count // TOKENS,),
-        [tile_of(half), tile_of(half), whole_spec(gain), whole_spec(bias)],
-        (x_own, x_peer, gain, bias),
+        [tile_of(half), tile_of(half), whole_spec(columns)],
+        (x_own, x_peer, columns),
         [tile_of(2 * half), tile_of(8)],
         [shape(2 * half, count), shape(8, count, dtype=f32)],
-        scalars=r[None].astype(jnp.int32),
-    )
-
-
-def norm_two(x_own, x_peer, low, other, out_bias, gain, bias, r):
+    )
+
+
+def norm_two(x_own, x_peer, low, other, columns):
     half, count = x_own.shape
 
-    def body(s_ref, own_ref, peer_ref, low_ref, other_ref, ob_ref, g_ref, b_ref, x_ref, h_ref, stat_ref):
+    def body(s_ref, own_ref, peer_ref, low_ref, other_ref, c_ref, x_ref, h_ref, stat_ref):
         own, peer = own_ref[...].astype(f32), peer_ref[...].astype(f32)
-        parts = [jnp.where(s_ref[0] == 0, own, peer), jnp.where(s_ref[0] == 0, peer, own)]
+        parts = [jnp.where(s_ref[ROW] == 0, own, peer), jnp.where(s_ref[ROW] == 0, peer, own)]
         for i in range(2):
             rows = slice(i * half, (i + 1) * half)
-            branch = low_ref[rows, :].astype(f32) + other_ref[rows, :].astype(f32) + ob_ref[rows, :]
+            branch = low_ref[rows, :].astype(f32) + other_ref[rows, :].astype(f32) + c_ref[rows, 2:3]
             parts[i] = parts[i] + branch
             x_ref[rows, :] = parts[i]
         center, inverse = norm_stats(parts)
@@ -916,16 +913,15 @@
         stat_ref[1:2, :] = inverse
         for i, part in enumerate(parts):
             rows = slice(i * half, (i + 1) * half)
-            h_ref[rows, :] = ((part - center) * inverse * g_ref[rows, :] + b_ref[rows, :]).astype(bf16)
+            h_ref[rows, :] = ((part - center) * inverse * c_ref[rows, 3:4] + c_ref[rows, 4:5]).astype(bf16)
 
     full = tile_of(2 * half)
     return call(
         body, "norm_two", (count // TOKENS,),
-        [tile_of(half), tile_of(half), full, full, whole_spec(out_bias), whole_spec(gain), whole_spec(bias)],
-        (x_own, x_peer, low, other, out_bias, gain, bias),
+        [tile_of(half), tile_of(half), full, full, whole_spec(columns)],
+        (x_own, x_peer, low, other, columns),
         [full, full, tile_of(8)],
         [shape(2 * half, count, dtype=f32), shape(2 * half, count), shape(8, count, dtype=f32)],
-        scalars=r[None].astype(jnp.int32),
     )
 
 
@@ -941,7 +937,7 @@
         ref[at] += total
 
 
-def norm_two_back(low, other, grad, x_mid, stats, gain):
+def norm_two_back(low, other, grad, x_mid, stats, columns):
     width, count = low.shape
 
     def body(_, low_ref, other_ref, g_ref, x_ref, stat_ref, gain_ref, mid_ref, branch_ref, sum_ref):
@@ -949,7 +945,7 @@
         incoming = low_ref[...].astype(f32) + other_ref[...].astype(f32)
         inverse = stat_ref[1:2, :]
         normed = (x_ref[...] - stat_ref[0:1, :]) * inverse
-        scaled = incoming * gain_ref[...]
+        scaled = incoming * gain_ref[:, 3:4]
         mean = jnp.sum(scaled, axis=0, keepdims=True) / width
         along = jnp.sum(scaled * normed, axis=0, keepdims=True) / width
         mid = g_ref[...].astype(f32) + inverse * (scaled - mean - normed * along)
@@ -963,21 +959,21 @@
     full = tile_of(width)
     return call(
         body, "norm_two_back", (count // TOKENS,),
-        [full, full, full, full, tile_of(8), whole_spec(gain)],
-        (low, other, grad, x_mid, stats, gain),
+        [full, full, full, full, tile_of(8), whole_spec(columns)],
+        (low, other, grad, x_mid, stats, columns),
         [full, full, pl.BlockSpec((3, width, 128), lambda i, s: (0, 0, 0))],
         [shape(width, count, dtype=f32), shape(width, count), shape(3, width, 128, dtype=f32)],
     )
 
 
-def norm_one_sums(mine, other, x_own, stats, gain, r):
+def norm_one_sums(mine, other, x_own, stats, columns):
     half, count = x_own.shape
 
     def body(_, m_ref, o_ref, x_ref, stat_ref, gain_ref, row_ref, sum_ref):
         first = pl.program_id(0) == 0
         incoming = m_ref[...] + o_ref[...].astype(f32)
         normed = (x_ref[...].astype(f32) - stat_ref[0:1, :]) * stat_ref[1:2, :]
-        scaled = incoming * gain_ref[...]
+        scaled = incoming * gain_ref[:, 0:1]
         row_ref[...] = jnp.zeros_like(row_ref)
         row_ref[0:1, :] = jnp.sum(scaled, axis=0, keepdims=True)
         row_ref[1:2, :] = jnp.sum(scaled * normed, axis=0, keepdims=True)
@@ -986,45 +982,44 @@
 
     return call(
         body, "norm_one_sums", (count // TOKENS,),
-        [tile_of(half, lambda s: s[0]), tile_of(half), tile_of(half), tile_of(8), whole_spec(gain)],
-        (mine, other, x_own, stats, gain),
+        [tile_of(half, lambda s: s[ROW]), tile_of(half), tile_of(half), tile_of(8), pl.BlockSpec((half, columns.shape[1]), lambda i, s: (s[ROW], 0))],
+        (mine, other, x_own, stats, columns),
         [tile_of(8), pl.BlockSpec((2, half, 128), lambda i, s: (0, 0, 0))],
         [shape(8, count, dtype=f32), shape(2, half, 128, dtype=f32)],
-        scalars=r[None].astype(jnp.int32),
-    )
-
-
-def norm_one_back(mine, other, x_own, stats, gain, mid_grad, sums, sums_peer, r):
+    )
+
+
+def norm_one_back(mine, other, x_own, stats, columns, mid_grad, sums, sums_peer):
     half, count = x_own.shape
 
     def body(_, m_ref, o_ref, x_ref, stat_ref, gain_ref, mid_ref, a_ref, b_ref, out_ref):
         inverse = stat_ref[1:2, :]
         normed = (x_ref[...].astype(f32) - stat_ref[0:1, :]) * inverse
-        scaled = (m_ref[...] + o_ref[...].astype(f32)) * gain_ref[...]
+        scaled = (m_ref[...] + o_ref[...].astype(f32)) * gain_ref[:, 0:1]
         means = (a_ref[...] + b_ref[...]) / (2 * half)
         out_ref[...] = mid_ref[...] + inverse * (scaled - means[0:1, :] - normed * means[1:2, :])
 
-    mine_tile = tile_of(half, lambda s: s[0])
+    mine_tile = tile_of(half, lambda s: s[ROW])
     return call(
         body, "norm_one_back", (count // TOKENS,),
-        [mine_tile, tile_of(half), tile_of(half), tile_of(8), whole_spec(gain), mine_tile, tile_of(8), tile_of(8)],
-        (mine, other, x_own, stats, gain, mid_grad, sums, sums_peer),
-        tile_of(half), shape(half, count, dtype=f32), scalars=r[None].astype(jnp.int32),
-    )
-
-
-def block_result(x_mid, part, other, bias, r):
+        [mine_tile, tile_of(half), tile_of(half), tile_of(8), pl.BlockSpec((half, columns.shape[1]), lambda i, s: (s[ROW], 0)), mine_tile, tile_of(8), tile_of(8)],
+        (mine, other, x_own, stats, columns, mid_grad, sums, sums_peer),
+        tile_of(half), shape(half, count, dtype=f32),
+    )
+
+
+def block_result(x_mid, part, other, columns):
     half, count = other.shape
 
     def body(_, x_ref, p_ref, o_ref, b_ref, out_ref):
-        out_ref[...] = (x_ref[...] + (p_ref[...].astype(f32) + o_ref[...].astype(f32)) + b_ref[...]).astype(bf16)
-
-    mine_tile = tile_of(half, lambda s: s[0])
+        out_ref[...] = (x_ref[...] + (p_ref[...].astype(f32) + o_ref[...].astype(f32)) + b_ref[:, 6:7]).astype(bf16)
+
+    mine_tile = tile_of(half, lambda s: s[ROW])
     return call(
         body, "block_result", (count // TOKENS,),
-        [mine_tile, mine_tile, tile_of(half), whole_spec(bias)],
-        (x_mid, part, other, bias),
-        tile_of(half), shape(half, count), scalars=r[None].astype(jnp.int32),
+        [mine_tile, mine_tile, tile_of(half), pl.BlockSpec((half, columns.shape[1]), lambda i, s: (s[ROW], 0))],
+        (x_mid, part, other, columns),
+        tile_of(half), shape(half, count),
     )
 
 
@@ -1036,8 +1031,8 @@
         first = after(self.got[0], *marks)
         self.got = [first, dp_xor(first, 1), dp_xor(first, 2)]
 
-    def rest(self, *marks):
-        self.got.append(dp_xor(after(self.got[2], *marks), 1))
+    def rest(self, first, *marks):
+        self.got.append(dp_xor(after(self.got[first], *marks), 3 - first))
         return self.got
 
 
@@ -1048,19 +1043,18 @@
         self.fast = lax.axis_size("dp") == 8
         tied = lambda marks: [(own, other, after(right, *marks), part) for own, other, right, part in sources]
         if not self.fast:
-            self.grad = weight_grad(tied(marks), jnp.arange(4, dtype=jnp.int32), 4)
+            self.grad = weight_grad(tied(marks), lambda i, s: i, 4, 4)
             return
-        self.y, self.lo, self.hi = k % 2, (k // 2) % 2, k // 4
         if y_first:
-            send, parts, mask = 2 * (1 - self.y) + jnp.arange(2), 4, 1
-            keep = 2 * self.y + jnp.arange(2)
+            send, keep = (lambda i, s: 2 * (1 - s[LOW_Y]) + i), (lambda i, s: 2 * s[LOW_Y] + i)
+            blocks, parts, mask = 2, 4, 1
         else:
-            send, parts, mask = (1 - self.lo) + 2 * jnp.arange(4), 8, 2
-            keep = self.lo + 2 * jnp.arange(4)
+            send, keep = (lambda i, s: 1 - s[LOW_Z] + 2 * i), (lambda i, s: s[LOW_Z] + 2 * i)
+            blocks, parts, mask = 4, 8, 2
         shaped = lambda v: v.reshape(2, 2, self.rows // 8, self.width)
-        sent = weight_grad(tied(marks), send.astype(jnp.int32), parts)
+        sent = weight_grad(tied(marks), send, blocks, parts)
         self.got, self.sent = dp_xor(shaped(sent), mask), [sent]
-        self.kept = lambda *marks: shaped(weight_grad(tied(marks), keep.astype(jnp.int32), parts))
+        self.kept = lambda *marks: shaped(weight_grad(tied(marks), keep, blocks, parts))
 
     def hold(self, *marks):
         if self.fast:
@@ -1075,7 +1069,7 @@
 
     def sum_one(self, *marks):
         if self.fast:
-            axis, at, mask = (1, self.lo, 2) if self.y_first else (0, self.y, 1)
+            axis, at, mask = (1, LOW_Z, 2) if self.y_first else (0, LOW_Y, 1)
             self.keep, send = halved(after(self.keep, *marks), self.got, axis, at)
             self.got = dp_xor(send, mask)
             return [self.keep]
@@ -1083,7 +1077,7 @@
 
     def sum_two(self, *marks):
         if self.fast:
-            self.keep, send = halved(after(self.keep, *marks), self.got, 0, self.hi)
+            self.keep, send = halved(after(self.keep, *marks), self.got, 0, HIGH_Z)
             self.got = dp_xor(send, 4)
             return [self.keep]
         return []
@@ -1103,14 +1097,14 @@
 
     def spread_one(self, *marks):
         if self.fast:
-            self.keep = chosen(self.y == self.r, after(self.keep, *marks), self.got)
+            self.keep = chosen(after(self.keep, *marks), self.got)
             self.got = dp_xor(self.keep, 4)
             return [self.keep]
         return []
 
     def spread_two(self, *marks):
         if self.fast:
-            self.keep = paired(self.hi, after(self.keep, *marks), self.got, 0)
+            self.keep = paired(HIGH_Z, after(self.keep, *marks), self.got, 0)
             self.got = dp_xor(self.keep, 2 if self.y_last else 1)
             return [self.keep]
         return []
@@ -1118,10 +1112,10 @@
     def spread_three(self, *marks):
         if self.fast:
             if self.y_last:
-                self.keep = paired(self.lo, after(self.keep, *marks), self.got, 1)
+                self.keep = paired(LOW_Z, after(self.keep, *marks), self.got, 1)
                 self.got = dp_xor(self.keep, 1)
             else:
-                self.keep = paired(self.y, after(self.keep, *marks), self.got, 0)
+                self.keep = paired(LOW_Y, after(self.keep, *marks), self.got, 0)
                 self.got = dp_xor(self.keep, 2)
             return [self.keep]
         return []
@@ -1130,7 +1124,7 @@
         if not self.fast:
             return list(marks)
         less = most - HEAD_DIM
-        at = self.y if self.y_last else self.lo
+        at = LOW_Y if self.y_last else LOW_Z
         self.keep = after(self.keep, *marks)
         tails = tails_of(self.keep, self.got, at, self.y_last, most, less - spare, less)
         self.tails = col_swap(tails)
@@ -1143,46 +1137,20 @@
             both = self.result()
             cut = lambda i: [v[:, i * most : (i + 1) * most] for v in both]
             return jnp.stack([from_slots(c, *cut(i), 1, spare).astype(f32) for i in range(self.width // most)])
-        at = self.y if self.y_last else self.lo
+        at = LOW_Y if self.y_last else LOW_Z
         keep = after(self.keep, *marks)
-        return unslotted(keep, self.got, self.tails, at, self.y_last, c, most, size)
+        return unslotted(keep, self.got, self.tails, at, self.y_last, most, size)
 
     def wide(self, *marks):
         if self.fast:
-            return widened(after(self.keep, *marks), self.got, self.y if self.y_last else self.lo, self.y_last)
-        return jnp.concatenate(self.result(*marks), axis=1).astype(f32)
-
-    def result(self, *marks):
-        if not self.fast:
-            halves = self.grad.reshape(2, self.rows // 2, self.width)
-            keep, got = pick(halves, self.r, 0), row_swap(pick(halves, 1 - self.r, 0))
-            both = lax.psum(ordered(self.r, keep[None], got[None], 0), "dp")
-            return both[0], both[1]
-        keep, got = after(self.keep, *marks), self.got
-        if self.y_last:
-            keep, got = [v.reshape(self.rows // 2, self.width) for v in (keep, got)]
-            return jnp.where(self.y == 0, keep, got), jnp.where(self.y == 0, got, keep)
-        both = paired(self.lo, keep, got, 2).reshape(2, self.rows // 2, self.width)
+            return widened(after(self.keep, *marks), self.got, LOW_Y if self.y_last else LOW_Z, self.y_last)
+        return jnp.concatenate(self.result(), axis=1).astype(f32)
+
+    def result(self):
+        halves = self.grad.reshape(2, self.rows // 2, self.width)
+        keep, got = pick(halves, self.r, 0), row_swap(pick(halves, 1 - self.r, 0))
+        both = lax.psum(ordered(self.r, keep[None], got[None], 0), "dp")
         return both[0], both[1]
-
-
-class Whole:
-    def __init__(self, source, r):
-        self.source, self.r, self.sums = source, r, {}
-
-    def part(self, mine, *marks):
-        own, other, right, part = self.source
-        first = 2 * (self.r if mine else 1 - self.r)
-        order = (first + jnp.arange(2)).astype(jnp.int32)
-        grad = weight_grad([(own, other, after(right, *marks), part)], order, 4)
-        self.sums[mine] = lax.psum(grad.reshape(-1, grad.shape[-1]), "dp")
-        return [grad]
-
-    def swap(self, *marks):
-        self.got = row_swap(after(self.sums[False], *marks))
-
-    def wide(self, *marks):
-        return side_by_side(after(self.sums[True], *marks), self.got, self.r)
 
 
 def hop(value, mask):
@@ -1220,32 +1188,36 @@
     column = lambda v: v.astype(f32)[:, None]
 
     y, z = k % 2, (k // 2) % 2
+    at = jnp.arange(8)
+    held = (r, c, y, z, (k // 4) % 2, 2 * z + y, 1 - r, (y == r).astype(r.dtype))
+    Here.places = sum(jnp.where(at == i, value, 0) for i, value in enumerate(held)).astype(jnp.int32)
     qkv_tail = col_swap(qkv_weight[:, :, :spare])
     proj_turned = proj_weight.T
-    qkv_sent, fc_sent, proj_sent = pack(qkv_weight, qkv_tail, fc_weight, proj_turned, c, r, 2 * z + y, most)
+    qkv_sent = pack_heads(qkv_weight, qkv_tail, most)
+    fc_sent, proj_sent = pack(after(fc_weight, qkv_sent), proj_turned)
     qkv_fetch = Fetch(qkv_sent)
     x_peer = row_swap(after(x_own, qkv_sent))
-    vectors = jnp.stack([ln1_gain, ln1_bias, out_bias, ln2_gain, ln2_bias])
-    vectors = ordered(r, vectors, row_swap(vectors), 1).astype(f32)
-    gain_one, bias_one, bias_out, gain_two, bias_two = [vectors[i][:, None] for i in range(5)]
-
+    vectors = after(jnp.stack([ln1_gain, ln1_bias, out_bias, ln2_gain, ln2_bias]), qkv_sent)
+    vectors = ordered(r, vectors, row_swap(vectors), 1)
+    both = jnp.stack([half_of(r, fc_bias, 0), jnp.concatenate([proj_bias, proj_bias])])
+    columns = jnp.concatenate([vectors, both, jnp.zeros_like(both[:1])]).astype(f32).T
+    qv_bias = after(qv_bias, qkv_sent)
     bias_first, bias_second = head_slots(c, qv_bias, col_swap(qv_bias[:, :spare]), 1, most)
     bias_mine = jnp.where(r == 0, bias_first, bias_second).astype(f32)
     bias_mine = jnp.stack([bias_mine[0], jnp.zeros_like(bias_mine[0]), bias_mine[1]])[:, :, None]
 
-    out_first, out_second = head_slots(c, after(out_weight, qkv_sent), col_swap(out_weight[:spare]), 0, most)
+    out_weight = after(out_weight, qkv_sent)
+    out_first, out_second = head_slots(c, out_weight, col_swap(out_weight[:spare]), 0, most)
     out_mine = jnp.where(r == 0, out_first, out_second)
     out_sent = jnp.where(r == 0, out_second, out_first)
-    fc_bias_mine = column(half_of(r, fc_bias, 0))
-    gain_half, proj_bias_half = column(ln1_gain), column(proj_bias)
     ff_size = fc_weight.shape[1] // 2
-    qkv_full = own_rows(after(qkv_weight, out_sent), qkv_tail, c, r, most)
+    qkv_full = own_rows(after(qkv_weight, fc_sent, out_sent), qkv_tail, most)
     qkv_fetch.more(qkv_full)
-    fc_full = own_rows(after(fc_weight, qkv_fetch.got[0]), None, c, r, ff_size)
-    qkv_fetch.rest(fc_full)
-    proj_full = own_rows(after(proj_turned, fc_full, *qkv_fetch.got[1:3]), None, c, r, ff_size)
-
-    lengths = seq_lengths[0]
+    fc_full = own_rows(after(fc_weight, qkv_fetch.got[0]), None, ff_size)
+    qkv_fetch.rest(2, fc_full)
+    proj_full = own_rows(after(proj_turned, fc_full, *qkv_fetch.got[1:3]), None, ff_size)
+
+    lengths = after(seq_lengths, qkv_sent)[0]
     group = 2 * tokens
     places = jnp.arange(group, dtype=jnp.int32)
     ends = jnp.cumsum(lengths, dtype=jnp.int32)
@@ -1254,31 +1226,29 @@
     ).reshape(group // BLK, BLK)
     info = jnp.concatenate([(c * (tokens // BLK))[None].astype(jnp.int32), first[:, 0] // BLK])
 
-    columns = [gain_one, bias_one, bias_out, gain_two, bias_two, bias_mine, fc_bias_mine, gain_half, proj_bias_half]
-    h_one, stats_one = norm_one(after(x_own, proj_full, info, *columns), x_peer, gain_one, bias_one, r)
-    h_one_peer = col_swap(h_one)
-    fc_fetch = Fetch(after(fc_sent, h_one))
-    proj_fetch = Fetch(after(proj_sent, h_one))
-    out_got = row_swap(after(out_sent, h_one))
-    grad_got = row_swap(after(grad_own, h_one))
-    qkv_full = all_rows(after(qkv_full, h_one), qkv_fetch.got, r, y, z)
+    h_one, stats_one = norm_one(after(x_own, proj_full, info, bias_mine), x_peer, columns)
+    qkv_full = all_rows(after(qkv_full, h_one), qkv_fetch.got)
+    h_one_peer = col_swap(after(h_one, qkv_full))
+    out_got = row_swap(after(out_sent, qkv_full))
+    fc_fetch = Fetch(after(fc_sent, qkv_full))
+    proj_fetch = Fetch(after(proj_sent, qkv_full))
     projected = project(qkv_full, h_one, h_one_peer, bias_mine)
-    fc_fetch.more(projected)
-    proj_fetch.more(projected)
     out_full = ordered(r, after(out_mine, projected), out_got, 1)
-    mark = [out_full, fc_fetch.got[0], proj_fetch.got[0]]
-    attended, log_totals = attend(info, after(projected, *mark), first, heads)
-    fc_fetch.rest(attended)
-    proj_fetch.rest(attended)
-    other = mapped(out_full, after(attended, *fc_fetch.got[1:3], *proj_fetch.got[1:3]), 1, True)
+    attended, log_totals = attend(info, after(projected, out_full), first, heads)
+    fc_fetch.more(attended)
+    proj_fetch.more(attended)
+    other = mapped(out_full, after(attended, fc_fetch.got[0], proj_fetch.got[0]), 1, True)
     low = mapped(out_full, attended, 0, True, col_swap(other))
     branch_other = row_swap(low)
-    fc_full = all_rows(after(fc_full, low), fc_fetch.got, r, y, z)
-    proj_full = all_rows(after(proj_full, fc_full), proj_fetch.got, r, y, z)
-    x_mid, h_two, stats_two = norm_two(x_own, x_peer, after(low, proj_full), branch_other, bias_out, gain_two, bias_two, r)
+    grad_got = row_swap(after(grad_own, low))
+    fc_fetch.rest(1, low)
+    proj_fetch.rest(2, low)
+    fc_full = all_rows(after(fc_full, low), fc_fetch.got)
+    proj_full = all_rows(after(proj_full, fc_full), proj_fetch.got)
+    x_mid, h_two, stats_two = norm_two(x_own, x_peer, after(low, proj_full), branch_other, columns)
     h_two_peer = col_swap(h_two)
-    activated, slope = hidden(fc_full, h_two, h_two_peer, fc_bias_mine)
-    grad_full = paired(r, after(grad_own, activated), grad_got, 0).reshape(2 * half, tokens)
+    activated, slope = hidden(fc_full, h_two, h_two_peer, columns)
+    grad_full = paired(ROW, after(grad_own, activated), grad_got, 0).reshape(2 * half, tokens)
     grad_peer = col_swap(grad_full)
 
     mark = [grad_peer]
@@ -1286,84 +1256,84 @@
     mark = [pre_grad]
     h_two_other = mapped(fc_full, after(pre_grad, *mark), 1, False)
     mark = [h_two_other]
+    fc_total = Total([(h_two, h_two_peer, pre_grad, (0, ff_size))], r, k, False, True, *mark)
+    mark = fc_total.sent_marks()
+    low = mapped(fc_full, after(pre_grad, *mark), 0, False, col_swap(h_two_other))
+    low_other, mark = row_swap(low), [low]
     proj_total = Total([(grad_full, grad_peer, activated, (0, ff_size))], r, k, True, False, *mark)
     mark = proj_total.sent_marks()
-    low = mapped(fc_full, after(pre_grad, *mark), 0, False, col_swap(h_two_other))
-    low_other, mark = row_swap(low), [low]
-    fc_total = Total([(h_two, h_two_peer, pre_grad, (0, ff_size))], r, k, False, True, *mark)
-    mark = fc_total.sent_marks()
+    part_other = mapped(proj_full, after(activated, *mark), 1, False)
+    mark = [part_other]
+    mark = proj_total.hold(*mark)
     mark = fc_total.hold(*mark)
-    mark = proj_total.hold(*mark)
+    mark = fc_total.sum_one(*mark)
+    mid_grad, branch_grad, sums_two = norm_two_back(
+        after(low, *mark), low_other, grad_full, x_mid, stats_two, columns
+    )
+    branch_peer, mark = col_swap(branch_grad), [branch_grad]
     mark = proj_total.sum_one(*mark)
-    mid_grad, branch_grad, sums_two = norm_two_back(
-        after(low, *mark), low_other, grad_full, x_mid, stats_two, gain_two
-    )
-    branch_peer, mark = col_swap(branch_grad), [branch_grad]
-    mark = fc_total.sum_one(*mark)
     attended_grad = attended_back(out_full, after(branch_grad, *mark), branch_peer)
     mark = [attended_grad]
     parts = attend_back(info, projected, attended, after(attended_grad, *mark), log_totals, first, heads)
     mark = [parts]
+    three_other = mapped_three(qkv_full, after(parts, *mark), 1)
+    mark = [three_other]
+    oq_total = Total([(branch_grad, branch_peer, attended, (0, most)), (h_one, h_one_peer, parts, (2, most))], r, k, True, True, *mark)
+    mark = oq_total.sent_marks()
+    mark = fc_total.sum_two(*mark)
+    mark = proj_total.sum_two(*mark)
     kv_total = Total([(h_one, h_one_peer, parts, (0, 2 * most))], r, k, True, False, *mark)
     mark = kv_total.sent_marks()
-    three_other = mapped_three(qkv_full, after(parts, *mark), 1)
-    mark = [three_other]
-    mark = proj_total.sum_two(*mark)
-    mark = fc_total.sum_two(*mark)
-    oq_total = Total([(branch_grad, branch_peer, attended, (0, most)), (h_one, h_one_peer, parts, (2, most))], r, k, True, True, *mark)
-    mark = oq_total.sent_marks()
+    proj_part = mapped(proj_full, after(activated, *mark), 0, False, col_swap(part_other))
+    mark = [proj_part]
     mark = oq_total.hold(*mark)
+    mark = oq_total.sum_one(*mark)
     mine = mapped_three(qkv_full, after(parts, *mark), 0, col_swap(three_other))
     mark = [mine]
+    send = half_rows(after(mine, *mark), PEER)
+    one_other, mark = row_swap(send), [send]
     mark = kv_total.hold(*mark)
-    send = half_rows(after(mine, *mark), 1 - r)
-    one_other, mark = row_swap(send), [send]
     mark = kv_total.sum_one(*mark)
     mark = proj_total.sum_three(*mark)
-    mark = oq_total.sum_one(*mark)
     mark = fc_total.sum_three(*mark)
+    mark = oq_total.sum_two(*mark)
     mark = kv_total.sum_two(*mark)
+    mark = oq_total.sum_three(*mark)
     mark = proj_total.spread_one(*mark)
-    mark = oq_total.sum_two(*mark)
+    mark = fc_total.spread_one(*mark)
+    sums, sums_one = norm_one_sums(after(mine, *mark), one_other, x_own, stats_one, columns)
+    sums_peer, mark = row_swap(sums), [sums]
     mark = kv_total.sum_three(*mark)
-    sums, sums_one = norm_one_sums(after(mine, *mark), one_other, x_own, stats_one, gain_half, r)
-    sums_peer, mark = row_swap(sums), [sums]
+    mark = oq_total.spread_one(*mark)
     packed = packed_sums(sums_two, after(sums_one, *mark), grad_own, hidden_sums, parts, most)
     packed_peer, mark = col_swap(packed), [packed]
-    mark = fc_total.spread_one(*mark)
-    mark = oq_total.sum_three(*mark)
     packed = sums_added(after(packed, *mark), packed_peer, 8)
     packed_peer, mark = hop(packed, 2), [packed]
-    x_grad = norm_one_back(after(mine, *mark), one_other, x_own, stats_one, gain_half, mid_grad, sums, sums_peer, r)
-    mark = [x_grad]
-    mark = oq_total.spread_one(*mark)
+    mark = proj_total.spread_two(*mark)
+    mark = kv_total.spread_one(*mark)
     packed = hop_added(packed, packed_peer, *mark)
     packed_peer, mark = hop(packed, 1), [packed]
-    mark = proj_total.spread_two(*mark)
-    mark = kv_total.spread_one(*mark)
+    x_grad = norm_one_back(after(mine, *mark), one_other, x_own, stats_one, columns, mid_grad, sums, sums_peer)
+    mark = [x_grad]
     mark = fc_total.spread_two(*mark)
-    part_other = mapped(proj_full, after(activated, *mark), 1, False)
-    mark = [part_other]
+    mark = kv_total.spread_two(*mark)
+    mark = oq_total.spread_two(*mark)
+    mark = kv_total.spread_three(*mark)
     packed = hop_added(packed, packed_peer, *mark)
     packed_peer, mark = hop(packed, 4), [packed]
-    mark = kv_total.spread_two(*mark)
-    mark = oq_total.spread_two(*mark)
-    mark = proj_total.spread_three(*mark)
-    mark = kv_total.spread_three(*mark)
     mark = oq_total.spread_three(*mark)
     packed = hop_added(packed, packed_peer, *mark)
     if n_dp != 8:
         for i in range(n_dp.bit_length() - 1):
             packed = sums_added(packed, dp_xor(packed, 1 << i), 16)
     packed_peer, mark = row_swap(packed), [packed]
-    mark = fc_total.spread_three(*mark)
+    mark = proj_total.spread_three(*mark)
     packed_peer = after(packed_peer, *mark)
     mark = [packed_peer]
-    proj_part = mapped(proj_full, after(activated, *mark), 0, False, col_swap(part_other))
-    mark = [proj_part]
+    mark = fc_total.spread_three(*mark)
     mark = kv_total.tail(most, spare, *mark)
     mark = oq_total.tail(most, spare, *mark)
-    send = half_rows(after(proj_part, *mark), 1 - r)
+    send = half_rows(after(proj_part, *mark), PEER)
     block_other, mark = row_swap(send), [send]
     whole = oq_total.slots(c, most, spare, *mark)
     out_weight_grad = whole[0]
@@ -1373,7 +1343,7 @@
     k_weight_grad = whole[0]
     v_weight_grad = whole[1]
     mark = [whole]
-    block_out = block_result(after(x_mid, *mark), proj_part, block_other, proj_bias_half, r)
+    block_out = block_result(after(x_mid, *mark), proj_part, block_other, columns)
     mark = [block_out]
     proj_weight_grad = proj_total.wide(*mark).T
     mark = [proj_weight_grad]

time: 805 us -> 772 us (0.959)
  Pallas kernels: 326 us -> 378 us
  waiting for transfers between devices: 287 us -> 249 us
  local copies, waits for them, and re-layouts: 81.7 us -> 46.9 us
  starting transfers between devices: 83.9 us -> 73.6 us
    ppermute x13, waiting for transfers between devices: 52.1 us -> 10.7 us  [row_swap(): return lax.ppermute(value, 'row', SWAP)]
    pallas_call x68 -> x69, Pallas kernels: 269 us -> 302 us  [call(): pl.pallas_call(body, grid_spec=pltpu.PrefetchScalarGridSpec(num_scalar_pr...]
    unnamed x184 -> x174, local copies, waits for them, and re-layouts: 61.1 us -> 33.6 us
    ppermute x36, starting transfers between devices: 57.6 us -> 47.4 us  [dp_xor(): lax.ppermute(value, 'dp', [(i, i ^ mask) for i in range(lax.axis_size('dp...]
  transfers between devices with their start and end apart: 68 -> 68, of which waited for: 34 -> 31; matrix products, arithmetic and copies ran while one was open for 5% -> 4% of each run, Pallas kernels for 35% -> 42%
where the time goes in v4:
time: 772 us; the launch traced here: 767 us
  Pallas kernels  378 us (49%)
  waiting for transfers between devices  249 us (32%)
  starting transfers between devices  73.6 us (10%)
  local copies, waits for them, and re-layouts  46.9 us (6%)
  other arithmetic  17 us (2%)
    pallas_call x69, Pallas kernels, call(): pl.pallas_call(body, grid_spec=pltpu.PrefetchScalarGridSpec(num_scalar_pr...  302 us
    ppermute x36, waiting for transfers between devices, dp_xor(): lax.ppermute(value, 'dp', [(i, i ^ mask) for i in range(lax.axis_size('dp...  223 us
    ppermute x36, starting transfers between devices, dp_xor(): lax.ppermute(value, 'dp', [(i, i ^ mask) for i in range(lax.axis_size('dp...  47.4 us
    unnamed x174, local copies, waits for them, and re-layouts  33.6 us
    pallas_call x1, Pallas kernels, attend(): pl.pallas_call(functools.partial(attend_kernel, heads, blocks), grid_spec...  31.5 us
    pallas_call x1, Pallas kernels, attend_back(): pl.pallas_call(functools.partial(attend_back_kernel, heads, blocks), grid...  30.7 us
    ppermute x13, starting transfers between devices, row_swap(): return lax.ppermute(value, 'row', SWAP)  20 us
    ppermute x15, waiting for transfers between devices, col_swap(): return lax.ppermute(value, 'col', SWAP)  15.7 us
  transfers between devices with their start and end apart: 68, of which 31 were waited for; matrix products, arithmetic and copies ran while one was open for 4% of the time, Pallas kernels for 42%

profile of v4, /device:TPU:0, one launch (start us, length us, event | category | flops | bytes accessed | tf_op | source)
XLA Modules:
  0.0 766.7 jit_solution(169385119257148954)
XLA Ops:
  9.5 3.9 pack_heads.1
  20.2 4.1 pack.1
  27.1 5.3 own_rows.3.h_ref
  35.8 5.2 own_rows.4.h_ref
  41.0 7.6 collective-permute-done.5.refs_2_
  50.6 5.3 own_rows.5.h_ref
  60.7 3.4 norm_one.1
  64.1 4.5 all_rows.3
  74.6 13.0 %project.1.q_ref.k_ref.v_ref = bf16[1344,1536]{1,0:T(8,128)(2,1)S(1)} custom-call(s32[8]{0:T(128)S(1)} %copy-done.41, bf16[3,1600,448]{2,1,0:T(8,128)(2,1)} %bitcast.65, bf16[1600,768]{1,0:T(8,128)(2,1)S(1)} %get-tuple-element.148.own_ref, bf16[1600,768]{1,0:T(8,128)(2,1)} %collective-permute-done.9.other_ref, f32[3,448,1]{2,1,0:T(8,128)S(1)} %copy-done.39), custom_call_target="tpu_custom_call" | custom-call | tf_op jit(solution)/shard_map/project/pallas_call | solution.py:215
  92.2 31.5 %attend.1 = (bf16[448,1536]{1,0:T(8,128)(2,1)S(1)}, f32[8,1536]{1,0:T(8,128)S(1)}) custom-call(s32[7]{0:T(128)S(1)} %pad_add_fusion.info_ref, bf16[1344,1536]{1,0:T(8,128)(2,1)S(1)} %project.1.q_ref.k_ref.v_ref, bf16[1344,1536]{1,0:T(8,128)(2,1)S(1)} %project.1.q_ref.k_ref.v_ref, bf16[1344,1536]{1,0:T(8,128)(2,1)S(1)} %project.1.q_ref.k_ref.v_ref, ...), custom_call_target="tpu_custom_call" | custom-call | tf_op jit(solution)/shard_map/attend/pallas_call | solution.py:90
  127.2 4.7 collective-permute-done.13.refs_0_
  138.4 14.9 %collective-permute-done.14.refs_1_ = bf16[200,1600]{1,0:T(8,128)(2,1)S(1)} collective-permute-done((bf16[200,1600]{1,0:T(8,128)(2,1)}, bf16[200,1600]{1,0:T(8,128)(2,1)S(1)}, u32[]{:S(2)}, u32[]{:S(2)}) %collective-permute-start.14) | collective-permute-done | bytes 640032 | tf_op jit(solution)/shard_map/ppermute | solution.py:455
  156.9 11.8 %collective-permute-done.15.refs_2_ = bf16[200,1600]{1,0:T(8,128)(2,1)S(1)} collective-permute-done((bf16[200,1600]{1,0:T(8,128)(2,1)}, bf16[200,1600]{1,0:T(8,128)(2,1)S(1)}, u32[]{:S(2)}, u32[]{:S(2)}) %collective-permute-start.15) | collective-permute-done | bytes 640032 | tf_op jit(solution)/shard_map/ppermute | solution.py:455
  168.7 13.1 %collective-permute-done.16.refs_3_ = bf16[200,1600]{1,0:T(8,128)(2,1)S(1)} collective-permute-done((bf16[200,1600]{1,0:T(8,128)(2,1)S(1)}, bf16[200,1600]{1,0:T(8,128)(2,1)S(1)}, u32[]{:S(2)}, u32[]{:S(2)}) %collective-permute-start.16) | collective-permute-done | bytes 640032 | tf_op jit(solution)/shard_map/ppermute | solution.py:455
  182.6 4.9 all_rows.4
  187.5 4.5 all_rows.5
  192.1 6.2 norm_two.1
  198.8 4.2 collective-permute-done.21.other_ref
  203.0 19.2 %hidden.1 = (bf16[1600,1536]{1,0:T(8,128)(2,1)S(1)}, f32[1600,1536]{1,0:T(8,128)}) custom-call(s32[8]{0:T(128)S(1)} %copy-done.42, bf16[1600,1600]{1,0:T(8,128)(2,1)} %bitcast.55, bf16[1600,768]{1,0:T(8,128)(2,1)S(1)} %get-tuple-element.165.own_ref, bf16[1600,768]{1,0:T(8,128)(2,1)S(1)} %collective-permute-done.21.other_ref, f32[1600,8]{1,0:T(8,128)S(1)} %bitcast.87), custom_call_target="tpu_custom_call" | custom-call | tf_op jit(solution)/shard_map/hidden/pallas_call | solution.py:215
  222.2 5.5 collective-permute-done.22.b_ref
  230.0 4.7 collective-permute-done.23.other_ref
  236.1 17.1 %hidden_back.1 = (bf16[1600,1536]{1,0:T(8,128)(2,1)}, f32[1600,128]{1,0:T(8,128)}) custom-call(s32[8]{0:T(128)} %fusion.14.s_ref._, bf16[1600,1600]{1,0:T(8,128)(2,1)} %bitcast.60, bf16[1600,768]{1,0:T(8,128)(2,1)} %bitcast.77, bf16[1600,768]{1,0:T(8,128)(2,1)} %copy-done.62, f32[1600,1536]{1,0:T(8,128)} %get-tuple-element.169.s_ref), custom_call_target="tpu_custom_call" | custom-call | tf_op jit(solution)/shard_map/hidden_back/pallas_call | solution.py:215
  255.6 6.8 mapped.8
  262.5 11.3 %weight_grad.8 = bf16[4,200,1600]{2,1,0:T(8,128)(2,1)} custom-call(s32[8]{0:T(128)} %fusion.14.s_ref._, bf16[8,200,768]{2,1,0:T(8,128)(2,1)} %bitcast.96, bf16[8,200,768]{2,1,0:T(8,128)(2,1)} %bitcast.98, bf16[1600,1536]{1,0:T(8,128)(2,1)} %get-tuple-element.177.t_ref.refs_2_), custom_call_target="tpu_custom_call" | custom-call | tf_op jit(solution)/shard_map/weight_grad/pallas_call | solution.py:215
  275.5 8.6 %mapped.9.low_ref = bf16[1600,768]{1,0:T(8,128)(2,1)} custom-call(s32[8]{0:T(128)S(1)} %copy-done.44, bf16[1600,1600]{1,0:T(8,128)(2,1)} %bitcast.56, bf16[1600,1536]{1,0:T(8,128)(2,1)S(1)} %bitcast.75, bf16[1600,768]{1,0:T(8,128)(2,1)} %collective-permute-done.24.refs_0_), custom_call_target="tpu_custom_call" | custom-call | tf_op jit(solution)/shard_map/mapped/pallas_call | solution.py:215
  284.6 10.0 %weight_grad.9 = bf16[2,400,1600]{2,1,0:T(8,128)(2,1)} custom-call(s32[8]{0:T(128)} %fusion.14.s_ref._, bf16[4,400,768]{2,1,0:T(8,128)(2,1)} %bitcast.78, bf16[4,400,768]{2,1,0:T(8,128)(2,1)} %bitcast.126, bf16[1600,1536]{1,0:T(8,128)(2,1)} %copy-done.6), custom_call_target="tpu_custom_call" | custom-call | tf_op jit(solution)/shard_map/weight_grad/pallas_call | solution.py:215
  298.8 6.8 mapped.10
  305.6 9.4 %weight_grad.10 = bf16[2,400,1600]{2,1,0:T(8,128)(2,1)} custom-call(s32[8]{0:T(128)} %fusion.14.s_ref._, bf16[4,400,768]{2,1,0:T(8,128)(2,1)} %bitcast.79, bf16[4,400,768]{2,1,0:T(8,128)(2,1)} %bitcast.127, bf16[1600,1536]{1,0:T(8,128)(2,1)} %copy-done.6), custom_call_target="tpu_custom_call" | custom-call | tf_op jit(solution)/shard_map/weight_grad/pallas_call | solution.py:215
  315.0 10.9 %weight_grad.11 = bf16[4,200,1600]{2,1,0:T(8,128)(2,1)} custom-call(s32[8]{0:T(128)} %fusion.14.s_ref._, bf16[8,200,768]{2,1,0:T(8,128)(2,1)} %bitcast.97, bf16[8,200,768]{2,1,0:T(8,128)(2,1)} %bitcast.99, bf16[1600,1536]{1,0:T(8,128)(2,1)} %get-tuple-element.177.t_ref.refs_2_), custom_call_target="tpu_custom_call" | custom-call | tf_op jit(solution)/shard_map/weight_grad/pallas_call | solution.py:215
  325.9 8.3 %collective-permute-done.25.b_ref.d_ref = bf16[2,2,200,1600]{3,2,1,0:T(8,128)(2,1)} collective-permute-done((bf16[2,2,200,1600]{3,2,1,0:T(8,128)(2,1)}, bf16[2,2,200,1600]{3,2,1,0:T(8,128)(2,1)}, u32[]{:S(2)}, u32[]{:S(2)}) %collective-permute-start.25) | collective-permute-done | bytes 2560032 | tf_op jit(solution)/shard_map/ppermute | solution.py:455
  339.7 10.2 %norm_two_back.1 = (f32[1600,768]{1,0:T(8,128)}, bf16[1600,768]{1,0:T(8,128)(2,1)S(1)}, f32[3,1600,128]{2,1,0:T(8,128)S(1)}) custom-call(s32[8]{0:T(128)S(1)} %copy-done.46, bf16[1600,768]{1,0:T(8,128)(2,1)} %mapped.9.low_ref, bf16[1600,768]{1,0:T(8,128)(2,1)} %collective-permute-done.26.other_ref, bf16[1600,768]{1,0:T(8,128)(2,1)S(1)} %bitcast.80, ...), custom_call_target="tpu_custom_call" | custom-call | tf_op jit(solution)/shard_map/norm_two_back/pallas_call | solution.py:215
  359.5 3.5 attended_back.1.g_ref
  363.0 30.7 %attend_back.1.p_ref.refs_5_.refs_2_ = bf16[1344,1536]{1,0:T(8,128)(2,1)S(1)} custom-call(s32[7]{0:T(128)S(1)} %pad_add_fusion.info_ref, bf16[1344,1536]{1,0:T(8,128)(2,1)S(1)} %copy-done.4, bf16[1344,1536]{1,0:T(8,128)(2,1)S(1)} %copy-done.4, bf16[1344,1536]{1,0:T(8,128)(2,1)S(1)} %copy-done.4, bf16[448,1536]{1,0:T(8,128)(2,1)S(1)} %copy-done.13, ...), custom_call_target="tpu_custom_call" | custom-call | tf_op jit(solution)/shard_map/attend_back/pallas_call | solution.py:178
  393.8 6.4 mapped_three.2
  400.3 7.6 weight_grad.12
  414.8 7.2 weight_grad.13
  424.1 3.8 collective-permute-start.35
  427.9 7.5 mapped.11.a_ref.p_ref
  436.8 7.5 weight_grad.14
  449.9 7.0 mapped_three.3.a_ref.m_ref
  461.8 6.9 weight_grad.15
  468.7 3.9 collective-permute-done.34.b_ref.d_ref
  480.1 5.9 collective-permute-done.36.b_ref
  488.5 6.8 collective-permute-done.37.b_ref.d_ref
  498.8 18.1 %collective-permute-done.38.b_ref.d_ref = bf16[2,200,896]{2,1,0:T(8,128)(2,1)S(1)} collective-permute-done((bf16[2,200,896]{2,1,0:T(8,128)(2,1)S(1)}, bf16[2,200,896]{2,1,0:T(8,128)(2,1)S(1)}, u32[]{:S(2)}, u32[]{:S(2)}) %collective-permute-start.38) | collective-permute-done | bytes 716832 | tf_op jit(solution)/shard_map/ppermute | solution.py:455
  528.0 37.4 %collective-permute-done.43.b_ref = bf16[200,896]{1,0:T(8,128)(2,1)S(1)} collective-permute-done((bf16[200,896]{1,0:T(8,128)(2,1)S(1)}, bf16[200,896]{1,0:T(8,128)(2,1)S(1)}, u32[]{:S(2)}, u32[]{:S(2)}) %collective-permute-start.43) | collective-permute-done | bytes 358432 | tf_op jit(solution)/shard_map/ppermute | solution.py:455
  569.9 5.0 packed_sums.1.a_ref
  586.9 3.3 collective-permute-done.48.b_ref
  590.8 3.4 norm_one_back.1
  594.2 7.5 collective-permute-done.50.b_ref
  605.6 3.3 collective-permute-done.51.b_ref
  610.4 28.0 %collective-permute-done.52.b_ref = bf16[200,896]{1,0:T(8,128)(2,1)S(1)} collective-permute-done((bf16[200,896]{1,0:T(8,128)(2,1)S(1)}, bf16[200,896]{1,0:T(8,128)(2,1)S(1)}, u32[]{:S(2)}, u32[]{:S(2)}) %collective-permute-start.52) | collective-permute-done | bytes 358432 | tf_op jit(solution)/shard_map/ppermute | solution.py:455
  639.1 4.3 collective-permute-start.55
  644.6 3.5 collective-permute-done.54.b_ref
  649.9 12.7 %collective-permute-done.55.b_ref = bf16[2,200,896]{2,1,0:T(8,128)(2,1)S(1)} collective-permute-done((bf16[2,200,896]{2,1,0:T(8,128)(2,1)S(1)}, bf16[2,200,896]{2,1,0:T(8,128)(2,1)S(1)}, u32[]{:S(2)}, u32[]{:S(2)}) %collective-permute-start.55) | collective-permute-done | bytes 716832 | tf_op jit(solution)/shard_map/ppermute | solution.py:455
  666.7 4.8 paired.16.a_ref.c_ref
  677.2 16.1 %collective-permute-done.60.b_ref.d_ref = bf16[2,2,200,896]{3,2,1,0:T(8,128)(2,1)S(1)} collective-permute-done((bf16[2,2,200,896]{3,2,1,0:T(8,128)(2,1)S(1)}, bf16[2,2,200,896]{3,2,1,0:T(8,128)(2,1)S(1)}, u32[]{:S(2)}, u32[]{:S(2)}) %collective-permute-start.60) | collective-permute-done | bytes 1433632 | tf_op jit(solution)/shard_map/ppermute | solution.py:455
  694.5 3.3 collective-permute-done.61.b_ref.d_ref
  714.8 4.1 copy.52
  719.0 7.5 pad_maximum_fusion
  728.9 3.9 block_result.1
  732.8 16.5 %collective-permute-done.66.b_ref.d_ref = bf16[2,2,200,1600]{3,2,1,0:T(8,128)(2,1)} collective-permute-done((bf16[2,2,200,1600]{3,2,1,0:T(8,128)(2,1)}, bf16[2,2,200,1600]{3,2,1,0:T(8,128)(2,1)}, u32[]{:S(2)}, u32[]{:S(2)}) %collective-permute-start.66) | collective-permute-done | bytes 2560032 | tf_op jit(solution)/shard_map/ppermute | solution.py:455
  749.3 8.8 %widened.2 = f32[800,3200]{1,0:T(8,128)} custom-call(s32[8]{0:T(128)S(1)} %copy-done.50, bf16[2,2,200,1600]{3,2,1,0:T(8,128)(2,1)} %paired.16.a_ref.c_ref, bf16[2,2,200,1600]{3,2,1,0:T(8,128)(2,1)} %collective-permute-done.66.b_ref.d_ref, bf16[2,2,200,1600]{3,2,1,0:T(8,128)(2,1)} %paired.16.a_ref.c_ref, ...), custom_call_target="tpu_custom_call" | custom-call | tf_op jit(solution)/shard_map/widened/pallas_call | solution.py:215
  758.1 8.5 %widened.3 = f32[800,3200]{1,0:T(8,128)} custom-call(s32[8]{0:T(128)S(1)} %copy-done.50, bf16[2,2,200,1600]{3,2,1,0:T(8,128)(2,1)} %paired.17.a_ref.c_ref, bf16[2,2,200,1600]{3,2,1,0:T(8,128)(2,1)} %collective-permute-done.67.b_ref.d_ref, bf16[2,2,200,1600]{3,2,1,0:T(8,128)(2,1)} %paired.17.a_ref.c_ref, ...), custom_call_target="tpu_custom_call" | custom-call | tf_op jit(solution)/shard_map/widened/pallas_call | solution.py:215
  (378 shorter events, 183.6 us)
Async XLA Ops:
  2.0 6.4 collective-permute-start
  14.6 17.8 %collective-permute-start.3 = (bf16[3,200,448]{2,1,0:T(8,128)(2,1)}, bf16[3,200,448]{2,1,0:T(8,128)(2,1)}, u32[]{:S(2)}, u32[]{:S(2)}) collective-permute-start(bf16[3,200,448]{2,1,0:T(8,128)(2,1)} %pack_heads.1), channel_id=1, source_target_pairs={{0,2},{2,0},{1,3},{3,1},{4,6},{6,4},{5,7},{7,5},{8,10},{10,8},{9,1... | collective-permute-start | bytes 1612808 | tf_op jit(solution)/shard_map/ppermute | solution.py:447
  17.0 7.3 collective-permute-start.2
  17.3 16.8 %collective-permute-start.6 = (bf16[2,32]{1,0:T(2,128)(2,1)S(1)}, bf16[2,32]{1,0:T(2,128)(2,1)S(1)}, u32[]{:S(2)}, u32[]{:S(2)}) collective-permute-start(bf16[2,32]{1,0:T(2,128)(2,1)S(1)} %slice.115), channel_id=1, source_target_pairs={{0,1},{1,0},{2,3},{3,2},{4,5},{5,4},{6,7},{7,6},{8,9},{9,8},{10,11... | collective-permute-start | bytes 392 | tf_op jit(solution)/shard_map/ppermute | solution.py:451
  18.0 32.1 %collective-permute-start.7 = (bf16[5,800]{1,0:T(8,128)(2,1)S(1)}, bf16[5,800]{1,0:T(8,128)(2,1)S(1)}, u32[]{:S(2)}, u32[]{:S(2)}) collective-permute-start(bf16[5,800]{1,0:T(8,128)(2,1)S(1)} %stack.37), channel_id=1, source_target_pairs={{0,2},{2,0},{1,3},{3,1},{4,6},{6,4},{5,7},{7,5},{8,10},{10,8},{9,1... | collective-permute-start | bytes 24008 | tf_op jit(solution)/shard_map/ppermute | solution.py:447
  18.2 40.2 %collective-permute-start.1 = (bf16[800,768]{1,0:T(8,128)(2,1)S(1)}, bf16[800,768]{1,0:T(8,128)(2,1)S(1)}, u32[]{:S(2)}, u32[]{:S(2)}) collective-permute-start(bf16[800,768]{1,0:T(8,128)(2,1)S(1)} %bitcast.104), channel_id=1, source_target_pairs={{0,2},{2,0},{1,3},{3,1},{4,6},{6,4},{5,7},{7,5},{8,10},{10,8},{9,1... | collective-permute-start | bytes 3686408 | tf_op jit(solution)/shard_map/ppermute | solution.py:447
  32.4 16.2 %collective-permute-start.5 = (bf16[3,200,448]{2,1,0:T(8,128)(2,1)}, bf16[3,200,448]{2,1,0:T(8,128)(2,1)}, u32[]{:S(2)}, u32[]{:S(2)}) collective-permute-start(bf16[3,200,448]{2,1,0:T(8,128)(2,1)} %collective-permute-done.3.refs_0_), channel_id=1, source_target_pairs={{0,8},{4,12},{8,0},{12,4},{16,24},{20,28},{24,16},{28,20},{1,9},{5... | collective-permute-start | bytes 1612808 | tf_op jit(solution)/shard_map/ppermute | solution.py:455
  34.3 16.2 %collective-permute-start.4 = (bf16[3,200,448]{2,1,0:T(8,128)(2,1)}, bf16[3,200,448]{2,1,0:T(8,128)(2,1)}, u32[]{:S(2)}, u32[]{:S(2)}) collective-permute-start(bf16[3,200,448]{2,1,0:T(8,128)(2,1)} %collective-permute-done.3.refs_0_), channel_id=1, source_target_pairs={{0,4},{4,0},{8,12},{12,8},{16,20},{20,16},{24,28},{28,24},{1,5},{5... | collective-permute-start | bytes 1612808 | tf_op jit(solution)/shard_map/ppermute | solution.py:455
  48.6 15.5 %collective-permute-start.8 = (bf16[3,200,448]{2,1,0:T(8,128)(2,1)}, bf16[3,200,448]{2,1,0:T(8,128)(2,1)}, u32[]{:S(2)}, u32[]{:S(2)}) collective-permute-start(bf16[3,200,448]{2,1,0:T(8,128)(2,1)} %collective-permute-done.5.refs_2_), channel_id=1, source_target_pairs={{0,4},{4,0},{8,12},{12,8},{16,20},{20,16},{24,28},{28,24},{1,5},{5... | collective-permute-start | bytes 1612808 | tf_op jit(solution)/shard_map/ppermute | solution.py:455
  68.6 4.9 collective-permute-start.9
  68.7 21.0 %collective-permute-start.10 = (bf16[448,800]{1,0:T(8,128)(2,1)}, bf16[448,800]{1,0:T(8,128)(2,1)}, u32[]{:S(2)}, u32[]{:S(2)}) collective-permute-start(bf16[448,800]{1,0:T(8,128)(2,1)} %get-tuple-element.150), channel_id=1, source_target_pairs={{0,2},{2,0},{1,3},{3,1},{4,6},{6,4},{5,7},{7,5},{8,10},{10,8},{9,1... | collective-permute-start | bytes 2150408 | tf_op jit(solution)/shard_map/ppermute | solution.py:447
  70.4 54.0 %collective-permute-start.12 = (bf16[200,1600]{1,0:T(8,128)(2,1)}, bf16[200,1600]{1,0:T(8,128)(2,1)}, u32[]{:S(2)}, u32[]{:S(2)}) collective-permute-start(bf16[200,1600]{1,0:T(8,128)(2,1)} %get-tuple-element.156), channel_id=1, source_target_pairs={{0,2},{2,0},{1,3},{3,1},{4,6},{6,4},{5,7},{7,5},{8,10},{10,8},{9,1... | collective-permute-start | bytes 1920008 | tf_op jit(solution)/shard_map/ppermute | solution.py:447
  70.8 53.6 %collective-permute-start.11 = (bf16[200,1600]{1,0:T(8,128)(2,1)}, bf16[200,1600]{1,0:T(8,128)(2,1)}, u32[]{:S(2)}, u32[]{:S(2)}) collective-permute-start(bf16[200,1600]{1,0:T(8,128)(2,1)} %get-tuple-element.153), channel_id=1, source_target_pairs={{0,2},{2,0},{1,3},{3,1},{4,6},{6,4},{5,7},{7,5},{8,10},{10,8},{9,1... | collective-permute-start | bytes 1920008 | tf_op jit(solution)/shard_map/ppermute | solution.py:447
  127.1 4.7 collective-permute-start.13
  134.7 57.4 %collective-permute-start.20 = (bf16[1600,768]{1,0:T(8,128)(2,1)S(1)}, bf16[1600,768]{1,0:T(8,128)(2,1)}, u32[]{:S(2)}, u32[]{:S(2)}) collective-permute-start(bf16[1600,768]{1,0:T(8,128)(2,1)S(1)} %mapped.7.low_ref), channel_id=1, source_target_pairs={{0,2},{2,0},{1,3},{3,1},{4,6},{6,4},{5,7},{7,5},{8,10},{10,8},{9,1... | collective-permute-start | bytes 7372808 | tf_op jit(solution)/shard_map/ppermute | solution.py:447
  136.3 16.9 %collective-permute-start.14 = (bf16[200,1600]{1,0:T(8,128)(2,1)}, bf16[200,1600]{1,0:T(8,128)(2,1)S(1)}, u32[]{:S(2)}, u32[]{:S(2)}) collective-permute-start(bf16[200,1600]{1,0:T(8,128)(2,1)} %collective-permute-done.11.refs_0_), channel_id=1, source_target_pairs={{0,4},{4,0},{8,12},{12,8},{16,20},{20,16},{24,28},{28,24},{1,5},{5... | collective-permute-start | bytes 1920008 | tf_op jit(solution)/shard_map/ppermute | solution.py:455
  136.3 18.8 %collective-permute-start.18 = (bf16[200,1600]{1,0:T(8,128)(2,1)}, bf16[200,1600]{1,0:T(8,128)(2,1)}, u32[]{:S(2)}, u32[]{:S(2)}) collective-permute-start(bf16[200,1600]{1,0:T(8,128)(2,1)} %collective-permute-done.12.refs_0_), channel_id=1, source_target_pairs={{0,8},{4,12},{8,0},{12,4},{16,24},{20,28},{24,16},{28,20},{1,9},{5... | collective-permute-start | bytes 1920008 | tf_op jit(solution)/shard_map/ppermute | solution.py:455
  137.9 30.7 %collective-permute-start.15 = (bf16[200,1600]{1,0:T(8,128)(2,1)}, bf16[200,1600]{1,0:T(8,128)(2,1)S(1)}, u32[]{:S(2)}, u32[]{:S(2)}) collective-permute-start(bf16[200,1600]{1,0:T(8,128)(2,1)} %collective-permute-done.11.refs_0_), channel_id=1, source_target_pairs={{0,8},{4,12},{8,0},{12,4},{16,24},{20,28},{24,16},{28,20},{1,9},{5... | collective-permute-start | bytes 1920008 | tf_op jit(solution)/shard_map/ppermute | solution.py:455
  153.3 28.5 %collective-permute-start.16 = (bf16[200,1600]{1,0:T(8,128)(2,1)S(1)}, bf16[200,1600]{1,0:T(8,128)(2,1)S(1)}, u32[]{:S(2)}, u32[]{:S(2)}) collective-permute-start(bf16[200,1600]{1,0:T(8,128)(2,1)S(1)} %collective-permute-done.14.refs_1_), channel_id=1, source_target_pairs={{0,8},{4,12},{8,0},{12,4},{16,24},{20,28},{24,16},{28,20},{1,9},{5... | collective-permute-start | bytes 1920008 | tf_op jit(solution)/shard_map/ppermute | solution.py:455
  154.8 32.7 %collective-permute-start.17 = (bf16[200,1600]{1,0:T(8,128)(2,1)}, bf16[200,1600]{1,0:T(8,128)(2,1)}, u32[]{:S(2)}, u32[]{:S(2)}) collective-permute-start(bf16[200,1600]{1,0:T(8,128)(2,1)} %collective-permute-done.12.refs_0_), channel_id=1, source_target_pairs={{0,4},{4,0},{8,12},{12,8},{16,20},{20,16},{24,28},{28,24},{1,5},{5... | collective-permute-start | bytes 1920008 | tf_op jit(solution)/shard_map/ppermute | solution.py:455
  155.1 32.4 %collective-permute-start.19 = (bf16[200,1600]{1,0:T(8,128)(2,1)}, bf16[200,1600]{1,0:T(8,128)(2,1)}, u32[]{:S(2)}, u32[]{:S(2)}) collective-permute-start(bf16[200,1600]{1,0:T(8,128)(2,1)} %collective-permute-done.18.refs_2_), channel_id=1, source_target_pairs={{0,4},{4,0},{8,12},{12,8},{16,20},{20,16},{24,28},{28,24},{1,5},{5... | collective-permute-start | bytes 1920008 | tf_op jit(solution)/shard_map/ppermute | solution.py:455
  198.3 4.7 collective-permute-start.21
  198.3 29.4 %collective-permute-start.22 = (bf16[800,768]{1,0:T(8,128)(2,1)S(1)}, bf16[800,768]{1,0:T(8,128)(2,1)S(1)}, u32[]{:S(2)}, u32[]{:S(2)}) collective-permute-start(bf16[800,768]{1,0:T(8,128)(2,1)S(1)} %bitcast.115), channel_id=1, source_target_pairs={{0,2},{2,0},{1,3},{3,1},{4,6},{6,4},{5,7},{7,5},{8,10},{10,8},{9,1... | collective-permute-start | bytes 3686408 | tf_op jit(solution)/shard_map/ppermute | solution.py:447
  230.0 4.7 collective-permute-start.23
  262.4 13.1 %collective-permute-start.24 = (bf16[1600,768]{1,0:T(8,128)(2,1)}, bf16[1600,768]{1,0:T(8,128)(2,1)}, u32[]{:S(2)}, u32[]{:S(2)}) collective-permute-start(bf16[1600,768]{1,0:T(8,128)(2,1)} %mapped.8), channel_id=1, source_target_pairs={{0,1},{1,0},{2,3},{3,2},{4,5},{5,4},{6,7},{7,6},{8,9},{9,8},{10,11... | collective-permute-start | bytes 7372808 | tf_op jit(solution)/shard_map/ppermute | solution.py:451
  273.8 60.3 %collective-permute-start.25 = (bf16[2,2,200,1600]{3,2,1,0:T(8,128)(2,1)}, bf16[2,2,200,1600]{3,2,1,0:T(8,128)(2,1)}, u32[]{:S(2)}, u32[]{:S(2)}) collective-permute-start(bf16[2,2,200,1600]{3,2,1,0:T(8,128)(2,1)} %bitcast.138), channel_id=1, source_target_pairs={{0,8},{4,12},{8,0},{12,4},{16,24},{20,28},{24,16},{28,20},{1,9},{5... | collective-permute-start | bytes 7680008 | tf_op jit(solution)/shard_map/ppermute | solution.py:455
  284.0 55.7 %collective-permute-start.26 = (bf16[1600,768]{1,0:T(8,128)(2,1)}, bf16[1600,768]{1,0:T(8,128)(2,1)}, u32[]{:S(2)}, u32[]{:S(2)}) collective-permute-start(bf16[1600,768]{1,0:T(8,128)(2,1)} %mapped.9.low_ref), channel_id=1, source_target_pairs={{0,2},{2,0},{1,3},{3,1},{4,6},{6,4},{5,7},{7,5},{8,10},{10,8},{9,1... | collective-permute-start | bytes 7372808 | tf_op jit(solution)/shard_map/ppermute | solution.py:447
  294.6 59.8 %collective-permute-start.27 = (bf16[2,2,200,1600]{3,2,1,0:T(8,128)(2,1)}, bf16[2,2,200,1600]{3,2,1,0:T(8,128)(2,1)}, u32[]{:S(2)}, u32[]{:S(2)}) collective-permute-start(bf16[2,2,200,1600]{3,2,1,0:T(8,128)(2,1)} %bitcast.137), channel_id=1, source_target_pairs={{0,4},{4,0},{8,12},{12,8},{16,20},{20,16},{24,28},{28,24},{1,5},{5... | collective-permute-start | bytes 7680008 | tf_op jit(solution)/shard_map/ppermute | solution.py:455
  351.3 8.1 %collective-permute-start.28 = (bf16[1600,768]{1,0:T(8,128)(2,1)S(1)}, bf16[1600,768]{1,0:T(8,128)(2,1)S(1)}, u32[]{:S(2)}, u32[]{:S(2)}) collective-permute-start(bf16[1600,768]{1,0:T(8,128)(2,1)S(1)} %get-tuple-element.184.own_ref), channel_id=1, source_target_pairs={{0,1},{1,0},{2,3},{3,2},{4,5},{5,4},{6,7},{7,6},{8,9},{9,8},{10,11... | collective-permute-start | bytes 7372808 | tf_op jit(solution)/shard_map/ppermute | solution.py:451
  351.3 76.6 %collective-permute-start.31 = (bf16[1600,768]{1,0:T(8,128)(2,1)}, bf16[1600,768]{1,0:T(8,128)(2,1)}, u32[]{:S(2)}, u32[]{:S(2)}) collective-permute-start(bf16[1600,768]{1,0:T(8,128)(2,1)} %mapped.10), channel_id=1, source_target_pairs={{0,1},{1,0},{2,3},{3,2},{4,5},{5,4},{6,7},{7,6},{8,9},{9,8},{10,11... | collective-permute-start | bytes 7372808 | tf_op jit(solution)/shard_map/ppermute | solution.py:451
  351.8 56.1 %collective-permute-start.29 = (bf16[2,200,1600]{2,1,0:T(8,128)(2,1)}, bf16[2,200,1600]{2,1,0:T(8,128)(2,1)}, u32[]{:S(2)}, u32[]{:S(2)}) collective-permute-start(bf16[2,200,1600]{2,1,0:T(8,128)(2,1)} %get-tuple-element.190), channel_id=1, source_target_pairs={{0,4},{4,0},{8,12},{12,8},{16,20},{20,16},{24,28},{28,24},{1,5},{5... | collective-permute-start | bytes 3840008 | tf_op jit(solution)/shard_map/ppermute | solution.py:455
  358.8 52.1 %collective-permute-start.30 = (bf16[2,200,1600]{2,1,0:T(8,128)(2,1)}, bf16[2,200,1600]{2,1,0:T(8,128)(2,1)}, u32[]{:S(2)}, u32[]{:S(2)}) collective-permute-start(bf16[2,200,1600]{2,1,0:T(8,128)(2,1)} %get-tuple-element.193), channel_id=1, source_target_pairs={{0,8},{4,12},{8,0},{12,4},{16,24},{20,28},{24,16},{28,20},{1,9},{5... | collective-permute-start | bytes 3840008 | tf_op jit(solution)/shard_map/ppermute | solution.py:455
  400.2 49.7 %collective-permute-start.33 = (bf16[1600,768]{1,0:T(8,128)(2,1)}, bf16[1600,768]{1,0:T(8,128)(2,1)}, u32[]{:S(2)}, u32[]{:S(2)}) collective-permute-start(bf16[1600,768]{1,0:T(8,128)(2,1)} %mapped_three.2), channel_id=1, source_target_pairs={{0,1},{1,0},{2,3},{3,2},{4,5},{5,4},{6,7},{7,6},{8,9},{9,8},{10,11... | collective-permute-start | bytes 7372808 | tf_op jit(solution)/shard_map/ppermute | solution.py:451
  407.9 36.4 %collective-permute-start.32 = (bf16[2,2,200,896]{3,2,1,0:T(8,128)(2,1)}, bf16[2,2,200,896]{3,2,1,0:T(8,128)(2,1)}, u32[]{:S(2)}, u32[]{:S(2)}) collective-permute-start(bf16[2,2,200,896]{3,2,1,0:T(8,128)(2,1)} %bitcast.141), channel_id=1, source_target_pairs={{0,4},{4,0},{8,12},{12,8},{16,20},{20,16},{24,28},{28,24},{1,5},{5... | collective-permute-start | bytes 4300808 | tf_op jit(solution)/shard_map/ppermute | solution.py:455
  422.1 50.5 %collective-permute-start.34 = (bf16[2,2,200,896]{3,2,1,0:T(8,128)(2,1)}, bf16[2,2,200,896]{3,2,1,0:T(8,128)(2,1)}, u32[]{:S(2)}, u32[]{:S(2)}) collective-permute-start(bf16[2,2,200,896]{3,2,1,0:T(8,128)(2,1)} %bitcast.140), channel_id=1, source_target_pairs={{0,4},{4,0},{8,12},{12,8},{16,20},{20,16},{24,28},{28,24},{1,5},{5... | collective-permute-start | bytes 4300808 | tf_op jit(solution)/shard_map/ppermute | solution.py:455
  424.1 53.5 %collective-permute-start.35 = (bf16[200,1600]{1,0:T(8,128)(2,1)}, bf16[200,1600]{1,0:T(8,128)(2,1)}, u32[]{:S(2)}, u32[]{:S(2)}) collective-permute-start(bf16[200,1600]{1,0:T(8,128)(2,1)} %bitcast.123), channel_id=1, source_target_pairs={{0,16},{4,20},{8,24},{12,28},{16,0},{20,4},{24,8},{28,12},{1,17},{... | collective-permute-start | bytes 1920008 | tf_op jit(solution)/shard_map/ppermute | solution.py:455
  427.9 58.1 %collective-permute-start.36 = (bf16[200,1600]{1,0:T(8,128)(2,1)}, bf16[200,1600]{1,0:T(8,128)(2,1)}, u32[]{:S(2)}, u32[]{:S(2)}) collective-permute-start(bf16[200,1600]{1,0:T(8,128)(2,1)} %bitcast.122), channel_id=1, source_target_pairs={{0,16},{4,20},{8,24},{12,28},{16,0},{20,4},{24,8},{28,12},{1,17},{... | collective-permute-start | bytes 1920008 | tf_op jit(solution)/shard_map/ppermute | solution.py:455
  448.6 46.7 %collective-permute-start.37 = (bf16[2,200,896]{2,1,0:T(8,128)(2,1)}, bf16[2,200,896]{2,1,0:T(8,128)(2,1)S(1)}, u32[]{:S(2)}, u32[]{:S(2)}) collective-permute-start(bf16[2,200,896]{2,1,0:T(8,128)(2,1)} %get-tuple-element.209), channel_id=1, source_target_pairs={{0,8},{4,12},{8,0},{12,4},{16,24},{20,28},{24,16},{28,20},{1,9},{5... | collective-permute-start | bytes 2150408 | tf_op jit(solution)/shard_map/ppermute | solution.py:455
  459.6 66.1 %collective-permute-start.42 = (bf16[800,768]{1,0:T(8,128)(2,1)}, bf16[800,768]{1,0:T(8,128)(2,1)S(1)}, u32[]{:S(2)}, u32[]{:S(2)}) collective-permute-start(bf16[800,768]{1,0:T(8,128)(2,1)} %half_rows.2), channel_id=1, source_target_pairs={{0,2},{2,0},{1,3},{3,1},{4,6},{6,4},{5,7},{7,5},{8,10},{10,8},{9,1... | collective-permute-start | bytes 3686408 | tf_op jit(solution)/shard_map/ppermute | solution.py:447
  476.1 40.8 %collective-permute-start.38 = (bf16[2,200,896]{2,1,0:T(8,128)(2,1)S(1)}, bf16[2,200,896]{2,1,0:T(8,128)(2,1)S(1)}, u32[]{:S(2)}, u32[]{:S(2)}) collective-permute-start(bf16[2,200,896]{2,1,0:T(8,128)(2,1)S(1)} %get-tuple-element.212), channel_id=1, source_target_pairs={{0,8},{4,12},{8,0},{12,4},{16,24},{20,28},{24,16},{28,20},{1,9},{5... | collective-permute-start | bytes 2150408 | tf_op jit(solution)/shard_map/ppermute | solution.py:455
  479.4 41.3 %collective-permute-start.40 = (bf16[200,1600]{1,0:T(8,128)(2,1)S(1)}, bf16[200,1600]{1,0:T(8,128)(2,1)S(1)}, u32[]{:S(2)}, u32[]{:S(2)}) collective-permute-start(bf16[200,1600]{1,0:T(8,128)(2,1)S(1)} %added.4.a_ref), channel_id=1, source_target_pairs={{2,4},{4,2},{10,12},{12,10},{18,20},{20,18},{26,28},{28,26},{3,5},... | collective-permute-start | bytes 1920008 | tf_op jit(solution)/shard_map/ppermute | solution.py:1094
  487.8 34.1 %collective-permute-start.41 = (bf16[200,1600]{1,0:T(8,128)(2,1)S(1)}, bf16[200,1600]{1,0:T(8,128)(2,1)S(1)}, u32[]{:S(2)}, u32[]{:S(2)}) collective-permute-start(bf16[200,1600]{1,0:T(8,128)(2,1)S(1)} %added.5.a_ref), channel_id=1, source_target_pairs={{2,4},{4,2},{10,12},{12,10},{18,20},{20,18},{26,28},{28,26},{3,5},... | collective-permute-start | bytes 1920008 | tf_op jit(solution)/shard_map/ppermute | solution.py:1094
  496.0 24.0 %collective-permute-start.39 = (bf16[200,896]{1,0:T(8,128)(2,1)S(1)}, bf16[200,896]{1,0:T(8,128)(2,1)S(1)}, u32[]{:S(2)}, u32[]{:S(2)}) collective-permute-start(bf16[200,896]{1,0:T(8,128)(2,1)S(1)} %bitcast.125), channel_id=1, source_target_pairs={{0,16},{4,20},{8,24},{12,28},{16,0},{20,4},{24,8},{28,12},{1,17},{... | collective-permute-start | bytes 1075208 | tf_op jit(solution)/shard_map/ppermute | solution.py:455
  517.5 47.8 %collective-permute-start.43 = (bf16[200,896]{1,0:T(8,128)(2,1)S(1)}, bf16[200,896]{1,0:T(8,128)(2,1)S(1)}, u32[]{:S(2)}, u32[]{:S(2)}) collective-permute-start(bf16[200,896]{1,0:T(8,128)(2,1)S(1)} %bitcast.124), channel_id=1, source_target_pairs={{0,16},{4,20},{8,24},{12,28},{16,0},{20,4},{24,8},{28,12},{1,17},{... | collective-permute-start | bytes 1075208 | tf_op jit(solution)/shard_map/ppermute | solution.py:455
  521.3 58.4 %collective-permute-start.46 = (bf16[200,1600]{1,0:T(8,128)(2,1)S(1)}, bf16[200,1600]{1,0:T(8,128)(2,1)}, u32[]{:S(2)}, u32[]{:S(2)}) collective-permute-start(bf16[200,1600]{1,0:T(8,128)(2,1)S(1)} %chosen.4.a_ref), channel_id=1, source_target_pairs={{0,16},{4,20},{8,24},{12,28},{16,0},{20,4},{24,8},{28,12},{1,17},{... | collective-permute-start | bytes 1920008 | tf_op jit(solution)/shard_map/ppermute | solution.py:455
  522.5 79.2 %collective-permute-start.50 = (bf16[200,1600]{1,0:T(8,128)(2,1)S(1)}, bf16[200,1600]{1,0:T(8,128)(2,1)}, u32[]{:S(2)}, u32[]{:S(2)}) collective-permute-start(bf16[200,1600]{1,0:T(8,128)(2,1)S(1)} %chosen.5.a_ref), channel_id=1, source_target_pairs={{0,16},{4,20},{8,24},{12,28},{16,0},{20,4},{24,8},{28,12},{1,17},{... | collective-permute-start | bytes 1920008 | tf_op jit(solution)/shard_map/ppermute | solution.py:455
  525.0 42.4 %collective-permute-start.44 = (bf16[200,896]{1,0:T(8,128)(2,1)S(1)}, bf16[200,896]{1,0:T(8,128)(2,1)S(1)}, u32[]{:S(2)}, u32[]{:S(2)}) collective-permute-start(bf16[200,896]{1,0:T(8,128)(2,1)S(1)} %added.6.a_ref), channel_id=1, source_target_pairs={{2,4},{4,2},{10,12},{12,10},{18,20},{20,18},{26,28},{28,26},{3,5},... | collective-permute-start | bytes 1075208 | tf_op jit(solution)/shard_map/ppermute | solution.py:1094
  565.9 16.0 %collective-permute-start.47 = (bf16[200,896]{1,0:T(8,128)(2,1)S(1)}, bf16[200,896]{1,0:T(8,128)(2,1)}, u32[]{:S(2)}, u32[]{:S(2)}) collective-permute-start(bf16[200,896]{1,0:T(8,128)(2,1)S(1)} %added.7.a_ref), channel_id=1, source_target_pairs={{2,4},{4,2},{10,12},{12,10},{18,20},{20,18},{26,28},{28,26},{3,5},... | collective-permute-start | bytes 1075208 | tf_op jit(solution)/shard_map/ppermute | solution.py:1094
  576.7 13.5 %collective-permute-start.48 = (f32[16,1600]{1,0:T(8,128)S(1)}, f32[16,1600]{1,0:T(8,128)S(1)}, u32[]{:S(2)}, u32[]{:S(2)}) collective-permute-start(f32[16,1600]{1,0:T(8,128)S(1)} %sums_added.4.a_ref), channel_id=1, source_target_pairs={{0,8},{4,12},{8,0},{12,4},{16,24},{20,28},{24,16},{28,20},{1,9},{5... | collective-permute-start | bytes 307208 | tf_op jit(solution)/shard_map/ppermute | solution.py:455
  576.8 14.0 %collective-permute-start.49 = (f32[8,768]{1,0:T(8,128)S(1)}, f32[8,768]{1,0:T(8,128)S(1)}, u32[]{:S(2)}, u32[]{:S(2)}) collective-permute-start(f32[8,768]{1,0:T(8,128)S(1)} %get-tuple-element.220.a_ref), channel_id=1, source_target_pairs={{0,2},{2,0},{1,3},{3,1},{4,6},{6,4},{5,7},{7,5},{8,10},{10,8},{9,1... | collective-permute-start | bytes 73736 | tf_op jit(solution)/shard_map/ppermute | solution.py:447
  583.5 25.4 %collective-permute-start.51 = (bf16[200,896]{1,0:T(8,128)(2,1)S(1)}, bf16[200,896]{1,0:T(8,128)(2,1)S(1)}, u32[]{:S(2)}, u32[]{:S(2)}) collective-permute-start(bf16[200,896]{1,0:T(8,128)(2,1)S(1)} %chosen.7.a_ref), channel_id=1, source_target_pairs={{0,16},{4,20},{8,24},{12,28},{16,0},{20,4},{24,8},{28,12},{1,17},{... | collective-permute-start | bytes 1075208 | tf_op jit(solution)/shard_map/ppermute | solution.py:455
  585.5 81.3 %collective-permute-start.58 = (bf16[2,200,1600]{2,1,0:T(8,128)(2,1)S(1)}, bf16[2,200,1600]{2,1,0:T(8,128)(2,1)}, u32[]{:S(2)}, u32[]{:S(2)}) collective-permute-start(bf16[2,200,1600]{2,1,0:T(8,128)(2,1)S(1)} %paired.10.a_ref), channel_id=1, source_target_pairs={{0,4},{4,0},{8,12},{12,8},{16,20},{20,16},{24,28},{28,24},{1,5},{5... | collective-permute-start | bytes 3840008 | tf_op jit(solution)/shard_map/ppermute | solution.py:455
  603.5 68.1 %collective-permute-start.59 = (bf16[2,200,1600]{2,1,0:T(8,128)(2,1)S(1)}, bf16[2,200,1600]{2,1,0:T(8,128)(2,1)S(1)}, u32[]{:S(2)}, u32[]{:S(2)}) collective-permute-start(bf16[2,200,1600]{2,1,0:T(8,128)(2,1)S(1)} %paired.11.a_ref), channel_id=1, source_target_pairs={{0,8},{4,12},{8,0},{12,4},{16,24},{20,28},{24,16},{28,20},{1,9},{5... | collective-permute-start | bytes 3840008 | tf_op jit(solution)/shard_map/ppermute | solution.py:455
  603.5 34.9 %collective-permute-start.52 = (bf16[200,896]{1,0:T(8,128)(2,1)S(1)}, bf16[200,896]{1,0:T(8,128)(2,1)S(1)}, u32[]{:S(2)}, u32[]{:S(2)}) collective-permute-start(bf16[200,896]{1,0:T(8,128)(2,1)S(1)} %chosen.6.a_ref), channel_id=1, source_target_pairs={{0,16},{4,20},{8,24},{12,28},{16,0},{20,4},{24,8},{28,12},{1,17},{... | collective-permute-start | bytes 1075208 | tf_op jit(solution)/shard_map/ppermute | solution.py:455
  609.6 34.2 %collective-permute-start.53 = (bf16[2,200,896]{2,1,0:T(8,128)(2,1)S(1)}, bf16[2,200,896]{2,1,0:T(8,128)(2,1)S(1)}, u32[]{:S(2)}, u32[]{:S(2)}) collective-permute-start(bf16[2,200,896]{2,1,0:T(8,128)(2,1)S(1)} %paired.12.a_ref), channel_id=1, source_target_pairs={{0,4},{4,0},{8,12},{12,8},{16,20},{20,16},{24,28},{28,24},{1,5},{5... | collective-permute-start | bytes 2150408 | tf_op jit(solution)/shard_map/ppermute | solution.py:455
  639.1 23.5 %collective-permute-start.55 = (bf16[2,200,896]{2,1,0:T(8,128)(2,1)S(1)}, bf16[2,200,896]{2,1,0:T(8,128)(2,1)S(1)}, u32[]{:S(2)}, u32[]{:S(2)}) collective-permute-start(bf16[2,200,896]{2,1,0:T(8,128)(2,1)S(1)} %paired.13.a_ref), channel_id=1, source_target_pairs={{0,8},{4,12},{8,0},{12,4},{16,24},{20,28},{24,16},{28,20},{1,9},{5... | collective-permute-start | bytes 2150408 | tf_op jit(solution)/shard_map/ppermute | solution.py:455
  643.4 4.7 collective-permute-start.54
  648.6 15.3 %collective-permute-start.56 = (f32[16,1600]{1,0:T(8,128)S(1)}, f32[16,1600]{1,0:T(8,128)S(1)}, u32[]{:S(2)}, u32[]{:S(2)}) collective-permute-start(f32[16,1600]{1,0:T(8,128)S(1)} %sums_added.6.a_ref), channel_id=1, source_target_pairs={{0,16},{4,20},{8,24},{12,28},{16,0},{20,4},{24,8},{28,12},{1,17},{... | collective-permute-start | bytes 307208 | tf_op jit(solution)/shard_map/ppermute | solution.py:455
  648.7 44.6 %collective-permute-start.60 = (bf16[2,2,200,896]{3,2,1,0:T(8,128)(2,1)S(1)}, bf16[2,2,200,896]{3,2,1,0:T(8,128)(2,1)S(1)}, u32[]{:S(2)}, u32[]{:S(2)}) collective-permute-start(bf16[2,2,200,896]{3,2,1,0:T(8,128)(2,1)S(1)} %paired.14.a_ref.c_ref), channel_id=1, source_target_pairs={{0,8},{4,12},{8,0},{12,4},{16,24},{20,28},{24,16},{28,20},{1,9},{5... | collective-permute-start | bytes 4300808 | tf_op jit(solution)/shard_map/ppermute | solution.py:455
  663.4 34.4 %collective-permute-start.61 = (bf16[2,2,200,896]{3,2,1,0:T(8,128)(2,1)S(1)}, bf16[2,2,200,896]{3,2,1,0:T(8,128)(2,1)S(1)}, u32[]{:S(2)}, u32[]{:S(2)}) collective-permute-start(bf16[2,2,200,896]{3,2,1,0:T(8,128)(2,1)S(1)} %paired.15.a_ref.c_ref), channel_id=1, source_target_pairs={{0,4},{4,0},{8,12},{12,8},{16,20},{20,16},{24,28},{28,24},{1,5},{5... | collective-permute-start | bytes 4300808 | tf_op jit(solution)/shard_map/ppermute | solution.py:455
  664.5 7.1 collective-permute-start.57
  671.5 77.7 %collective-permute-start.66 = (bf16[2,2,200,1600]{3,2,1,0:T(8,128)(2,1)}, bf16[2,2,200,1600]{3,2,1,0:T(8,128)(2,1)}, u32[]{:S(2)}, u32[]{:S(2)}) collective-permute-start(bf16[2,2,200,1600]{3,2,1,0:T(8,128)(2,1)} %paired.16.a_ref.c_ref), channel_id=1, source_target_pairs={{0,8},{4,12},{8,0},{12,4},{16,24},{20,28},{24,16},{28,20},{1,9},{5... | collective-permute-start | bytes 7680008 | tf_op jit(solution)/shard_map/ppermute | solution.py:455
  674.2 83.9 %collective-permute-start.67 = (bf16[2,2,200,1600]{3,2,1,0:T(8,128)(2,1)}, bf16[2,2,200,1600]{3,2,1,0:T(8,128)(2,1)}, u32[]{:S(2)}, u32[]{:S(2)}) collective-permute-start(bf16[2,2,200,1600]{3,2,1,0:T(8,128)(2,1)} %paired.17.a_ref.c_ref), channel_id=1, source_target_pairs={{0,4},{4,0},{8,12},{12,8},{16,20},{20,16},{24,28},{28,24},{1,5},{5... | collective-permute-start | bytes 7680008 | tf_op jit(solution)/shard_map/ppermute | solution.py:455
  701.2 25.3 %collective-permute-start.64 = (bf16[800,768]{1,0:T(8,128)(2,1)}, bf16[800,768]{1,0:T(8,128)(2,1)}, u32[]{:S(2)}, u32[]{:S(2)}) collective-permute-start(bf16[800,768]{1,0:T(8,128)(2,1)} %half_rows.3), channel_id=1, source_target_pairs={{0,2},{2,0},{1,3},{3,1},{4,6},{6,4},{5,7},{7,5},{8,10},{10,8},{9,1... | collective-permute-start | bytes 3686408 | tf_op jit(solution)/shard_map/ppermute | solution.py:447
  (91 other events, 930.2 us)

commit v5 on v4

--- a/solution.py
+++ b/solution.py
@@ -1345,10 +1345,10 @@
     mark = [whole]
     block_out = block_result(after(x_mid, *mark), proj_part, block_other, columns)
     mark = [block_out]
+    fc_weight_grad = fc_total.wide(*mark)
+    mark = [fc_weight_grad]
     proj_weight_grad = proj_total.wide(*mark).T
     mark = [proj_weight_grad]
-    fc_weight_grad = fc_total.wide(*mark)
-    mark = [fc_weight_grad]
 
     own = half_of(r, packed, 1)
     fc_bias_grad = ordered(r, packed[8], packed_peer[8], 0)

time: 772 us -> 776 us (level)
  no operation moved by 1% of the time
where the time goes in v5:
time: 776 us; the launch traced here: 772 us
  Pallas kernels  378 us (49%)
  waiting for transfers between devices  246 us (32%)
  starting transfers between devices  81.2 us (10%)
  local copies, waits for them, and re-layouts  46.9 us (6%)
  other arithmetic  17 us (2%)
    pallas_call x69, Pallas kernels, call(): pl.pallas_call(body, grid_spec=pltpu.PrefetchScalarGridSpec(num_scalar_pr...  302 us
    ppermute x36, waiting for transfers between devices, dp_xor(): lax.ppermute(value, 'dp', [(i, i ^ mask) for i in range(lax.axis_size('dp...  220 us
    ppermute x36, starting transfers between devices, dp_xor(): lax.ppermute(value, 'dp', [(i, i ^ mask) for i in range(lax.axis_size('dp...  55.1 us
    unnamed x174, local copies, waits for them, and re-layouts  33.6 us
    pallas_call x1, Pallas kernels, attend(): pl.pallas_call(functools.partial(attend_kernel, heads, blocks), grid_spec...  31.5 us
    pallas_call x1, Pallas kernels, attend_back(): pl.pallas_call(functools.partial(attend_back_kernel, heads, blocks), grid...  30.7 us
    ppermute x13, starting transfers between devices, row_swap(): return lax.ppermute(value, 'row', SWAP)  19.9 us
    ppermute x15, waiting for transfers between devices, col_swap(): return lax.ppermute(value, 'col', SWAP)  15.7 us
  transfers between devices with their start and end apart: 68, of which 31 were waited for; matrix products, arithmetic and copies ran while one was open for 4% of the time, Pallas kernels for 42%

profile of v5, /device:TPU:0, one launch (start us, length us, event | category | flops | bytes accessed | tf_op | source)
XLA Modules:
  0.0 771.5 jit_solution(4205255849777044429)
XLA Ops:
  9.5 3.9 pack_heads.1
  20.2 4.1 pack.1
  27.1 5.3 own_rows.3.h_ref
  35.8 5.2 own_rows.4.h_ref
  41.0 7.6 collective-permute-done.5.refs_2_
  50.6 5.3 own_rows.5.h_ref
  60.7 3.4 norm_one.1
  64.1 4.5 all_rows.3
  74.6 13.0 %project.1.q_ref.k_ref.v_ref = bf16[1344,1536]{1,0:T(8,128)(2,1)S(1)} custom-call(s32[8]{0:T(128)S(1)} %copy-done.41, bf16[3,1600,448]{2,1,0:T(8,128)(2,1)} %bitcast.65, bf16[1600,768]{1,0:T(8,128)(2,1)S(1)} %get-tuple-element.148.own_ref, bf16[1600,768]{1,0:T(8,128)(2,1)} %collective-permute-done.9.other_ref, f32[3,448,1]{2,1,0:T(8,128)S(1)} %copy-done.39), custom_call_target="tpu_custom_call" | custom-call | tf_op jit(solution)/shard_map/project/pallas_call | solution.py:215
  92.2 31.5 %attend.1 = (bf16[448,1536]{1,0:T(8,128)(2,1)S(1)}, f32[8,1536]{1,0:T(8,128)S(1)}) custom-call(s32[7]{0:T(128)S(1)} %pad_add_fusion.info_ref, bf16[1344,1536]{1,0:T(8,128)(2,1)S(1)} %project.1.q_ref.k_ref.v_ref, bf16[1344,1536]{1,0:T(8,128)(2,1)S(1)} %project.1.q_ref.k_ref.v_ref, bf16[1344,1536]{1,0:T(8,128)(2,1)S(1)} %project.1.q_ref.k_ref.v_ref, ...), custom_call_target="tpu_custom_call" | custom-call | tf_op jit(solution)/shard_map/attend/pallas_call | solution.py:90
  127.2 4.7 collective-permute-done.13.refs_0_
  138.4 14.9 %collective-permute-done.14.refs_1_ = bf16[200,1600]{1,0:T(8,128)(2,1)S(1)} collective-permute-done((bf16[200,1600]{1,0:T(8,128)(2,1)}, bf16[200,1600]{1,0:T(8,128)(2,1)S(1)}, u32[]{:S(2)}, u32[]{:S(2)}) %collective-permute-start.14) | collective-permute-done | bytes 640032 | tf_op jit(solution)/shard_map/ppermute | solution.py:455
  156.9 11.8 %collective-permute-done.15.refs_2_ = bf16[200,1600]{1,0:T(8,128)(2,1)S(1)} collective-permute-done((bf16[200,1600]{1,0:T(8,128)(2,1)}, bf16[200,1600]{1,0:T(8,128)(2,1)S(1)}, u32[]{:S(2)}, u32[]{:S(2)}) %collective-permute-start.15) | collective-permute-done | bytes 640032 | tf_op jit(solution)/shard_map/ppermute | solution.py:455
  168.7 13.1 %collective-permute-done.16.refs_3_ = bf16[200,1600]{1,0:T(8,128)(2,1)S(1)} collective-permute-done((bf16[200,1600]{1,0:T(8,128)(2,1)S(1)}, bf16[200,1600]{1,0:T(8,128)(2,1)S(1)}, u32[]{:S(2)}, u32[]{:S(2)}) %collective-permute-start.16) | collective-permute-done | bytes 640032 | tf_op jit(solution)/shard_map/ppermute | solution.py:455
  182.6 4.9 all_rows.4
  187.5 4.5 all_rows.5
  192.1 6.2 norm_two.1
  198.8 4.2 collective-permute-done.21.other_ref
  203.0 19.2 %hidden.1 = (bf16[1600,1536]{1,0:T(8,128)(2,1)S(1)}, f32[1600,1536]{1,0:T(8,128)}) custom-call(s32[8]{0:T(128)S(1)} %copy-done.42, bf16[1600,1600]{1,0:T(8,128)(2,1)} %bitcast.55, bf16[1600,768]{1,0:T(8,128)(2,1)S(1)} %get-tuple-element.165.own_ref, bf16[1600,768]{1,0:T(8,128)(2,1)S(1)} %collective-permute-done.21.other_ref, f32[1600,8]{1,0:T(8,128)S(1)} %bitcast.87), custom_call_target="tpu_custom_call" | custom-call | tf_op jit(solution)/shard_map/hidden/pallas_call | solution.py:215
  222.2 5.5 collective-permute-done.22.b_ref
  230.0 4.7 collective-permute-done.23.other_ref
  236.1 17.1 %hidden_back.1 = (bf16[1600,1536]{1,0:T(8,128)(2,1)}, f32[1600,128]{1,0:T(8,128)}) custom-call(s32[8]{0:T(128)} %fusion.14.s_ref._, bf16[1600,1600]{1,0:T(8,128)(2,1)} %bitcast.60, bf16[1600,768]{1,0:T(8,128)(2,1)} %bitcast.77, bf16[1600,768]{1,0:T(8,128)(2,1)} %copy-done.62, f32[1600,1536]{1,0:T(8,128)} %get-tuple-element.169.s_ref), custom_call_target="tpu_custom_call" | custom-call | tf_op jit(solution)/shard_map/hidden_back/pallas_call | solution.py:215
  255.6 6.8 mapped.8
  262.5 11.3 %weight_grad.8 = bf16[4,200,1600]{2,1,0:T(8,128)(2,1)} custom-call(s32[8]{0:T(128)} %fusion.14.s_ref._, bf16[8,200,768]{2,1,0:T(8,128)(2,1)} %bitcast.96, bf16[8,200,768]{2,1,0:T(8,128)(2,1)} %bitcast.98, bf16[1600,1536]{1,0:T(8,128)(2,1)} %get-tuple-element.177.t_ref.refs_2_), custom_call_target="tpu_custom_call" | custom-call | tf_op jit(solution)/shard_map/weight_grad/pallas_call | solution.py:215
  275.5 8.6 %mapped.9.low_ref = bf16[1600,768]{1,0:T(8,128)(2,1)} custom-call(s32[8]{0:T(128)S(1)} %copy-done.44, bf16[1600,1600]{1,0:T(8,128)(2,1)} %bitcast.56, bf16[1600,1536]{1,0:T(8,128)(2,1)S(1)} %bitcast.75, bf16[1600,768]{1,0:T(8,128)(2,1)} %collective-permute-done.24.refs_0_), custom_call_target="tpu_custom_call" | custom-call | tf_op jit(solution)/shard_map/mapped/pallas_call | solution.py:215
  284.6 10.0 %weight_grad.9 = bf16[2,400,1600]{2,1,0:T(8,128)(2,1)} custom-call(s32[8]{0:T(128)} %fusion.14.s_ref._, bf16[4,400,768]{2,1,0:T(8,128)(2,1)} %bitcast.78, bf16[4,400,768]{2,1,0:T(8,128)(2,1)} %bitcast.126, bf16[1600,1536]{1,0:T(8,128)(2,1)} %copy-done.6), custom_call_target="tpu_custom_call" | custom-call | tf_op jit(solution)/shard_map/weight_grad/pallas_call | solution.py:215
  298.8 6.8 mapped.10
  305.6 9.4 %weight_grad.10 = bf16[2,400,1600]{2,1,0:T(8,128)(2,1)} custom-call(s32[8]{0:T(128)} %fusion.14.s_ref._, bf16[4,400,768]{2,1,0:T(8,128)(2,1)} %bitcast.79, bf16[4,400,768]{2,1,0:T(8,128)(2,1)} %bitcast.127, bf16[1600,1536]{1,0:T(8,128)(2,1)} %copy-done.6), custom_call_target="tpu_custom_call" | custom-call | tf_op jit(solution)/shard_map/weight_grad/pallas_call | solution.py:215
  315.0 10.9 %weight_grad.11 = bf16[4,200,1600]{2,1,0:T(8,128)(2,1)} custom-call(s32[8]{0:T(128)} %fusion.14.s_ref._, bf16[8,200,768]{2,1,0:T(8,128)(2,1)} %bitcast.97, bf16[8,200,768]{2,1,0:T(8,128)(2,1)} %bitcast.99, bf16[1600,1536]{1,0:T(8,128)(2,1)} %get-tuple-element.177.t_ref.refs_2_), custom_call_target="tpu_custom_call" | custom-call | tf_op jit(solution)/shard_map/weight_grad/pallas_call | solution.py:215
  325.9 8.3 %collective-permute-done.25.b_ref.d_ref = bf16[2,2,200,1600]{3,2,1,0:T(8,128)(2,1)} collective-permute-done((bf16[2,2,200,1600]{3,2,1,0:T(8,128)(2,1)}, bf16[2,2,200,1600]{3,2,1,0:T(8,128)(2,1)}, u32[]{:S(2)}, u32[]{:S(2)}) %collective-permute-start.25) | collective-permute-done | bytes 2560032 | tf_op jit(solution)/shard_map/ppermute | solution.py:455
  339.7 10.2 %norm_two_back.1 = (f32[1600,768]{1,0:T(8,128)}, bf16[1600,768]{1,0:T(8,128)(2,1)S(1)}, f32[3,1600,128]{2,1,0:T(8,128)S(1)}) custom-call(s32[8]{0:T(128)S(1)} %copy-done.46, bf16[1600,768]{1,0:T(8,128)(2,1)} %mapped.9.low_ref, bf16[1600,768]{1,0:T(8,128)(2,1)} %collective-permute-done.26.other_ref, bf16[1600,768]{1,0:T(8,128)(2,1)S(1)} %bitcast.80, ...), custom_call_target="tpu_custom_call" | custom-call | tf_op jit(solution)/shard_map/norm_two_back/pallas_call | solution.py:215
  354.4 3.3 halved.9
  359.5 3.5 attended_back.1.g_ref
  363.0 30.7 %attend_back.1.p_ref.refs_5_.refs_2_ = bf16[1344,1536]{1,0:T(8,128)(2,1)S(1)} custom-call(s32[7]{0:T(128)S(1)} %pad_add_fusion.info_ref, bf16[1344,1536]{1,0:T(8,128)(2,1)S(1)} %copy-done.4, bf16[1344,1536]{1,0:T(8,128)(2,1)S(1)} %copy-done.4, bf16[1344,1536]{1,0:T(8,128)(2,1)S(1)} %copy-done.4, bf16[448,1536]{1,0:T(8,128)(2,1)S(1)} %copy-done.13, ...), custom_call_target="tpu_custom_call" | custom-call | tf_op jit(solution)/shard_map/attend_back/pallas_call | solution.py:178
  393.8 6.4 mapped_three.2
  400.3 7.6 weight_grad.12
  414.8 7.2 weight_grad.13
  424.1 4.7 collective-permute-start.35
  428.8 7.5 mapped.11.a_ref.p_ref
  437.7 7.5 weight_grad.14
  452.6 7.0 mapped_three.3.a_ref.m_ref
  464.5 6.9 weight_grad.15
  480.1 6.8 collective-permute-done.36.b_ref
  489.3 6.0 collective-permute-done.37.b_ref.d_ref
  496.1 5.4 collective-permute-start.39
  501.5 15.9 %collective-permute-done.38.b_ref.d_ref = bf16[2,200,896]{2,1,0:T(8,128)(2,1)S(1)} collective-permute-done((bf16[2,200,896]{2,1,0:T(8,128)(2,1)S(1)}, bf16[2,200,896]{2,1,0:T(8,128)(2,1)S(1)}, u32[]{:S(2)}, u32[]{:S(2)}) %collective-permute-start.38) | collective-permute-done | bytes 716832 | tf_op jit(solution)/shard_map/ppermute | solution.py:455
  518.1 4.7 collective-permute-start.43
  530.7 37.3 %collective-permute-done.43.b_ref = bf16[200,896]{1,0:T(8,128)(2,1)S(1)} collective-permute-done((bf16[200,896]{1,0:T(8,128)(2,1)S(1)}, bf16[200,896]{1,0:T(8,128)(2,1)S(1)}, u32[]{:S(2)}, u32[]{:S(2)}) %collective-permute-start.43) | collective-permute-done | bytes 358432 | tf_op jit(solution)/shard_map/ppermute | solution.py:455
  572.6 5.0 packed_sums.1.a_ref
  589.6 3.3 collective-permute-done.48.b_ref
  593.6 3.4 norm_one_back.1
  596.9 7.5 collective-permute-done.50.b_ref
  612.3 28.8 %collective-permute-done.52.b_ref = bf16[200,896]{1,0:T(8,128)(2,1)S(1)} collective-permute-done((bf16[200,896]{1,0:T(8,128)(2,1)S(1)}, bf16[200,896]{1,0:T(8,128)(2,1)S(1)}, u32[]{:S(2)}, u32[]{:S(2)}) %collective-permute-start.52) | collective-permute-done | bytes 358432 | tf_op jit(solution)/shard_map/ppermute | solution.py:455
  641.8 4.3 collective-permute-start.55
  652.6 12.7 %collective-permute-done.55.b_ref = bf16[2,200,896]{2,1,0:T(8,128)(2,1)S(1)} collective-permute-done((bf16[2,200,896]{2,1,0:T(8,128)(2,1)S(1)}, bf16[2,200,896]{2,1,0:T(8,128)(2,1)S(1)}, u32[]{:S(2)}, u32[]{:S(2)}) %collective-permute-start.55) | collective-permute-done | bytes 716832 | tf_op jit(solution)/shard_map/ppermute | solution.py:455
  669.6 4.8 paired.16.a_ref.c_ref
  680.0 16.0 %collective-permute-done.60.b_ref.d_ref = bf16[2,2,200,896]{3,2,1,0:T(8,128)(2,1)S(1)} collective-permute-done((bf16[2,2,200,896]{3,2,1,0:T(8,128)(2,1)S(1)}, bf16[2,2,200,896]{3,2,1,0:T(8,128)(2,1)S(1)}, u32[]{:S(2)}, u32[]{:S(2)}) %collective-permute-start.60) | collective-permute-done | bytes 1433632 | tf_op jit(solution)/shard_map/ppermute | solution.py:455
  697.2 3.3 collective-permute-done.61.b_ref.d_ref
  717.6 4.1 copy.52
  721.7 7.5 pad_maximum_fusion
  731.6 3.9 block_result.1
  735.5 18.6 %collective-permute-done.66.b_ref.d_ref = bf16[2,2,200,1600]{3,2,1,0:T(8,128)(2,1)} collective-permute-done((bf16[2,2,200,1600]{3,2,1,0:T(8,128)(2,1)}, bf16[2,2,200,1600]{3,2,1,0:T(8,128)(2,1)}, u32[]{:S(2)}, u32[]{:S(2)}) %collective-permute-start.66) | collective-permute-done | bytes 2560032 | tf_op jit(solution)/shard_map/ppermute | solution.py:455
  754.1 8.5 %widened.2 = f32[800,3200]{1,0:T(8,128)} custom-call(s32[8]{0:T(128)S(1)} %copy-done.50, bf16[2,2,200,1600]{3,2,1,0:T(8,128)(2,1)} %paired.17.a_ref.c_ref, bf16[2,2,200,1600]{3,2,1,0:T(8,128)(2,1)} %collective-permute-done.66.b_ref.d_ref, bf16[2,2,200,1600]{3,2,1,0:T(8,128)(2,1)} %paired.17.a_ref.c_ref, ...), custom_call_target="tpu_custom_call" | custom-call | tf_op jit(solution)/shard_map/widened/pallas_call | solution.py:215
  762.6 8.8 %widened.3 = f32[800,3200]{1,0:T(8,128)} custom-call(s32[8]{0:T(128)S(1)} %copy-done.50, bf16[2,2,200,1600]{3,2,1,0:T(8,128)(2,1)} %paired.16.a_ref.c_ref, bf16[2,2,200,1600]{3,2,1,0:T(8,128)(2,1)} %collective-permute-done.67.b_ref.d_ref, bf16[2,2,200,1600]{3,2,1,0:T(8,128)(2,1)} %paired.16.a_ref.c_ref, ...), custom_call_target="tpu_custom_call" | custom-call | tf_op jit(solution)/shard_map/widened/pallas_call | solution.py:215
  (378 shorter events, 184.2 us)
Async XLA Ops:
  2.0 6.4 collective-permute-start
  14.6 17.8 %collective-permute-start.3 = (bf16[3,200,448]{2,1,0:T(8,128)(2,1)}, bf16[3,200,448]{2,1,0:T(8,128)(2,1)}, u32[]{:S(2)}, u32[]{:S(2)}) collective-permute-start(bf16[3,200,448]{2,1,0:T(8,128)(2,1)} %pack_heads.1), channel_id=1, source_target_pairs={{0,2},{2,0},{1,3},{3,1},{4,6},{6,4},{5,7},{7,5},{8,10},{10,8},{9,1... | collective-permute-start | bytes 1612808 | tf_op jit(solution)/shard_map/ppermute | solution.py:447
  17.0 7.3 collective-permute-start.2
  17.3 16.8 %collective-permute-start.6 = (bf16[2,32]{1,0:T(2,128)(2,1)S(1)}, bf16[2,32]{1,0:T(2,128)(2,1)S(1)}, u32[]{:S(2)}, u32[]{:S(2)}) collective-permute-start(bf16[2,32]{1,0:T(2,128)(2,1)S(1)} %slice.115), channel_id=1, source_target_pairs={{0,1},{1,0},{2,3},{3,2},{4,5},{5,4},{6,7},{7,6},{8,9},{9,8},{10,11... | collective-permute-start | bytes 392 | tf_op jit(solution)/shard_map/ppermute | solution.py:451
  18.0 32.1 %collective-permute-start.7 = (bf16[5,800]{1,0:T(8,128)(2,1)S(1)}, bf16[5,800]{1,0:T(8,128)(2,1)S(1)}, u32[]{:S(2)}, u32[]{:S(2)}) collective-permute-start(bf16[5,800]{1,0:T(8,128)(2,1)S(1)} %stack.37), channel_id=1, source_target_pairs={{0,2},{2,0},{1,3},{3,1},{4,6},{6,4},{5,7},{7,5},{8,10},{10,8},{9,1... | collective-permute-start | bytes 24008 | tf_op jit(solution)/shard_map/ppermute | solution.py:447
  18.2 40.2 %collective-permute-start.1 = (bf16[800,768]{1,0:T(8,128)(2,1)S(1)}, bf16[800,768]{1,0:T(8,128)(2,1)S(1)}, u32[]{:S(2)}, u32[]{:S(2)}) collective-permute-start(bf16[800,768]{1,0:T(8,128)(2,1)S(1)} %bitcast.104), channel_id=1, source_target_pairs={{0,2},{2,0},{1,3},{3,1},{4,6},{6,4},{5,7},{7,5},{8,10},{10,8},{9,1... | collective-permute-start | bytes 3686408 | tf_op jit(solution)/shard_map/ppermute | solution.py:447
  32.4 16.2 %collective-permute-start.5 = (bf16[3,200,448]{2,1,0:T(8,128)(2,1)}, bf16[3,200,448]{2,1,0:T(8,128)(2,1)}, u32[]{:S(2)}, u32[]{:S(2)}) collective-permute-start(bf16[3,200,448]{2,1,0:T(8,128)(2,1)} %collective-permute-done.3.refs_0_), channel_id=1, source_target_pairs={{0,8},{4,12},{8,0},{12,4},{16,24},{20,28},{24,16},{28,20},{1,9},{5... | collective-permute-start | bytes 1612808 | tf_op jit(solution)/shard_map/ppermute | solution.py:455
  34.3 16.2 %collective-permute-start.4 = (bf16[3,200,448]{2,1,0:T(8,128)(2,1)}, bf16[3,200,448]{2,1,0:T(8,128)(2,1)}, u32[]{:S(2)}, u32[]{:S(2)}) collective-permute-start(bf16[3,200,448]{2,1,0:T(8,128)(2,1)} %collective-permute-done.3.refs_0_), channel_id=1, source_target_pairs={{0,4},{4,0},{8,12},{12,8},{16,20},{20,16},{24,28},{28,24},{1,5},{5... | collective-permute-start | bytes 1612808 | tf_op jit(solution)/shard_map/ppermute | solution.py:455
  48.6 15.5 %collective-permute-start.8 = (bf16[3,200,448]{2,1,0:T(8,128)(2,1)}, bf16[3,200,448]{2,1,0:T(8,128)(2,1)}, u32[]{:S(2)}, u32[]{:S(2)}) collective-permute-start(bf16[3,200,448]{2,1,0:T(8,128)(2,1)} %collective-permute-done.5.refs_2_), channel_id=1, source_target_pairs={{0,4},{4,0},{8,12},{12,8},{16,20},{20,16},{24,28},{28,24},{1,5},{5... | collective-permute-start | bytes 1612808 | tf_op jit(solution)/shard_map/ppermute | solution.py:455
  68.6 4.9 collective-permute-start.9
  68.7 21.0 %collective-permute-start.10 = (bf16[448,800]{1,0:T(8,128)(2,1)}, bf16[448,800]{1,0:T(8,128)(2,1)}, u32[]{:S(2)}, u32[]{:S(2)}) collective-permute-start(bf16[448,800]{1,0:T(8,128)(2,1)} %get-tuple-element.150), channel_id=1, source_target_pairs={{0,2},{2,0},{1,3},{3,1},{4,6},{6,4},{5,7},{7,5},{8,10},{10,8},{9,1... | collective-permute-start | bytes 2150408 | tf_op jit(solution)/shard_map/ppermute | solution.py:447
  70.4 54.0 %collective-permute-start.12 = (bf16[200,1600]{1,0:T(8,128)(2,1)}, bf16[200,1600]{1,0:T(8,128)(2,1)}, u32[]{:S(2)}, u32[]{:S(2)}) collective-permute-start(bf16[200,1600]{1,0:T(8,128)(2,1)} %get-tuple-element.156), channel_id=1, source_target_pairs={{0,2},{2,0},{1,3},{3,1},{4,6},{6,4},{5,7},{7,5},{8,10},{10,8},{9,1... | collective-permute-start | bytes 1920008 | tf_op jit(solution)/shard_map/ppermute | solution.py:447
  70.8 53.6 %collective-permute-start.11 = (bf16[200,1600]{1,0:T(8,128)(2,1)}, bf16[200,1600]{1,0:T(8,128)(2,1)}, u32[]{:S(2)}, u32[]{:S(2)}) collective-permute-start(bf16[200,1600]{1,0:T(8,128)(2,1)} %get-tuple-element.153), channel_id=1, source_target_pairs={{0,2},{2,0},{1,3},{3,1},{4,6},{6,4},{5,7},{7,5},{8,10},{10,8},{9,1... | collective-permute-start | bytes 1920008 | tf_op jit(solution)/shard_map/ppermute | solution.py:447
  127.1 4.7 collective-permute-start.13
  134.7 57.4 %collective-permute-start.20 = (bf16[1600,768]{1,0:T(8,128)(2,1)S(1)}, bf16[1600,768]{1,0:T(8,128)(2,1)}, u32[]{:S(2)}, u32[]{:S(2)}) collective-permute-start(bf16[1600,768]{1,0:T(8,128)(2,1)S(1)} %mapped.7.low_ref), channel_id=1, source_target_pairs={{0,2},{2,0},{1,3},{3,1},{4,6},{6,4},{5,7},{7,5},{8,10},{10,8},{9,1... | collective-permute-start | bytes 7372808 | tf_op jit(solution)/shard_map/ppermute | solution.py:447
  136.3 16.9 %collective-permute-start.14 = (bf16[200,1600]{1,0:T(8,128)(2,1)}, bf16[200,1600]{1,0:T(8,128)(2,1)S(1)}, u32[]{:S(2)}, u32[]{:S(2)}) collective-permute-start(bf16[200,1600]{1,0:T(8,128)(2,1)} %collective-permute-done.11.refs_0_), channel_id=1, source_target_pairs={{0,4},{4,0},{8,12},{12,8},{16,20},{20,16},{24,28},{28,24},{1,5},{5... | collective-permute-start | bytes 1920008 | tf_op jit(solution)/shard_map/ppermute | solution.py:455
  136.3 18.8 %collective-permute-start.18 = (bf16[200,1600]{1,0:T(8,128)(2,1)}, bf16[200,1600]{1,0:T(8,128)(2,1)}, u32[]{:S(2)}, u32[]{:S(2)}) collective-permute-start(bf16[200,1600]{1,0:T(8,128)(2,1)} %collective-permute-done.12.refs_0_), channel_id=1, source_target_pairs={{0,8},{4,12},{8,0},{12,4},{16,24},{20,28},{24,16},{28,20},{1,9},{5... | collective-permute-start | bytes 1920008 | tf_op jit(solution)/shard_map/ppermute | solution.py:455
  137.9 30.7 %collective-permute-start.15 = (bf16[200,1600]{1,0:T(8,128)(2,1)}, bf16[200,1600]{1,0:T(8,128)(2,1)S(1)}, u32[]{:S(2)}, u32[]{:S(2)}) collective-permute-start(bf16[200,1600]{1,0:T(8,128)(2,1)} %collective-permute-done.11.refs_0_), channel_id=1, source_target_pairs={{0,8},{4,12},{8,0},{12,4},{16,24},{20,28},{24,16},{28,20},{1,9},{5... | collective-permute-start | bytes 1920008 | tf_op jit(solution)/shard_map/ppermute | solution.py:455
  153.3 28.5 %collective-permute-start.16 = (bf16[200,1600]{1,0:T(8,128)(2,1)S(1)}, bf16[200,1600]{1,0:T(8,128)(2,1)S(1)}, u32[]{:S(2)}, u32[]{:S(2)}) collective-permute-start(bf16[200,1600]{1,0:T(8,128)(2,1)S(1)} %collective-permute-done.14.refs_1_), channel_id=1, source_target_pairs={{0,8},{4,12},{8,0},{12,4},{16,24},{20,28},{24,16},{28,20},{1,9},{5... | collective-permute-start | bytes 1920008 | tf_op jit(solution)/shard_map/ppermute | solution.py:455
  154.8 32.7 %collective-permute-start.17 = (bf16[200,1600]{1,0:T(8,128)(2,1)}, bf16[200,1600]{1,0:T(8,128)(2,1)}, u32[]{:S(2)}, u32[]{:S(2)}) collective-permute-start(bf16[200,1600]{1,0:T(8,128)(2,1)} %collective-permute-done.12.refs_0_), channel_id=1, source_target_pairs={{0,4},{4,0},{8,12},{12,8},{16,20},{20,16},{24,28},{28,24},{1,5},{5... | collective-permute-start | bytes 1920008 | tf_op jit(solution)/shard_map/ppermute | solution.py:455
  155.1 32.4 %collective-permute-start.19 = (bf16[200,1600]{1,0:T(8,128)(2,1)}, bf16[200,1600]{1,0:T(8,128)(2,1)}, u32[]{:S(2)}, u32[]{:S(2)}) collective-permute-start(bf16[200,1600]{1,0:T(8,128)(2,1)} %collective-permute-done.18.refs_2_), channel_id=1, source_target_pairs={{0,4},{4,0},{8,12},{12,8},{16,20},{20,16},{24,28},{28,24},{1,5},{5... | collective-permute-start | bytes 1920008 | tf_op jit(solution)/shard_map/ppermute | solution.py:455
  198.3 4.7 collective-permute-start.21
  198.3 29.4 %collective-permute-start.22 = (bf16[800,768]{1,0:T(8,128)(2,1)S(1)}, bf16[800,768]{1,0:T(8,128)(2,1)S(1)}, u32[]{:S(2)}, u32[]{:S(2)}) collective-permute-start(bf16[800,768]{1,0:T(8,128)(2,1)S(1)} %bitcast.115), channel_id=1, source_target_pairs={{0,2},{2,0},{1,3},{3,1},{4,6},{6,4},{5,7},{7,5},{8,10},{10,8},{9,1... | collective-permute-start | bytes 3686408 | tf_op jit(solution)/shard_map/ppermute | solution.py:447
  230.0 4.7 collective-permute-start.23
  262.4 13.1 %collective-permute-start.24 = (bf16[1600,768]{1,0:T(8,128)(2,1)}, bf16[1600,768]{1,0:T(8,128)(2,1)}, u32[]{:S(2)}, u32[]{:S(2)}) collective-permute-start(bf16[1600,768]{1,0:T(8,128)(2,1)} %mapped.8), channel_id=1, source_target_pairs={{0,1},{1,0},{2,3},{3,2},{4,5},{5,4},{6,7},{7,6},{8,9},{9,8},{10,11... | collective-permute-start | bytes 7372808 | tf_op jit(solution)/shard_map/ppermute | solution.py:451
  273.8 60.3 %collective-permute-start.25 = (bf16[2,2,200,1600]{3,2,1,0:T(8,128)(2,1)}, bf16[2,2,200,1600]{3,2,1,0:T(8,128)(2,1)}, u32[]{:S(2)}, u32[]{:S(2)}) collective-permute-start(bf16[2,2,200,1600]{3,2,1,0:T(8,128)(2,1)} %bitcast.138), channel_id=1, source_target_pairs={{0,8},{4,12},{8,0},{12,4},{16,24},{20,28},{24,16},{28,20},{1,9},{5... | collective-permute-start | bytes 7680008 | tf_op jit(solution)/shard_map/ppermute | solution.py:455
  284.0 55.7 %collective-permute-start.26 = (bf16[1600,768]{1,0:T(8,128)(2,1)}, bf16[1600,768]{1,0:T(8,128)(2,1)}, u32[]{:S(2)}, u32[]{:S(2)}) collective-permute-start(bf16[1600,768]{1,0:T(8,128)(2,1)} %mapped.9.low_ref), channel_id=1, source_target_pairs={{0,2},{2,0},{1,3},{3,1},{4,6},{6,4},{5,7},{7,5},{8,10},{10,8},{9,1... | collective-permute-start | bytes 7372808 | tf_op jit(solution)/shard_map/ppermute | solution.py:447
  294.6 59.8 %collective-permute-start.27 = (bf16[2,2,200,1600]{3,2,1,0:T(8,128)(2,1)}, bf16[2,2,200,1600]{3,2,1,0:T(8,128)(2,1)}, u32[]{:S(2)}, u32[]{:S(2)}) collective-permute-start(bf16[2,2,200,1600]{3,2,1,0:T(8,128)(2,1)} %bitcast.137), channel_id=1, source_target_pairs={{0,4},{4,0},{8,12},{12,8},{16,20},{20,16},{24,28},{28,24},{1,5},{5... | collective-permute-start | bytes 7680008 | tf_op jit(solution)/shard_map/ppermute | solution.py:455
  351.3 8.1 %collective-permute-start.28 = (bf16[1600,768]{1,0:T(8,128)(2,1)S(1)}, bf16[1600,768]{1,0:T(8,128)(2,1)S(1)}, u32[]{:S(2)}, u32[]{:S(2)}) collective-permute-start(bf16[1600,768]{1,0:T(8,128)(2,1)S(1)} %get-tuple-element.184.own_ref), channel_id=1, source_target_pairs={{0,1},{1,0},{2,3},{3,2},{4,5},{5,4},{6,7},{7,6},{8,9},{9,8},{10,11... | collective-permute-start | bytes 7372808 | tf_op jit(solution)/shard_map/ppermute | solution.py:451
  351.3 77.4 %collective-permute-start.31 = (bf16[1600,768]{1,0:T(8,128)(2,1)}, bf16[1600,768]{1,0:T(8,128)(2,1)}, u32[]{:S(2)}, u32[]{:S(2)}) collective-permute-start(bf16[1600,768]{1,0:T(8,128)(2,1)} %mapped.10), channel_id=1, source_target_pairs={{0,1},{1,0},{2,3},{3,2},{4,5},{5,4},{6,7},{7,6},{8,9},{9,8},{10,11... | collective-permute-start | bytes 7372808 | tf_op jit(solution)/shard_map/ppermute | solution.py:451
  351.8 56.1 %collective-permute-start.29 = (bf16[2,200,1600]{2,1,0:T(8,128)(2,1)}, bf16[2,200,1600]{2,1,0:T(8,128)(2,1)}, u32[]{:S(2)}, u32[]{:S(2)}) collective-permute-start(bf16[2,200,1600]{2,1,0:T(8,128)(2,1)} %get-tuple-element.190), channel_id=1, source_target_pairs={{0,4},{4,0},{8,12},{12,8},{16,20},{20,16},{24,28},{28,24},{1,5},{5... | collective-permute-start | bytes 3840008 | tf_op jit(solution)/shard_map/ppermute | solution.py:455
  358.8 52.1 %collective-permute-start.30 = (bf16[2,200,1600]{2,1,0:T(8,128)(2,1)}, bf16[2,200,1600]{2,1,0:T(8,128)(2,1)}, u32[]{:S(2)}, u32[]{:S(2)}) collective-permute-start(bf16[2,200,1600]{2,1,0:T(8,128)(2,1)} %get-tuple-element.193), channel_id=1, source_target_pairs={{0,8},{4,12},{8,0},{12,4},{16,24},{20,28},{24,16},{28,20},{1,9},{5... | collective-permute-start | bytes 3840008 | tf_op jit(solution)/shard_map/ppermute | solution.py:455
  400.2 52.4 %collective-permute-start.33 = (bf16[1600,768]{1,0:T(8,128)(2,1)}, bf16[1600,768]{1,0:T(8,128)(2,1)}, u32[]{:S(2)}, u32[]{:S(2)}) collective-permute-start(bf16[1600,768]{1,0:T(8,128)(2,1)} %mapped_three.2), channel_id=1, source_target_pairs={{0,1},{1,0},{2,3},{3,2},{4,5},{5,4},{6,7},{7,6},{8,9},{9,8},{10,11... | collective-permute-start | bytes 7372808 | tf_op jit(solution)/shard_map/ppermute | solution.py:451
  407.9 37.3 %collective-permute-start.32 = (bf16[2,2,200,896]{3,2,1,0:T(8,128)(2,1)}, bf16[2,2,200,896]{3,2,1,0:T(8,128)(2,1)}, u32[]{:S(2)}, u32[]{:S(2)}) collective-permute-start(bf16[2,2,200,896]{3,2,1,0:T(8,128)(2,1)} %bitcast.141), channel_id=1, source_target_pairs={{0,4},{4,0},{8,12},{12,8},{16,20},{20,16},{24,28},{28,24},{1,5},{5... | collective-permute-start | bytes 4300808 | tf_op jit(solution)/shard_map/ppermute | solution.py:455
  422.0 50.6 %collective-permute-start.34 = (bf16[2,2,200,896]{3,2,1,0:T(8,128)(2,1)}, bf16[2,2,200,896]{3,2,1,0:T(8,128)(2,1)}, u32[]{:S(2)}, u32[]{:S(2)}) collective-permute-start(bf16[2,2,200,896]{3,2,1,0:T(8,128)(2,1)} %bitcast.140), channel_id=1, source_target_pairs={{0,4},{4,0},{8,12},{12,8},{16,20},{20,16},{24,28},{28,24},{1,5},{5... | collective-permute-start | bytes 4300808 | tf_op jit(solution)/shard_map/ppermute | solution.py:455
  424.1 53.5 %collective-permute-start.35 = (bf16[200,1600]{1,0:T(8,128)(2,1)}, bf16[200,1600]{1,0:T(8,128)(2,1)}, u32[]{:S(2)}, u32[]{:S(2)}) collective-permute-start(bf16[200,1600]{1,0:T(8,128)(2,1)} %bitcast.123), channel_id=1, source_target_pairs={{0,16},{4,20},{8,24},{12,28},{16,0},{20,4},{24,8},{28,12},{1,17},{... | collective-permute-start | bytes 1920008 | tf_op jit(solution)/shard_map/ppermute | solution.py:455
  428.7 58.1 %collective-permute-start.36 = (bf16[200,1600]{1,0:T(8,128)(2,1)}, bf16[200,1600]{1,0:T(8,128)(2,1)}, u32[]{:S(2)}, u32[]{:S(2)}) collective-permute-start(bf16[200,1600]{1,0:T(8,128)(2,1)} %bitcast.122), channel_id=1, source_target_pairs={{0,16},{4,20},{8,24},{12,28},{16,0},{20,4},{24,8},{28,12},{1,17},{... | collective-permute-start | bytes 1920008 | tf_op jit(solution)/shard_map/ppermute | solution.py:455
  449.4 46.0 %collective-permute-start.37 = (bf16[2,200,896]{2,1,0:T(8,128)(2,1)}, bf16[2,200,896]{2,1,0:T(8,128)(2,1)S(1)}, u32[]{:S(2)}, u32[]{:S(2)}) collective-permute-start(bf16[2,200,896]{2,1,0:T(8,128)(2,1)} %get-tuple-element.209), channel_id=1, source_target_pairs={{0,8},{4,12},{8,0},{12,4},{16,24},{20,28},{24,16},{28,20},{1,9},{5... | collective-permute-start | bytes 2150408 | tf_op jit(solution)/shard_map/ppermute | solution.py:455
  462.3 66.1 %collective-permute-start.42 = (bf16[800,768]{1,0:T(8,128)(2,1)}, bf16[800,768]{1,0:T(8,128)(2,1)S(1)}, u32[]{:S(2)}, u32[]{:S(2)}) collective-permute-start(bf16[800,768]{1,0:T(8,128)(2,1)} %half_rows.2), channel_id=1, source_target_pairs={{0,2},{2,0},{1,3},{3,1},{4,6},{6,4},{5,7},{7,5},{8,10},{10,8},{9,1... | collective-permute-start | bytes 3686408 | tf_op jit(solution)/shard_map/ppermute | solution.py:447
  476.1 41.3 %collective-permute-start.38 = (bf16[2,200,896]{2,1,0:T(8,128)(2,1)S(1)}, bf16[2,200,896]{2,1,0:T(8,128)(2,1)S(1)}, u32[]{:S(2)}, u32[]{:S(2)}) collective-permute-start(bf16[2,200,896]{2,1,0:T(8,128)(2,1)S(1)} %get-tuple-element.212), channel_id=1, source_target_pairs={{0,8},{4,12},{8,0},{12,4},{16,24},{20,28},{24,16},{28,20},{1,9},{5... | collective-permute-start | bytes 2150408 | tf_op jit(solution)/shard_map/ppermute | solution.py:455
  479.4 44.1 %collective-permute-start.40 = (bf16[200,1600]{1,0:T(8,128)(2,1)S(1)}, bf16[200,1600]{1,0:T(8,128)(2,1)S(1)}, u32[]{:S(2)}, u32[]{:S(2)}) collective-permute-start(bf16[200,1600]{1,0:T(8,128)(2,1)S(1)} %added.4.a_ref), channel_id=1, source_target_pairs={{2,4},{4,2},{10,12},{12,10},{18,20},{20,18},{26,28},{28,26},{3,5},... | collective-permute-start | bytes 1920008 | tf_op jit(solution)/shard_map/ppermute | solution.py:1094
  488.6 35.5 %collective-permute-start.41 = (bf16[200,1600]{1,0:T(8,128)(2,1)S(1)}, bf16[200,1600]{1,0:T(8,128)(2,1)S(1)}, u32[]{:S(2)}, u32[]{:S(2)}) collective-permute-start(bf16[200,1600]{1,0:T(8,128)(2,1)S(1)} %added.5.a_ref), channel_id=1, source_target_pairs={{2,4},{4,2},{10,12},{12,10},{18,20},{20,18},{26,28},{28,26},{3,5},... | collective-permute-start | bytes 1920008 | tf_op jit(solution)/shard_map/ppermute | solution.py:1094
  496.1 26.7 %collective-permute-start.39 = (bf16[200,896]{1,0:T(8,128)(2,1)S(1)}, bf16[200,896]{1,0:T(8,128)(2,1)S(1)}, u32[]{:S(2)}, u32[]{:S(2)}) collective-permute-start(bf16[200,896]{1,0:T(8,128)(2,1)S(1)} %bitcast.125), channel_id=1, source_target_pairs={{0,16},{4,20},{8,24},{12,28},{16,0},{20,4},{24,8},{28,12},{1,17},{... | collective-permute-start | bytes 1075208 | tf_op jit(solution)/shard_map/ppermute | solution.py:455
  518.1 50.0 %collective-permute-start.43 = (bf16[200,896]{1,0:T(8,128)(2,1)S(1)}, bf16[200,896]{1,0:T(8,128)(2,1)S(1)}, u32[]{:S(2)}, u32[]{:S(2)}) collective-permute-start(bf16[200,896]{1,0:T(8,128)(2,1)S(1)} %bitcast.124), channel_id=1, source_target_pairs={{0,16},{4,20},{8,24},{12,28},{16,0},{20,4},{24,8},{28,12},{1,17},{... | collective-permute-start | bytes 1075208 | tf_op jit(solution)/shard_map/ppermute | solution.py:455
  524.1 58.4 %collective-permute-start.46 = (bf16[200,1600]{1,0:T(8,128)(2,1)S(1)}, bf16[200,1600]{1,0:T(8,128)(2,1)}, u32[]{:S(2)}, u32[]{:S(2)}) collective-permute-start(bf16[200,1600]{1,0:T(8,128)(2,1)S(1)} %chosen.4.a_ref), channel_id=1, source_target_pairs={{0,16},{4,20},{8,24},{12,28},{16,0},{20,4},{24,8},{28,12},{1,17},{... | collective-permute-start | bytes 1920008 | tf_op jit(solution)/shard_map/ppermute | solution.py:455
  524.8 79.6 %collective-permute-start.50 = (bf16[200,1600]{1,0:T(8,128)(2,1)S(1)}, bf16[200,1600]{1,0:T(8,128)(2,1)}, u32[]{:S(2)}, u32[]{:S(2)}) collective-permute-start(bf16[200,1600]{1,0:T(8,128)(2,1)S(1)} %chosen.5.a_ref), channel_id=1, source_target_pairs={{0,16},{4,20},{8,24},{12,28},{16,0},{20,4},{24,8},{28,12},{1,17},{... | collective-permute-start | bytes 1920008 | tf_op jit(solution)/shard_map/ppermute | solution.py:455
  527.7 42.4 %collective-permute-start.44 = (bf16[200,896]{1,0:T(8,128)(2,1)S(1)}, bf16[200,896]{1,0:T(8,128)(2,1)S(1)}, u32[]{:S(2)}, u32[]{:S(2)}) collective-permute-start(bf16[200,896]{1,0:T(8,128)(2,1)S(1)} %added.6.a_ref), channel_id=1, source_target_pairs={{2,4},{4,2},{10,12},{12,10},{18,20},{20,18},{26,28},{28,26},{3,5},... | collective-permute-start | bytes 1075208 | tf_op jit(solution)/shard_map/ppermute | solution.py:1094
  568.7 16.0 %collective-permute-start.47 = (bf16[200,896]{1,0:T(8,128)(2,1)S(1)}, bf16[200,896]{1,0:T(8,128)(2,1)}, u32[]{:S(2)}, u32[]{:S(2)}) collective-permute-start(bf16[200,896]{1,0:T(8,128)(2,1)S(1)} %added.7.a_ref), channel_id=1, source_target_pairs={{2,4},{4,2},{10,12},{12,10},{18,20},{20,18},{26,28},{28,26},{3,5},... | collective-permute-start | bytes 1075208 | tf_op jit(solution)/shard_map/ppermute | solution.py:1094
  579.5 13.5 %collective-permute-start.48 = (f32[16,1600]{1,0:T(8,128)S(1)}, f32[16,1600]{1,0:T(8,128)S(1)}, u32[]{:S(2)}, u32[]{:S(2)}) collective-permute-start(f32[16,1600]{1,0:T(8,128)S(1)} %sums_added.4.a_ref), channel_id=1, source_target_pairs={{0,8},{4,12},{8,0},{12,4},{16,24},{20,28},{24,16},{28,20},{1,9},{5... | collective-permute-start | bytes 307208 | tf_op jit(solution)/shard_map/ppermute | solution.py:455
  579.5 14.0 %collective-permute-start.49 = (f32[8,768]{1,0:T(8,128)S(1)}, f32[8,768]{1,0:T(8,128)S(1)}, u32[]{:S(2)}, u32[]{:S(2)}) collective-permute-start(f32[8,768]{1,0:T(8,128)S(1)} %get-tuple-element.220.a_ref), channel_id=1, source_target_pairs={{0,2},{2,0},{1,3},{3,1},{4,6},{6,4},{5,7},{7,5},{8,10},{10,8},{9,1... | collective-permute-start | bytes 73736 | tf_op jit(solution)/shard_map/ppermute | solution.py:447
  586.3 24.7 %collective-permute-start.51 = (bf16[200,896]{1,0:T(8,128)(2,1)S(1)}, bf16[200,896]{1,0:T(8,128)(2,1)S(1)}, u32[]{:S(2)}, u32[]{:S(2)}) collective-permute-start(bf16[200,896]{1,0:T(8,128)(2,1)S(1)} %chosen.7.a_ref), channel_id=1, source_target_pairs={{0,16},{4,20},{8,24},{12,28},{16,0},{20,4},{24,8},{28,12},{1,17},{... | collective-permute-start | bytes 1075208 | tf_op jit(solution)/shard_map/ppermute | solution.py:455
  588.2 81.4 %collective-permute-start.58 = (bf16[2,200,1600]{2,1,0:T(8,128)(2,1)S(1)}, bf16[2,200,1600]{2,1,0:T(8,128)(2,1)}, u32[]{:S(2)}, u32[]{:S(2)}) collective-permute-start(bf16[2,200,1600]{2,1,0:T(8,128)(2,1)S(1)} %paired.10.a_ref), channel_id=1, source_target_pairs={{0,4},{4,0},{8,12},{12,8},{16,20},{20,16},{24,28},{28,24},{1,5},{5... | collective-permute-start | bytes 3840008 | tf_op jit(solution)/shard_map/ppermute | solution.py:455
  606.2 68.2 %collective-permute-start.59 = (bf16[2,200,1600]{2,1,0:T(8,128)(2,1)S(1)}, bf16[2,200,1600]{2,1,0:T(8,128)(2,1)S(1)}, u32[]{:S(2)}, u32[]{:S(2)}) collective-permute-start(bf16[2,200,1600]{2,1,0:T(8,128)(2,1)S(1)} %paired.11.a_ref), channel_id=1, source_target_pairs={{0,8},{4,12},{8,0},{12,4},{16,24},{20,28},{24,16},{28,20},{1,9},{5... | collective-permute-start | bytes 3840008 | tf_op jit(solution)/shard_map/ppermute | solution.py:455
  606.3 34.9 %collective-permute-start.52 = (bf16[200,896]{1,0:T(8,128)(2,1)S(1)}, bf16[200,896]{1,0:T(8,128)(2,1)S(1)}, u32[]{:S(2)}, u32[]{:S(2)}) collective-permute-start(bf16[200,896]{1,0:T(8,128)(2,1)S(1)} %chosen.6.a_ref), channel_id=1, source_target_pairs={{0,16},{4,20},{8,24},{12,28},{16,0},{20,4},{24,8},{28,12},{1,17},{... | collective-permute-start | bytes 1075208 | tf_op jit(solution)/shard_map/ppermute | solution.py:455
  611.7 35.0 %collective-permute-start.53 = (bf16[2,200,896]{2,1,0:T(8,128)(2,1)S(1)}, bf16[2,200,896]{2,1,0:T(8,128)(2,1)S(1)}, u32[]{:S(2)}, u32[]{:S(2)}) collective-permute-start(bf16[2,200,896]{2,1,0:T(8,128)(2,1)S(1)} %paired.12.a_ref), channel_id=1, source_target_pairs={{0,4},{4,0},{8,12},{12,8},{16,20},{20,16},{24,28},{28,24},{1,5},{5... | collective-permute-start | bytes 2150408 | tf_op jit(solution)/shard_map/ppermute | solution.py:455
  641.8 23.5 %collective-permute-start.55 = (bf16[2,200,896]{2,1,0:T(8,128)(2,1)S(1)}, bf16[2,200,896]{2,1,0:T(8,128)(2,1)S(1)}, u32[]{:S(2)}, u32[]{:S(2)}) collective-permute-start(bf16[2,200,896]{2,1,0:T(8,128)(2,1)S(1)} %paired.13.a_ref), channel_id=1, source_target_pairs={{0,8},{4,12},{8,0},{12,4},{16,24},{20,28},{24,16},{28,20},{1,9},{5... | collective-permute-start | bytes 2150408 | tf_op jit(solution)/shard_map/ppermute | solution.py:455
  646.1 4.7 collective-permute-start.54
  651.4 15.4 %collective-permute-start.56 = (f32[16,1600]{1,0:T(8,128)S(1)}, f32[16,1600]{1,0:T(8,128)S(1)}, u32[]{:S(2)}, u32[]{:S(2)}) collective-permute-start(f32[16,1600]{1,0:T(8,128)S(1)} %sums_added.6.a_ref), channel_id=1, source_target_pairs={{0,16},{4,20},{8,24},{12,28},{16,0},{20,4},{24,8},{28,12},{1,17},{... | collective-permute-start | bytes 307208 | tf_op jit(solution)/shard_map/ppermute | solution.py:455
  651.4 44.6 %collective-permute-start.60 = (bf16[2,2,200,896]{3,2,1,0:T(8,128)(2,1)S(1)}, bf16[2,2,200,896]{3,2,1,0:T(8,128)(2,1)S(1)}, u32[]{:S(2)}, u32[]{:S(2)}) collective-permute-start(bf16[2,2,200,896]{3,2,1,0:T(8,128)(2,1)S(1)} %paired.14.a_ref.c_ref), channel_id=1, source_target_pairs={{0,8},{4,12},{8,0},{12,4},{16,24},{20,28},{24,16},{28,20},{1,9},{5... | collective-permute-start | bytes 4300808 | tf_op jit(solution)/shard_map/ppermute | solution.py:455
  666.1 34.4 %collective-permute-start.61 = (bf16[2,2,200,896]{3,2,1,0:T(8,128)(2,1)S(1)}, bf16[2,2,200,896]{3,2,1,0:T(8,128)(2,1)S(1)}, u32[]{:S(2)}, u32[]{:S(2)}) collective-permute-start(bf16[2,2,200,896]{3,2,1,0:T(8,128)(2,1)S(1)} %paired.15.a_ref.c_ref), channel_id=1, source_target_pairs={{0,4},{4,0},{8,12},{12,8},{16,20},{20,16},{24,28},{28,24},{1,5},{5... | collective-permute-start | bytes 4300808 | tf_op jit(solution)/shard_map/ppermute | solution.py:455
  667.4 7.0 collective-permute-start.57
  677.0 77.0 %collective-permute-start.66 = (bf16[2,2,200,1600]{3,2,1,0:T(8,128)(2,1)}, bf16[2,2,200,1600]{3,2,1,0:T(8,128)(2,1)}, u32[]{:S(2)}, u32[]{:S(2)}) collective-permute-start(bf16[2,2,200,1600]{3,2,1,0:T(8,128)(2,1)} %paired.17.a_ref.c_ref), channel_id=1, source_target_pairs={{0,4},{4,0},{8,12},{12,8},{16,20},{20,16},{24,28},{28,24},{1,5},{5... | collective-permute-start | bytes 7680008 | tf_op jit(solution)/shard_map/ppermute | solution.py:455
  678.6 84.0 %collective-permute-start.67 = (bf16[2,2,200,1600]{3,2,1,0:T(8,128)(2,1)}, bf16[2,2,200,1600]{3,2,1,0:T(8,128)(2,1)}, u32[]{:S(2)}, u32[]{:S(2)}) collective-permute-start(bf16[2,2,200,1600]{3,2,1,0:T(8,128)(2,1)} %paired.16.a_ref.c_ref), channel_id=1, source_target_pairs={{0,8},{4,12},{8,0},{12,4},{16,24},{20,28},{24,16},{28,20},{1,9},{5... | collective-permute-start | bytes 7680008 | tf_op jit(solution)/shard_map/ppermute | solution.py:455
  703.9 25.3 %collective-permute-start.64 = (bf16[800,768]{1,0:T(8,128)(2,1)}, bf16[800,768]{1,0:T(8,128)(2,1)}, u32[]{:S(2)}, u32[]{:S(2)}) collective-permute-start(bf16[800,768]{1,0:T(8,128)(2,1)} %half_rows.3), channel_id=1, source_target_pairs={{0,2},{2,0},{1,3},{3,1},{4,6},{6,4},{5,7},{7,5},{8,10},{10,8},{9,1... | collective-permute-start | bytes 3686408 | tf_op jit(solution)/shard_map/ppermute | solution.py:447
  (91 other events, 935.4 us)

commit v6 on v4

--- a/solution.py
+++ b/solution.py
@@ -47,7 +47,7 @@
     return jnp.transpose(x.astype(jnp.float32)).astype(jnp.bfloat16)
 
 
-def attend_kernel(heads, blocks, info_ref, q_ref, k_ref, v_ref, first_ref, o_ref, lse_ref, keys_ref):
+def attend_kernel(heads, blocks, info_ref, q_ref, k_ref, v_ref, first_ref, o_ref, lse_ref, keys_ref, queries_ref):
     i = pl.program_id(0)
     shift = info_ref[0]
 
@@ -57,29 +57,31 @@
             keys_ref[h] = turned(k_ref[head_rows(h), :])
 
     first = first_ref[pl.ds(i, 1), :]
-    scale = jnp.bfloat16(HEAD_DIM**-0.5)
+    queries_ref[...] = q_ref[...] * jnp.bfloat16(HEAD_DIM**-0.5)
+    ones = jnp.ones((16, BLK), jnp.bfloat16)
 
     def step(j, carry):
         place = pl.ds(pl.multiple_of(lax.rem(j + shift, blocks) * BLK, BLK), BLK)
         allowed = allowed_tile(i, j, first)
         out = []
         for h in range(heads):
-            top, total, acc = carry[h]
-            scores = nn(keys_ref[h, place, :], q_ref[head_rows(h), :] * scale)
+            top, acc = carry[h]
+            scores = nn(keys_ref[h, place, :], queries_ref[head_rows(h), :])
             scores = jnp.where(allowed, scores, NEG)
             new_top = jnp.maximum(top, jnp.max(scores, axis=0, keepdims=True))
             probs = jnp.exp(scores - new_top)
             shrink = jnp.exp(top - new_top)
-            total = total * shrink + jnp.sum(probs, axis=0, keepdims=True)
-            acc = acc * shrink + nn(v_ref[head_rows(h), place], probs.astype(jnp.bfloat16))
-            out.append((new_top, total, acc))
+            values = jnp.concatenate([v_ref[head_rows(h), place], ones], axis=0)
+            acc = acc * shrink + nn(values, probs.astype(jnp.bfloat16))
+            out.append((new_top, acc))
         return tuple(out)
 
     row = lambda value: jnp.full((1, BLK), value, jnp.float32)
-    start = tuple((row(NEG), row(0.0), jnp.zeros((HEAD_DIM, BLK), jnp.float32)) for h in range(heads))
+    start = tuple((row(NEG), jnp.zeros((HEAD_DIM + 16, BLK), jnp.float32)) for h in range(heads))
     done = lax.fori_loop(info_ref[1 + i], i + 1, step, start)
-    for h, (top, total, acc) in enumerate(done):
-        o_ref[head_rows(h), :] = (acc / total).astype(jnp.bfloat16)
+    for h, (top, acc) in enumerate(done):
+        total = acc[HEAD_DIM : HEAD_DIM + 1, :]
+        o_ref[head_rows(h), :] = (acc[:HEAD_DIM] / total).astype(jnp.bfloat16)
         lse_ref[h : h + 1, :] = top + jnp.log(total)
 
 
@@ -102,7 +104,10 @@
                 pl.BlockSpec((wide, BLK), lambda i, s: (0, at(i, s))),
                 pl.BlockSpec((8, BLK), lambda i, s: (0, i)),
             ],
-            scratch_shapes=[pltpu.VMEM((heads, tokens, HEAD_DIM), jnp.bfloat16)],
+            scratch_shapes=[
+                pltpu.VMEM((heads, tokens, HEAD_DIM), jnp.bfloat16),
+                pltpu.VMEM((wide, BLK), jnp.bfloat16),
+            ],
         ),
         out_shape=[
             jax.ShapeDtypeStruct((wide, tokens), jnp.bfloat16),
@@ -116,7 +121,7 @@
 
 def attend_back_kernel(
     heads, blocks, info_ref, q_ref, k_ref, v_ref, o_ref, g_ref, lse_ref, first_ref,
-    d_ref, keys_ref, values_ref, dk_acc, dv_acc,
+    d_ref, keys_ref, values_ref, queries_ref, dk_acc, dv_acc,
 ):
     i = pl.program_id(0)
     shift = info_ref[0]
@@ -130,7 +135,7 @@
         dv_acc[...] = jnp.zeros_like(dv_acc)
 
     first = first_ref[pl.ds(i, 1), :]
-    scale = jnp.bfloat16(HEAD_DIM**-0.5)
+    queries_ref[...] = q_ref[...] * jnp.bfloat16(HEAD_DIM**-0.5)
     centre = [
         jnp.sum(
             g_ref[head_rows(h), :].astype(jnp.float32) * o_ref[head_rows(h), :].astype(jnp.float32),
@@ -146,7 +151,7 @@
         out = []
         for h in range(heads):
             rows = head_rows(h)
-            query = q_ref[rows, :] * scale
+            query = queries_ref[rows, :]
             grad = g_ref[rows, :]
             scores = jnp.where(allowed, nn(keys_ref[h, place, :], query), NEG)
             probs = jnp.exp(scores - lse_ref[h : h + 1, :])
@@ -193,6 +198,7 @@
             scratch_shapes=[
                 pltpu.VMEM((heads, tokens, HEAD_DIM), jnp.bfloat16),
                 pltpu.VMEM((heads, tokens, HEAD_DIM), jnp.bfloat16),
+                pltpu.VMEM((wide, BLK), jnp.bfloat16),
                 pltpu.VMEM((wide, tokens), jnp.float32),
                 pltpu.VMEM((wide, tokens), jnp.float32),
             ],

time: 772 us -> 773 us (level)
  no operation moved by 1% of the time
where the time goes in v6:
time: 773 us; the launch traced here: 766 us
  Pallas kernels  377 us (49%)
  waiting for transfers between devices  254 us (33%)
  starting transfers between devices  68.7 us (9%)
  local copies, waits for them, and re-layouts  46.9 us (6%)
  other arithmetic  17 us (2%)
    pallas_call x69, Pallas kernels, call(): pl.pallas_call(body, grid_spec=pltpu.PrefetchScalarGridSpec(num_scalar_pr...  302 us
    ppermute x36, waiting for transfers between devices, dp_xor(): lax.ppermute(value, 'dp', [(i, i ^ mask) for i in range(lax.axis_size('dp...  228 us
    ppermute x36, starting transfers between devices, dp_xor(): lax.ppermute(value, 'dp', [(i, i ^ mask) for i in range(lax.axis_size('dp...  42.5 us
    unnamed x174, local copies, waits for them, and re-layouts  33.6 us
    pallas_call x1, Pallas kernels, attend(): pl.pallas_call(functools.partial(attend_kernel, heads, blocks), grid_spec...  30.8 us
    pallas_call x1, Pallas kernels, attend_back(): pl.pallas_call(functools.partial(attend_back_kernel, heads, blocks), grid...  30.8 us
    ppermute x13, starting transfers between devices, row_swap(): return lax.ppermute(value, 'row', SWAP)  20.1 us
    ppermute x15, waiting for transfers between devices, col_swap(): return lax.ppermute(value, 'col', SWAP)  15.5 us
  transfers between devices with their start and end apart: 68, of which 31 were waited for; matrix products, arithmetic and copies ran while one was open for 4% of the time, Pallas kernels for 42%

profile of v6, /device:TPU:0, one launch (start us, length us, event | category | flops | bytes accessed | tf_op | source)
XLA Modules:
  0.0 766.0 jit_solution(11891686937964994736)
XLA Ops:
  9.5 3.9 pack_heads.1
  20.2 4.1 pack.1
  27.1 5.3 own_rows.3.h_ref
  35.8 5.2 own_rows.4.h_ref
  41.0 7.6 collective-permute-done.5.refs_2_
  50.6 5.3 own_rows.5.h_ref
  60.7 3.4 norm_one.1
  64.1 4.5 all_rows.3
  74.6 13.0 %project.1.q_ref.k_ref.v_ref = bf16[1344,1536]{1,0:T(8,128)(2,1)S(1)} custom-call(s32[8]{0:T(128)S(1)} %copy-done.41, bf16[3,1600,448]{2,1,0:T(8,128)(2,1)} %bitcast.65, bf16[1600,768]{1,0:T(8,128)(2,1)S(1)} %get-tuple-element.148.own_ref, bf16[1600,768]{1,0:T(8,128)(2,1)} %collective-permute-done.9.other_ref, f32[3,448,1]{2,1,0:T(8,128)S(1)} %copy-done.39), custom_call_target="tpu_custom_call" | custom-call | tf_op jit(solution)/shard_map/project/pallas_call | solution.py:221
  92.2 30.8 %attend.1 = (bf16[448,1536]{1,0:T(8,128)(2,1)S(1)}, f32[8,1536]{1,0:T(8,128)S(1)}) custom-call(s32[7]{0:T(128)S(1)} %pad_add_fusion.info_ref, bf16[1344,1536]{1,0:T(8,128)(2,1)S(1)} %project.1.q_ref.k_ref.v_ref, bf16[1344,1536]{1,0:T(8,128)(2,1)S(1)} %project.1.q_ref.k_ref.v_ref, bf16[1344,1536]{1,0:T(8,128)(2,1)S(1)} %project.1.q_ref.k_ref.v_ref, ...), custom_call_target="tpu_custom_call" | custom-call | tf_op jit(solution)/shard_map/attend/pallas_call | solution.py:92
  126.5 4.7 collective-permute-done.13.refs_0_
  139.2 13.4 %collective-permute-done.14.refs_1_ = bf16[200,1600]{1,0:T(8,128)(2,1)S(1)} collective-permute-done((bf16[200,1600]{1,0:T(8,128)(2,1)}, bf16[200,1600]{1,0:T(8,128)(2,1)S(1)}, u32[]{:S(2)}, u32[]{:S(2)}) %collective-permute-start.14) | collective-permute-done | bytes 640032 | tf_op jit(solution)/shard_map/ppermute | solution.py:461
  156.0 13.6 %collective-permute-done.15.refs_2_ = bf16[200,1600]{1,0:T(8,128)(2,1)S(1)} collective-permute-done((bf16[200,1600]{1,0:T(8,128)(2,1)}, bf16[200,1600]{1,0:T(8,128)(2,1)S(1)}, u32[]{:S(2)}, u32[]{:S(2)}) %collective-permute-start.15) | collective-permute-done | bytes 640032 | tf_op jit(solution)/shard_map/ppermute | solution.py:461
  169.5 12.8 %collective-permute-done.16.refs_3_ = bf16[200,1600]{1,0:T(8,128)(2,1)S(1)} collective-permute-done((bf16[200,1600]{1,0:T(8,128)(2,1)S(1)}, bf16[200,1600]{1,0:T(8,128)(2,1)S(1)}, u32[]{:S(2)}, u32[]{:S(2)}) %collective-permute-start.16) | collective-permute-done | bytes 640032 | tf_op jit(solution)/shard_map/ppermute | solution.py:461
  183.2 4.9 all_rows.4
  188.1 4.5 all_rows.5
  192.7 6.2 norm_two.1
  199.5 4.1 collective-permute-done.21.other_ref
  203.6 19.2 %hidden.1 = (bf16[1600,1536]{1,0:T(8,128)(2,1)S(1)}, f32[1600,1536]{1,0:T(8,128)}) custom-call(s32[8]{0:T(128)S(1)} %copy-done.42, bf16[1600,1600]{1,0:T(8,128)(2,1)} %bitcast.55, bf16[1600,768]{1,0:T(8,128)(2,1)S(1)} %get-tuple-element.165.own_ref, bf16[1600,768]{1,0:T(8,128)(2,1)S(1)} %collective-permute-done.21.other_ref, f32[1600,8]{1,0:T(8,128)S(1)} %bitcast.87), custom_call_target="tpu_custom_call" | custom-call | tf_op jit(solution)/shard_map/hidden/pallas_call | solution.py:221
  222.8 5.5 collective-permute-done.22.b_ref
  230.5 4.7 collective-permute-done.23.other_ref
  236.6 17.1 %hidden_back.1 = (bf16[1600,1536]{1,0:T(8,128)(2,1)}, f32[1600,128]{1,0:T(8,128)}) custom-call(s32[8]{0:T(128)} %fusion.14.s_ref._, bf16[1600,1600]{1,0:T(8,128)(2,1)} %bitcast.60, bf16[1600,768]{1,0:T(8,128)(2,1)} %bitcast.77, bf16[1600,768]{1,0:T(8,128)(2,1)} %copy-done.62, f32[1600,1536]{1,0:T(8,128)} %get-tuple-element.169.s_ref), custom_call_target="tpu_custom_call" | custom-call | tf_op jit(solution)/shard_map/hidden_back/pallas_call | solution.py:221
  256.2 6.8 mapped.8
  263.1 11.3 %weight_grad.8 = bf16[4,200,1600]{2,1,0:T(8,128)(2,1)} custom-call(s32[8]{0:T(128)} %fusion.14.s_ref._, bf16[8,200,768]{2,1,0:T(8,128)(2,1)} %bitcast.96, bf16[8,200,768]{2,1,0:T(8,128)(2,1)} %bitcast.98, bf16[1600,1536]{1,0:T(8,128)(2,1)} %get-tuple-element.177.t_ref.refs_2_), custom_call_target="tpu_custom_call" | custom-call | tf_op jit(solution)/shard_map/weight_grad/pallas_call | solution.py:221
  276.0 8.6 %mapped.9.low_ref = bf16[1600,768]{1,0:T(8,128)(2,1)} custom-call(s32[8]{0:T(128)S(1)} %copy-done.44, bf16[1600,1600]{1,0:T(8,128)(2,1)} %bitcast.56, bf16[1600,1536]{1,0:T(8,128)(2,1)S(1)} %bitcast.75, bf16[1600,768]{1,0:T(8,128)(2,1)} %collective-permute-done.24.refs_0_), custom_call_target="tpu_custom_call" | custom-call | tf_op jit(solution)/shard_map/mapped/pallas_call | solution.py:221
  285.1 10.0 %weight_grad.9 = bf16[2,400,1600]{2,1,0:T(8,128)(2,1)} custom-call(s32[8]{0:T(128)} %fusion.14.s_ref._, bf16[4,400,768]{2,1,0:T(8,128)(2,1)} %bitcast.78, bf16[4,400,768]{2,1,0:T(8,128)(2,1)} %bitcast.126, bf16[1600,1536]{1,0:T(8,128)(2,1)} %copy-done.6), custom_call_target="tpu_custom_call" | custom-call | tf_op jit(solution)/shard_map/weight_grad/pallas_call | solution.py:221
  297.9 6.8 mapped.10
  304.7 9.4 %weight_grad.10 = bf16[2,400,1600]{2,1,0:T(8,128)(2,1)} custom-call(s32[8]{0:T(128)} %fusion.14.s_ref._, bf16[4,400,768]{2,1,0:T(8,128)(2,1)} %bitcast.79, bf16[4,400,768]{2,1,0:T(8,128)(2,1)} %bitcast.127, bf16[1600,1536]{1,0:T(8,128)(2,1)} %copy-done.6), custom_call_target="tpu_custom_call" | custom-call | tf_op jit(solution)/shard_map/weight_grad/pallas_call | solution.py:221
  314.1 10.9 %weight_grad.11 = bf16[4,200,1600]{2,1,0:T(8,128)(2,1)} custom-call(s32[8]{0:T(128)} %fusion.14.s_ref._, bf16[8,200,768]{2,1,0:T(8,128)(2,1)} %bitcast.97, bf16[8,200,768]{2,1,0:T(8,128)(2,1)} %bitcast.99, bf16[1600,1536]{1,0:T(8,128)(2,1)} %get-tuple-element.177.t_ref.refs_2_), custom_call_target="tpu_custom_call" | custom-call | tf_op jit(solution)/shard_map/weight_grad/pallas_call | solution.py:221
  325.0 9.7 %collective-permute-done.25.b_ref.d_ref = bf16[2,2,200,1600]{3,2,1,0:T(8,128)(2,1)} collective-permute-done((bf16[2,2,200,1600]{3,2,1,0:T(8,128)(2,1)}, bf16[2,2,200,1600]{3,2,1,0:T(8,128)(2,1)}, u32[]{:S(2)}, u32[]{:S(2)}) %collective-permute-start.25) | collective-permute-done | bytes 2560032 | tf_op jit(solution)/shard_map/ppermute | solution.py:461
  336.5 3.3 halved.8
  340.3 10.2 %norm_two_back.1 = (f32[1600,768]{1,0:T(8,128)}, bf16[1600,768]{1,0:T(8,128)(2,1)S(1)}, f32[3,1600,128]{2,1,0:T(8,128)S(1)}) custom-call(s32[8]{0:T(128)S(1)} %copy-done.46, bf16[1600,768]{1,0:T(8,128)(2,1)} %mapped.9.low_ref, bf16[1600,768]{1,0:T(8,128)(2,1)} %collective-permute-done.26.other_ref, bf16[1600,768]{1,0:T(8,128)(2,1)S(1)} %bitcast.80, ...), custom_call_target="tpu_custom_call" | custom-call | tf_op jit(solution)/shard_map/norm_two_back/pallas_call | solution.py:221
  355.0 3.3 halved.9
  360.0 3.5 attended_back.1.g_ref
  363.6 30.8 %attend_back.1.p_ref.refs_5_.refs_2_ = bf16[1344,1536]{1,0:T(8,128)(2,1)S(1)} custom-call(s32[7]{0:T(128)S(1)} %pad_add_fusion.info_ref, bf16[1344,1536]{1,0:T(8,128)(2,1)S(1)} %copy-done.4, bf16[1344,1536]{1,0:T(8,128)(2,1)S(1)} %copy-done.4, bf16[1344,1536]{1,0:T(8,128)(2,1)S(1)} %copy-done.4, bf16[448,1536]{1,0:T(8,128)(2,1)S(1)} %copy-done.13, ...), custom_call_target="tpu_custom_call" | custom-call | tf_op jit(solution)/shard_map/attend_back/pallas_call | solution.py:183
  394.5 6.4 mapped_three.2
  401.0 7.6 weight_grad.12
  415.7 7.2 weight_grad.13
  427.7 7.5 mapped.11.a_ref.p_ref
  436.6 7.5 weight_grad.14
  449.3 7.0 mapped_three.3.a_ref.m_ref
  461.2 6.9 weight_grad.15
  468.1 5.1 collective-permute-done.34.b_ref.d_ref
  479.3 6.2 collective-permute-done.36.b_ref
  488.0 7.1 collective-permute-done.37.b_ref.d_ref
  498.2 18.1 %collective-permute-done.38.b_ref.d_ref = bf16[2,200,896]{2,1,0:T(8,128)(2,1)S(1)} collective-permute-done((bf16[2,200,896]{2,1,0:T(8,128)(2,1)S(1)}, bf16[2,200,896]{2,1,0:T(8,128)(2,1)S(1)}, u32[]{:S(2)}, u32[]{:S(2)}) %collective-permute-start.38) | collective-permute-done | bytes 716832 | tf_op jit(solution)/shard_map/ppermute | solution.py:461
  527.4 37.3 %collective-permute-done.43.b_ref = bf16[200,896]{1,0:T(8,128)(2,1)S(1)} collective-permute-done((bf16[200,896]{1,0:T(8,128)(2,1)S(1)}, bf16[200,896]{1,0:T(8,128)(2,1)S(1)}, u32[]{:S(2)}, u32[]{:S(2)}) %collective-permute-start.43) | collective-permute-done | bytes 358432 | tf_op jit(solution)/shard_map/ppermute | solution.py:461
  569.3 5.0 packed_sums.1.a_ref
  586.4 3.3 collective-permute-done.48.b_ref
  590.3 3.4 norm_one_back.1
  593.6 7.5 collective-permute-done.50.b_ref
  609.0 28.9 %collective-permute-done.52.b_ref = bf16[200,896]{1,0:T(8,128)(2,1)S(1)} collective-permute-done((bf16[200,896]{1,0:T(8,128)(2,1)S(1)}, bf16[200,896]{1,0:T(8,128)(2,1)S(1)}, u32[]{:S(2)}, u32[]{:S(2)}) %collective-permute-start.52) | collective-permute-done | bytes 358432 | tf_op jit(solution)/shard_map/ppermute | solution.py:461
  638.5 4.3 collective-permute-start.55
  644.1 3.4 collective-permute-done.54.b_ref
  649.3 12.7 %collective-permute-done.55.b_ref = bf16[2,200,896]{2,1,0:T(8,128)(2,1)S(1)} collective-permute-done((bf16[2,200,896]{2,1,0:T(8,128)(2,1)S(1)}, bf16[2,200,896]{2,1,0:T(8,128)(2,1)S(1)}, u32[]{:S(2)}, u32[]{:S(2)}) %collective-permute-start.55) | collective-permute-done | bytes 716832 | tf_op jit(solution)/shard_map/ppermute | solution.py:461
  666.2 4.8 paired.16.a_ref.c_ref
  676.7 16.1 %collective-permute-done.60.b_ref.d_ref = bf16[2,2,200,896]{3,2,1,0:T(8,128)(2,1)S(1)} collective-permute-done((bf16[2,2,200,896]{3,2,1,0:T(8,128)(2,1)S(1)}, bf16[2,2,200,896]{3,2,1,0:T(8,128)(2,1)S(1)}, u32[]{:S(2)}, u32[]{:S(2)}) %collective-permute-start.60) | collective-permute-done | bytes 1433632 | tf_op jit(solution)/shard_map/ppermute | solution.py:461
  694.0 3.3 collective-permute-done.61.b_ref.d_ref
  714.3 4.1 copy.52
  718.4 7.5 pad_maximum_fusion
  728.3 3.9 block_result.1
  732.2 16.3 %collective-permute-done.66.b_ref.d_ref = bf16[2,2,200,1600]{3,2,1,0:T(8,128)(2,1)} collective-permute-done((bf16[2,2,200,1600]{3,2,1,0:T(8,128)(2,1)}, bf16[2,2,200,1600]{3,2,1,0:T(8,128)(2,1)}, u32[]{:S(2)}, u32[]{:S(2)}) %collective-permute-start.66) | collective-permute-done | bytes 2560032 | tf_op jit(solution)/shard_map/ppermute | solution.py:461
  748.6 8.8 %widened.2 = f32[800,3200]{1,0:T(8,128)} custom-call(s32[8]{0:T(128)S(1)} %copy-done.50, bf16[2,2,200,1600]{3,2,1,0:T(8,128)(2,1)} %paired.16.a_ref.c_ref, bf16[2,2,200,1600]{3,2,1,0:T(8,128)(2,1)} %collective-permute-done.66.b_ref.d_ref, bf16[2,2,200,1600]{3,2,1,0:T(8,128)(2,1)} %paired.16.a_ref.c_ref, ...), custom_call_target="tpu_custom_call" | custom-call | tf_op jit(solution)/shard_map/widened/pallas_call | solution.py:221
  757.4 8.5 %widened.3 = f32[800,3200]{1,0:T(8,128)} custom-call(s32[8]{0:T(128)S(1)} %copy-done.50, bf16[2,2,200,1600]{3,2,1,0:T(8,128)(2,1)} %paired.17.a_ref.c_ref, bf16[2,2,200,1600]{3,2,1,0:T(8,128)(2,1)} %collective-permute-done.67.b_ref.d_ref, bf16[2,2,200,1600]{3,2,1,0:T(8,128)(2,1)} %paired.17.a_ref.c_ref, ...), custom_call_target="tpu_custom_call" | custom-call | tf_op jit(solution)/shard_map/widened/pallas_call | solution.py:221
  (378 shorter events, 180.3 us)
Async XLA Ops:
  2.0 6.4 collective-permute-start
  14.6 17.8 %collective-permute-start.3 = (bf16[3,200,448]{2,1,0:T(8,128)(2,1)}, bf16[3,200,448]{2,1,0:T(8,128)(2,1)}, u32[]{:S(2)}, u32[]{:S(2)}) collective-permute-start(bf16[3,200,448]{2,1,0:T(8,128)(2,1)} %pack_heads.1), channel_id=1, source_target_pairs={{0,2},{2,0},{1,3},{3,1},{4,6},{6,4},{5,7},{7,5},{8,10},{10,8},{9,1... | collective-permute-start | bytes 1612808 | tf_op jit(solution)/shard_map/ppermute | solution.py:453
  17.0 7.3 collective-permute-start.2
  17.3 16.8 %collective-permute-start.6 = (bf16[2,32]{1,0:T(2,128)(2,1)S(1)}, bf16[2,32]{1,0:T(2,128)(2,1)S(1)}, u32[]{:S(2)}, u32[]{:S(2)}) collective-permute-start(bf16[2,32]{1,0:T(2,128)(2,1)S(1)} %slice.115), channel_id=1, source_target_pairs={{0,1},{1,0},{2,3},{3,2},{4,5},{5,4},{6,7},{7,6},{8,9},{9,8},{10,11... | collective-permute-start | bytes 392 | tf_op jit(solution)/shard_map/ppermute | solution.py:457
  18.0 32.1 %collective-permute-start.7 = (bf16[5,800]{1,0:T(8,128)(2,1)S(1)}, bf16[5,800]{1,0:T(8,128)(2,1)S(1)}, u32[]{:S(2)}, u32[]{:S(2)}) collective-permute-start(bf16[5,800]{1,0:T(8,128)(2,1)S(1)} %stack.37), channel_id=1, source_target_pairs={{0,2},{2,0},{1,3},{3,1},{4,6},{6,4},{5,7},{7,5},{8,10},{10,8},{9,1... | collective-permute-start | bytes 24008 | tf_op jit(solution)/shard_map/ppermute | solution.py:453
  18.2 40.2 %collective-permute-start.1 = (bf16[800,768]{1,0:T(8,128)(2,1)S(1)}, bf16[800,768]{1,0:T(8,128)(2,1)S(1)}, u32[]{:S(2)}, u32[]{:S(2)}) collective-permute-start(bf16[800,768]{1,0:T(8,128)(2,1)S(1)} %bitcast.104), channel_id=1, source_target_pairs={{0,2},{2,0},{1,3},{3,1},{4,6},{6,4},{5,7},{7,5},{8,10},{10,8},{9,1... | collective-permute-start | bytes 3686408 | tf_op jit(solution)/shard_map/ppermute | solution.py:453
  32.4 16.2 %collective-permute-start.5 = (bf16[3,200,448]{2,1,0:T(8,128)(2,1)}, bf16[3,200,448]{2,1,0:T(8,128)(2,1)}, u32[]{:S(2)}, u32[]{:S(2)}) collective-permute-start(bf16[3,200,448]{2,1,0:T(8,128)(2,1)} %collective-permute-done.3.refs_0_), channel_id=1, source_target_pairs={{0,8},{4,12},{8,0},{12,4},{16,24},{20,28},{24,16},{28,20},{1,9},{5... | collective-permute-start | bytes 1612808 | tf_op jit(solution)/shard_map/ppermute | solution.py:461
  34.3 16.2 %collective-permute-start.4 = (bf16[3,200,448]{2,1,0:T(8,128)(2,1)}, bf16[3,200,448]{2,1,0:T(8,128)(2,1)}, u32[]{:S(2)}, u32[]{:S(2)}) collective-permute-start(bf16[3,200,448]{2,1,0:T(8,128)(2,1)} %collective-permute-done.3.refs_0_), channel_id=1, source_target_pairs={{0,4},{4,0},{8,12},{12,8},{16,20},{20,16},{24,28},{28,24},{1,5},{5... | collective-permute-start | bytes 1612808 | tf_op jit(solution)/shard_map/ppermute | solution.py:461
  48.6 15.5 %collective-permute-start.8 = (bf16[3,200,448]{2,1,0:T(8,128)(2,1)}, bf16[3,200,448]{2,1,0:T(8,128)(2,1)}, u32[]{:S(2)}, u32[]{:S(2)}) collective-permute-start(bf16[3,200,448]{2,1,0:T(8,128)(2,1)} %collective-permute-done.5.refs_2_), channel_id=1, source_target_pairs={{0,4},{4,0},{8,12},{12,8},{16,20},{20,16},{24,28},{28,24},{1,5},{5... | collective-permute-start | bytes 1612808 | tf_op jit(solution)/shard_map/ppermute | solution.py:461
  68.6 4.9 collective-permute-start.9
  68.7 21.0 %collective-permute-start.10 = (bf16[448,800]{1,0:T(8,128)(2,1)}, bf16[448,800]{1,0:T(8,128)(2,1)}, u32[]{:S(2)}, u32[]{:S(2)}) collective-permute-start(bf16[448,800]{1,0:T(8,128)(2,1)} %get-tuple-element.150), channel_id=1, source_target_pairs={{0,2},{2,0},{1,3},{3,1},{4,6},{6,4},{5,7},{7,5},{8,10},{10,8},{9,1... | collective-permute-start | bytes 2150408 | tf_op jit(solution)/shard_map/ppermute | solution.py:453
  70.4 53.4 %collective-permute-start.12 = (bf16[200,1600]{1,0:T(8,128)(2,1)}, bf16[200,1600]{1,0:T(8,128)(2,1)}, u32[]{:S(2)}, u32[]{:S(2)}) collective-permute-start(bf16[200,1600]{1,0:T(8,128)(2,1)} %get-tuple-element.156), channel_id=1, source_target_pairs={{0,2},{2,0},{1,3},{3,1},{4,6},{6,4},{5,7},{7,5},{8,10},{10,8},{9,1... | collective-permute-start | bytes 1920008 | tf_op jit(solution)/shard_map/ppermute | solution.py:453
  70.8 52.9 %collective-permute-start.11 = (bf16[200,1600]{1,0:T(8,128)(2,1)}, bf16[200,1600]{1,0:T(8,128)(2,1)}, u32[]{:S(2)}, u32[]{:S(2)}) collective-permute-start(bf16[200,1600]{1,0:T(8,128)(2,1)} %get-tuple-element.153), channel_id=1, source_target_pairs={{0,2},{2,0},{1,3},{3,1},{4,6},{6,4},{5,7},{7,5},{8,10},{10,8},{9,1... | collective-permute-start | bytes 1920008 | tf_op jit(solution)/shard_map/ppermute | solution.py:453
  126.4 4.7 collective-permute-start.13
  134.0 58.6 %collective-permute-start.20 = (bf16[1600,768]{1,0:T(8,128)(2,1)S(1)}, bf16[1600,768]{1,0:T(8,128)(2,1)}, u32[]{:S(2)}, u32[]{:S(2)}) collective-permute-start(bf16[1600,768]{1,0:T(8,128)(2,1)S(1)} %mapped.7.low_ref), channel_id=1, source_target_pairs={{0,2},{2,0},{1,3},{3,1},{4,6},{6,4},{5,7},{7,5},{8,10},{10,8},{9,1... | collective-permute-start | bytes 7372808 | tf_op jit(solution)/shard_map/ppermute | solution.py:453
  135.7 16.9 %collective-permute-start.14 = (bf16[200,1600]{1,0:T(8,128)(2,1)}, bf16[200,1600]{1,0:T(8,128)(2,1)S(1)}, u32[]{:S(2)}, u32[]{:S(2)}) collective-permute-start(bf16[200,1600]{1,0:T(8,128)(2,1)} %collective-permute-done.11.refs_0_), channel_id=1, source_target_pairs={{0,4},{4,0},{8,12},{12,8},{16,20},{20,16},{24,28},{28,24},{1,5},{5... | collective-permute-start | bytes 1920008 | tf_op jit(solution)/shard_map/ppermute | solution.py:461
  137.2 18.5 %collective-permute-start.18 = (bf16[200,1600]{1,0:T(8,128)(2,1)}, bf16[200,1600]{1,0:T(8,128)(2,1)}, u32[]{:S(2)}, u32[]{:S(2)}) collective-permute-start(bf16[200,1600]{1,0:T(8,128)(2,1)} %collective-permute-done.12.refs_0_), channel_id=1, source_target_pairs={{0,8},{4,12},{8,0},{12,4},{16,24},{20,28},{24,16},{28,20},{1,9},{5... | collective-permute-start | bytes 1920008 | tf_op jit(solution)/shard_map/ppermute | solution.py:461
  138.8 30.8 %collective-permute-start.15 = (bf16[200,1600]{1,0:T(8,128)(2,1)}, bf16[200,1600]{1,0:T(8,128)(2,1)S(1)}, u32[]{:S(2)}, u32[]{:S(2)}) collective-permute-start(bf16[200,1600]{1,0:T(8,128)(2,1)} %collective-permute-done.11.refs_0_), channel_id=1, source_target_pairs={{0,8},{4,12},{8,0},{12,4},{16,24},{20,28},{24,16},{28,20},{1,9},{5... | collective-permute-start | bytes 1920008 | tf_op jit(solution)/shard_map/ppermute | solution.py:461
  152.6 29.8 %collective-permute-start.16 = (bf16[200,1600]{1,0:T(8,128)(2,1)S(1)}, bf16[200,1600]{1,0:T(8,128)(2,1)S(1)}, u32[]{:S(2)}, u32[]{:S(2)}) collective-permute-start(bf16[200,1600]{1,0:T(8,128)(2,1)S(1)} %collective-permute-done.14.refs_1_), channel_id=1, source_target_pairs={{0,8},{4,12},{8,0},{12,4},{16,24},{20,28},{24,16},{28,20},{1,9},{5... | collective-permute-start | bytes 1920008 | tf_op jit(solution)/shard_map/ppermute | solution.py:461
  153.9 34.1 %collective-permute-start.17 = (bf16[200,1600]{1,0:T(8,128)(2,1)}, bf16[200,1600]{1,0:T(8,128)(2,1)}, u32[]{:S(2)}, u32[]{:S(2)}) collective-permute-start(bf16[200,1600]{1,0:T(8,128)(2,1)} %collective-permute-done.12.refs_0_), channel_id=1, source_target_pairs={{0,4},{4,0},{8,12},{12,8},{16,20},{20,16},{24,28},{28,24},{1,5},{5... | collective-permute-start | bytes 1920008 | tf_op jit(solution)/shard_map/ppermute | solution.py:461
  155.7 32.4 %collective-permute-start.19 = (bf16[200,1600]{1,0:T(8,128)(2,1)}, bf16[200,1600]{1,0:T(8,128)(2,1)}, u32[]{:S(2)}, u32[]{:S(2)}) collective-permute-start(bf16[200,1600]{1,0:T(8,128)(2,1)} %collective-permute-done.18.refs_2_), channel_id=1, source_target_pairs={{0,4},{4,0},{8,12},{12,8},{16,20},{20,16},{24,28},{28,24},{1,5},{5... | collective-permute-start | bytes 1920008 | tf_op jit(solution)/shard_map/ppermute | solution.py:461
  198.9 4.7 collective-permute-start.21
  198.9 29.4 %collective-permute-start.22 = (bf16[800,768]{1,0:T(8,128)(2,1)S(1)}, bf16[800,768]{1,0:T(8,128)(2,1)S(1)}, u32[]{:S(2)}, u32[]{:S(2)}) collective-permute-start(bf16[800,768]{1,0:T(8,128)(2,1)S(1)} %bitcast.115), channel_id=1, source_target_pairs={{0,2},{2,0},{1,3},{3,1},{4,6},{6,4},{5,7},{7,5},{8,10},{10,8},{9,1... | collective-permute-start | bytes 3686408 | tf_op jit(solution)/shard_map/ppermute | solution.py:453
  230.5 4.7 collective-permute-start.23
  262.9 13.0 %collective-permute-start.24 = (bf16[1600,768]{1,0:T(8,128)(2,1)}, bf16[1600,768]{1,0:T(8,128)(2,1)}, u32[]{:S(2)}, u32[]{:S(2)}) collective-permute-start(bf16[1600,768]{1,0:T(8,128)(2,1)} %mapped.8), channel_id=1, source_target_pairs={{0,1},{1,0},{2,3},{3,2},{4,5},{5,4},{6,7},{7,6},{8,9},{9,8},{10,11... | collective-permute-start | bytes 7372808 | tf_op jit(solution)/shard_map/ppermute | solution.py:457
  274.4 60.3 %collective-permute-start.25 = (bf16[2,2,200,1600]{3,2,1,0:T(8,128)(2,1)}, bf16[2,2,200,1600]{3,2,1,0:T(8,128)(2,1)}, u32[]{:S(2)}, u32[]{:S(2)}) collective-permute-start(bf16[2,2,200,1600]{3,2,1,0:T(8,128)(2,1)} %bitcast.138), channel_id=1, source_target_pairs={{0,8},{4,12},{8,0},{12,4},{16,24},{20,28},{24,16},{28,20},{1,9},{5... | collective-permute-start | bytes 7680008 | tf_op jit(solution)/shard_map/ppermute | solution.py:461
  284.6 55.7 %collective-permute-start.26 = (bf16[1600,768]{1,0:T(8,128)(2,1)}, bf16[1600,768]{1,0:T(8,128)(2,1)}, u32[]{:S(2)}, u32[]{:S(2)}) collective-permute-start(bf16[1600,768]{1,0:T(8,128)(2,1)} %mapped.9.low_ref), channel_id=1, source_target_pairs={{0,2},{2,0},{1,3},{3,1},{4,6},{6,4},{5,7},{7,5},{8,10},{10,8},{9,1... | collective-permute-start | bytes 7372808 | tf_op jit(solution)/shard_map/ppermute | solution.py:453
  295.2 59.8 %collective-permute-start.27 = (bf16[2,2,200,1600]{3,2,1,0:T(8,128)(2,1)}, bf16[2,2,200,1600]{3,2,1,0:T(8,128)(2,1)}, u32[]{:S(2)}, u32[]{:S(2)}) collective-permute-start(bf16[2,2,200,1600]{3,2,1,0:T(8,128)(2,1)} %bitcast.137), channel_id=1, source_target_pairs={{0,4},{4,0},{8,12},{12,8},{16,20},{20,16},{24,28},{28,24},{1,5},{5... | collective-permute-start | bytes 7680008 | tf_op jit(solution)/shard_map/ppermute | solution.py:461
  351.9 8.1 %collective-permute-start.28 = (bf16[1600,768]{1,0:T(8,128)(2,1)S(1)}, bf16[1600,768]{1,0:T(8,128)(2,1)S(1)}, u32[]{:S(2)}, u32[]{:S(2)}) collective-permute-start(bf16[1600,768]{1,0:T(8,128)(2,1)S(1)} %get-tuple-element.184.own_ref), channel_id=1, source_target_pairs={{0,1},{1,0},{2,3},{3,2},{4,5},{5,4},{6,7},{7,6},{8,9},{9,8},{10,11... | collective-permute-start | bytes 7372808 | tf_op jit(solution)/shard_map/ppermute | solution.py:457
  351.9 72.9 %collective-permute-start.31 = (bf16[1600,768]{1,0:T(8,128)(2,1)}, bf16[1600,768]{1,0:T(8,128)(2,1)}, u32[]{:S(2)}, u32[]{:S(2)}) collective-permute-start(bf16[1600,768]{1,0:T(8,128)(2,1)} %mapped.10), channel_id=1, source_target_pairs={{0,1},{1,0},{2,3},{3,2},{4,5},{5,4},{6,7},{7,6},{8,9},{9,8},{10,11... | collective-permute-start | bytes 7372808 | tf_op jit(solution)/shard_map/ppermute | solution.py:457
  352.4 56.5 %collective-permute-start.29 = (bf16[2,200,1600]{2,1,0:T(8,128)(2,1)}, bf16[2,200,1600]{2,1,0:T(8,128)(2,1)}, u32[]{:S(2)}, u32[]{:S(2)}) collective-permute-start(bf16[2,200,1600]{2,1,0:T(8,128)(2,1)} %get-tuple-element.190), channel_id=1, source_target_pairs={{0,4},{4,0},{8,12},{12,8},{16,20},{20,16},{24,28},{28,24},{1,5},{5... | collective-permute-start | bytes 3840008 | tf_op jit(solution)/shard_map/ppermute | solution.py:461
  359.3 52.5 %collective-permute-start.30 = (bf16[2,200,1600]{2,1,0:T(8,128)(2,1)}, bf16[2,200,1600]{2,1,0:T(8,128)(2,1)}, u32[]{:S(2)}, u32[]{:S(2)}) collective-permute-start(bf16[2,200,1600]{2,1,0:T(8,128)(2,1)} %get-tuple-element.193), channel_id=1, source_target_pairs={{0,8},{4,12},{8,0},{12,4},{16,24},{20,28},{24,16},{28,20},{1,9},{5... | collective-permute-start | bytes 3840008 | tf_op jit(solution)/shard_map/ppermute | solution.py:461
  400.8 48.5 %collective-permute-start.33 = (bf16[1600,768]{1,0:T(8,128)(2,1)}, bf16[1600,768]{1,0:T(8,128)(2,1)}, u32[]{:S(2)}, u32[]{:S(2)}) collective-permute-start(bf16[1600,768]{1,0:T(8,128)(2,1)} %mapped_three.2), channel_id=1, source_target_pairs={{0,1},{1,0},{2,3},{3,2},{4,5},{5,4},{6,7},{7,6},{8,9},{9,8},{10,11... | collective-permute-start | bytes 7372808 | tf_op jit(solution)/shard_map/ppermute | solution.py:457
  408.5 35.5 %collective-permute-start.32 = (bf16[2,2,200,896]{3,2,1,0:T(8,128)(2,1)}, bf16[2,2,200,896]{3,2,1,0:T(8,128)(2,1)}, u32[]{:S(2)}, u32[]{:S(2)}) collective-permute-start(bf16[2,2,200,896]{3,2,1,0:T(8,128)(2,1)} %bitcast.141), channel_id=1, source_target_pairs={{0,4},{4,0},{8,12},{12,8},{16,20},{20,16},{24,28},{28,24},{1,5},{5... | collective-permute-start | bytes 4300808 | tf_op jit(solution)/shard_map/ppermute | solution.py:461
  423.0 50.3 %collective-permute-start.34 = (bf16[2,2,200,896]{3,2,1,0:T(8,128)(2,1)}, bf16[2,2,200,896]{3,2,1,0:T(8,128)(2,1)}, u32[]{:S(2)}, u32[]{:S(2)}) collective-permute-start(bf16[2,2,200,896]{3,2,1,0:T(8,128)(2,1)} %bitcast.140), channel_id=1, source_target_pairs={{0,4},{4,0},{8,12},{12,8},{16,20},{20,16},{24,28},{28,24},{1,5},{5... | collective-permute-start | bytes 4300808 | tf_op jit(solution)/shard_map/ppermute | solution.py:461
  424.7 52.1 %collective-permute-start.35 = (bf16[200,1600]{1,0:T(8,128)(2,1)}, bf16[200,1600]{1,0:T(8,128)(2,1)}, u32[]{:S(2)}, u32[]{:S(2)}) collective-permute-start(bf16[200,1600]{1,0:T(8,128)(2,1)} %bitcast.123), channel_id=1, source_target_pairs={{0,16},{4,20},{8,24},{12,28},{16,0},{20,4},{24,8},{28,12},{1,17},{... | collective-permute-start | bytes 1920008 | tf_op jit(solution)/shard_map/ppermute | solution.py:461
  424.7 60.8 %collective-permute-start.36 = (bf16[200,1600]{1,0:T(8,128)(2,1)}, bf16[200,1600]{1,0:T(8,128)(2,1)}, u32[]{:S(2)}, u32[]{:S(2)}) collective-permute-start(bf16[200,1600]{1,0:T(8,128)(2,1)} %bitcast.122), channel_id=1, source_target_pairs={{0,16},{4,20},{8,24},{12,28},{16,0},{20,4},{24,8},{28,12},{1,17},{... | collective-permute-start | bytes 1920008 | tf_op jit(solution)/shard_map/ppermute | solution.py:461
  448.3 46.8 %collective-permute-start.37 = (bf16[2,200,896]{2,1,0:T(8,128)(2,1)}, bf16[2,200,896]{2,1,0:T(8,128)(2,1)S(1)}, u32[]{:S(2)}, u32[]{:S(2)}) collective-permute-start(bf16[2,200,896]{2,1,0:T(8,128)(2,1)} %get-tuple-element.209), channel_id=1, source_target_pairs={{0,8},{4,12},{8,0},{12,4},{16,24},{20,28},{24,16},{28,20},{1,9},{5... | collective-permute-start | bytes 2150408 | tf_op jit(solution)/shard_map/ppermute | solution.py:461
  459.1 66.1 %collective-permute-start.42 = (bf16[800,768]{1,0:T(8,128)(2,1)}, bf16[800,768]{1,0:T(8,128)(2,1)S(1)}, u32[]{:S(2)}, u32[]{:S(2)}) collective-permute-start(bf16[800,768]{1,0:T(8,128)(2,1)} %half_rows.2), channel_id=1, source_target_pairs={{0,2},{2,0},{1,3},{3,1},{4,6},{6,4},{5,7},{7,5},{8,10},{10,8},{9,1... | collective-permute-start | bytes 3686408 | tf_op jit(solution)/shard_map/ppermute | solution.py:453
  476.7 39.6 %collective-permute-start.38 = (bf16[2,200,896]{2,1,0:T(8,128)(2,1)S(1)}, bf16[2,200,896]{2,1,0:T(8,128)(2,1)S(1)}, u32[]{:S(2)}, u32[]{:S(2)}) collective-permute-start(bf16[2,200,896]{2,1,0:T(8,128)(2,1)S(1)} %get-tuple-element.212), channel_id=1, source_target_pairs={{0,8},{4,12},{8,0},{12,4},{16,24},{20,28},{24,16},{28,20},{1,9},{5... | collective-permute-start | bytes 2150408 | tf_op jit(solution)/shard_map/ppermute | solution.py:461
  478.6 41.5 %collective-permute-start.40 = (bf16[200,1600]{1,0:T(8,128)(2,1)S(1)}, bf16[200,1600]{1,0:T(8,128)(2,1)S(1)}, u32[]{:S(2)}, u32[]{:S(2)}) collective-permute-start(bf16[200,1600]{1,0:T(8,128)(2,1)S(1)} %added.4.a_ref), channel_id=1, source_target_pairs={{2,4},{4,2},{10,12},{12,10},{18,20},{20,18},{26,28},{28,26},{3,5},... | collective-permute-start | bytes 1920008 | tf_op jit(solution)/shard_map/ppermute | solution.py:1100
  487.3 34.1 %collective-permute-start.41 = (bf16[200,1600]{1,0:T(8,128)(2,1)S(1)}, bf16[200,1600]{1,0:T(8,128)(2,1)S(1)}, u32[]{:S(2)}, u32[]{:S(2)}) collective-permute-start(bf16[200,1600]{1,0:T(8,128)(2,1)S(1)} %added.5.a_ref), channel_id=1, source_target_pairs={{2,4},{4,2},{10,12},{12,10},{18,20},{20,18},{26,28},{28,26},{3,5},... | collective-permute-start | bytes 1920008 | tf_op jit(solution)/shard_map/ppermute | solution.py:1100
  495.8 23.7 %collective-permute-start.39 = (bf16[200,896]{1,0:T(8,128)(2,1)S(1)}, bf16[200,896]{1,0:T(8,128)(2,1)S(1)}, u32[]{:S(2)}, u32[]{:S(2)}) collective-permute-start(bf16[200,896]{1,0:T(8,128)(2,1)S(1)} %bitcast.125), channel_id=1, source_target_pairs={{0,16},{4,20},{8,24},{12,28},{16,0},{20,4},{24,8},{28,12},{1,17},{... | collective-permute-start | bytes 1075208 | tf_op jit(solution)/shard_map/ppermute | solution.py:461
  517.1 47.7 %collective-permute-start.43 = (bf16[200,896]{1,0:T(8,128)(2,1)S(1)}, bf16[200,896]{1,0:T(8,128)(2,1)S(1)}, u32[]{:S(2)}, u32[]{:S(2)}) collective-permute-start(bf16[200,896]{1,0:T(8,128)(2,1)S(1)} %bitcast.124), channel_id=1, source_target_pairs={{0,16},{4,20},{8,24},{12,28},{16,0},{20,4},{24,8},{28,12},{1,17},{... | collective-permute-start | bytes 1075208 | tf_op jit(solution)/shard_map/ppermute | solution.py:461
  520.8 58.4 %collective-permute-start.46 = (bf16[200,1600]{1,0:T(8,128)(2,1)S(1)}, bf16[200,1600]{1,0:T(8,128)(2,1)}, u32[]{:S(2)}, u32[]{:S(2)}) collective-permute-start(bf16[200,1600]{1,0:T(8,128)(2,1)S(1)} %chosen.4.a_ref), channel_id=1, source_target_pairs={{0,16},{4,20},{8,24},{12,28},{16,0},{20,4},{24,8},{28,12},{1,17},{... | collective-permute-start | bytes 1920008 | tf_op jit(solution)/shard_map/ppermute | solution.py:461
  522.0 79.1 %collective-permute-start.50 = (bf16[200,1600]{1,0:T(8,128)(2,1)S(1)}, bf16[200,1600]{1,0:T(8,128)(2,1)}, u32[]{:S(2)}, u32[]{:S(2)}) collective-permute-start(bf16[200,1600]{1,0:T(8,128)(2,1)S(1)} %chosen.5.a_ref), channel_id=1, source_target_pairs={{0,16},{4,20},{8,24},{12,28},{16,0},{20,4},{24,8},{28,12},{1,17},{... | collective-permute-start | bytes 1920008 | tf_op jit(solution)/shard_map/ppermute | solution.py:461
  524.5 42.4 %collective-permute-start.44 = (bf16[200,896]{1,0:T(8,128)(2,1)S(1)}, bf16[200,896]{1,0:T(8,128)(2,1)S(1)}, u32[]{:S(2)}, u32[]{:S(2)}) collective-permute-start(bf16[200,896]{1,0:T(8,128)(2,1)S(1)} %added.6.a_ref), channel_id=1, source_target_pairs={{2,4},{4,2},{10,12},{12,10},{18,20},{20,18},{26,28},{28,26},{3,5},... | collective-permute-start | bytes 1075208 | tf_op jit(solution)/shard_map/ppermute | solution.py:1100
  565.4 16.0 %collective-permute-start.47 = (bf16[200,896]{1,0:T(8,128)(2,1)S(1)}, bf16[200,896]{1,0:T(8,128)(2,1)}, u32[]{:S(2)}, u32[]{:S(2)}) collective-permute-start(bf16[200,896]{1,0:T(8,128)(2,1)S(1)} %added.7.a_ref), channel_id=1, source_target_pairs={{2,4},{4,2},{10,12},{12,10},{18,20},{20,18},{26,28},{28,26},{3,5},... | collective-permute-start | bytes 1075208 | tf_op jit(solution)/shard_map/ppermute | solution.py:1100
  576.2 13.5 %collective-permute-start.48 = (f32[16,1600]{1,0:T(8,128)S(1)}, f32[16,1600]{1,0:T(8,128)S(1)}, u32[]{:S(2)}, u32[]{:S(2)}) collective-permute-start(f32[16,1600]{1,0:T(8,128)S(1)} %sums_added.4.a_ref), channel_id=1, source_target_pairs={{0,8},{4,12},{8,0},{12,4},{16,24},{20,28},{24,16},{28,20},{1,9},{5... | collective-permute-start | bytes 307208 | tf_op jit(solution)/shard_map/ppermute | solution.py:461
  576.3 14.0 %collective-permute-start.49 = (f32[8,768]{1,0:T(8,128)S(1)}, f32[8,768]{1,0:T(8,128)S(1)}, u32[]{:S(2)}, u32[]{:S(2)}) collective-permute-start(f32[8,768]{1,0:T(8,128)S(1)} %get-tuple-element.220.a_ref), channel_id=1, source_target_pairs={{0,2},{2,0},{1,3},{3,1},{4,6},{6,4},{5,7},{7,5},{8,10},{10,8},{9,1... | collective-permute-start | bytes 73736 | tf_op jit(solution)/shard_map/ppermute | solution.py:453
  583.0 25.0 %collective-permute-start.51 = (bf16[200,896]{1,0:T(8,128)(2,1)S(1)}, bf16[200,896]{1,0:T(8,128)(2,1)S(1)}, u32[]{:S(2)}, u32[]{:S(2)}) collective-permute-start(bf16[200,896]{1,0:T(8,128)(2,1)S(1)} %chosen.7.a_ref), channel_id=1, source_target_pairs={{0,16},{4,20},{8,24},{12,28},{16,0},{20,4},{24,8},{28,12},{1,17},{... | collective-permute-start | bytes 1075208 | tf_op jit(solution)/shard_map/ppermute | solution.py:461
  584.9 81.3 %collective-permute-start.58 = (bf16[2,200,1600]{2,1,0:T(8,128)(2,1)S(1)}, bf16[2,200,1600]{2,1,0:T(8,128)(2,1)}, u32[]{:S(2)}, u32[]{:S(2)}) collective-permute-start(bf16[2,200,1600]{2,1,0:T(8,128)(2,1)S(1)} %paired.10.a_ref), channel_id=1, source_target_pairs={{0,4},{4,0},{8,12},{12,8},{16,20},{20,16},{24,28},{28,24},{1,5},{5... | collective-permute-start | bytes 3840008 | tf_op jit(solution)/shard_map/ppermute | solution.py:461
  602.9 68.1 %collective-permute-start.59 = (bf16[2,200,1600]{2,1,0:T(8,128)(2,1)S(1)}, bf16[2,200,1600]{2,1,0:T(8,128)(2,1)S(1)}, u32[]{:S(2)}, u32[]{:S(2)}) collective-permute-start(bf16[2,200,1600]{2,1,0:T(8,128)(2,1)S(1)} %paired.11.a_ref), channel_id=1, source_target_pairs={{0,8},{4,12},{8,0},{12,4},{16,24},{20,28},{24,16},{28,20},{1,9},{5... | collective-permute-start | bytes 3840008 | tf_op jit(solution)/shard_map/ppermute | solution.py:461
  603.0 34.9 %collective-permute-start.52 = (bf16[200,896]{1,0:T(8,128)(2,1)S(1)}, bf16[200,896]{1,0:T(8,128)(2,1)S(1)}, u32[]{:S(2)}, u32[]{:S(2)}) collective-permute-start(bf16[200,896]{1,0:T(8,128)(2,1)S(1)} %chosen.6.a_ref), channel_id=1, source_target_pairs={{0,16},{4,20},{8,24},{12,28},{16,0},{20,4},{24,8},{28,12},{1,17},{... | collective-permute-start | bytes 1075208 | tf_op jit(solution)/shard_map/ppermute | solution.py:461
  608.7 34.7 %collective-permute-start.53 = (bf16[2,200,896]{2,1,0:T(8,128)(2,1)S(1)}, bf16[2,200,896]{2,1,0:T(8,128)(2,1)S(1)}, u32[]{:S(2)}, u32[]{:S(2)}) collective-permute-start(bf16[2,200,896]{2,1,0:T(8,128)(2,1)S(1)} %paired.12.a_ref), channel_id=1, source_target_pairs={{0,4},{4,0},{8,12},{12,8},{16,20},{20,16},{24,28},{28,24},{1,5},{5... | collective-permute-start | bytes 2150408 | tf_op jit(solution)/shard_map/ppermute | solution.py:461
  638.5 23.5 %collective-permute-start.55 = (bf16[2,200,896]{2,1,0:T(8,128)(2,1)S(1)}, bf16[2,200,896]{2,1,0:T(8,128)(2,1)S(1)}, u32[]{:S(2)}, u32[]{:S(2)}) collective-permute-start(bf16[2,200,896]{2,1,0:T(8,128)(2,1)S(1)} %paired.13.a_ref), channel_id=1, source_target_pairs={{0,8},{4,12},{8,0},{12,4},{16,24},{20,28},{24,16},{28,20},{1,9},{5... | collective-permute-start | bytes 2150408 | tf_op jit(solution)/shard_map/ppermute | solution.py:461
  642.8 4.7 collective-permute-start.54
  648.1 15.4 %collective-permute-start.56 = (f32[16,1600]{1,0:T(8,128)S(1)}, f32[16,1600]{1,0:T(8,128)S(1)}, u32[]{:S(2)}, u32[]{:S(2)}) collective-permute-start(f32[16,1600]{1,0:T(8,128)S(1)} %sums_added.6.a_ref), channel_id=1, source_target_pairs={{0,16},{4,20},{8,24},{12,28},{16,0},{20,4},{24,8},{28,12},{1,17},{... | collective-permute-start | bytes 307208 | tf_op jit(solution)/shard_map/ppermute | solution.py:461
  648.2 44.6 %collective-permute-start.60 = (bf16[2,2,200,896]{3,2,1,0:T(8,128)(2,1)S(1)}, bf16[2,2,200,896]{3,2,1,0:T(8,128)(2,1)S(1)}, u32[]{:S(2)}, u32[]{:S(2)}) collective-permute-start(bf16[2,2,200,896]{3,2,1,0:T(8,128)(2,1)S(1)} %paired.14.a_ref.c_ref), channel_id=1, source_target_pairs={{0,8},{4,12},{8,0},{12,4},{16,24},{20,28},{24,16},{28,20},{1,9},{5... | collective-permute-start | bytes 4300808 | tf_op jit(solution)/shard_map/ppermute | solution.py:461
  662.8 34.4 %collective-permute-start.61 = (bf16[2,2,200,896]{3,2,1,0:T(8,128)(2,1)S(1)}, bf16[2,2,200,896]{3,2,1,0:T(8,128)(2,1)S(1)}, u32[]{:S(2)}, u32[]{:S(2)}) collective-permute-start(bf16[2,2,200,896]{3,2,1,0:T(8,128)(2,1)S(1)} %paired.15.a_ref.c_ref), channel_id=1, source_target_pairs={{0,4},{4,0},{8,12},{12,8},{16,20},{20,16},{24,28},{28,24},{1,5},{5... | collective-permute-start | bytes 4300808 | tf_op jit(solution)/shard_map/ppermute | solution.py:461
  664.0 7.0 collective-permute-start.57
  671.0 77.6 %collective-permute-start.66 = (bf16[2,2,200,1600]{3,2,1,0:T(8,128)(2,1)}, bf16[2,2,200,1600]{3,2,1,0:T(8,128)(2,1)}, u32[]{:S(2)}, u32[]{:S(2)}) collective-permute-start(bf16[2,2,200,1600]{3,2,1,0:T(8,128)(2,1)} %paired.16.a_ref.c_ref), channel_id=1, source_target_pairs={{0,8},{4,12},{8,0},{12,4},{16,24},{20,28},{24,16},{28,20},{1,9},{5... | collective-permute-start | bytes 7680008 | tf_op jit(solution)/shard_map/ppermute | solution.py:461
  673.6 83.8 %collective-permute-start.67 = (bf16[2,2,200,1600]{3,2,1,0:T(8,128)(2,1)}, bf16[2,2,200,1600]{3,2,1,0:T(8,128)(2,1)}, u32[]{:S(2)}, u32[]{:S(2)}) collective-permute-start(bf16[2,2,200,1600]{3,2,1,0:T(8,128)(2,1)} %paired.17.a_ref.c_ref), channel_id=1, source_target_pairs={{0,4},{4,0},{8,12},{12,8},{16,20},{20,16},{24,28},{28,24},{1,5},{5... | collective-permute-start | bytes 7680008 | tf_op jit(solution)/shard_map/ppermute | solution.py:461
  700.6 25.3 %collective-permute-start.64 = (bf16[800,768]{1,0:T(8,128)(2,1)}, bf16[800,768]{1,0:T(8,128)(2,1)}, u32[]{:S(2)}, u32[]{:S(2)}) collective-permute-start(bf16[800,768]{1,0:T(8,128)(2,1)} %half_rows.3), channel_id=1, source_target_pairs={{0,2},{2,0},{1,3},{3,1},{4,6},{6,4},{5,7},{7,5},{8,10},{10,8},{9,1... | collective-permute-start | bytes 3686408 | tf_op jit(solution)/shard_map/ppermute | solution.py:453
  (91 other events, 923.3 us)
